TPU v7x, 32 devices: a whole 2x2x4 slice. The times are simulated.
32 devices in a mesh: dp: 8 (over y, x, core), tensor: 4 (over z).
Axes of the slice: x: 2, y: 2, z: 4, core: 2. Of those that a mesh axis runs over, the one named last changes fastest.
Arguments:
- tokens: bfloat16 [8, 1024, 2048], P('dp', 'tensor'), may hold values from -6 to 6
- seq_lengths: int32 [8, 4], P('dp'), may hold values from 0 to 1024, as said below
- attention_gain: bfloat16 [2048], P('dp'), may hold values from 0.5 to 1.5
- query_matrix: bfloat16 [2048, 2048], P('dp', 'tensor'), may hold values from -0.125 to 0.125
- key_matrix: bfloat16 [2048, 512], P('dp', 'tensor'), may hold values from -0.125 to 0.125
- value_matrix: bfloat16 [2048, 512], P('dp', 'tensor'), may hold values from -0.125 to 0.125
- output_weight: bfloat16 [2048, 2048], P('tensor', 'dp'), may hold values from -0.5 to 0.5
- feedforward_gain: bfloat16 [2048], P('dp'), may hold values from 0.5 to 1.5
- gate_weight: bfloat16 [2048, 8192], P('dp', 'tensor'), may hold values from -0.125 to 0.125
- up_weight: bfloat16 [2048, 8192], P('dp', 'tensor'), may hold values from -0.125 to 0.125
- down_weight: bfloat16 [8192, 2048], P('tensor', 'dp'), may hold values from -0.0625 to 0.0625
- cotangent: bfloat16 [8, 1024, 2048], P('dp', 'tensor'), may hold values from -6 to 6
Outputs:
- block_output: bfloat16 [8, 1024, 2048], P('dp', 'tensor')
- input_gradient: float32 [8, 1024, 2048], P('dp', 'tensor')
- attention_gain_gradient: float32 [2048], P('dp')
- query_weight_gradient: float32 [2048, 2048], P('dp', 'tensor')
- key_weight_gradient: float32 [2048, 512], P('dp', 'tensor')
- value_weight_gradient: float32 [2048, 512], P('dp', 'tensor')
- output_weight_gradient: float32 [2048, 2048], P('tensor', 'dp')
- feedforward_gain_gradient: float32 [2048], P('dp')
- gate_weight_gradient: float32 [2048, 8192], P('dp', 'tensor')
- up_weight_gradient: float32 [2048, 8192], P('dp', 'tensor')
- down_weight_gradient: float32 [8192, 2048], P('tensor', 'dp')
Inputs may be any that keep to these rules, and one draw needn't show every extreme that they name: `seq_lengths`: each row lists the lengths of 4 documents packed from the start of one slot of 1024 positions; a length may be 0 and a row sums to at most 1024. Row g belongs to data group g (one slot per group); in every group one slot's first document is longer than 896, and some slot's first document has exactly 1024 tokens.
All inputs are finite; a program needn't handle non-finite values.
Results may differ from a plain program's by a relative error of at most 0.023.
Values may be sent and summed in bfloat16 or wider, within the bound.
No kernel may reach another device: no remote copies, remote signals or barrier semaphores. Data moves between devices by JAX's collectives and lax.ppermute only.
A program may use at most 256 MiB of HBM per device.

v0:
```python
import jax
import jax.numpy as jnp
from jax import lax
from jax.sharding import PartitionSpec as P

QUERY_HEADS = 32
KEY_VALUE_HEADS = 8
HEAD_SIZE = 64
PIECES = 4


EPSILON = 1e-05
ROPE_BASE = 500000.0
NEGATIVE = -1e30


def layout(lengths, complete_rows):
    doc_ends = jnp.cumsum(lengths, axis=-1)
    row_index = jnp.arange(complete_rows, dtype=jnp.int32)
    piece_count = lengths.shape[-1]
    doc_ids = jnp.sum((row_index[None, :, None] >= doc_ends[:, None, :]).astype(jnp.int32), axis=2)
    starts = doc_ends - lengths
    chosen = doc_ids[:, :, None] == jnp.arange(piece_count, dtype=jnp.int32)[None, None, :]
    doc_begin = jnp.sum(jnp.where(chosen, starts[:, None, :], 0), axis=2) + jnp.where(
        doc_ids == piece_count, doc_ends[:, -1:], 0
    )
    return (doc_ids, row_index[None, :] - doc_begin)


def rope_tables(positions, head_dim):
    half_dim = head_dim // 2
    frequency = ROPE_BASE ** (-(jnp.arange(half_dim, dtype=jnp.float32) * (2.0 / head_dim)))
    angles = positions.astype(jnp.float32)[..., None] * frequency
    return (jnp.cos(angles), jnp.sin(angles))


def rotate(vectors, cosine, sine):
    half_dim = vectors.shape[-1] // 2
    first_half = vectors[..., :half_dim]
    second_half = vectors[..., half_dim:]
    return jnp.concatenate(
        [first_half * cosine - second_half * sine, second_half * cosine + first_half * sine],
        axis=-1,
    )


def unrotate(vectors, cosine, sine):
    half_dim = vectors.shape[-1] // 2
    first_half = vectors[..., :half_dim]
    second_half = vectors[..., half_dim:]
    return jnp.concatenate(
        [first_half * cosine + second_half * sine, second_half * cosine - first_half * sine],
        axis=-1,
    )


def norm_rows(values):
    inverse = lax.rsqrt(jnp.mean(values * values, axis=-1, keepdims=True) + EPSILON)
    return (values * inverse, inverse)


def norm_back(grad_normed, scaled, inverse, scale_row):
    grad_scaled = grad_normed * scale_row
    projection = jnp.mean(grad_scaled * scaled, axis=-1, keepdims=True)
    return (
        inverse * (grad_scaled - scaled * projection),
        jnp.sum(grad_normed * scaled, axis=(0, 1)),
    )


def contract(left, right, left_dim, right_dim):
    return lax.dot_general(
        left, right, (((left_dim,), (right_dim,)), ((), ())), preferred_element_type=jnp.float32
    )


def masked_scores(query_block, key_rows, doc_ids, first_row, last_row):
    scores = jnp.einsum(
        "qhgd,khd->hgqk", query_block, key_rows[:last_row], preferred_element_type=jnp.float32
    ) * HEAD_SIZE ** (-0.5)
    query_pos = jnp.arange(first_row, last_row, dtype=jnp.int32)
    key_pos = jnp.arange(last_row, dtype=jnp.int32)
    query_doc = doc_ids[first_row:last_row]
    key_doc = doc_ids[:last_row]
    allowed = (query_doc[:, None] == key_doc[None, :]) & (key_pos[None, :] <= query_pos[:, None])
    allowed = allowed & ((query_doc[:, None] < PIECES) | (key_pos[None, :] == query_pos[:, None]))
    return jnp.where(allowed[None, None], scores, NEGATIVE)


def attend_slot(query_rows, key_rows, value_rows, doc_ids, block_rows):
    complete_rows = query_rows.shape[0]
    outputs = []
    totals = []
    for first_row in range(0, complete_rows, block_rows):
        last_row = first_row + block_rows
        scores = masked_scores(
            query_rows[first_row:last_row], key_rows, doc_ids, first_row, last_row
        )
        row_peak = jnp.max(scores, axis=-1, keepdims=True)
        exp_scores = jnp.exp(scores - row_peak)
        row_total = jnp.sum(exp_scores, axis=-1, keepdims=True)
        soft_probs = (exp_scores / row_total).astype(jnp.bfloat16)
        block_out = jnp.einsum(
            "hgqk,khd->qhgd", soft_probs, value_rows[:last_row], preferred_element_type=jnp.float32
        )
        outputs.append(block_out.astype(jnp.bfloat16))
        totals.append((row_peak + jnp.log(row_total))[..., 0])
    return (jnp.concatenate(outputs, axis=0), jnp.concatenate(totals, axis=-1))


def attend_back(query_rows, key_rows, value_rows, doc_ids, totals, grad_rows, block_rows):
    complete_rows = query_rows.shape[0]
    score_scale = HEAD_SIZE ** (-0.5)
    grad_query_list = []
    grad_key = jnp.zeros(key_rows.shape, jnp.float32)
    grad_value = jnp.zeros(value_rows.shape, jnp.float32)
    for first_row in range(0, complete_rows, block_rows):
        last_row = first_row + block_rows
        query_block = query_rows[first_row:last_row]
        grad_block = grad_rows[first_row:last_row]
        scores = masked_scores(query_block, key_rows, doc_ids, first_row, last_row)
        soft_probs = jnp.exp(scores - totals[:, :, first_row:last_row, None])
        grad_probs = jnp.einsum(
            "qhgd,khd->hgqk", grad_block, value_rows[:last_row], preferred_element_type=jnp.float32
        )
        row_inner = jnp.sum(soft_probs * grad_probs, axis=-1, keepdims=True)
        grad_scores = (soft_probs * (grad_probs - row_inner)).astype(jnp.bfloat16)
        grad_query_list.append(
            jnp.einsum(
                "hgqk,khd->qhgd",
                grad_scores,
                key_rows[:last_row],
                preferred_element_type=jnp.float32,
            )
            * score_scale
        )
        key_part = (
            jnp.einsum(
                "hgqk,qhgd->khd", grad_scores, query_block, preferred_element_type=jnp.float32
            )
            * score_scale
        )
        value_part = jnp.einsum(
            "hgqk,qhgd->khd",
            soft_probs.astype(jnp.bfloat16),
            grad_block,
            preferred_element_type=jnp.float32,
        )
        padding = ((0, complete_rows - last_row), (0, 0), (0, 0))
        grad_key = grad_key + jnp.pad(key_part, padding)
        grad_value = grad_value + jnp.pad(value_part, padding)
    return (jnp.concatenate(grad_query_list, axis=0), grad_key, grad_value)


def per_device(
    tokens,
    seq_lengths,
    attention_gain,
    query_matrix,
    key_matrix,
    value_matrix,
    output_weight,
    feedforward_gain,
    gate_weight,
    up_weight,
    down_weight,
    cotangent,
):
    slot_count, local_rows, model_width = tokens.shape
    complete_rows = local_rows * lax.axis_size("tensor")
    block_rows = min(512, complete_rows)
    kv_heads = key_matrix.shape[1] // HEAD_SIZE
    group_width = QUERY_HEADS // KEY_VALUE_HEADS
    doc_ids, positions = layout(seq_lengths, complete_rows)
    cosine_table, sine_table = rope_tables(positions, HEAD_SIZE)
    flat_count = slot_count * complete_rows

    def attention_weights():
        return (
            lax.all_gather(attention_gain, "dp", axis=0, tiled=True),
            lax.all_gather(query_matrix, "dp", axis=0, tiled=True),
            lax.all_gather(key_matrix, "dp", axis=0, tiled=True),
            lax.all_gather(value_matrix, "dp", axis=0, tiled=True),
            lax.all_gather(output_weight, "dp", axis=1, tiled=True),
        )

    def feedforward_weights():
        return (
            lax.all_gather(feedforward_gain, "dp", axis=0, tiled=True),
            lax.all_gather(gate_weight, "dp", axis=0, tiled=True),
            lax.all_gather(up_weight, "dp", axis=0, tiled=True),
            lax.all_gather(down_weight, "dp", axis=1, tiled=True),
        )

    inputs = tokens.astype(jnp.float32)
    gain_one, query_full, key_full, value_full, output_full = attention_weights()
    scaled_one, inverse_one = norm_rows(inputs)
    normed_one = (scaled_one * gain_one.astype(jnp.float32)).astype(jnp.bfloat16)
    whole_one = lax.all_gather(normed_one, "tensor", axis=1, tiled=True)
    flattened_first = whole_one.reshape(flat_count, model_width)
    query_linear = jnp.dot(flattened_first, query_full, preferred_element_type=jnp.float32).reshape(
        slot_count, complete_rows, kv_heads, group_width, HEAD_SIZE
    )
    query_rot = rotate(
        query_linear, cosine_table[:, :, None, None], sine_table[:, :, None, None]
    ).astype(jnp.bfloat16)
    key_linear = jnp.dot(flattened_first, key_full, preferred_element_type=jnp.float32).reshape(
        slot_count, complete_rows, kv_heads, HEAD_SIZE
    )
    key_rot = rotate(key_linear, cosine_table[:, :, None], sine_table[:, :, None]).astype(
        jnp.bfloat16
    )
    value_every_head = (
        jnp.dot(flattened_first, value_full, preferred_element_type=jnp.float32)
        .astype(jnp.bfloat16)
        .reshape(slot_count, complete_rows, kv_heads, HEAD_SIZE)
    )

    def forward_slot(slot_items):
        return attend_slot(slot_items[0], slot_items[1], slot_items[2], slot_items[3], block_rows)

    attended, totals = lax.map(forward_slot, (query_rot, key_rot, value_every_head, doc_ids))
    attended_flat = attended.reshape(flat_count, kv_heads * group_width * HEAD_SIZE)
    branch_one = jnp.dot(attended_flat, output_full, preferred_element_type=jnp.float32).reshape(
        slot_count, complete_rows, model_width
    )
    mixed_one = lax.psum_scatter(
        branch_one.astype(jnp.bfloat16), "tensor", scatter_dimension=1, tiled=True
    ).astype(jnp.float32)
    hidden_res = inputs + mixed_one
    gain_two, gate_full, up_full, down_full = feedforward_weights()
    scaled_two, inverse_two = norm_rows(hidden_res)
    normed_two = (scaled_two * gain_two.astype(jnp.float32)).astype(jnp.bfloat16)
    whole_two = lax.all_gather(normed_two, "tensor", axis=1, tiled=True)
    flat_two = whole_two.reshape(flat_count, model_width)
    gate_lin = jnp.dot(flat_two, gate_full, preferred_element_type=jnp.float32)
    up_lin = jnp.dot(flat_two, up_full, preferred_element_type=jnp.float32)
    sigmoid_gate = jax.nn.sigmoid(gate_lin)
    silu_gate = gate_lin * sigmoid_gate
    product = (silu_gate * up_lin).astype(jnp.bfloat16)
    branch_two = jnp.dot(product, down_full, preferred_element_type=jnp.float32).reshape(
        slot_count, complete_rows, model_width
    )
    mixed_two = lax.psum_scatter(
        branch_two.astype(jnp.bfloat16), "tensor", scatter_dimension=1, tiled=True
    ).astype(jnp.float32)
    block_output = (hidden_res + mixed_two).astype(jnp.bfloat16)
    grad_rows = cotangent.astype(jnp.float32)
    whole_grad = lax.all_gather(cotangent, "tensor", axis=1, tiled=True).reshape(
        flat_count, model_width
    )
    gain_two, gate_full, up_full, down_full = feedforward_weights()
    grad_product = contract(whole_grad, down_full, 1, 1)
    down_grad = contract(product, whole_grad, 0, 0)
    grad_gate = (
        grad_product * up_lin * sigmoid_gate * (1.0 + gate_lin * (1.0 - sigmoid_gate))
    ).astype(jnp.bfloat16)
    grad_up = (grad_product * silu_gate).astype(jnp.bfloat16)
    gate_grad = contract(flat_two, grad_gate, 0, 0)
    up_grad = contract(flat_two, grad_up, 0, 0)
    grad_normed_two = (
        contract(grad_gate, gate_full, 1, 1) + contract(grad_up, up_full, 1, 1)
    ).reshape(slot_count, complete_rows, model_width)
    local_two = lax.psum_scatter(
        grad_normed_two.astype(jnp.bfloat16), "tensor", scatter_dimension=1, tiled=True
    ).astype(jnp.float32)
    back_two, gain_two_part = norm_back(
        local_two, scaled_two, inverse_two, gain_two.astype(jnp.float32)
    )
    grad_hidden = grad_rows + back_two
    summed_two = (
        lax.psum_scatter(
            gain_two_part.astype(jnp.bfloat16), "dp", scatter_dimension=0, tiled=True
        ).astype(jnp.float32),
        lax.psum_scatter(
            gate_grad.astype(jnp.bfloat16), "dp", scatter_dimension=0, tiled=True
        ).astype(jnp.float32),
        lax.psum_scatter(
            up_grad.astype(jnp.bfloat16), "dp", scatter_dimension=0, tiled=True
        ).astype(jnp.float32),
        lax.psum_scatter(
            down_grad.astype(jnp.bfloat16), "dp", scatter_dimension=1, tiled=True
        ).astype(jnp.float32),
    )
    grad_branch = grad_hidden.astype(jnp.bfloat16)
    whole_branch = lax.all_gather(grad_branch, "tensor", axis=1, tiled=True).reshape(
        flat_count, model_width
    )
    gain_one, query_full, key_full, value_full, output_full = attention_weights()
    output_grad = contract(attended_flat, whole_branch, 0, 0)
    grad_attended = (
        contract(whole_branch, output_full, 1, 1)
        .astype(jnp.bfloat16)
        .reshape(slot_count, complete_rows, kv_heads, group_width, HEAD_SIZE)
    )

    def backward_slot(slot_items):
        return attend_back(
            slot_items[0],
            slot_items[1],
            slot_items[2],
            slot_items[3],
            slot_items[4],
            slot_items[5],
            block_rows,
        )

    grad_query_rot, grad_key_rot, grad_value_all = lax.map(
        backward_slot, (query_rot, key_rot, value_every_head, doc_ids, totals, grad_attended)
    )
    grad_query = (
        unrotate(grad_query_rot, cosine_table[:, :, None, None], sine_table[:, :, None, None])
        .astype(jnp.bfloat16)
        .reshape(flat_count, kv_heads * group_width * HEAD_SIZE)
    )
    grad_key = (
        unrotate(grad_key_rot, cosine_table[:, :, None], sine_table[:, :, None])
        .astype(jnp.bfloat16)
        .reshape(flat_count, kv_heads * HEAD_SIZE)
    )
    grad_value = grad_value_all.astype(jnp.bfloat16).reshape(flat_count, kv_heads * HEAD_SIZE)
    query_grad = contract(flattened_first, grad_query, 0, 0)
    key_grad = contract(flattened_first, grad_key, 0, 0)
    value_grad = contract(flattened_first, grad_value, 0, 0)
    grad_normed_one = (
        contract(grad_query, query_full, 1, 1)
        + contract(grad_key, key_full, 1, 1)
        + contract(grad_value, value_full, 1, 1)
    )
    local_one = lax.psum_scatter(
        grad_normed_one.reshape(slot_count, complete_rows, model_width).astype(jnp.bfloat16),
        "tensor",
        scatter_dimension=1,
        tiled=True,
    ).astype(jnp.float32)
    back_one, gain_one_part = norm_back(
        local_one, scaled_one, inverse_one, gain_one.astype(jnp.float32)
    )
    input_gradient = grad_hidden + back_one
    summed_one = (
        lax.psum_scatter(
            gain_one_part.astype(jnp.bfloat16), "dp", scatter_dimension=0, tiled=True
        ).astype(jnp.float32),
        lax.psum_scatter(
            query_grad.astype(jnp.bfloat16), "dp", scatter_dimension=0, tiled=True
        ).astype(jnp.float32),
        lax.psum_scatter(
            key_grad.astype(jnp.bfloat16), "dp", scatter_dimension=0, tiled=True
        ).astype(jnp.float32),
        lax.psum_scatter(
            value_grad.astype(jnp.bfloat16), "dp", scatter_dimension=0, tiled=True
        ).astype(jnp.float32),
        lax.psum_scatter(
            output_grad.astype(jnp.bfloat16), "dp", scatter_dimension=1, tiled=True
        ).astype(jnp.float32),
    )
    gain_totals = lax.psum((summed_one[0], summed_two[0]), "tensor")
    return (
        block_output,
        input_gradient,
        gain_totals[0],
        summed_one[1],
        summed_one[2],
        summed_one[3],
        summed_one[4],
        gain_totals[1],
        summed_two[1],
        summed_two[2],
        summed_two[3],
    )


def solution(mesh):
    return jax.shard_map(
        per_device,
        mesh=mesh,
        in_specs=(
            P("dp", "tensor", None),
            P("dp", None),
            P("dp"),
            P("dp", "tensor"),
            P("dp", "tensor"),
            P("dp", "tensor"),
            P("tensor", "dp"),
            P("dp"),
            P("dp", "tensor"),
            P("dp", "tensor"),
            P("tensor", "dp"),
            P("dp", "tensor", None),
        ),
        out_specs=(
            P("dp", "tensor", None),
            P("dp", "tensor", None),
            P("dp"),
            P("dp", "tensor"),
            P("dp", "tensor"),
            P("dp", "tensor"),
            P("tensor", "dp"),
            P("dp"),
            P("dp", "tensor"),
            P("dp", "tensor"),
            P("tensor", "dp"),
        ),
        check_vma=False,
    )
```

profile of v0, /device:TPU:0, one launch (start us, length us, event | category | flops | bytes accessed | tf_op | source)
XLA Modules:
  0.0 1354.1 jit_solution(10319265628988538467)
XLA Ops:
  51.2 73.0 %all-gather.12.cloned.1.call-done = bf16[1,1024,2048]{2,1,0:T(8,128)(2,1)} async-done(((bf16[1,256,2048]{2,1,0:T(8,128)(2,1)}), bf16[1,1024,2048]{2,1,0:T(8,128)(2,1)}) %all-gather.12.cloned.1.call-update) | async-done | bytes 4194320 | tf_op jit(solution)/shard_map/all_gather | solution.py:199
  182.5 66.1 %reduce-scatter.12.cloned.1.call-done = bf16[1,256,2048]{2,1,0:T(8,128)(2,1)} async-done(((bf16[1,1024,2048]{2,1,0:T(8,128)(2,1)}), bf16[1,256,2048]{2,1,0:T(8,128)(2,1)}) %reduce-scatter.12.cloned.1.call-update) | async-done | bytes 1048592 | tf_op jit(solution)/shard_map/reduce_scatter | solution.py:227
  255.2 50.3 %all-gather.22.cloned.1.call-done = bf16[2048,2048]{1,0:T(8,128)(2,1)} async-done(((bf16[256,2048]{1,0:T(8,128)(2,1)}), bf16[2048,2048]{1,0:T(8,128)(2,1)}) %all-gather.22.cloned.1.call-update) | async-done | bytes 8388624 | tf_op jit(solution)/shard_map/all_gather | solution.py:191
  305.5 82.9 %all-gather.18.cloned.1.call-done = bf16[1,1024,2048]{2,1,0:T(8,128)(2,1)} async-done(((bf16[1,256,2048]{2,1,0:T(8,128)(2,1)}), bf16[1,1024,2048]{2,1,0:T(8,128)(2,1)}) %all-gather.18.cloned.1.call-update) | async-done | bytes 4194320 | tf_op jit(solution)/shard_map/all_gather | solution.py:234
  388.4 14.8 %fusion.29 = f32[1024,2048]{1,0:T(8,128)} fusion(bf16[2048,2048]{1,0:T(8,128)(2,1)} %all-gather.22.cloned.1.call-done, bf16[1,1024,2048]{2,1,0:T(8,128)(2,1)} %all-gather.18.cloned.1.call-done), kind=kOutput, calls=%fused_computation.48 | convolution fusion | flops 8589934592 | bytes 20971520 | tf_op jit(solution)/shard_map/dot_general | solution.py:237
  403.2 40.2 %all-gather.20.cloned.1.call-done = bf16[2048,2048]{1,0:T(8,128)(2,1)} async-done(((bf16[256,2048]{1,0:T(8,128)(2,1)}), bf16[2048,2048]{1,0:T(8,128)(2,1)}) %all-gather.20.cloned.1.call-update) | async-done | bytes 8388624 | tf_op jit(solution)/shard_map/all_gather | solution.py:190
  443.4 14.4 %fusion.31 = f32[1024,2048]{1,0:T(8,128)} fusion(bf16[2048,2048]{1,0:T(8,128)(2,1)} %all-gather.20.cloned.1.call-done, bf16[1,1024,2048]{2,1,0:T(8,128)(2,1)} %all-gather.18.cloned.1.call-done), kind=kOutput, calls=%fused_computation.50 | convolution fusion | flops 8589934592 | bytes 20971520 | tf_op jit(solution)/shard_map/dot_general | solution.py:236
  457.7 68.1 %all-gather.26.cloned.1.call-done = bf16[1,1024,2048]{2,1,0:T(8,128)(2,1)} async-done(((bf16[1,256,2048]{2,1,0:T(8,128)(2,1)}), bf16[1,1024,2048]{2,1,0:T(8,128)(2,1)}) %all-gather.26.cloned.1.call-update) | async-done | bytes 4194320 | tf_op jit(solution)/shard_map/all_gather | solution.py:249
  525.8 56.6 %all-gather.24.cloned.1.call-done = bf16[2048,2048]{1,0:T(8,128)(2,1)} async-done(((bf16[2048,256]{1,0:T(8,128)(2,1)}), bf16[2048,2048]{1,0:T(8,128)(2,1)}) %all-gather.24.cloned.1.call-update) | async-done | bytes 8388624 | tf_op jit(solution)/shard_map/all_gather | solution.py:192
  582.4 21.9 %multiply_convert_fusion = (bf16[1024,2048]{1,0:T(8,128)(2,1)}, bf16[1024,2048]{1,0:T(8,128)(2,1)}, bf16[1024,2048]{1,0:T(8,128)(2,1)}) fusion(f32[1024,2048]{1,0:T(8,128)} %fusion.31, f32[1024,2048]{1,0:T(8,128)} %fusion.29, bf16[2048,2048]{1,0:T(8,128)(2,1)} %all-gather.24.cloned.1.call-done, bf16[1,1024,2048]{2,1,0:T(8,128)(2,1)} %all-gather.26.cloned.1.call-done), kind=kOutput, calls=%fused_computation.22 | convolution fusion | flops 8621391872 | bytes 41943040 | tf_op jit(solution)/shard_map/dot_general | solution.py:72
  630.2 76.9 %reduce-scatter.16.cloned.1.call-done = bf16[1,256,2048]{2,1,0:T(8,128)(2,1)} async-done(((bf16[1,1024,2048]{2,1,0:T(8,128)(2,1)}), bf16[1,256,2048]{2,1,0:T(8,128)(2,1)}) %reduce-scatter.16.cloned.1.call-update) | async-done | bytes 1048592 | tf_op jit(solution)/shard_map/reduce_scatter | solution.py:264
  713.7 14.2 %convolution_convert_fusion.1 = bf16[2048,2048]{1,0:T(8,128)(2,1)} fusion(bf16[1024,2048]{1,0:T(8,128)(2,1)} %get-tuple-element.70, bf16[1,1024,2048]{2,1,0:T(8,128)(2,1)} %all-gather.18.cloned.1.call-done), kind=kOutput, calls=%fused_computation.31 | convolution fusion | flops 8594128896 | bytes 16777216 | tf_op jit(solution)/shard_map/dot_general | solution.py:72
  728.0 14.1 %convolution_convert_fusion.2 = bf16[2048,2048]{1,0:T(8,128)(2,1)} fusion(bf16[1024,2048]{1,0:T(8,128)(2,1)} %get-tuple-element.71, bf16[1,1024,2048]{2,1,0:T(8,128)(2,1)} %all-gather.18.cloned.1.call-done), kind=kOutput, calls=%fused_computation.32 | convolution fusion | flops 8594128896 | bytes 16777216 | tf_op jit(solution)/shard_map/dot_general | solution.py:72
  742.2 14.5 %convolution_convert_fusion = bf16[2048,2048]{1,0:T(8,128)(2,1)} fusion(bf16[1024,2048]{1,0:T(8,128)(2,1)} %get-tuple-element.72, bf16[1,1024,2048]{2,1,0:T(8,128)(2,1)} %all-gather.26.cloned.1.call-done), kind=kOutput, calls=%fused_computation.30 | convolution fusion | flops 8594128896 | bytes 16777216 | tf_op jit(solution)/shard_map/dot_general | solution.py:72
  757.4 37.6 %all-gather.28.cloned.1.call-done = bf16[1,1024,2048]{2,1,0:T(8,128)(2,1)} async-done(((bf16[1,256,2048]{2,1,0:T(8,128)(2,1)}), bf16[1,1024,2048]{2,1,0:T(8,128)(2,1)}) %all-gather.28.cloned.1.call-update) | async-done | bytes 4194320 | tf_op jit(solution)/shard_map/all_gather | solution.py:286
  909.1 34.2 %reduce-scatter.28.cloned.1.call-done = bf16[256,2048]{1,0:T(8,128)(2,1)} async-done(((bf16[2048,2048]{1,0:T(8,128)(2,1)}), bf16[256,2048]{1,0:T(8,128)(2,1)}) %reduce-scatter.28.cloned.1.call-update) | async-done | bytes 1048592 | tf_op jit(solution)/shard_map/reduce_scatter | solution.py:275
  946.2 71.8 %reduce-scatter.32.cloned.1.call-done = bf16[2048,256]{1,0:T(8,128)(2,1)} async-done(((bf16[2048,2048]{1,0:T(8,128)(2,1)}), bf16[2048,256]{1,0:T(8,128)(2,1)}) %reduce-scatter.32.cloned.1.call-update) | async-done | bytes 1048592 | tf_op jit(solution)/shard_map/reduce_scatter | solution.py:281
  1020.7 34.7 %reduce-scatter.24.cloned.1.call-done = bf16[256,128]{1,0:T(8,128)(2,1)} async-done(((bf16[2048,128]{1,0:T(8,128)(2,1)}), bf16[256,128]{1,0:T(8,128)(2,1)}) %reduce-scatter.24.cloned.1.call-update) | async-done | bytes 65552 | tf_op jit(solution)/shard_map/reduce_scatter | solution.py:350
  1056.9 36.1 %reduce-scatter.22.cloned.1.call-done = bf16[256,128]{1,0:T(8,128)(2,1)} async-done(((bf16[2048,128]{1,0:T(8,128)(2,1)}), bf16[256,128]{1,0:T(8,128)(2,1)}) %reduce-scatter.22.cloned.1.call-update) | async-done | bytes 65552 | tf_op jit(solution)/shard_map/reduce_scatter | solution.py:347
  1094.5 43.2 %reduce-scatter.26.cloned.1.call-done = bf16[512,256]{1,0:T(8,128)(2,1)} async-done(((bf16[512,2048]{1,0:T(8,128)(2,1)}), bf16[512,256]{1,0:T(8,128)(2,1)}) %reduce-scatter.26.cloned.1.call-update) | async-done | bytes 262160 | tf_op jit(solution)/shard_map/reduce_scatter | solution.py:353
  1139.5 43.2 %reduce-scatter.20.cloned.1.call-done = bf16[256,512]{1,0:T(8,128)(2,1)} async-done(((bf16[2048,512]{1,0:T(8,128)(2,1)}), bf16[256,512]{1,0:T(8,128)(2,1)}) %reduce-scatter.20.cloned.1.call-update) | async-done | bytes 262160 | tf_op jit(solution)/shard_map/reduce_scatter | solution.py:344
  1184.5 77.4 %reduce-scatter.18.cloned.1.call-done = bf16[1,256,2048]{2,1,0:T(8,128)(2,1)} async-done(((bf16[1,1024,2048]{2,1,0:T(8,128)(2,1)}), bf16[1,256,2048]{2,1,0:T(8,128)(2,1)}) %reduce-scatter.18.cloned.1.call-update) | async-done | bytes 1048592 | tf_op jit(solution)/shard_map/reduce_scatter | solution.py:330
  1264.0 14.0 %all-reduce.5 = (bf16[2048]{0:T(1024)(128)(2,1)S(1)}, bf16[2048]{0:T(1024)(128)(2,1)S(1)}) all-reduce(bf16[2048]{0:T(1024)(128)(2,1)S(1)} %get-tuple-element.54, bf16[2048]{0:T(1024)(128)(2,1)S(1)} %copy-done.56), channel_id=6, replica_groups=mesh['dp'=8,'tensor'=4] {'dp'}, use_global_device_ids=true, to_apply=%region_18.19.clone | all-reduce | flops 4096 | bytes 16384
  1290.0 51.7 %reduce-scatter.14.cloned.1.call-done = bf16[1,256,2048]{2,1,0:T(8,128)(2,1)} async-done(((bf16[1,1024,2048]{2,1,0:T(8,128)(2,1)}), bf16[1,256,2048]{2,1,0:T(8,128)(2,1)}) %reduce-scatter.14.cloned.1.call-update) | async-done | bytes 1048592 | tf_op jit(solution)/shard_map/reduce_scatter | solution.py:244
  (281 shorter events, 285.8 us)
Async XLA Ops:
  7.2 40.0 %all-gather.14.cloned.1.call-start = ((), (), s32[]{:S(2)}) async-start(), calls=%async_computation.12 | async-start | bytes 2359296 | tf_op jit(solution)/shard_map/all_gather | solution.py:181
  7.9 116.2 %all-gather.12.cloned.1.call-start = ((), (), s32[]{:S(2)}) async-start(), calls=%async_computation.11 | async-start | bytes 5242880 | tf_op jit(solution)/shard_map/all_gather | solution.py:199
  23.1 142.9 %all-gather.16.cloned.1.call-start = ((), (), s32[]{:S(2)}) async-start(), calls=%async_computation.13 | async-start | bytes 2359296 | tf_op jit(solution)/shard_map/all_gather | solution.py:184
  23.9 224.8 %reduce-scatter.12.cloned.1.call-start = ((), (), s32[]{:S(2)}) async-start(), calls=%async_computation.14 | async-start | bytes 5242880 | tf_op jit(solution)/shard_map/reduce_scatter | solution.py:227
  173.0 132.5 %all-gather.22.cloned.1.call-start = ((), (), s32[]{:S(2)}) async-start(), calls=%async_computation.17 | async-start | bytes 9437184 | tf_op jit(solution)/shard_map/all_gather | solution.py:191
  173.6 214.7 %all-gather.18.cloned.1.call-start = ((), (), s32[]{:S(2)}) async-start(), calls=%async_computation.15 | async-start | bytes 5242880 | tf_op jit(solution)/shard_map/all_gather | solution.py:234
  182.5 527.3 %copy-start.38 = (f32[8,1,256]{2,1,0:T(1,128)}, f32[8,1,256]{2,1,0:T(1,128)S(1)}, u32[]{:S(2)}) copy-start(f32[8,1,256]{2,1,0:T(1,128)S(1)} %convert_element_type.321) | copy-start | bytes 24580
  250.3 459.5 %copy-start.52 = (f32[256]{0:T(256)}, f32[256]{0:T(256)S(1)}, u32[]{:S(2)}) copy-start(f32[256]{0:T(256)S(1)} %add_rsqrt_fusion) | copy-start | bytes 3076
  252.9 190.4 %all-gather.20.cloned.1.call-start = ((), (), s32[]{:S(2)}) async-start(), calls=%async_computation.16 | async-start | bytes 9437184 | tf_op jit(solution)/shard_map/all_gather | solution.py:190
  253.7 272.1 %all-gather.26.cloned.1.call-start = ((), (), s32[]{:S(2)}) async-start(), calls=%async_computation.20 | async-start | bytes 5242880 | tf_op jit(solution)/shard_map/all_gather | solution.py:249
  254.4 327.9 %all-gather.24.cloned.1.call-start = ((), (), s32[]{:S(2)}) async-start(), calls=%async_computation.18 | async-start | bytes 9437184 | tf_op jit(solution)/shard_map/all_gather | solution.py:192
  255.2 451.9 %reduce-scatter.16.cloned.1.call-start = ((), (), s32[]{:S(2)}) async-start(), calls=%async_computation.21 | async-start | bytes 5242880 | tf_op jit(solution)/shard_map/reduce_scatter | solution.py:264
  630.1 164.9 %all-gather.28.cloned.1.call-start = ((), (), s32[]{:S(2)}) async-start(), calls=%async_computation.22 | async-start | bytes 5242880 | tf_op jit(solution)/shard_map/all_gather | solution.py:286
  713.7 192.5 %reduce-scatter.30.cloned.1.call-start = ((), (), s32[]{:S(2)}) async-start(), calls=%async_computation.29 | async-start | bytes 9437184 | tf_op jit(solution)/shard_map/reduce_scatter | solution.py:278
  728.0 215.4 %reduce-scatter.28.cloned.1.call-start = ((), (), s32[]{:S(2)}) async-start(), calls=%async_computation.28 | async-start | bytes 9437184 | tf_op jit(solution)/shard_map/reduce_scatter | solution.py:275
  742.1 275.9 %reduce-scatter.32.cloned.1.call-start = ((), (), s32[]{:S(2)}) async-start(), calls=%async_computation.30 | async-start | bytes 9437184 | tf_op jit(solution)/shard_map/reduce_scatter | solution.py:281
  756.7 298.7 %reduce-scatter.24.cloned.1.call-start = ((), (), s32[]{:S(2)}) async-start(), calls=%async_computation.26 | async-start | bytes 589824 | tf_op jit(solution)/shard_map/reduce_scatter | solution.py:350
  841.3 251.8 %reduce-scatter.22.cloned.1.call-start = ((), (), s32[]{:S(2)}) async-start(), calls=%async_computation.25 | async-start | bytes 589824 | tf_op jit(solution)/shard_map/reduce_scatter | solution.py:347
  860.8 277.0 %reduce-scatter.26.cloned.1.call-start = ((), (), s32[]{:S(2)}) async-start(), calls=%async_computation.27 | async-start | bytes 2359296 | tf_op jit(solution)/shard_map/reduce_scatter | solution.py:353
  867.1 315.7 %reduce-scatter.20.cloned.1.call-start = ((), (), s32[]{:S(2)}) async-start(), calls=%async_computation.24 | async-start | bytes 2359296 | tf_op jit(solution)/shard_map/reduce_scatter | solution.py:344
  882.0 379.9 %reduce-scatter.18.cloned.1.call-start = ((), (), s32[]{:S(2)}) async-start(), calls=%async_computation.23 | async-start | bytes 5242880 | tf_op jit(solution)/shard_map/reduce_scatter | solution.py:330
  890.1 451.5 %reduce-scatter.14.cloned.1.call-start = ((), (), s32[]{:S(2)}) async-start(), calls=%async_computation.19 | async-start | bytes 5242880 | tf_op jit(solution)/shard_map/reduce_scatter | solution.py:244
  946.2 395.5 %copy-start.8 = (bf16[1,256,2048]{2,1,0:T(8,128)(2,1)S(1)}, bf16[1,256,2048]{2,1,0:T(8,128)(2,1)}, u32[]{:S(2)}) copy-start(bf16[1,256,2048]{2,1,0:T(8,128)(2,1)} %param.23) | copy-start | bytes 3145732
  946.2 395.5 %copy-start.39 = (f32[8,1,256]{2,1,0:T(1,128)S(1)}, f32[8,1,256]{2,1,0:T(1,128)}, u32[]{:S(2)}) copy-start(f32[8,1,256]{2,1,0:T(1,128)} %copy-done.38) | copy-start | bytes 24580
  (69 other events, 3568.4 us)
Sparse Core Ops, SparseCore 0:
  9.9 31.2 all-gather.13
  43.4 80.7 all-gather.11
  126.1 26.7 all-gather.15
  173.1 75.4 reduce-scatter.11
  250.6 54.8 all-gather.21
  307.6 80.7 all-gather.17
  390.4 52.9 all-gather.19
  445.0 80.7 all-gather.25
  527.8 54.4 all-gather.23
  630.3 76.7 reduce-scatter.15
  713.8 81.2 all-gather.27
  798.4 69.7 reduce-scatter.29
  872.1 71.2 reduce-scatter.27
  946.7 71.2 reduce-scatter.31
  1021.2 34.1 reduce-scatter.23
  1058.9 34.0 reduce-scatter.21
  1096.5 41.2 reduce-scatter.25
  1141.5 41.1 reduce-scatter.19
  1185.1 76.7 reduce-scatter.17
  1264.0 77.5 reduce-scatter.13
where the time goes:
time: 1360 us; the launch traced here: 1350 us
  waiting for transfers between devices  948 us (70%)
  matrix products  234 us (17%)
  other arithmetic  67.1 us (5%)
  blocking collectives  64.9 us (5%)
  local copies, waits for them, and re-layouts  22.5 us (2%)
  between operations  16.4 us (1%)
    dot_general x14, matrix products, contract(): lax.dot_general(left, right, (((left_dim,), (right_dim,)), ((), ())), pre...  119 us
    all_gather x1, waiting for transfers between devices, per_device(): whole_two = lax.all_gather(normed_two, 'tensor', axis=1, tiled=True)  82.9 us
    reduce_scatter x1, waiting for transfers between devices, per_device(): lax.psum_scatter(grad_normed_one.reshape(slot_count, complete_rows, model...  77.4 us
    reduce_scatter x1, waiting for transfers between devices, per_device(): lax.psum_scatter(grad_normed_two.astype(jnp.bfloat16), 'tensor', scatter_...  76.9 us
    all_gather x1, waiting for transfers between devices, per_device(): whole_one = lax.all_gather(normed_one, 'tensor', axis=1, tiled=True)  73 us
    reduce_scatter x1, waiting for transfers between devices, per_device(): lax.psum_scatter(down_grad.astype(jnp.bfloat16), 'dp', scatter_dimension=...  71.8 us
    all_gather x1, waiting for transfers between devices, per_device(): lax.all_gather(cotangent, 'tensor', axis=1, tiled=True)  68.1 us
    reduce_scatter x1, waiting for transfers between devices, per_device(): lax.psum_scatter(branch_one.astype(jnp.bfloat16), 'tensor', scatter_dimen...  66.1 us
  transfers between devices with their start and end apart: 20, of which 17 were waited for; matrix products, arithmetic and copies ran while one was open for 18% of the time, Pallas kernels for 0%

commit v1 on v0

v1 whole, which is shorter than its diff:
```python
import jax
import jax.numpy as jnp
from jax import lax
from jax.sharding import PartitionSpec as P

QUERY_HEADS = 32
KEY_VALUE_HEADS = 8
HEAD_SIZE = 64
PIECES = 4


EPSILON = 1e-05
ROPE_BASE = 500000.0
NEGATIVE = -1e30


def layout(lengths, complete_rows):
    doc_ends = jnp.cumsum(lengths, axis=-1)
    row_index = jnp.arange(complete_rows, dtype=jnp.int32)
    piece_count = lengths.shape[-1]
    doc_ids = jnp.sum((row_index[None, :, None] >= doc_ends[:, None, :]).astype(jnp.int32), axis=2)
    starts = doc_ends - lengths
    chosen = doc_ids[:, :, None] == jnp.arange(piece_count, dtype=jnp.int32)[None, None, :]
    doc_begin = jnp.sum(jnp.where(chosen, starts[:, None, :], 0), axis=2) + jnp.where(
        doc_ids == piece_count, doc_ends[:, -1:], 0
    )
    return (doc_ids, row_index[None, :] - doc_begin)


def rope_tables(positions, head_dim):
    half_dim = head_dim // 2
    frequency = ROPE_BASE ** (-(jnp.arange(half_dim, dtype=jnp.float32) * (2.0 / head_dim)))
    angles = positions.astype(jnp.float32)[..., None] * frequency
    return (jnp.cos(angles), jnp.sin(angles))


def rotate(vectors, cosine, sine):
    half_dim = vectors.shape[-1] // 2
    first_half = vectors[..., :half_dim]
    second_half = vectors[..., half_dim:]
    return jnp.concatenate(
        [first_half * cosine - second_half * sine, second_half * cosine + first_half * sine],
        axis=-1,
    )


def unrotate(vectors, cosine, sine):
    half_dim = vectors.shape[-1] // 2
    first_half = vectors[..., :half_dim]
    second_half = vectors[..., half_dim:]
    return jnp.concatenate(
        [first_half * cosine + second_half * sine, second_half * cosine - first_half * sine],
        axis=-1,
    )


def norm_rows(values):
    inverse = lax.rsqrt(jnp.mean(values * values, axis=-1, keepdims=True) + EPSILON)
    return (values * inverse, inverse)


def norm_back(grad_normed, scaled, inverse, scale_row):
    grad_scaled = grad_normed * scale_row
    projection = jnp.mean(grad_scaled * scaled, axis=-1, keepdims=True)
    return (
        inverse * (grad_scaled - scaled * projection),
        jnp.sum(grad_normed * scaled, axis=(0, 1)),
    )


def contract(left, right, left_dim, right_dim):
    return lax.dot_general(
        left, right, (((left_dim,), (right_dim,)), ((), ())), preferred_element_type=jnp.float32
    )


def masked_scores(query_block, key_rows, doc_ids, first_row, last_row):
    scores = jnp.einsum(
        "qhgd,khd->hgqk", query_block, key_rows[:last_row], preferred_element_type=jnp.float32
    ) * HEAD_SIZE ** (-0.5)
    query_pos = jnp.arange(first_row, last_row, dtype=jnp.int32)
    key_pos = jnp.arange(last_row, dtype=jnp.int32)
    query_doc = doc_ids[first_row:last_row]
    key_doc = doc_ids[:last_row]
    allowed = (query_doc[:, None] == key_doc[None, :]) & (key_pos[None, :] <= query_pos[:, None])
    allowed = allowed & ((query_doc[:, None] < PIECES) | (key_pos[None, :] == query_pos[:, None]))
    return jnp.where(allowed[None, None], scores, NEGATIVE)


def attend_slot(query_rows, key_rows, value_rows, doc_ids, block_rows):
    complete_rows = query_rows.shape[0]
    outputs = []
    totals = []
    for first_row in range(0, complete_rows, block_rows):
        last_row = first_row + block_rows
        scores = masked_scores(
            query_rows[first_row:last_row], key_rows, doc_ids, first_row, last_row
        )
        row_peak = jnp.max(scores, axis=-1, keepdims=True)
        exp_scores = jnp.exp(scores - row_peak)
        row_total = jnp.sum(exp_scores, axis=-1, keepdims=True)
        soft_probs = (exp_scores / row_total).astype(jnp.bfloat16)
        block_out = jnp.einsum(
            "hgqk,khd->qhgd", soft_probs, value_rows[:last_row], preferred_element_type=jnp.float32
        )
        outputs.append(block_out.astype(jnp.bfloat16))
        totals.append((row_peak + jnp.log(row_total))[..., 0])
    return (jnp.concatenate(outputs, axis=0), jnp.concatenate(totals, axis=-1))


def attend_back(query_rows, key_rows, value_rows, doc_ids, totals, grad_rows, block_rows):
    complete_rows = query_rows.shape[0]
    score_scale = HEAD_SIZE ** (-0.5)
    grad_query_list = []
    grad_key = jnp.zeros(key_rows.shape, jnp.float32)
    grad_value = jnp.zeros(value_rows.shape, jnp.float32)
    for first_row in range(0, complete_rows, block_rows):
        last_row = first_row + block_rows
        query_block = query_rows[first_row:last_row]
        grad_block = grad_rows[first_row:last_row]
        scores = masked_scores(query_block, key_rows, doc_ids, first_row, last_row)
        soft_probs = jnp.exp(scores - totals[:, :, first_row:last_row, None])
        grad_probs = jnp.einsum(
            "qhgd,khd->hgqk", grad_block, value_rows[:last_row], preferred_element_type=jnp.float32
        )
        row_inner = jnp.sum(soft_probs * grad_probs, axis=-1, keepdims=True)
        grad_scores = (soft_probs * (grad_probs - row_inner)).astype(jnp.bfloat16)
        grad_query_list.append(
            jnp.einsum(
                "hgqk,khd->qhgd",
                grad_scores,
                key_rows[:last_row],
                preferred_element_type=jnp.float32,
            )
            * score_scale
        )
        key_part = (
            jnp.einsum(
                "hgqk,qhgd->khd", grad_scores, query_block, preferred_element_type=jnp.float32
            )
            * score_scale
        )
        value_part = jnp.einsum(
            "hgqk,qhgd->khd",
            soft_probs.astype(jnp.bfloat16),
            grad_block,
            preferred_element_type=jnp.float32,
        )
        padding = ((0, complete_rows - last_row), (0, 0), (0, 0))
        grad_key = grad_key + jnp.pad(key_part, padding)
        grad_value = grad_value + jnp.pad(value_part, padding)
    return (jnp.concatenate(grad_query_list, axis=0), grad_key, grad_value)


def swap_columns(values, place, count):
    width = values.shape[-1] // count
    blocks = [values[:, j * width : (j + 1) * width] for j in range(count)]
    step = 1
    while step < count:
        bit = (place & step) != 0
        blocks = [jnp.where(bit, blocks[j ^ step], blocks[j]) for j in range(count)]
        step *= 2
    return jnp.concatenate(blocks, axis=-1)


def partner(value, step):
    count = lax.axis_size("dp")
    return lax.ppermute(value, "dp", [(i, i ^ step) for i in range(count)])


def dp_steps(turn):
    count = lax.axis_size("dp")
    steps = []
    step = 2
    while step < count:
        steps.append(step)
        step *= 2
    turn = turn % max(1, len(steps))
    return steps[turn:] + steps[:turn]


def gather_dp(piece, turn):
    held = {0: piece}
    for step in dp_steps(turn) + [1]:
        held.update({j ^ step: partner(value, step) for j, value in held.items()})
    return [held[j] for j in range(len(held))]


def reduce_dp(parts, turn):
    held = dict(enumerate(parts))
    for step in [1] + dp_steps(turn)[::-1]:
        kept = {}
        for j in held:
            if not j & step:
                moved = partner(held[j ^ step].astype(jnp.bfloat16), step)
                kept[j] = held[j].astype(jnp.float32) + moved.astype(jnp.float32)
        held = kept
    return held[0]


def gather_ring(block, shift):
    count = lax.axis_size("tensor")
    held = [block]
    for _ in range(count - 1):
        held.append(
            lax.ppermute(held[-1], "tensor", [(i, (i + shift) % count) for i in range(count)])
        )
    return held


def reduce_ring(parts, shift):
    count = lax.axis_size("tensor")
    total = parts[1 % count].astype(jnp.float32)
    for j in range(1, count):
        moved = lax.ppermute(
            total.astype(jnp.bfloat16), "tensor", [(i, (i + shift) % count) for i in range(count)]
        )
        total = moved.astype(jnp.float32) + parts[(j + 1) % count].astype(jnp.float32)
    return total


def exchange(parts, shift):
    count = lax.axis_size("tensor")
    return [parts[0]] + [
        lax.ppermute(parts[j], "tensor", [(i, (i + shift * j) % count) for i in range(count)])
        for j in range(1, count)
    ]


def halves(values, count, axis):
    return jnp.split(values, count, axis=axis)


def back_norm(grad_normed, scaled, inverse, scale_row):
    grad_scaled = grad_normed * scale_row
    projection = jnp.mean(grad_scaled * scaled, axis=-1, keepdims=True)
    return inverse * (grad_scaled - scaled * projection)


def per_device(
    tokens,
    seq_lengths,
    attention_gain,
    query_matrix,
    key_matrix,
    value_matrix,
    output_weight,
    feedforward_gain,
    gate_weight,
    up_weight,
    down_weight,
    cotangent,
):
    dp_count = lax.axis_size("dp")
    ring = lax.axis_size("tensor")
    dp_place = lax.axis_index("dp")
    ring_place = lax.axis_index("tensor")
    _, local_rows, model_width = tokens.shape
    complete_rows = local_rows * ring
    block_rows = min(512, complete_rows)
    query_width = query_matrix.shape[1]
    key_width = key_matrix.shape[1]
    kv_heads = key_width // HEAD_SIZE
    group_width = QUERY_HEADS // KEY_VALUE_HEADS
    doc_ids, positions = layout(seq_lengths, complete_rows)
    doc_ids = doc_ids[0]
    cosine, sine = rope_tables(positions[0], HEAD_SIZE)
    f32 = jnp.float32
    b16 = jnp.bfloat16

    local_tokens = swap_columns(tokens[0], dp_place, dp_count)
    local_cotangent = swap_columns(cotangent[0], dp_place, dp_count)

    token_chunks = gather_ring(local_tokens, 1)
    gains = jnp.concatenate(
        gather_dp(jnp.stack([attention_gain, feedforward_gain]), 0), axis=1
    ).astype(f32)
    gain_one, gain_two = gains[0], gains[1]
    joint_matrix = jnp.concatenate([query_matrix, key_matrix, value_matrix], axis=1)
    joint_full = jnp.concatenate(gather_dp(joint_matrix, 0), axis=0)
    output_ring = jnp.concatenate(gather_ring(output_weight, -1), axis=0)
    output_full = jnp.concatenate(gather_dp(output_ring, 1), axis=1)
    gate_full = jnp.concatenate(gather_dp(gate_weight, 0), axis=0)
    up_full = jnp.concatenate(gather_dp(up_weight, 1), axis=0)
    down_a, down_b = halves(down_weight, 2, 0)
    down_full = jnp.concatenate(
        [
            jnp.concatenate(gather_dp(down_a, 0), axis=1),
            jnp.concatenate(gather_dp(down_b, 1), axis=1),
        ],
        axis=0,
    )
    cotangent_chunks = gather_ring(local_cotangent, 1)

    def to_absolute(values):
        flipped = values.reshape((ring, local_rows) + values.shape[1:])[::-1]
        return jnp.roll(flipped, ring_place + 1, axis=0).reshape(values.shape)

    def to_relative(values):
        view = values.reshape((ring, local_rows) + values.shape[1:])
        return jnp.roll(view, -(ring_place + 1), axis=0)[::-1].reshape(values.shape)

    normed_chunks = []
    for chunk in token_chunks:
        scaled, _ = norm_rows(chunk.astype(f32))
        normed_chunks.append((scaled * gain_one).astype(b16))
    normed_one = jnp.concatenate(normed_chunks, axis=0)
    joint = to_absolute(jnp.dot(normed_one, joint_full, preferred_element_type=f32))
    query_rot = rotate(
        joint[:, :query_width].reshape(complete_rows, kv_heads, group_width, HEAD_SIZE),
        cosine[:, None, None],
        sine[:, None, None],
    ).astype(b16)
    key_rot = rotate(
        joint[:, query_width : query_width + key_width].reshape(complete_rows, kv_heads, HEAD_SIZE),
        cosine[:, None],
        sine[:, None],
    ).astype(b16)
    value_rows = (
        joint[:, query_width + key_width :].astype(b16).reshape(complete_rows, kv_heads, HEAD_SIZE)
    )
    attended, totals = attend_slot(query_rot, key_rot, value_rows, doc_ids, block_rows)
    attended = to_relative(attended.reshape(complete_rows, query_width))
    attended_local = jnp.concatenate(exchange(halves(attended, ring, 0), -1), axis=1)
    inputs = local_tokens.astype(f32)
    scaled_one, inverse_one = norm_rows(inputs)
    hidden_res = inputs + jnp.dot(attended_local, output_full, preferred_element_type=f32)

    scaled_two, inverse_two = norm_rows(hidden_res)
    normed_two = jnp.concatenate(gather_ring((scaled_two * gain_two).astype(b16), 1), axis=0)
    gate_lin = jnp.dot(normed_two, gate_full, preferred_element_type=f32)
    up_lin = jnp.dot(normed_two, up_full, preferred_element_type=f32)
    sigmoid_gate = jax.nn.sigmoid(gate_lin)
    product = (gate_lin * sigmoid_gate * up_lin).astype(b16)
    gate_kept = gate_lin.astype(b16)
    up_kept = up_lin.astype(b16)
    branch_two = jnp.dot(product, down_full, preferred_element_type=f32).astype(b16)
    mixed_two = reduce_ring(halves(branch_two, ring, 0), 1)
    block_output = (hidden_res + mixed_two).astype(b16)

    whole_cotangent = jnp.concatenate(cotangent_chunks, axis=0)
    grad_product = contract(whole_cotangent, down_full, 1, 1)
    gate_lin = gate_kept.astype(f32)
    up_lin = up_kept.astype(f32)
    sigmoid_gate = jax.nn.sigmoid(gate_lin)
    grad_gate = (
        grad_product * up_lin * sigmoid_gate * (1.0 + gate_lin * (1.0 - sigmoid_gate))
    ).astype(b16)
    grad_up = (grad_product * gate_lin * sigmoid_gate).astype(b16)
    grad_normed_two = (
        contract(grad_gate, gate_full, 1, 1) + contract(grad_up, up_full, 1, 1)
    ).astype(b16)
    local_two = reduce_ring(halves(grad_normed_two, ring, 0), 1)
    gate_grad = contract(normed_two, grad_gate, 0, 0).astype(b16)
    up_grad = contract(normed_two, grad_up, 0, 0).astype(b16)
    down_grad = contract(product, whole_cotangent, 0, 0).astype(b16)
    gate_out = reduce_dp(halves(gate_grad, dp_count, 0), 0)
    up_out = reduce_dp(halves(up_grad, dp_count, 0), 1)
    grad_a, grad_b = halves(down_grad, 2, 0)
    down_out = jnp.concatenate(
        [
            reduce_dp(halves(grad_a, dp_count, 1), 0),
            reduce_dp(halves(grad_b, dp_count, 1), 1),
        ],
        axis=0,
    )
    gain_two_part = jnp.sum(local_two * scaled_two, axis=0)
    grad_hidden = local_cotangent.astype(f32) + back_norm(
        local_two, scaled_two, inverse_two, gain_two
    )

    grad_branch = grad_hidden.astype(b16)
    grad_attended_local = contract(grad_branch, output_full, 1, 1).astype(b16)
    grad_attended = jnp.concatenate(exchange(halves(grad_attended_local, ring, 1), 1), axis=0)
    output_grad = contract(attended_local, grad_branch, 0, 0).astype(b16)
    output_part = reduce_dp(halves(output_grad, dp_count, 1), 1)
    output_out = reduce_ring(halves(output_part, ring, 0), -1)
    grad_attended = to_absolute(grad_attended).reshape(
        complete_rows, kv_heads, group_width, HEAD_SIZE
    )
    grad_query_rot, grad_key_rot, grad_value = attend_back(
        query_rot, key_rot, value_rows, doc_ids, totals, grad_attended, block_rows
    )
    grad_query = unrotate(grad_query_rot, cosine[:, None, None], sine[:, None, None])
    grad_key = unrotate(grad_key_rot, cosine[:, None], sine[:, None])
    grad_joint = to_relative(
        jnp.concatenate(
            [
                grad_query.reshape(complete_rows, query_width).astype(b16),
                grad_key.reshape(complete_rows, key_width).astype(b16),
                grad_value.reshape(complete_rows, key_width).astype(b16),
            ],
            axis=1,
        )
    )
    grad_normed_one = contract(grad_joint, joint_full, 1, 1).astype(b16)
    local_one = reduce_ring(halves(grad_normed_one, ring, 0), 1)
    joint_grad = contract(normed_one, grad_joint, 0, 0).astype(b16)
    joint_out = reduce_dp(halves(joint_grad, dp_count, 0), 0)
    gain_one_part = jnp.sum(local_one * scaled_one, axis=0)
    input_gradient = grad_hidden + back_norm(local_one, scaled_one, inverse_one, gain_one)

    gain_parts = jnp.stack([gain_one_part, gain_two_part])
    width = model_width // dp_count
    held = {j: gain_parts[:, j * width : (j + 1) * width] for j in range(dp_count)}
    for step in [1] + dp_steps(0)[::-1]:
        held = {j: held[j] + partner(held[j ^ step], step) for j in held if not j & step}
    gain_out = held[0]
    for shift in range(1, ring):
        gain_out = gain_out + lax.ppermute(
            held[0], "tensor", [(i, (i + shift) % ring) for i in range(ring)]
        )
    return (
        swap_columns(block_output, dp_place, dp_count)[None],
        swap_columns(input_gradient, dp_place, dp_count)[None],
        gain_out[0],
        joint_out[:, :query_width],
        joint_out[:, query_width : query_width + key_width],
        joint_out[:, query_width + key_width :],
        output_out,
        gain_out[1],
        gate_out,
        up_out,
        down_out,
    )


def solution(mesh):
    return jax.shard_map(
        per_device,
        mesh=mesh,
        in_specs=(
            P("dp", "tensor", None),
            P("dp", None),
            P("dp"),
            P("dp", "tensor"),
            P("dp", "tensor"),
            P("dp", "tensor"),
            P("tensor", "dp"),
            P("dp"),
            P("dp", "tensor"),
            P("dp", "tensor"),
            P("tensor", "dp"),
            P("dp", "tensor", None),
        ),
        out_specs=(
            P("dp", "tensor", None),
            P("dp", "tensor", None),
            P("dp"),
            P("dp", "tensor"),
            P("dp", "tensor"),
            P("dp", "tensor"),
            P("tensor", "dp"),
            P("dp"),
            P("dp", "tensor"),
            P("dp", "tensor"),
            P("tensor", "dp"),
        ),
        check_vma=False,
    )
```

time: 1360 us -> 975 us (0.72)
  waiting for transfers between devices: 948 us -> 436 us
  local copies, waits for them, and re-layouts: 22.5 us -> 112 us
  starting transfers between devices: 1.28 us -> 89.6 us
  blocking collectives: 64.9 us -> 0 us
  other arithmetic: 67.1 us -> 99.2 us
    reduce_scatter x11 -> x0, waiting for transfers between devices: 535 us -> none  [the longest x1 77.4 us: per_device(): lax.psum_scatter(grad_normed_one.reshape(slot_count, complete_rows, model...]
    ppermute x0 -> x131, waiting for transfers between devices: none -> 436 us  [the longest x98 188 us: partner(): return lax.ppermute(value, 'dp', [(i, i ^ step) for i in range(count)])]
    all_gather x9 -> x0, waiting for transfers between devices: 409 us -> none  [the longest x1 82.9 us: per_device(): whole_two = lax.all_gather(normed_two, 'tensor', axis=1, tiled=True)]
    ppermute x0 -> x131, starting transfers between devices: none -> 89.6 us  [the longest x98 50.2 us: partner(): return lax.ppermute(value, 'dp', [(i, i ^ step) for i in range(count)])]
    all_gather x4 -> x0, blocking collectives: 39 us -> none  [the longest x1 11.1 us: attention_weights(): lax.all_gather(key_matrix, 'dp', axis=0, tiled=True)]
    unnamed x149 -> x304, local copies, waits for them, and re-layouts: 17.6 us -> 55.8 us
    concatenate x0 -> x12, other arithmetic: none -> 17.7 us  [the longest x2 10.5 us: to_relative(): return jnp.roll(view, -(ring_place + 1), axis=0)[::-1].reshape(values.shape)]
    unnamed x1 -> x0, blocking collectives: 14 us -> none
  transfers between devices with their start and end apart: 20 -> 131, of which waited for: 17 -> 49; matrix products, arithmetic and copies ran while one was open for 18% -> 38% of each run, Pallas kernels for 0% -> 0%
where the time goes in v1:
time: 975 us; the launch traced here: 966 us
  waiting for transfers between devices  436 us (45%)
  matrix products  226 us (23%)
  local copies, waits for them, and re-layouts  112 us (11%)
  other arithmetic  99.2 us (10%)
  starting transfers between devices  89.6 us (9%)
    ppermute x98, waiting for transfers between devices, partner(): return lax.ppermute(value, 'dp', [(i, i ^ step) for i in range(count)])  188 us
    ppermute x12, waiting for transfers between devices, reduce_ring(): lax.ppermute(total.astype(jnp.bfloat16), 'tensor', [(i, (i + shift) % cou...  137 us
    dot_general x10, matrix products, contract(): lax.dot_general(left, right, (((left_dim,), (right_dim,)), ((), ())), pre...  106 us
    ppermute x12, waiting for transfers between devices, gather_ring(): lax.ppermute(held[-1], 'tensor', [(i, (i + shift) % count) for i in range...  100 us
    unnamed x304, local copies, waits for them, and re-layouts  55.8 us
    ppermute x98, starting transfers between devices, partner(): return lax.ppermute(value, 'dp', [(i, i ^ step) for i in range(count)])  50.2 us
    dot_general x2, matrix products, attend_back(): jnp.einsum('qhgd,khd->hgqk', grad_block, value_rows[:last_row], preferred...  20.8 us
  transfers between devices with their start and end apart: 131, of which 49 were waited for; matrix products, arithmetic and copies ran while one was open for 38% of the time, Pallas kernels for 0%

profile of v1, /device:TPU:0, one launch (start us, length us, event | category | flops | bytes accessed | tf_op | source)
XLA Modules:
  0.0 965.9 jit_solution(17387159372800003352)
XLA Ops:
  67.7 13.4 %collective-permute-done.22 = bf16[512,256]{1,0:T(8,128)(2,1)S(1)} collective-permute-done((bf16[512,256]{1,0:T(8,128)(2,1)S(1)}, bf16[512,256]{1,0:T(8,128)(2,1)S(1)}, u32[]{:S(2)}, u32[]{:S(2)}) %collective-permute-start.22) | collective-permute-done | bytes 262176 | tf_op jit(solution)/shard_map/ppermute | solution.py:206
  87.8 12.1 %collective-permute-done.57 = bf16[1024,256]{1,0:T(8,128)(2,1)S(1)} collective-permute-done((bf16[1024,256]{1,0:T(8,128)(2,1)S(1)}, bf16[1024,256]{1,0:T(8,128)(2,1)S(1)}, u32[]{:S(2)}, u32[]{:S(2)}) %collective-permute-start.57) | collective-permute-done | bytes 524320 | tf_op jit(solution)/shard_map/ppermute | solution.py:168
  120.0 16.9 %collective-permute-done.26 = bf16[2048,256]{1,0:T(8,128)(2,1)} collective-permute-done((bf16[2048,256]{1,0:T(8,128)(2,1)S(1)}, bf16[2048,256]{1,0:T(8,128)(2,1)}, u32[]{:S(2)}, u32[]{:S(2)}) %collective-permute-start.26) | collective-permute-done | bytes 1048608 | tf_op jit(solution)/shard_map/ppermute | solution.py:168
  144.4 18.9 %collective-permute-done.28 = bf16[2048,256]{1,0:T(8,128)(2,1)} collective-permute-done((bf16[2048,256]{1,0:T(8,128)(2,1)}, bf16[2048,256]{1,0:T(8,128)(2,1)}, u32[]{:S(2)}, u32[]{:S(2)}) %collective-permute-start.28) | collective-permute-done | bytes 1048608 | tf_op jit(solution)/shard_map/ppermute | solution.py:168
  275.2 13.0 %collective-permute-done.38 = bf16[256,2048]{1,0:T(8,128)(2,1)S(1)} collective-permute-done((bf16[256,2048]{1,0:T(8,128)(2,1)S(1)}, bf16[256,2048]{1,0:T(8,128)(2,1)S(1)}, u32[]{:S(2)}, u32[]{:S(2)}) %collective-permute-start.38) | collective-permute-done | bytes 1048608 | tf_op jit(solution)/shard_map/ppermute | solution.py:168
  309.2 13.1 %collective-permute-done.65 = bf16[256,2048]{1,0:T(8,128)(2,1)S(1)} collective-permute-done((bf16[256,2048]{1,0:T(8,128)(2,1)S(1)}, bf16[256,2048]{1,0:T(8,128)(2,1)S(1)}, u32[]{:S(2)}, u32[]{:S(2)}) %collective-permute-start.65) | collective-permute-done | bytes 1048608 | tf_op jit(solution)/shard_map/ppermute | solution.py:206
  322.4 22.2 %collective-permute-done.31 = bf16[256,2048]{1,0:T(8,128)(2,1)S(1)} collective-permute-done((bf16[256,2048]{1,0:T(8,128)(2,1)S(1)}, bf16[256,2048]{1,0:T(8,128)(2,1)S(1)}, u32[]{:S(2)}, u32[]{:S(2)}) %collective-permute-start.31) | collective-permute-done | bytes 1048608 | tf_op jit(solution)/shard_map/ppermute | solution.py:206
  346.3 42.6 %collective-permute-done.32 = bf16[256,2048]{1,0:T(8,128)(2,1)S(1)} collective-permute-done((bf16[256,2048]{1,0:T(8,128)(2,1)S(1)}, bf16[256,2048]{1,0:T(8,128)(2,1)S(1)}, u32[]{:S(2)}, u32[]{:S(2)}) %collective-permute-start.32) | collective-permute-done | bytes 1048608 | tf_op jit(solution)/shard_map/ppermute | solution.py:206
  388.8 14.1 %fusion.128 = f32[1024,2048]{1,0:T(8,128)} fusion(bf16[2048,2048]{1,0:T(8,128)(2,1)S(1)} %constant_dynamic-update-slice_fusion.52, bf16[256,2048]{1,0:T(8,128)(2,1)S(1)} %collective-permute-done.32, bf16[256,2048]{1,0:T(8,128)(2,1)S(1)} %collective-permute-done.31, bf16[256,2048]{1,0:T(8,128)(2,1)S(1)} %collective-permute-done.30, ...), kind=kOutput, calls=%fused_computation.442 | convolution fusion | flops 8606711808 | bytes 20971520 | tf_op jit(solution)/shard_map/dot_general | solution.py:332
  403.0 14.0 %fusion.129 = f32[1024,2048]{1,0:T(8,128)} fusion(bf16[2048,2048]{1,0:T(8,128)(2,1)S(1)} %constant_dynamic-update-slice_fusion.44, bf16[256,2048]{1,0:T(8,128)(2,1)S(1)} %collective-permute-done.32, bf16[256,2048]{1,0:T(8,128)(2,1)S(1)} %collective-permute-done.31, bf16[256,2048]{1,0:T(8,128)(2,1)S(1)} %collective-permute-done.30, ...), kind=kOutput, calls=%fused_computation.443 | convolution fusion | flops 8606711808 | bytes 20971520 | tf_op jit(solution)/shard_map/dot_general | solution.py:331
  416.9 26.6 %fusion.10 = (bf16[1024,2048]{1,0:T(8,128)(2,1)}, bf16[1024,2048]{1,0:T(8,128)(2,1)}, bf16[1024,2048]{1,0:T(8,128)(2,1)}) fusion(f32[1024,2048]{1,0:T(8,128)} %fusion.128, f32[1024,2048]{1,0:T(8,128)} %fusion.129, bf16[1024,2048]{1,0:T(8,128)(2,1)} %constant_dynamic-update-slice_fusion.68, bf16[1024,2048]{1,0:T(8,128)(2,1)} %constant_dynamic-update-slice_fusion.60, ...), kind=kOutput, calls=%fused_computation.19 | convolution fusion | flops 8671723520 | bytes 41943040 | tf_op jit(solution)/shard_map/dot_general | solution.py:72
  443.5 14.7 %fusion.144 = f32[1024,2048]{1,0:T(8,128)} fusion(bf16[1024,2048]{1,0:T(8,128)(2,1)} %get-tuple-element.60, bf16[2048,2048]{1,0:T(8,128)(2,1)} %copy-done.91), kind=kOutput, calls=%fused_computation.458 | convolution fusion | flops 8589934592 | bytes 20971520 | tf_op jit(solution)/shard_map/dot_general | solution.py:72
  492.5 12.7 %add_convert_fusion = bf16[1024,2048]{1,0:T(8,128)(2,1)S(1)} fusion(f32[1024,2048]{1,0:T(8,128)} %fusion.144, bf16[1024,2048]{1,0:T(8,128)(2,1)S(1)} %copy-done.113, bf16[2048,2048]{1,0:T(8,128)(2,1)} %copy-done.92), kind=kOutput, calls=%fused_computation.32 | convolution fusion | flops 8594128896 | bytes 25165824 | tf_op jit(solution)/shard_map/dot_general | solution.py:72
  505.2 13.2 %convolution_convert_fusion.2 = bf16[2048,2048]{1,0:T(8,128)(2,1)S(1)} fusion(bf16[1024,2048]{1,0:T(8,128)(2,1)} %get-tuple-element.58, bf16[256,2048]{1,0:T(8,128)(2,1)} %copy-done.110, bf16[256,2048]{1,0:T(8,128)(2,1)} %copy-done.106, bf16[256,2048]{1,0:T(8,128)(2,1)S(1)} %copy-done.105, bf16[256,2048]{1,0:T(8,128)(2,1)S(1)} %multiply_convert_fusion.1), kind=kOutput, calls=%fused_computation.39 | convolution fusion | flops 8610906112 | bytes 16777216 | tf_op jit(solution)/shard_map/dot_general | solution.py:72
  521.2 14.6 %fusion.28 = bf16[1024,2048]{1,0:T(8,128)(2,1)} fusion(bf16[1024,2048]{1,0:T(8,128)(2,1)} %get-tuple-element.59, bf16[1024,2048]{1,0:T(8,128)(2,1)} %constant_dynamic-update-slice_fusion.68, bf16[1024,2048]{1,0:T(8,128)(2,1)} %constant_dynamic-update-slice_fusion.60), kind=kOutput, calls=%fused_computation.53 | convolution fusion | flops 8608808960 | bytes 16777216 | tf_op jit(solution)/shard_map/dot_general | solution.py:337
  550.3 14.9 %collective-permute-done.61 = bf16[256,2048]{1,0:T(8,128)(2,1)S(1)} collective-permute-done((bf16[256,2048]{1,0:T(8,128)(2,1)S(1)}, bf16[256,2048]{1,0:T(8,128)(2,1)S(1)}, u32[]{:S(2)}, u32[]{:S(2)}) %collective-permute-start.61) | collective-permute-done | bytes 1048608 | tf_op jit(solution)/shard_map/ppermute | solution.py:215
  587.5 21.0 %collective-permute-done.123 = bf16[1024,256]{1,0:T(8,128)(2,1)S(1)} collective-permute-done((bf16[1024,256]{1,0:T(8,128)(2,1)S(1)}, bf16[1024,256]{1,0:T(8,128)(2,1)S(1)}, u32[]{:S(2)}, u32[]{:S(2)}) %collective-permute-start.123) | collective-permute-done | bytes 524320 | tf_op jit(solution)/shard_map/ppermute | solution.py:168
  617.4 20.1 %collective-permute-done.68 = bf16[256,2048]{1,0:T(8,128)(2,1)S(1)} collective-permute-done((bf16[256,2048]{1,0:T(8,128)(2,1)S(1)}, bf16[256,2048]{1,0:T(8,128)(2,1)S(1)}, u32[]{:S(2)}, u32[]{:S(2)}) %collective-permute-start.68) | collective-permute-done | bytes 1048608 | tf_op jit(solution)/shard_map/ppermute | solution.py:215
  640.0 12.4 %collective-permute-done.129 = bf16[1024,256]{1,0:T(8,128)(2,1)S(1)} collective-permute-done((bf16[1024,256]{1,0:T(8,128)(2,1)S(1)}, bf16[1024,256]{1,0:T(8,128)(2,1)S(1)}, u32[]{:S(2)}, u32[]{:S(2)}) %collective-permute-start.129) | collective-permute-done | bytes 524320 | tf_op jit(solution)/shard_map/ppermute | solution.py:168
  684.1 19.9 %collective-permute-done.63 = bf16[256,2048]{1,0:T(8,128)(2,1)S(1)} collective-permute-done((bf16[256,2048]{1,0:T(8,128)(2,1)S(1)}, bf16[256,2048]{1,0:T(8,128)(2,1)S(1)}, u32[]{:S(2)}, u32[]{:S(2)}) %collective-permute-start.63) | collective-permute-done | bytes 1048608 | tf_op jit(solution)/shard_map/ppermute | solution.py:215
  774.9 15.5 %fusion = (f32[2,4,512]{2,1,0:T(4,128)}, f32[2,1024,512,4]{2,1,3,0:T(8,128)}) fusion(f32[2,4,512,1024]{2,3,1,0:T(8,128)} %get-tuple-element.157, f32[2,4,512]{2,1,0:T(4,128)S(1)} %bitcast.202, bf16[1024,2,64,1]{0,2,3,1:T(8,128)(2,1)} %bitcast.199, bf16[512,2,4,64]{0,3,2,1:T(8,128)(2,1)} %slice.291), kind=kOutput, calls=%fused_computation.2 | convolution fusion | flops 549449728 | bytes 34373632 | tf_op jit(solution)/shard_map/qhgd,khd->hgqk/dot_general | solution.py:123
  860.9 16.9 %collective-permute-done.73 = bf16[256,2048]{1,0:T(8,128)(2,1)S(1)} collective-permute-done((bf16[256,2048]{1,0:T(8,128)(2,1)S(1)}, bf16[256,2048]{1,0:T(8,128)(2,1)S(1)}, u32[]{:S(2)}, u32[]{:S(2)}) %collective-permute-start.73) | collective-permute-done | bytes 1048608 | tf_op jit(solution)/shard_map/ppermute | solution.py:215
  890.8 18.8 %collective-permute-done.74 = bf16[256,2048]{1,0:T(8,128)(2,1)S(1)} collective-permute-done((bf16[256,2048]{1,0:T(8,128)(2,1)S(1)}, bf16[256,2048]{1,0:T(8,128)(2,1)S(1)}, u32[]{:S(2)}, u32[]{:S(2)}) %collective-permute-start.74) | collective-permute-done | bytes 1048608 | tf_op jit(solution)/shard_map/ppermute | solution.py:215
  922.0 18.9 %collective-permute-done.100 = bf16[512,256]{1,0:T(8,128)(2,1)S(1)} collective-permute-done((bf16[512,256]{1,0:T(8,128)(2,1)S(1)}, bf16[512,256]{1,0:T(8,128)(2,1)S(1)}, u32[]{:S(2)}, u32[]{:S(2)}) %collective-permute-start.100) | collective-permute-done | bytes 262176 | tf_op jit(solution)/shard_map/ppermute | solution.py:215
  (738 shorter events, 541.9 us)
Async XLA Ops:
  138.4 119.5 %collective-permute-start.36 = (bf16[256,2048]{1,0:T(8,128)(2,1)}, bf16[256,2048]{1,0:T(8,128)(2,1)}, u32[]{:S(2)}, u32[]{:S(2)}) collective-permute-start(bf16[256,2048]{1,0:T(8,128)(2,1)} %param.22), channel_id=1, source_target_pairs={{0,16},{4,20},{8,24},{12,28},{16,0},{20,4},{24,8},{28,12},{1,17},{... | collective-permute-start | bytes 3145736 | tf_op jit(solution)/shard_map/ppermute | solution.py:168
  140.0 118.1 %collective-permute-start.41 = (bf16[256,2048]{1,0:T(8,128)(2,1)}, bf16[256,2048]{1,0:T(8,128)(2,1)}, u32[]{:S(2)}, u32[]{:S(2)}) collective-permute-start(bf16[256,2048]{1,0:T(8,128)(2,1)} %param.23), channel_id=1, source_target_pairs={{0,8},{4,12},{8,0},{12,4},{16,24},{20,28},{24,16},{28,20},{1,9},{5... | collective-permute-start | bytes 3145736 | tf_op jit(solution)/shard_map/ppermute | solution.py:168
  163.3 63.4 %collective-permute-start.27 = (bf16[2048,256]{1,0:T(8,128)(2,1)}, bf16[2048,256]{1,0:T(8,128)(2,1)}, u32[]{:S(2)}, u32[]{:S(2)}) collective-permute-start(bf16[2048,256]{1,0:T(8,128)(2,1)} %collective-permute-done.26), channel_id=1, source_target_pairs={{0,4},{4,0},{8,12},{12,8},{16,20},{20,16},{24,28},{28,24},{1,5},{5... | collective-permute-start | bytes 3145736 | tf_op jit(solution)/shard_map/ppermute | solution.py:168
  163.3 80.7 %collective-permute-start.29 = (bf16[2048,256]{1,0:T(8,128)(2,1)}, bf16[2048,256]{1,0:T(8,128)(2,1)}, u32[]{:S(2)}, u32[]{:S(2)}) collective-permute-start(bf16[2048,256]{1,0:T(8,128)(2,1)} %collective-permute-done.28), channel_id=1, source_target_pairs={{0,4},{4,0},{8,12},{12,8},{16,20},{20,16},{24,28},{28,24},{1,5},{5... | collective-permute-start | bytes 3145736 | tf_op jit(solution)/shard_map/ppermute | solution.py:168
  299.7 44.9 %collective-permute-start.31 = (bf16[256,2048]{1,0:T(8,128)(2,1)S(1)}, bf16[256,2048]{1,0:T(8,128)(2,1)S(1)}, u32[]{:S(2)}, u32[]{:S(2)}) collective-permute-start(bf16[256,2048]{1,0:T(8,128)(2,1)S(1)} %collective-permute-done.30), channel_id=1, source_target_pairs={{0,1},{1,2},{2,3},{3,0},{4,5},{5,6},{6,7},{7,4},{8,9},{9,10},{10,1... | collective-permute-start | bytes 3145736 | tf_op jit(solution)/shard_map/ppermute | solution.py:206
  299.9 46.2 %collective-permute-start.39 = (bf16[256,2048]{1,0:T(8,128)(2,1)S(1)}, bf16[256,2048]{1,0:T(8,128)(2,1)S(1)}, u32[]{:S(2)}, u32[]{:S(2)}) collective-permute-start(bf16[256,2048]{1,0:T(8,128)(2,1)S(1)} %collective-permute-done.38), channel_id=1, source_target_pairs={{0,4},{4,0},{8,12},{12,8},{16,20},{20,16},{24,28},{28,24},{1,5},{5... | collective-permute-start | bytes 3145736 | tf_op jit(solution)/shard_map/ppermute | solution.py:168
  322.2 94.7 %collective-permute-start.66 = (bf16[256,2048]{1,0:T(8,128)(2,1)S(1)}, bf16[256,2048]{1,0:T(8,128)(2,1)}, u32[]{:S(2)}, u32[]{:S(2)}) collective-permute-start(bf16[256,2048]{1,0:T(8,128)(2,1)S(1)} %collective-permute-done.65), channel_id=1, source_target_pairs={{0,1},{1,2},{2,3},{3,0},{4,5},{5,6},{6,7},{7,4},{8,9},{9,10},{10,1... | collective-permute-start | bytes 3145736 | tf_op jit(solution)/shard_map/ppermute | solution.py:206
  344.7 44.1 %collective-permute-start.32 = (bf16[256,2048]{1,0:T(8,128)(2,1)S(1)}, bf16[256,2048]{1,0:T(8,128)(2,1)S(1)}, u32[]{:S(2)}, u32[]{:S(2)}) collective-permute-start(bf16[256,2048]{1,0:T(8,128)(2,1)S(1)} %collective-permute-done.31), channel_id=1, source_target_pairs={{0,1},{1,2},{2,3},{3,0},{4,5},{5,6},{6,7},{7,4},{8,9},{9,10},{10,1... | collective-permute-start | bytes 3145736 | tf_op jit(solution)/shard_map/ppermute | solution.py:206
  475.1 45.6 %collective-permute-start.121 = (bf16[1024,256]{1,0:T(8,128)(2,1)}, bf16[1024,256]{1,0:T(8,128)(2,1)}, u32[]{:S(2)}, u32[]{:S(2)}) collective-permute-start(bf16[1024,256]{1,0:T(8,128)(2,1)} %get-tuple-element.69), channel_id=1, source_target_pairs={{0,4},{4,0},{8,12},{12,8},{16,20},{20,16},{24,28},{28,24},{1,5},{5... | collective-permute-start | bytes 1572872 | tf_op jit(solution)/shard_map/ppermute | solution.py:168
  475.1 62.1 %collective-permute-start.118 = (bf16[1024,256]{1,0:T(8,128)(2,1)}, bf16[1024,256]{1,0:T(8,128)(2,1)}, u32[]{:S(2)}, u32[]{:S(2)}) collective-permute-start(bf16[1024,256]{1,0:T(8,128)(2,1)} %get-tuple-element.71), channel_id=1, source_target_pairs={{0,4},{4,0},{8,12},{12,8},{16,20},{20,16},{24,28},{28,24},{1,5},{5... | collective-permute-start | bytes 1572872 | tf_op jit(solution)/shard_map/ppermute | solution.py:168
  492.0 46.9 %collective-permute-start.114 = (bf16[256,2048]{1,0:T(8,128)(2,1)}, bf16[256,2048]{1,0:T(8,128)(2,1)}, u32[]{:S(2)}, u32[]{:S(2)}) collective-permute-start(bf16[256,2048]{1,0:T(8,128)(2,1)} %get-tuple-element.75), channel_id=1, source_target_pairs={{0,4},{4,0},{8,12},{12,8},{16,20},{20,16},{24,28},{28,24},{1,5},{5... | collective-permute-start | bytes 3145736 | tf_op jit(solution)/shard_map/ppermute | solution.py:168
  492.0 49.2 %collective-permute-start.111 = (bf16[256,2048]{1,0:T(8,128)(2,1)}, bf16[256,2048]{1,0:T(8,128)(2,1)}, u32[]{:S(2)}, u32[]{:S(2)}) collective-permute-start(bf16[256,2048]{1,0:T(8,128)(2,1)} %get-tuple-element.77), channel_id=1, source_target_pairs={{0,4},{4,0},{8,12},{12,8},{16,20},{20,16},{24,28},{28,24},{1,5},{5... | collective-permute-start | bytes 3145736 | tf_op jit(solution)/shard_map/ppermute | solution.py:168
  538.9 47.3 %collective-permute-start.67 = (bf16[256,2048]{1,0:T(8,128)(2,1)S(1)}, bf16[256,2048]{1,0:T(8,128)(2,1)S(1)}, u32[]{:S(2)}, u32[]{:S(2)}) collective-permute-start(bf16[256,2048]{1,0:T(8,128)(2,1)S(1)} %split.319), channel_id=1, source_target_pairs={{0,1},{1,2},{2,3},{3,0},{4,5},{5,6},{6,7},{7,4},{8,9},{9,10},{10,1... | collective-permute-start | bytes 3145736 | tf_op jit(solution)/shard_map/ppermute | solution.py:215
  565.9 43.2 %collective-permute-start.113 = (bf16[256,2048]{1,0:T(8,128)(2,1)S(1)}, bf16[256,2048]{1,0:T(8,128)(2,1)S(1)}, u32[]{:S(2)}, u32[]{:S(2)}) collective-permute-start(bf16[256,2048]{1,0:T(8,128)(2,1)S(1)} %copy-done.60), channel_id=1, source_target_pairs={{0,4},{4,0},{8,12},{12,8},{16,20},{20,16},{24,28},{28,24},{1,5},{5... | collective-permute-start | bytes 3145736 | tf_op jit(solution)/shard_map/ppermute | solution.py:168
  609.1 51.6 %collective-permute-start.124 = (bf16[1024,256]{1,0:T(8,128)(2,1)S(1)}, bf16[1024,256]{1,0:T(8,128)(2,1)S(1)}, u32[]{:S(2)}, u32[]{:S(2)}) collective-permute-start(bf16[1024,256]{1,0:T(8,128)(2,1)S(1)} %get-tuple-element.68), channel_id=1, source_target_pairs={{0,4},{4,0},{8,12},{12,8},{16,20},{20,16},{24,28},{28,24},{1,5},{5... | collective-permute-start | bytes 1572872 | tf_op jit(solution)/shard_map/ppermute | solution.py:168
  612.9 106.2 %collective-permute-start.110 = (bf16[256,2048]{1,0:T(8,128)(2,1)}, bf16[256,2048]{1,0:T(8,128)(2,1)}, u32[]{:S(2)}, u32[]{:S(2)}) collective-permute-start(bf16[256,2048]{1,0:T(8,128)(2,1)} %get-tuple-element.74), channel_id=1, source_target_pairs={{0,4},{4,0},{8,12},{12,8},{16,20},{20,16},{24,28},{28,24},{1,5},{5... | collective-permute-start | bytes 3145736 | tf_op jit(solution)/shard_map/ppermute | solution.py:168
  612.9 47.0 %collective-permute-start.62 = (bf16[256,2048]{1,0:T(8,128)(2,1)S(1)}, bf16[256,2048]{1,0:T(8,128)(2,1)S(1)}, u32[]{:S(2)}, u32[]{:S(2)}) collective-permute-start(bf16[256,2048]{1,0:T(8,128)(2,1)S(1)} %add_convert_fusion.16), channel_id=1, source_target_pairs={{0,1},{1,2},{2,3},{3,0},{4,5},{5,6},{6,7},{7,4},{8,9},{9,10},{10,1... | collective-permute-start | bytes 3145736 | tf_op jit(solution)/shard_map/ppermute | solution.py:215
  660.7 73.7 %collective-permute-start.103 = (bf16[256,2048]{1,0:T(8,128)(2,1)}, bf16[256,2048]{1,0:T(8,128)(2,1)}, u32[]{:S(2)}, u32[]{:S(2)}) collective-permute-start(bf16[256,2048]{1,0:T(8,128)(2,1)} %get-tuple-element.80), channel_id=1, source_target_pairs={{0,4},{4,0},{8,12},{12,8},{16,20},{20,16},{24,28},{28,24},{1,5},{5... | collective-permute-start | bytes 3145736 | tf_op jit(solution)/shard_map/ppermute | solution.py:168
  660.9 62.6 %collective-permute-start.112 = (bf16[256,2048]{1,0:T(8,128)(2,1)}, bf16[256,2048]{1,0:T(8,128)(2,1)}, u32[]{:S(2)}, u32[]{:S(2)}) collective-permute-start(bf16[256,2048]{1,0:T(8,128)(2,1)} %get-tuple-element.78), channel_id=1, source_target_pairs={{0,8},{4,12},{8,0},{12,4},{16,24},{20,28},{24,16},{28,20},{1,9},{5... | collective-permute-start | bytes 3145736 | tf_op jit(solution)/shard_map/ppermute | solution.py:168
  682.4 52.6 %collective-permute-start.105 = (bf16[256,2048]{1,0:T(8,128)(2,1)}, bf16[256,2048]{1,0:T(8,128)(2,1)}, u32[]{:S(2)}, u32[]{:S(2)}) collective-permute-start(bf16[256,2048]{1,0:T(8,128)(2,1)} %get-tuple-element.84), channel_id=1, source_target_pairs={{0,16},{4,20},{8,24},{12,28},{16,0},{20,4},{24,8},{28,12},{1,17},{... | collective-permute-start | bytes 3145736 | tf_op jit(solution)/shard_map/ppermute | solution.py:168
  735.0 120.2 %collective-permute-start.97 = (bf16[2048,256]{1,0:T(8,128)(2,1)}, bf16[2048,256]{1,0:T(8,128)(2,1)}, u32[]{:S(2)}, u32[]{:S(2)}) collective-permute-start(bf16[2048,256]{1,0:T(8,128)(2,1)} %get-tuple-element.87), channel_id=1, source_target_pairs={{0,4},{4,0},{8,12},{12,8},{16,20},{20,16},{24,28},{28,24},{1,5},{5... | collective-permute-start | bytes 3145736 | tf_op jit(solution)/shard_map/ppermute | solution.py:168
  743.2 136.7 %collective-permute-start.96 = (bf16[2048,256]{1,0:T(8,128)(2,1)}, bf16[2048,256]{1,0:T(8,128)(2,1)}, u32[]{:S(2)}, u32[]{:S(2)}) collective-permute-start(bf16[2048,256]{1,0:T(8,128)(2,1)} %get-tuple-element.88), channel_id=1, source_target_pairs={{0,4},{4,0},{8,12},{12,8},{16,20},{20,16},{24,28},{28,24},{1,5},{5... | collective-permute-start | bytes 3145736 | tf_op jit(solution)/shard_map/ppermute | solution.py:168
  748.2 107.6 %collective-permute-start.94 = (bf16[2048,256]{1,0:T(8,128)(2,1)}, bf16[2048,256]{1,0:T(8,128)(2,1)}, u32[]{:S(2)}, u32[]{:S(2)}) collective-permute-start(bf16[2048,256]{1,0:T(8,128)(2,1)} %get-tuple-element.89), channel_id=1, source_target_pairs={{0,4},{4,0},{8,12},{12,8},{16,20},{20,16},{24,28},{28,24},{1,5},{5... | collective-permute-start | bytes 3145736 | tf_op jit(solution)/shard_map/ppermute | solution.py:168
  860.2 51.5 %collective-permute-start.93 = (bf16[2048,256]{1,0:T(8,128)(2,1)S(1)}, bf16[2048,256]{1,0:T(8,128)(2,1)S(1)}, u32[]{:S(2)}, u32[]{:S(2)}) collective-permute-start(bf16[2048,256]{1,0:T(8,128)(2,1)S(1)} %copy-done.59), channel_id=1, source_target_pairs={{0,4},{4,0},{8,12},{12,8},{16,20},{20,16},{24,28},{28,24},{1,5},{5... | collective-permute-start | bytes 3145736 | tf_op jit(solution)/shard_map/ppermute | solution.py:168
  (234 other events, 5182.2 us)

commit v2 on v1

v2 whole, which is shorter than its diff:
```python
import functools

import jax
import jax.numpy as jnp
from jax import lax
from jax.experimental import pallas as pl
from jax.experimental.pallas import tpu as pltpu
from jax.sharding import PartitionSpec as P

QUERY_HEADS = 32
KEY_VALUE_HEADS = 8
HEAD_SIZE = 64
PIECES = 4


EPSILON = 1e-05
ROPE_BASE = 500000.0
NEGATIVE = -1e30
KERNEL_VMEM = 60 * 1024 * 1024
SMALL_COST = pl.CostEstimate(flops=1, bytes_accessed=1, transcendentals=0)


def layout(lengths, complete_rows):
    doc_ends = jnp.cumsum(lengths, axis=-1)
    row_index = jnp.arange(complete_rows, dtype=jnp.int32)
    piece_count = lengths.shape[-1]
    doc_ids = jnp.sum((row_index[None, :, None] >= doc_ends[:, None, :]).astype(jnp.int32), axis=2)
    starts = doc_ends - lengths
    chosen = doc_ids[:, :, None] == jnp.arange(piece_count, dtype=jnp.int32)[None, None, :]
    doc_begin = jnp.sum(jnp.where(chosen, starts[:, None, :], 0), axis=2) + jnp.where(
        doc_ids == piece_count, doc_ends[:, -1:], 0
    )
    return (doc_ids, row_index[None, :] - doc_begin)


def rope_tables(positions, head_dim):
    half_dim = head_dim // 2
    frequency = ROPE_BASE ** (-(jnp.arange(half_dim, dtype=jnp.float32) * (2.0 / head_dim)))
    angles = positions.astype(jnp.float32)[..., None] * frequency
    return (jnp.cos(angles), jnp.sin(angles))


def norm_rows(values):
    inverse = lax.rsqrt(jnp.mean(values * values, axis=-1, keepdims=True) + EPSILON)
    return (values * inverse, inverse)


def dot_nt(left, right):
    return lax.dot_general(
        left, right, (((1,), (1,)), ((), ())), preferred_element_type=jnp.float32
    )


def dot_nn(left, right):
    return jnp.dot(left, right, preferred_element_type=jnp.float32)


def dot_tn(left, right):
    return lax.dot_general(
        left, right, (((0,), (0,)), ((), ())), preferred_element_type=jnp.float32
    )


def swap_halves(values):
    lane = lax.broadcasted_iota(jnp.int32, values.shape, 1)
    half = HEAD_SIZE // 2
    return jnp.where(
        lane % HEAD_SIZE < half, pltpu.roll(values, 128 - half, 1), pltpu.roll(values, half, 1)
    )


def turned(values, cosine, sine, rotated, start):
    if start >= rotated:
        return values
    result = values * cosine + swap_halves(values) * sine
    if start + 128 <= rotated:
        return result
    lane = lax.broadcasted_iota(jnp.int32, values.shape, 1)
    return jnp.where(lane < rotated - start, result, values)


def project_kernel(
    query_width, rotated, x_ref, gain_ref, weight_ref, cos_ref, sin_ref, normed_ref, joint_ref
):
    step = pl.program_id(0)

    @pl.when(step == 0)
    def _():
        values = x_ref[...].astype(jnp.float32)
        inverse = lax.rsqrt(jnp.mean(values * values, axis=-1, keepdims=True) + EPSILON)
        normed_ref[...] = (values * inverse * gain_ref[...]).astype(jnp.bfloat16)

    width = weight_ref.shape[1]
    product = dot_nn(normed_ref[...], weight_ref[...])
    for index in range(pl.cdiv(query_width + 2 * (rotated - query_width), width)):

        @pl.when(step == index)
        def _():
            for start in range(0, width, 128):
                column = index * width + start
                part = turned(
                    product[:, start : start + 128], cos_ref[...], sin_ref[...], rotated, column
                )
                if column < query_width:
                    part = part * HEAD_SIZE ** (-0.5)
                joint_ref[:, start : start + 128] = part.astype(jnp.bfloat16)


def project(x, gain, weight, cosine, sine, index, query_width, rotated):
    rows, depth = x.shape
    total = 2 * rotated - query_width
    width = tile_of(total, 256)
    return pl.pallas_call(
        functools.partial(project_kernel, query_width, rotated),
        grid=(total // width,),
        in_specs=[
            pl.BlockSpec((rows, depth), lambda i: (0, 0)),
            pl.BlockSpec((1, depth), lambda i: (0, 0)),
            pl.BlockSpec((depth, width), lambda i: (0, i)),
            pl.BlockSpec((rows, 128), lambda i: (index, 0)),
            pl.BlockSpec((rows, 128), lambda i: (index, 0)),
        ],
        out_specs=[
            pl.BlockSpec((rows, depth), lambda i: (0, 0)),
            pl.BlockSpec((rows, width), lambda i: (0, i)),
        ],
        out_shape=[
            jax.ShapeDtypeStruct((rows, depth), jnp.bfloat16),
            jax.ShapeDtypeStruct((rows, total), jnp.bfloat16),
        ],
        compiler_params=pltpu.CompilerParams(vmem_limit_bytes=KERNEL_VMEM),
        cost_estimate=SMALL_COST,
        name="project",
    )(x, gain, weight, cosine, sine)


def ring_offset(place, chunk, count, rows):
    return pl.multiple_of(lax.rem(place - chunk + count, count) * rows, rows)


def forward_kernel(
    count, place_ref, q_ref, kv_ref, docq_ref, dock_ref, o_ref, lse_ref, bias, scores
):
    chunk = pl.program_id(0)
    place = place_ref[0]
    rows = q_ref.shape[0]
    kv_width = kv_ref.shape[1] // 2
    heads = kv_width // HEAD_SIZE
    group = q_ref.shape[1] // kv_width
    row_index = lax.broadcasted_iota(jnp.int32, (rows, rows), 0)
    column_index = lax.broadcasted_iota(jnp.int32, (rows, rows), 1)

    def score(j, peaks):
        offset = ring_offset(place, j, count, rows)
        same = dock_ref[pl.ds(offset, rows), :] == docq_ref[...]
        same = same & ((row_index <= column_index) | (j < chunk))
        bias[...] = jnp.where(same, 0.0, NEGATIVE)
        result = []
        for head in range(heads * group):
            h = head // group
            keys = kv_ref[pl.ds(offset, rows), h * HEAD_SIZE : (h + 1) * HEAD_SIZE]
            query = q_ref[:, head * HEAD_SIZE : (head + 1) * HEAD_SIZE]
            block = dot_nt(keys, query) + bias[...]
            scores[head, j] = block
            result.append(jnp.maximum(peaks[head], jnp.max(block, axis=0, keepdims=True)))
        return tuple(result)

    peaks = lax.fori_loop(
        0,
        chunk + 1,
        score,
        tuple(jnp.full((1, rows), NEGATIVE, jnp.float32) for _ in range(heads * group)),
    )
    for h in range(heads):
        first_value = kv_width + h * HEAD_SIZE

        def mix(j, carry):
            offset = ring_offset(place, j, count, rows)
            values = kv_ref[pl.ds(offset, rows), first_value : first_value + HEAD_SIZE]
            values = jnp.concatenate([values, jnp.ones_like(values)], axis=1)
            result = []
            for g in range(group):
                probs = jnp.exp(scores[h * group + g, j] - peaks[h * group + g])
                total = carry[g][1] + jnp.sum(probs, axis=0, keepdims=True)
                result.append(
                    (carry[g][0] + dot_tn(probs.astype(jnp.bfloat16), values), total)
                )
            return tuple(result)

        sums = lax.fori_loop(
            0,
            chunk + 1,
            mix,
            tuple(
                (
                    jnp.zeros((rows, 2 * HEAD_SIZE), jnp.float32),
                    jnp.zeros((1, rows), jnp.float32),
                )
                for _ in range(group)
            ),
        )
        for g in range(group):
            head = h * group + g
            mixed, total = sums[g]
            o_ref[:, head * HEAD_SIZE : (head + 1) * HEAD_SIZE] = (
                mixed[:, :HEAD_SIZE] / mixed[:, HEAD_SIZE:]
            ).astype(jnp.bfloat16)
            lse_ref[head : head + 1, :] = peaks[head] + jnp.log(total)


def attention_forward(joint, docs, place, count, query_width, kv_width):
    total_rows = joint.shape[0]
    rows = total_rows // count
    heads = query_width // HEAD_SIZE
    padded = max(8, heads)
    group = query_width // kv_width

    def chunk_row(c, place_ref):
        return lax.rem(place_ref[0] - c + count, count)

    spec = pltpu.PrefetchScalarGridSpec(
        num_scalar_prefetch=1,
        grid=(count,),
        in_specs=[
            pl.BlockSpec((rows, query_width), lambda c, p: (chunk_row(c, p), 0)),
            pl.BlockSpec(
                (total_rows, 2 * kv_width), lambda c, p: (0, query_width // (2 * kv_width))
            ),
            pl.BlockSpec((1, rows), lambda c, p: (0, chunk_row(c, p))),
            pl.BlockSpec((total_rows, 1), lambda c, p: (0, 0)),
        ],
        out_specs=[
            pl.BlockSpec((rows, query_width), lambda c, p: (chunk_row(c, p), 0)),
            pl.BlockSpec((padded, rows), lambda c, p: (0, chunk_row(c, p))),
        ],
        scratch_shapes=[
            pltpu.VMEM((rows, rows), jnp.float32),
            pltpu.VMEM((heads, count, rows, rows), jnp.float32),
        ],
    )
    return pl.pallas_call(
        functools.partial(forward_kernel, count),
        grid_spec=spec,
        out_shape=[
            jax.ShapeDtypeStruct((total_rows, query_width), jnp.bfloat16),
            jax.ShapeDtypeStruct((padded, total_rows), jnp.float32),
        ],
        compiler_params=pltpu.CompilerParams(vmem_limit_bytes=KERNEL_VMEM),
        cost_estimate=SMALL_COST,
        name="attend",
    )(place, joint, joint, docs[None, :], docs[:, None])


def backward_kernel(
    count,
    place_ref,
    q_ref,
    kv_ref,
    o_ref,
    do_ref,
    lse_ref,
    docq_ref,
    dock_ref,
    cos_ref,
    sin_ref,
    out_ref,
    bias,
    sum_q,
    sum_kv,
):
    chunk = pl.program_id(0)
    place = place_ref[0]
    rows, query_width = q_ref.shape
    kv_width = kv_ref.shape[1] // 2
    heads = kv_width // HEAD_SIZE
    group = query_width // kv_width
    row_index = lax.broadcasted_iota(jnp.int32, (rows, rows), 0)
    column_index = lax.broadcasted_iota(jnp.int32, (rows, rows), 1)

    @pl.when(chunk == 0)
    def _():
        sum_kv[...] = jnp.zeros_like(sum_kv)

    sum_q[...] = jnp.zeros_like(sum_q)
    padded = lse_ref.shape[0]
    owner = lax.broadcasted_iota(jnp.int32, (padded, query_width), 0)
    head_of = lax.broadcasted_iota(jnp.int32, (padded, query_width), 1) // HEAD_SIZE
    selector = jnp.where(owner == head_of, 1.0, 0.0).astype(jnp.bfloat16)
    both = o_ref[...].astype(jnp.float32) * do_ref[...].astype(jnp.float32)
    high = both.astype(jnp.bfloat16)
    low = (both - high.astype(jnp.float32)).astype(jnp.bfloat16)
    inner = dot_nt(selector, high) + dot_nt(selector, low)

    def block(j, carry):
        offset = ring_offset(place, j, count, rows)
        same = dock_ref[pl.ds(offset, rows), :] == docq_ref[...]
        same = same & ((row_index <= column_index) | (j < chunk))
        bias[...] = jnp.where(same, 0.0, NEGATIVE)
        for h in range(heads):
            keys = kv_ref[pl.ds(offset, rows), h * HEAD_SIZE : (h + 1) * HEAD_SIZE]
            first_value = kv_width + h * HEAD_SIZE
            values = kv_ref[pl.ds(offset, rows), first_value : first_value + HEAD_SIZE]
            key_sum = jnp.zeros((rows, HEAD_SIZE), jnp.float32)
            value_sum = jnp.zeros((rows, HEAD_SIZE), jnp.float32)
            for g in range(group):
                head = h * group + g
                lanes = slice(head * HEAD_SIZE, (head + 1) * HEAD_SIZE)
                query = q_ref[:, lanes]
                grad = do_ref[:, lanes]
                probs = jnp.exp(dot_nt(keys, query) + bias[...] - lse_ref[head : head + 1, :])
                grad_probs = dot_nt(values, grad)
                grad_scores = (probs * (grad_probs - inner[head : head + 1, :])).astype(
                    jnp.bfloat16
                )
                value_sum += dot_nn(probs.astype(jnp.bfloat16), grad)
                key_sum += dot_nn(grad_scores, query)
                sum_q[:, lanes] += dot_tn(grad_scores, keys)
            sum_kv[pl.ds(offset, rows), h * HEAD_SIZE : (h + 1) * HEAD_SIZE] += key_sum
            sum_kv[pl.ds(offset, rows), first_value : first_value + HEAD_SIZE] += value_sum
        return carry

    lax.fori_loop(0, chunk + 1, block, 0)
    offset = ring_offset(place, chunk, count, rows)
    own = pl.ds(offset, rows)
    for start in range(0, query_width, 128):
        part = turned(
            sum_q[:, start : start + 128], cos_ref[own, :], -sin_ref[own, :], query_width, start
        )
        out_ref[own, start : start + 128] = (part * HEAD_SIZE ** (-0.5)).astype(jnp.bfloat16)

    @pl.when(chunk == count - 1)
    def _():
        for start in range(0, 2 * kv_width, 128):
            part = turned(
                sum_kv[:, start : start + 128], cos_ref[...], -sin_ref[...], kv_width, start
            )
            out_ref[:, query_width + start : query_width + start + 128] = part.astype(jnp.bfloat16)


def attention_backward(
    joint, attended, grad_attended, lse, docs, cosine, sine, place, count, query_width, kv_width
):
    total_rows, total_width = joint.shape
    rows = total_rows // count
    heads = query_width // HEAD_SIZE
    padded = lse.shape[0]

    def chunk_row(c, place_ref):
        return lax.rem(place_ref[0] - c + count, count)

    own = pl.BlockSpec((rows, query_width), lambda c, p: (chunk_row(c, p), 0))
    table = pl.BlockSpec((total_rows, 128), lambda c, p: (0, 0))
    spec = pltpu.PrefetchScalarGridSpec(
        num_scalar_prefetch=1,
        grid=(count,),
        in_specs=[
            own,
            pl.BlockSpec(
                (total_rows, 2 * kv_width), lambda c, p: (0, query_width // (2 * kv_width))
            ),
            own,
            own,
            pl.BlockSpec((padded, rows), lambda c, p: (0, chunk_row(c, p))),
            pl.BlockSpec((1, rows), lambda c, p: (0, chunk_row(c, p))),
            pl.BlockSpec((total_rows, 1), lambda c, p: (0, 0)),
            table,
            table,
        ],
        out_specs=pl.BlockSpec((total_rows, total_width), lambda c, p: (0, 0)),
        scratch_shapes=[
            pltpu.VMEM((rows, rows), jnp.float32),
            pltpu.VMEM((rows, query_width), jnp.float32),
            pltpu.VMEM((total_rows, 2 * kv_width), jnp.float32),
        ],
    )
    return pl.pallas_call(
        functools.partial(backward_kernel, count),
        grid_spec=spec,
        out_shape=jax.ShapeDtypeStruct((total_rows, total_width), jnp.bfloat16),
        compiler_params=pltpu.CompilerParams(vmem_limit_bytes=KERNEL_VMEM),
        cost_estimate=SMALL_COST,
        name="attend_back",
    )(
        place,
        joint,
        joint,
        attended,
        grad_attended,
        lse,
        docs[None, :],
        docs[:, None],
        cosine,
        sine,
    )


def tile_of(size, limit=512):
    tile = limit
    while size % tile:
        tile //= 2
    return tile


def transposed_kernel(x_ref, weight_ref, out_ref):
    out_ref[...] = dot_nt(x_ref[...], weight_ref[...]).astype(out_ref.dtype)


def transposed_product(x, weight, dtype):
    rows, depth = x.shape
    width = weight.shape[0]
    tile = tile_of(width)
    return pl.pallas_call(
        transposed_kernel,
        grid=(width // tile,),
        in_specs=[
            pl.BlockSpec((rows, depth), lambda t: (0, 0)),
            pl.BlockSpec((tile, depth), lambda t: (t, 0)),
        ],
        out_specs=pl.BlockSpec((rows, tile), lambda t: (0, t)),
        out_shape=jax.ShapeDtypeStruct((rows, width), dtype),
        compiler_params=pltpu.CompilerParams(vmem_limit_bytes=KERNEL_VMEM),
        cost_estimate=SMALL_COST,
        name="transposed",
    )(x, weight)


def join_kernel(axis, *refs):
    place = 0
    for ref in refs[:-1]:
        size = ref.shape[axis]
        if axis == 0:
            refs[-1][place : place + size, :] = ref[...]
        else:
            refs[-1][:, place : place + size] = ref[...]
        place += size


def join(parts, axis):
    shape = list(parts[0].shape)
    shape[axis] = sum(part.shape[axis] for part in parts)
    return pl.pallas_call(
        functools.partial(join_kernel, axis),
        out_shape=jax.ShapeDtypeStruct(tuple(shape), parts[0].dtype),
        compiler_params=pltpu.CompilerParams(vmem_limit_bytes=KERNEL_VMEM),
        cost_estimate=SMALL_COST,
        name="join",
    )(*parts)


def attended_kernel(o_ref, weight_ref, tokens_ref, gain_ref, hidden_ref, normed_ref):
    step = pl.program_id(0)
    tile = weight_ref.shape[0]
    columns = pl.ds(pl.multiple_of(step * tile, tile), tile)
    hidden_ref[:, columns] = tokens_ref[...].astype(jnp.float32) + dot_nt(
        o_ref[...], weight_ref[...]
    )

    @pl.when(step == pl.num_programs(0) - 1)
    def _():
        values = hidden_ref[...]
        inverse = lax.rsqrt(jnp.mean(values * values, axis=-1, keepdims=True) + EPSILON)
        normed_ref[...] = (values * inverse * gain_ref[...]).astype(jnp.bfloat16)


def after_attention(attended, weight, tokens, gain):
    rows, depth = attended.shape
    width = weight.shape[0]
    tile = tile_of(width)
    whole = pl.BlockSpec((rows, width), lambda t: (0, 0))
    return pl.pallas_call(
        attended_kernel,
        grid=(width // tile,),
        in_specs=[
            pl.BlockSpec((rows, depth), lambda t: (0, 0)),
            pl.BlockSpec((tile, depth), lambda t: (t, 0)),
            pl.BlockSpec((rows, tile), lambda t: (0, t)),
            pl.BlockSpec((1, width), lambda t: (0, 0)),
        ],
        out_specs=[whole, whole],
        out_shape=[
            jax.ShapeDtypeStruct((rows, width), jnp.float32),
            jax.ShapeDtypeStruct((rows, width), jnp.bfloat16),
        ],
        compiler_params=pltpu.CompilerParams(vmem_limit_bytes=KERNEL_VMEM),
        cost_estimate=SMALL_COST,
        name="after_attention",
    )(attended, weight, tokens, gain)


def join_rows(parts, out_ref):
    rows = parts[0].shape[0]
    for index, part in enumerate(parts):
        out_ref[index * rows : (index + 1) * rows, :] = part[...]


def up_kernel(parts, *refs):
    gate_ref, up_ref = refs[parts : parts + 2]
    a_ref, u_ref, g_ref, x_out = refs[-4:]

    @pl.when(pl.program_id(0) == 0)
    def _():
        join_rows(refs[:parts], x_out)

    gate = dot_nn(x_out[...], gate_ref[...])
    up = dot_nn(x_out[...], up_ref[...])
    a_ref[...] = gate.astype(jnp.bfloat16)
    u_ref[...] = up.astype(jnp.bfloat16)
    g_ref[...] = (gate * jax.nn.sigmoid(gate) * up).astype(jnp.bfloat16)


def up_chunk(xs, weight, kept, index, count):
    rows = len(xs) * xs[0].shape[0]
    depth, width = weight.shape
    hidden = width // 2
    tile = tile_of(hidden)
    tiles = hidden // tile
    specs = [pl.BlockSpec(xs[0].shape, lambda t: (0, 0))] * len(xs)
    specs.append(pl.BlockSpec((depth, tile), lambda t: (0, t)))
    specs.append(pl.BlockSpec((depth, tile), lambda t: (0, tiles + t)))
    operands = [*xs, weight, weight]
    shapes = [jax.ShapeDtypeStruct((rows * count, hidden), jnp.bfloat16)] * 3 + [
        jax.ShapeDtypeStruct((rows * count, depth), jnp.bfloat16)
    ]
    aliases = {}
    if kept is not None:
        specs.extend([pl.BlockSpec(memory_space=pl.ANY)] * 4)
        aliases = {len(operands) + i: i for i in range(4)}
        operands.extend(kept)
    return pl.pallas_call(
        functools.partial(up_kernel, len(xs)),
        grid=(tiles,),
        in_specs=specs,
        out_specs=[pl.BlockSpec((rows, tile), lambda t: (index, t))] * 3
        + [pl.BlockSpec((rows, depth), lambda t: (index, 0))],
        out_shape=shapes,
        input_output_aliases=aliases,
        compiler_params=pltpu.CompilerParams(vmem_limit_bytes=KERNEL_VMEM),
        cost_estimate=SMALL_COST,
        name="up_chunk",
    )(*operands)


def down_kernel(parts, tiles, *refs):
    down_ref, a_ref, u_ref, gate_ref, up_ref = refs[parts : parts + 5]
    da_ref, du_ref, e_out, dx_ref, da_kept, du_kept = refs[-6:]
    step = pl.program_id(0)

    @pl.when(step == 0)
    def _():
        join_rows(refs[:parts], e_out)

    @pl.when(step < tiles)
    def _():
        grad = dot_nn(e_out[...], down_ref[...])
        gate = a_ref[...].astype(jnp.float32)
        up = u_ref[...].astype(jnp.float32)
        sigmoid = jax.nn.sigmoid(gate)
        da = (grad * up * sigmoid * (1.0 + gate * (1.0 - sigmoid))).astype(jnp.bfloat16)
        du = (grad * gate * sigmoid).astype(jnp.bfloat16)
        da_ref[...] = da
        du_ref[...] = du
        tile = da.shape[1]
        for index in range(tiles):

            @pl.when(step == index)
            def _():
                da_kept[:, index * tile : (index + 1) * tile] = da
                du_kept[:, index * tile : (index + 1) * tile] = du

    @pl.when(step >= tiles)
    def _():
        dx_ref[...] = (
            dot_nt(da_kept[...], gate_ref[...]) + dot_nt(du_kept[...], up_ref[...])
        ).astype(jnp.bfloat16)


def down_chunk(es, down_weight, a, u, weight, kept, index, count):
    rows = len(es) * es[0].shape[0]
    depth, width = weight.shape
    hidden = width // 2
    tile = tile_of(hidden)
    tiles = hidden // tile
    row_tile = tile_of(depth)

    def column(t):
        return jnp.minimum(t, tiles - 1)

    def row(t):
        return jnp.maximum(t - tiles, 0)

    specs = [pl.BlockSpec(es[0].shape, lambda t: (0, 0))] * len(es) + [
        pl.BlockSpec((depth, tile), lambda t: (0, column(t))),
        pl.BlockSpec((rows, tile), lambda t: (index, column(t))),
        pl.BlockSpec((rows, tile), lambda t: (index, column(t))),
        pl.BlockSpec((row_tile, hidden), lambda t: (row(t), 0)),
        pl.BlockSpec((row_tile, hidden), lambda t: (row(t), 1)),
    ]
    operands = [*es, down_weight, a, u, weight, weight]
    shapes = [
        jax.ShapeDtypeStruct((rows * count, hidden), jnp.bfloat16),
        jax.ShapeDtypeStruct((rows * count, hidden), jnp.bfloat16),
        jax.ShapeDtypeStruct((rows * count, depth), jnp.bfloat16),
        jax.ShapeDtypeStruct((rows, depth), jnp.bfloat16),
    ]
    aliases = {}
    if kept is not None:
        specs.extend([pl.BlockSpec(memory_space=pl.ANY)] * 3)
        aliases = {len(operands) + i: i for i in range(3)}
        operands.extend(kept)
    return pl.pallas_call(
        functools.partial(down_kernel, len(es), tiles),
        grid=(tiles + depth // row_tile,),
        in_specs=specs,
        out_specs=[
            pl.BlockSpec((rows, tile), lambda t: (index, column(t))),
            pl.BlockSpec((rows, tile), lambda t: (index, column(t))),
            pl.BlockSpec((rows, depth), lambda t: (index, 0)),
            pl.BlockSpec((rows, row_tile), lambda t: (0, row(t))),
        ],
        out_shape=shapes,
        input_output_aliases=aliases,
        scratch_shapes=[
            pltpu.VMEM((rows, hidden), jnp.bfloat16),
            pltpu.VMEM((rows, hidden), jnp.bfloat16),
        ],
        compiler_params=pltpu.CompilerParams(vmem_limit_bytes=KERNEL_VMEM),
        cost_estimate=SMALL_COST,
        name="down_chunk",
    )(*operands)


def weight_kernel(count, core_ref, x_ref, *refs):
    out_ref = refs[-1]
    column = 0
    for y_ref in refs[:count]:
        width = y_ref.shape[1]
        piece = 1024 if width % 1024 == 0 else width
        for first in range(0, width, piece):
            total = dot_tn(x_ref[...], y_ref[:, first : first + piece])
            place = slice(column + first, column + first + piece)
            if len(refs) > count + 1:
                total += refs[count][:, place].astype(jnp.float32)
            out_ref[:, place] = total.astype(jnp.bfloat16)
        column += width


def weight_product(x, ys, core, count, received):
    rows, depth = x.shape
    tile = depth // count
    total = sum(y.shape[1] for y in ys)
    side = 1 if received is None else 0
    block = pl.BlockSpec((tile, total), lambda t, c: (t, 0))
    specs = [pl.BlockSpec((rows, tile), lambda t, c: (0, 2 * t + lax.rem(c[0] + side, 2)))]
    specs += [pl.BlockSpec((rows, y.shape[1]), lambda t, c: (0, 0)) for y in ys]
    operands = [x, *ys]
    if received is not None:
        specs.append(block)
        operands.append(received)
    return pl.pallas_call(
        functools.partial(weight_kernel, len(ys)),
        grid_spec=pltpu.PrefetchScalarGridSpec(
            num_scalar_prefetch=1, grid=(count // 2,), in_specs=specs, out_specs=block
        ),
        out_shape=jax.ShapeDtypeStruct((depth // 2, total), jnp.bfloat16),
        compiler_params=pltpu.CompilerParams(vmem_limit_bytes=KERNEL_VMEM),
        cost_estimate=SMALL_COST,
        name="weight_product",
    )(core, *operands)


def residual_kernel(
    e_ref, hidden_ref, first_ref, second_ref, gain_ref, weight_ref, dh_ref, dz_ref, do_ref
):
    @pl.when(pl.program_id(0) == 0)
    def _():
        values = hidden_ref[...]
        inverse = lax.rsqrt(jnp.mean(values * values, axis=-1, keepdims=True) + EPSILON)
        scaled = values * inverse
        grad = first_ref[...].astype(jnp.float32) + second_ref[...].astype(jnp.float32)
        grad = grad * gain_ref[...]
        projection = jnp.mean(grad * scaled, axis=-1, keepdims=True)
        total = e_ref[...].astype(jnp.float32) + inverse * (grad - scaled * projection)
        dh_ref[...] = total
        dz_ref[...] = total.astype(jnp.bfloat16)

    do_ref[...] = dot_nn(dz_ref[...], weight_ref[...]).astype(jnp.bfloat16)


def residual_gradient(e, hidden_res, first, second, gain, weight):
    rows, depth = e.shape
    width = weight.shape[1]
    tile = tile_of(width)
    whole = pl.BlockSpec((rows, depth), lambda t: (0, 0))
    return pl.pallas_call(
        residual_kernel,
        grid=(width // tile,),
        in_specs=[
            whole,
            whole,
            whole,
            whole,
            pl.BlockSpec((1, depth), lambda t: (0, 0)),
            pl.BlockSpec((depth, tile), lambda t: (0, t)),
        ],
        out_specs=[whole, whole, pl.BlockSpec((rows, tile), lambda t: (0, t))],
        out_shape=[
            jax.ShapeDtypeStruct((rows, depth), jnp.float32),
            jax.ShapeDtypeStruct((rows, depth), jnp.bfloat16),
            jax.ShapeDtypeStruct((rows, width), jnp.bfloat16),
        ],
        compiler_params=pltpu.CompilerParams(vmem_limit_bytes=KERNEL_VMEM),
        cost_estimate=SMALL_COST,
        name="residual_gradient",
    )(e, hidden_res, first, second, gain, weight)


def tie(value, *others):
    return lax.optimization_barrier((value, others))[0]


def together(*values):
    return lax.optimization_barrier(values)


class Mover:
    def __init__(self):
        self.dp_count = lax.axis_size("dp")
        self.ring = lax.axis_size("tensor")
        self.groups = [list(range(core, self.dp_count, 2)) for core in range(2)]

    def swap(self, value, step):
        return lax.ppermute(value, "dp", [(i, i ^ step) for i in range(self.dp_count)])

    def gather(self, shard):
        return lax.all_gather(shard, "dp", axis=0, tiled=True)

    def scatter(self, total):
        return lax.psum_scatter(
            total, "dp", scatter_dimension=0, tiled=True, axis_index_groups=self.groups
        )

    def hop(self, value, shift=1):
        return lax.ppermute(
            value, "tensor", [(i, (i + shift) % self.ring) for i in range(self.ring)]
        )

    def spread(self, value):
        ring = self.ring
        return [value] + [
            lax.ppermute(value, "tensor", [(i, (i - j) % ring) for i in range(ring)])
            for j in range(1, ring)
        ]

    def exchange(self, parts, shift):
        ring = self.ring
        return [parts[0]] + [
            lax.ppermute(parts[j], "tensor", [(i, (i + shift * j) % ring) for i in range(ring)])
            for j in range(1, ring)
        ]


def add(first, second):
    return (first.astype(jnp.float32) + second.astype(jnp.float32)).astype(jnp.bfloat16)


def back_norm(grad_normed, scaled, inverse, scale_row):
    grad_scaled = grad_normed * scale_row
    projection = jnp.mean(grad_scaled * scaled, axis=-1, keepdims=True)
    return inverse * (grad_scaled - scaled * projection)


def per_device(
    tokens,
    seq_lengths,
    attention_gain,
    query_matrix,
    key_matrix,
    value_matrix,
    output_weight,
    feedforward_gain,
    gate_weight,
    up_weight,
    down_weight,
    cotangent,
):
    mover = Mover()
    dp_count = mover.dp_count
    ring = mover.ring
    core = (lax.axis_index("dp") % 2).astype(jnp.int32).reshape(1)
    ring_place = lax.axis_index("tensor")
    _, local_rows, model_width = tokens.shape
    complete_rows = local_rows * ring
    query_width = query_matrix.shape[1]
    key_width = key_matrix.shape[1]
    joint_width = query_width + 2 * key_width
    hidden = gate_weight.shape[1]
    f32 = jnp.float32
    b16 = jnp.bfloat16

    doc_ids, positions = layout(seq_lengths, complete_rows)
    row_index = jnp.arange(complete_rows, dtype=jnp.int32)
    doc_ids = jnp.where(doc_ids[0] < PIECES, doc_ids[0], PIECES + row_index)

    def to_relative(values):
        view = values.reshape((ring, local_rows) + values.shape[1:])
        return jnp.roll(view, -(ring_place + 1), axis=0)[::-1].reshape(values.shape)

    doc_ids = to_relative(doc_ids)
    cosine, sine = rope_tables(to_relative(positions[0]), HEAD_SIZE)
    cosine_table = jnp.tile(cosine, (1, 128 // cosine.shape[1]))
    sine_table = jnp.tile(jnp.concatenate([-sine, sine], axis=1), (1, 128 // HEAD_SIZE))
    place = ring_place.astype(jnp.int32).reshape(1)

    local_tokens = tokens[0]
    local_cotangent = cotangent[0]
    joint_matrix = jnp.concatenate([query_matrix, key_matrix, value_matrix], axis=1)
    own_gains = jnp.stack([attention_gain, feedforward_gain], axis=1)
    joint_full = mover.gather(
        jnp.concatenate([joint_matrix, jnp.pad(own_gains, ((0, 0), (0, 126)))], axis=1)
    )
    token = mover.hop(local_tokens)
    output_parts = mover.spread(output_weight.T)
    up_shard = jnp.concatenate([gate_weight, up_weight], axis=1)
    down_shard = down_weight.T
    token, output_ring, cosine_table, sine_table, doc_ids, up_shard, down_shard = together(
        token, join(output_parts, 1), cosine_table, sine_table, doc_ids, up_shard, down_shard
    )
    output_full = mover.gather(output_ring)
    up_full = mover.gather(tie(up_shard, output_ring))
    down_full = mover.gather(tie(down_shard, output_ring))
    gains = joint_full[:, joint_width : joint_width + 2].T.astype(f32)
    gain_one, gain_two = gains[:1], gains[1:]

    def projection(x, index):
        return project(
            x,
            gain_one,
            joint_full,
            cosine_table,
            sine_table,
            index,
            query_width,
            query_width + key_width,
        )

    projected = [projection(local_tokens, 0)]
    for j in range(1, ring):
        if j + 1 < ring:
            moved = mover.hop(token)
        else:
            moved = mover.hop(local_cotangent)
        projected.append(projection(tie(token, projected[-1]), j))
        if j + 1 < ring:
            token, projected[-1] = together(moved, projected[-1])
    cotangent_chunks = [local_cotangent, moved]
    joint = join([p[1] for p in projected], 0)
    attended, totals = attention_forward(joint, doc_ids, place, ring, query_width, key_width)
    cotangent_chunks[1], attended = together(cotangent_chunks[1], attended)
    attended_parts = together(*mover.exchange(jnp.split(attended, ring, axis=0), -1))
    attended_local = join(attended_parts, 1)
    hidden_res, normed_two = after_attention(
        attended_local, output_full, local_tokens, gain_two
    )

    def upward(chunks, kept, index):
        return up_chunk(chunks, up_full, kept, index, ring // 2)

    def downward(chunks, kept, index):
        result = down_chunk(
            chunks, down_full, gate_all, up_all, up_full, kept, index, ring // 2
        )
        return result[:3], jnp.split(result[3], 2, axis=0)

    normed_chunks = [normed_two]
    kept = None
    for j in range(1, ring):
        moved = mover.hop(normed_chunks[-1])
        if j % 2 and j > 1:
            kept = upward(normed_chunks[j - 3 : j - 1], kept, (j - 3) // 2)
            moved, kept = together(moved, kept)
        normed_chunks.append(moved)
    moved = mover.hop(cotangent_chunks[-1])
    kept = upward(normed_chunks[ring - 2 :], kept, ring // 2 - 1)
    moved, kept = together(moved, kept)
    cotangent_chunks.append(moved)
    gate_all, up_all, product, normed_all = kept
    kept = None
    grads = []
    for j in range(3, ring):
        moved = mover.hop(cotangent_chunks[-1])
        if j % 2:
            kept, parts = downward(cotangent_chunks[j - 3 : j - 1], kept, (j - 3) // 2)
            moved, kept, parts = together(moved, kept, parts)
            grads.extend(parts)
        cotangent_chunks.append(moved)
    total = grads[1]
    moved = mover.hop(total)
    kept, parts = downward(tie(cotangent_chunks[ring - 2 :], total), kept, ring // 2 - 1)
    moved, kept, parts = together(moved, kept, parts)
    grads.extend(parts)
    grad_gate, grad_up, cotangent_all = kept

    def weights(x, ys, received=None):
        return weight_product(x, ys, core, dp_count, received)

    for j in range(2, ring):
        total = add(moved, grads[j])
        moved = mover.hop(total)
        if j == 2:
            down_part = weights(tie(cotangent_all, total), [product])
            up_part = weights(tie(normed_all, down_part), [grad_gate, grad_up])
            moved, down_part, up_part = together(moved, down_part, up_part)
            down_part = mover.swap(down_part, 1)
            up_part = mover.swap(up_part, 1)
        if j == 3:
            branch = transposed_product(tie(product, total), down_full, b16)
            down_part = weights(tie(cotangent_all, branch), [product], down_part)
            moved, branch, down_part = together(moved, branch, down_part)
    down_out = mover.scatter(down_part)
    grad_hidden, grad_branch, grad_attended_local = residual_gradient(
        local_cotangent, hidden_res, moved, grads[0], gain_two, output_full
    )

    grad_attended = mover.exchange(jnp.split(grad_attended_local, ring, axis=1), 1)
    up_part = weights(tie(normed_all, grad_branch), [grad_gate, grad_up], up_part)
    output_part = weights(tie(grad_branch, up_part), [attended_local])
    grad_attended, up_part, output_part = together(grad_attended, up_part, output_part)
    up_out = mover.scatter(tie(up_part, down_part))
    output_part = mover.swap(output_part, 1)
    branch_parts = jnp.split(branch, ring, axis=0)
    moved = mover.hop(tie(branch_parts[1], grad_attended))
    grad_joint = attention_backward(
        joint,
        attended,
        join(grad_attended, 0),
        totals,
        doc_ids,
        cosine_table,
        sine_table,
        place,
        ring,
        query_width,
        key_width,
    )
    branch_moved, grad_joint = together(moved, grad_joint)
    grads = jnp.split(transposed_product(grad_joint, joint_full, b16), ring, axis=0)
    normed_one = join([p[0] for p in projected], 0)
    moved = grads[0]
    for j in range(1, ring):
        total = grads[1] if j == 1 else add(moved, grads[j])
        moved = mover.hop(total)
        if j == 1:
            joint_part = weights(tie(normed_one, total), [grad_joint])
            output_part = weights(
                tie(grad_branch, joint_part), [attended_local], output_part
            )
            moved, joint_part, output_part = together(moved, joint_part, output_part)
            joint_part = mover.swap(joint_part, 1)
            output_out = mover.scatter(tie(output_part, up_part))
        if j == 2:
            joint_part = weights(tie(normed_one, total), [grad_joint], joint_part)
            moved, joint_part, up_out = together(moved, joint_part, up_out)
            joint_out = mover.scatter(tie(joint_part, output_part))
    scaled_one, inverse_one = norm_rows(local_tokens.astype(f32))
    local_one = moved.astype(f32) + grads[0].astype(f32)
    input_gradient = grad_hidden + back_norm(local_one, scaled_one, inverse_one, gain_one)
    branch_moved = tie(branch_moved, moved)
    for j in range(2, ring):
        branch_moved = mover.hop(add(branch_moved, branch_parts[j]))
    block_output = (
        hidden_res + (branch_moved.astype(f32) + branch_parts[0].astype(f32))
    ).astype(b16)
    output_parts = jnp.split(output_out, ring, axis=1)
    moved = output_parts[0]
    for j in range(1, ring):
        moved = mover.hop(output_parts[1] if j == 1 else add(moved, output_parts[j]), -1)
    output_out = (moved.astype(f32) + output_parts[0].astype(f32)).T
    joint_out = joint_out.astype(f32)

    gate_out = up_out[:, :hidden].astype(f32)
    up_out = up_out[:, hidden:].astype(f32)
    sums = jnp.stack(
        [
            jnp.sum(joint_out * joint_matrix.astype(f32), axis=1) / attention_gain.astype(f32),
            jnp.sum(gate_out * gate_weight.astype(f32) + up_out * up_weight.astype(f32), axis=1)
            / feedforward_gain.astype(f32),
        ]
    )
    gain_out = sums
    for shift in range(1, ring):
        gain_out = gain_out + lax.ppermute(
            sums, "tensor", [(i, (i + shift) % ring) for i in range(ring)]
        )
    return (
        block_output[None],
        input_gradient[None],
        gain_out[0],
        joint_out[:, :query_width],
        joint_out[:, query_width : query_width + key_width],
        joint_out[:, query_width + key_width :],
        output_out,
        gain_out[1],
        gate_out,
        up_out,
        down_out.astype(f32).T,
    )


def solution(mesh):
    return jax.shard_map(
        per_device,
        mesh=mesh,
        in_specs=(
            P("dp", "tensor", None),
            P("dp", None),
            P("dp"),
            P("dp", "tensor"),
            P("dp", "tensor"),
            P("dp", "tensor"),
            P("tensor", "dp"),
            P("dp"),
            P("dp", "tensor"),
            P("dp", "tensor"),
            P("tensor", "dp"),
            P("dp", "tensor", None),
        ),
        out_specs=(
            P("dp", "tensor", None),
            P("dp", "tensor", None),
            P("dp"),
            P("dp", "tensor"),
            P("dp", "tensor"),
            P("dp", "tensor"),
            P("tensor", "dp"),
            P("dp"),
            P("dp", "tensor"),
            P("dp", "tensor"),
            P("tensor", "dp"),
        ),
        check_vma=False,
    )
```

time: 975 us -> 783 us (0.80)
  Pallas kernels: 0 us -> 277 us
  matrix products: 226 us -> 0 us
  local copies, waits for them, and re-layouts: 112 us -> 34.5 us
  waiting for transfers between devices: 436 us -> 362 us
  other arithmetic: 99.2 us -> 38.4 us
  starting transfers between devices: 89.6 us -> 45.6 us
  between operations: 3.62 us -> 14.9 us
    pallas_call x0 -> x27, Pallas kernels: none -> 277 us  [the longest x8 70.8 us: weight_product(): pl.pallas_call(functools.partial(weight_kernel, len(ys)), grid_spec=pltpu...]
    ppermute x131 -> x37, waiting for transfers between devices: 436 us -> 192 us  [the longest x21 139 us: hop(): lax.ppermute(value, 'tensor', [(i, (i + shift) % self.ring) for i in rang...]
    dot_general x27 -> x0, matrix products: 226 us -> none  [the longest x10 106 us: contract(): lax.dot_general(left, right, (((left_dim,), (right_dim,)), ((), ())), pre...]
    reduce_scatter x0 -> x4, waiting for transfers between devices: none -> 168 us  [scatter(): lax.psum_scatter(total, 'dp', scatter_dimension=0, tiled=True, axis_index...]
    ppermute x131 -> x37, starting transfers between devices: 89.6 us -> 45.3 us  [the longest x21 27.1 us: hop(): lax.ppermute(value, 'tensor', [(i, (i + shift) % self.ring) for i in rang...]
    unnamed x304 -> x74, local copies, waits for them, and re-layouts: 55.8 us -> 11.5 us
    convert_element_type x24 -> x9, other arithmetic: 36.8 us -> 15.7 us  [the longest x8 14.6 us: add(): (first.astype(jnp.float32) + second.astype(jnp.float32)).astype(jnp.bfloa...]
    add x15 -> x1, other arithmetic: 14.7 us -> 0.01 us  [per_device(): gain_out + lax.ppermute(sums, 'tensor', [(i, (i + shift) % ring) for i in...]
  transfers between devices with their start and end apart: 131 -> 45, of which waited for: 49 -> 16; matrix products, arithmetic and copies ran while one was open for 38% -> 8% of each run, Pallas kernels for 0% -> 36%
where the time goes in v2:
time: 783 us; the launch traced here: 773 us
  waiting for transfers between devices  362 us (46%)
  Pallas kernels  277 us (35%)
  starting transfers between devices  45.6 us (6%)
  other arithmetic  38.4 us (5%)
  local copies, waits for them, and re-layouts  34.5 us (4%)
  between operations  14.9 us (2%)
    reduce_scatter x4, waiting for transfers between devices, scatter(): lax.psum_scatter(total, 'dp', scatter_dimension=0, tiled=True, axis_index...  168 us
    ppermute x21, waiting for transfers between devices, hop(): lax.ppermute(value, 'tensor', [(i, (i + shift) % self.ring) for i in rang...  139 us
    pallas_call x8, Pallas kernels, weight_product(): pl.pallas_call(functools.partial(weight_kernel, len(ys)), grid_spec=pltpu...  70.8 us
    pallas_call x2, Pallas kernels, down_chunk(): pl.pallas_call(functools.partial(down_kernel, len(es), tiles), grid=(tile...  47.2 us
    ppermute x3, waiting for transfers between devices, spread(): lax.ppermute(value, 'tensor', [(i, (i - j) % ring) for i in range(ring)])  34.7 us
    pallas_call x1, Pallas kernels, attention_backward(): pl.pallas_call(functools.partial(backward_kernel, count), grid_spec=spec,...  34.2 us
    pallas_call x2, Pallas kernels, up_chunk(): pl.pallas_call(functools.partial(up_kernel, len(xs)), grid=(tiles,), in_s...  29.3 us
    ppermute x21, starting transfers between devices, hop(): lax.ppermute(value, 'tensor', [(i, (i + shift) % self.ring) for i in rang...  27.1 us
  transfers between devices with their start and end apart: 45, of which 16 were waited for; matrix products, arithmetic and copies ran while one was open for 8% of the time, Pallas kernels for 36%

profile of v2, /device:TPU:0, one launch (start us, length us, event | category | flops | bytes accessed | tf_op | source)
XLA Modules:
  0.0 773.0 jit_solution(10953299784025391851)
XLA Ops:
  27.2 34.7 %collective-permute-done.3.refs_2_ = bf16[256,512]{1,0:T(8,128)(2,1)} collective-permute-done((bf16[256,512]{1,0:T(8,128)(2,1)S(1)}, bf16[256,512]{1,0:T(8,128)(2,1)}, u32[]{:S(2)}, u32[]{:S(2)}) %collective-permute-start.3) | collective-permute-done | bytes 262176 | tf_op jit(solution)/shard_map/ppermute | solution.py:750
  81.8 10.1 %collective-permute-done.5.x_ref = bf16[256,2048]{1,0:T(8,128)(2,1)} collective-permute-done((bf16[256,2048]{1,0:T(8,128)(2,1)}, bf16[256,2048]{1,0:T(8,128)(2,1)}, u32[]{:S(2)}, u32[]{:S(2)}) %collective-permute-start.5) | collective-permute-done | bytes 1048608 | tf_op jit(solution)/shard_map/ppermute | solution.py:743
  97.5 22.6 %collective-permute-done.6.x_ref = bf16[256,2048]{1,0:T(8,128)(2,1)} collective-permute-done((bf16[256,2048]{1,0:T(8,128)(2,1)}, bf16[256,2048]{1,0:T(8,128)(2,1)}, u32[]{:S(2)}, u32[]{:S(2)}) %collective-permute-start.6) | collective-permute-done | bytes 1048608 | tf_op jit(solution)/shard_map/ppermute | solution.py:743
  129.7 20.1 %attend.1 = (bf16[1024,512]{1,0:T(8,128)(2,1)}, f32[8,1024]{1,0:T(8,128)}) custom-call(s32[1]{0:T(128)} %bitcast.1.place_ref, bf16[1024,768]{1,0:T(8,128)(2,1)} %join.6.q_ref.kv_ref, bf16[1024,768]{1,0:T(8,128)(2,1)} %join.6.q_ref.kv_ref, s32[1,1024]{1,0:T(1,128)} %bitcast.50, s32[1024,1]{1,0:T(8,128)} %copy.102.dock_ref), custom_call_target="tpu_custom_call" | custom-call | flops 1 | bytes 1 | tf_op jit(solution)/shard_map/attend/pallas_call | solution.py:241
  181.4 22.2 %collective-permute-done.11.refs_1_ = bf16[256,2048]{1,0:T(8,128)(2,1)S(1)} collective-permute-done((bf16[256,2048]{1,0:T(8,128)(2,1)}, bf16[256,2048]{1,0:T(8,128)(2,1)S(1)}, u32[]{:S(2)}, u32[]{:S(2)}) %collective-permute-start.11) | collective-permute-done | bytes 1048608 | tf_op jit(solution)/shard_map/ppermute | solution.py:743
  205.3 22.7 %collective-permute-done.12.refs_0_ = bf16[256,2048]{1,0:T(8,128)(2,1)S(1)} collective-permute-done((bf16[256,2048]{1,0:T(8,128)(2,1)S(1)}, bf16[256,2048]{1,0:T(8,128)(2,1)S(1)}, u32[]{:S(2)}, u32[]{:S(2)}) %collective-permute-start.12) | collective-permute-done | bytes 1048608 | tf_op jit(solution)/shard_map/ppermute | solution.py:743
  230.9 15.0 %up_chunk.2 = (bf16[1024,2048]{1,0:T(8,128)(2,1)}, bf16[1024,2048]{1,0:T(8,128)(2,1)}, bf16[1024,2048]{1,0:T(8,128)(2,1)}, bf16[1024,2048]{1,0:T(8,128)(2,1)}) custom-call(bf16[256,2048]{1,0:T(8,128)(2,1)} %get-tuple-element.150.refs_0_, bf16[256,2048]{1,0:T(8,128)(2,1)} %copy-done.18, ...), custom_call_target="tpu_custom_call" | custom-call | flops 1 | bytes 1 | tf_op jit(solution)/shard_map/up_chunk/pallas_call | solution.py:529
  246.0 10.0 %collective-permute-done.13.refs_1_ = bf16[256,2048]{1,0:T(8,128)(2,1)} collective-permute-done((bf16[256,2048]{1,0:T(8,128)(2,1)S(1)}, bf16[256,2048]{1,0:T(8,128)(2,1)}, u32[]{:S(2)}, u32[]{:S(2)}) %collective-permute-start.13) | collective-permute-done | bytes 1048608 | tf_op jit(solution)/shard_map/ppermute | solution.py:743
  256.0 14.2 %up_chunk.3 = (bf16[1024,2048]{1,0:T(8,128)(2,1)}, bf16[1024,2048]{1,0:T(8,128)(2,1)}, bf16[1024,2048]{1,0:T(8,128)(2,1)}, bf16[1024,2048]{1,0:T(8,128)(2,1)}) custom-call(bf16[256,2048]{1,0:T(8,128)(2,1)} %copy-done.17, bf16[256,2048]{1,0:T(8,128)(2,1)} %collective-permute-done.13.refs_1_, ...), custom_call_target="tpu_custom_call", output_to_operand_aliasing={{0}: (4, {}), {1}: (5, {}), {2}: (6, {}), {3}: (7, {})} | custom-call | flops 1 | bytes 1 | tf_op jit(solution)/shard_map/up_chunk/pallas_call | solution.py:529
  274.2 23.6 %down_chunk.2 = (bf16[1024,2048]{1,0:T(8,128)(2,1)}, bf16[1024,2048]{1,0:T(8,128)(2,1)}, bf16[1024,2048]{1,0:T(8,128)(2,1)}, bf16[512,2048]{1,0:T(8,128)(2,1)}) custom-call(bf16[256,2048]{1,0:T(8,128)(2,1)} %bitcast.39, bf16[256,2048]{1,0:T(8,128)(2,1)} %copy-done.15, bf16[2048,2048]{1,0:T(8,128)(2,1)} %all-gather.11.cloned.1.call-done.refs_2_.weight_ref, ...), custom_call_target="tpu_custom_call" | custom-call | flops 1 | bytes 1 | tf_op jit(solution)/shard_map/down_chunk/pallas_call | solution.py:610
  303.5 23.6 %down_chunk.3 = (bf16[1024,2048]{1,0:T(8,128)(2,1)}, bf16[1024,2048]{1,0:T(8,128)(2,1)}, bf16[1024,2048]{1,0:T(8,128)(2,1)}, bf16[512,2048]{1,0:T(8,128)(2,1)}) custom-call(bf16[256,2048]{1,0:T(8,128)(2,1)} %copy-done.12, bf16[256,2048]{1,0:T(8,128)(2,1)} %copy-done.13, ...), custom_call_target="tpu_custom_call", output_to_operand_aliasing={{0}: (7, {}), {1}: (8, {}), {2}: (9, {})} | custom-call | flops 1 | bytes 1 | tf_op jit(solution)/shard_map/down_chunk/pallas_call | solution.py:610
  332.4 8.7 %weight_product.8 = bf16[1024,2048]{1,0:T(8,128)(2,1)} custom-call(s32[1]{0:T(128)} %bitcast.13.core_ref, bf16[1024,2048]{1,0:T(8,128)(2,1)} %get-tuple-element.198.x_ref, bf16[1024,2048]{1,0:T(8,128)(2,1)} %get-tuple-element.197.refs_0_.x_ref), custom_call_target="tpu_custom_call" | custom-call | flops 1 | bytes 1 | tf_op jit(solution)/shard_map/weight_product/pallas_call | solution.py:659
  341.0 14.6 %weight_product.9 = bf16[1024,4096]{1,0:T(8,128)(2,1)} custom-call(s32[1]{0:T(128)} %bitcast.13.core_ref, bf16[1024,2048]{1,0:T(8,128)(2,1)} %get-tuple-element.205.x_ref, bf16[1024,2048]{1,0:T(8,128)(2,1)} %get-tuple-element.193.refs_0_, bf16[1024,2048]{1,0:T(8,128)(2,1)} %get-tuple-element.194.refs_1_), custom_call_target="tpu_custom_call" | custom-call | flops 1 | bytes 1 | tf_op jit(solution)/shard_map/weight_product/pallas_call | solution.py:659
  357.9 13.4 %transposed.2 = bf16[1024,2048]{1,0:T(8,128)(2,1)} custom-call(bf16[1024,2048]{1,0:T(8,128)(2,1)} %get-tuple-element.197.refs_0_.x_ref, bf16[2048,2048]{1,0:T(8,128)(2,1)} %all-gather.11.cloned.1.call-done.refs_2_.weight_ref), custom_call_target="tpu_custom_call" | custom-call | flops 1 | bytes 1 | tf_op jit(solution)/shard_map/transposed/pallas_call | solution.py:412
  375.1 9.5 %weight_product.10 = bf16[1024,2048]{1,0:T(8,128)(2,1)} custom-call(s32[1]{0:T(128)} %bitcast.13.core_ref, bf16[1024,2048]{1,0:T(8,128)(2,1)} %get-tuple-element.198.x_ref, bf16[1024,2048]{1,0:T(8,128)(2,1)} %get-tuple-element.197.refs_0_.x_ref, bf16[1024,2048]{1,0:T(8,128)(2,1)} %collective-permute-done.18.refs_1_), custom_call_target="tpu_custom_call" | custom-call | flops 1 | bytes 1 | tf_op jit(solution)/shard_map/weight_product/pallas_call | solution.py:659
  385.6 9.7 %residual_gradient.1 = (f32[256,2048]{1,0:T(8,128)}, bf16[256,2048]{1,0:T(8,128)(2,1)}, bf16[256,2048]{1,0:T(8,128)(2,1)}) custom-call(bf16[256,2048]{1,0:T(8,128)(2,1)} %bitcast.40, f32[256,2048]{1,0:T(8,128)} %get-tuple-element.148.hidden_ref, bf16[256,2048]{1,0:T(8,128)(2,1)} %copy-done.20, bf16[256,2048]{1,0:T(8,128)(2,1)} %get-tuple-element.202.second_ref, ...), custom_call_target="tpu_custom_call" | custom-call | flops 1 | bytes 1 | tf_op jit(solution)/shard_map/residual_gradient/pallas_call | solution.py:694
  401.7 15.3 %weight_product.11 = bf16[1024,4096]{1,0:T(8,128)(2,1)} custom-call(s32[1]{0:T(128)} %bitcast.13.core_ref, bf16[1024,2048]{1,0:T(8,128)(2,1)} %get-tuple-element.205.x_ref, bf16[1024,2048]{1,0:T(8,128)(2,1)} %get-tuple-element.193.refs_0_, bf16[1024,2048]{1,0:T(8,128)(2,1)} %get-tuple-element.194.refs_1_, bf16[1024,4096]{1,0:T(8,128)(2,1)} %collective-permute-done.22.refs_2_), custom_call_target="tpu_custom_call" | custom-call | flops 1 | bytes 1 | tf_op jit(solution)/shard_map/weight_product/pallas_call | solution.py:659
  428.5 34.2 %attend_back.1.x_ref.refs_0_ = bf16[1024,768]{1,0:T(8,128)(2,1)} custom-call(s32[1]{0:T(128)} %bitcast.1.place_ref, bf16[1024,768]{1,0:T(8,128)(2,1)} %join.6.q_ref.kv_ref, bf16[1024,768]{1,0:T(8,128)(2,1)} %join.6.q_ref.kv_ref, bf16[1024,512]{1,0:T(8,128)(2,1)} %get-tuple-element.142.o_ref, bf16[1024,512]{1,0:T(8,128)(2,1)} %join.8.do_ref, ...), custom_call_target="tpu_custom_call" | custom-call | flops 1 | bytes 1 | tf_op jit(solution)/shard_map/attend_back/pallas_call | solution.py:376
  488.1 10.9 %collective-permute-done.24 = bf16[256,2048]{1,0:T(8,128)(2,1)S(1)} collective-permute-done((bf16[256,2048]{1,0:T(8,128)(2,1)S(1)}, bf16[256,2048]{1,0:T(8,128)(2,1)S(1)}, u32[]{:S(2)}, u32[]{:S(2)}) %collective-permute-start.24) | collective-permute-done | bytes 1048608 | tf_op jit(solution)/shard_map/ppermute | solution.py:743
  504.4 45.9 %reduce-scatter.9.cloned.1.call-done = bf16[256,2048]{1,0:T(8,128)(2,1)} async-done(((bf16[1024,2048]{1,0:T(8,128)(2,1)}), bf16[256,2048]{1,0:T(8,128)(2,1)}) %reduce-scatter.9.cloned.1.call-update) | async-done | bytes 1048592 | tf_op jit(solution)/shard_map/reduce_scatter | solution.py:738
  565.6 74.4 %reduce-scatter.5.cloned.1.call-done = bf16[256,4096]{1,0:T(8,128)(2,1)} async-done(((bf16[1024,4096]{1,0:T(8,128)(2,1)}), bf16[256,4096]{1,0:T(8,128)(2,1)}) %reduce-scatter.5.cloned.1.call-update) | async-done | bytes 2097168 | tf_op jit(solution)/shard_map/reduce_scatter | solution.py:738
  647.8 47.9 %reduce-scatter.11.cloned.1.call-done = bf16[256,2048]{1,0:T(8,128)(2,1)} async-done(((bf16[1024,2048]{1,0:T(8,128)(2,1)}), bf16[256,2048]{1,0:T(8,128)(2,1)}) %reduce-scatter.11.cloned.1.call-update) | async-done | bytes 1048592 | tf_op jit(solution)/shard_map/reduce_scatter | solution.py:738
  711.2 20.7 %collective-permute-done.29 = bf16[256,2048]{1,0:T(8,128)(2,1)S(1)} collective-permute-done((bf16[256,2048]{1,0:T(8,128)(2,1)S(1)}, bf16[256,2048]{1,0:T(8,128)(2,1)S(1)}, u32[]{:S(2)}, u32[]{:S(2)}) %collective-permute-start.29) | collective-permute-done | bytes 1048608 | tf_op jit(solution)/shard_map/ppermute | solution.py:743
  744.3 16.5 %collective-permute-done.30 = bf16[256,2048]{1,0:T(8,128)(2,1)} collective-permute-done((bf16[256,2048]{1,0:T(8,128)(2,1)}, bf16[256,2048]{1,0:T(8,128)(2,1)}, u32[]{:S(2)}, u32[]{:S(2)}) %collective-permute-start.30) | collective-permute-done | bytes 1048608 | tf_op jit(solution)/shard_map/ppermute | solution.py:743
  (237 shorter events, 217.7 us)
Async XLA Ops:
  7.2 60.6 %all-gather.5.cloned.1.call-start = ((), (), s32[]{:S(2)}) async-start(), calls=%async_computation.4 | async-start | bytes 4128768 | tf_op jit(solution)/shard_map/all_gather | solution.py:735
  10.8 161.7 %all-gather.7.cloned.1.call-start = ((), (), s32[]{:S(2)}) async-start(), calls=%async_computation.5 | async-start | bytes 9437184 | tf_op jit(solution)/shard_map/all_gather | solution.py:735
  17.1 44.9 %collective-permute-start.3 = (bf16[256,512]{1,0:T(8,128)(2,1)S(1)}, bf16[256,512]{1,0:T(8,128)(2,1)}, u32[]{:S(2)}, u32[]{:S(2)}) collective-permute-start(bf16[256,512]{1,0:T(8,128)(2,1)S(1)} %bitcast.46), channel_id=1, source_target_pairs={{0,2},{1,3},{2,0},{3,1},{4,6},{5,7},{6,4},{7,5},{8,10},{9,11},{10,... | collective-permute-start | bytes 786440 | tf_op jit(solution)/shard_map/ppermute | solution.py:750
  17.1 44.9 %collective-permute-start.4 = (bf16[256,512]{1,0:T(8,128)(2,1)S(1)}, bf16[256,512]{1,0:T(8,128)(2,1)}, u32[]{:S(2)}, u32[]{:S(2)}) collective-permute-start(bf16[256,512]{1,0:T(8,128)(2,1)S(1)} %bitcast.47), channel_id=1, source_target_pairs={{0,1},{1,2},{2,3},{3,0},{4,5},{5,6},{6,7},{7,4},{8,9},{9,10},{10,1... | collective-permute-start | bytes 786440 | tf_op jit(solution)/shard_map/ppermute | solution.py:750
  18.1 46.1 %collective-permute-start.1 = (bf16[256,2048]{1,0:T(8,128)(2,1)}, bf16[256,2048]{1,0:T(8,128)(2,1)}, u32[]{:S(2)}, u32[]{:S(2)}) collective-permute-start(bf16[256,2048]{1,0:T(8,128)(2,1)} %bitcast.36), channel_id=1, source_target_pairs={{0,1},{1,2},{2,3},{3,0},{4,5},{5,6},{6,7},{7,4},{8,9},{9,10},{10,1... | collective-permute-start | bytes 3145736 | tf_op jit(solution)/shard_map/ppermute | solution.py:743
  64.3 166.6 %all-gather.9.cloned.1.call-start = ((), (), s32[]{:S(2)}) async-start(), calls=%async_computation.6 | async-start | bytes 18874368 | tf_op jit(solution)/shard_map/all_gather | solution.py:735
  65.1 209.2 %all-gather.11.cloned.1.call-start = ((), (), s32[]{:S(2)}) async-start(), calls=%async_computation.7 | async-start | bytes 9437184 | tf_op jit(solution)/shard_map/all_gather | solution.py:735
  65.6 484.7 %reduce-scatter.9.cloned.1.call-start = ((), (), s32[]{:S(2)}) async-start(), calls=%async_computation.10 | async-start | bytes 5242880 | tf_op jit(solution)/shard_map/reduce_scatter | solution.py:738
  91.9 28.2 %collective-permute-start.6 = (bf16[256,2048]{1,0:T(8,128)(2,1)}, bf16[256,2048]{1,0:T(8,128)(2,1)}, u32[]{:S(2)}, u32[]{:S(2)}) collective-permute-start(bf16[256,2048]{1,0:T(8,128)(2,1)} %collective-permute-done.5.x_ref), channel_id=1, source_target_pairs={{0,1},{1,2},{2,3},{3,0},{4,5},{5,6},{6,7},{7,4},{8,9},{9,10},{10,1... | collective-permute-start | bytes 3145736 | tf_op jit(solution)/shard_map/ppermute | solution.py:743
  91.9 57.9 %collective-permute-start = (bf16[256,2048]{1,0:T(8,128)(2,1)S(1)}, bf16[256,2048]{1,0:T(8,128)(2,1)S(1)}, u32[]{:S(2)}, u32[]{:S(2)}) collective-permute-start(bf16[256,2048]{1,0:T(8,128)(2,1)S(1)} %bitcast.41), channel_id=1, source_target_pairs={{0,1},{1,2},{2,3},{3,0},{4,5},{5,6},{6,7},{7,4},{8,9},{9,10},{10,1... | collective-permute-start | bytes 3145736 | tf_op jit(solution)/shard_map/ppermute | solution.py:743
  228.0 28.0 %collective-permute-start.13 = (bf16[256,2048]{1,0:T(8,128)(2,1)S(1)}, bf16[256,2048]{1,0:T(8,128)(2,1)}, u32[]{:S(2)}, u32[]{:S(2)}) collective-permute-start(bf16[256,2048]{1,0:T(8,128)(2,1)S(1)} %collective-permute-done.12.refs_0_), channel_id=1, source_target_pairs={{0,1},{1,2},{2,3},{3,0},{4,5},{5,6},{6,7},{7,4},{8,9},{9,10},{10,1... | collective-permute-start | bytes 3145736 | tf_op jit(solution)/shard_map/ppermute | solution.py:743
  228.5 45.3 %collective-permute-start.10 = (bf16[256,2048]{1,0:T(8,128)(2,1)S(1)}, bf16[256,2048]{1,0:T(8,128)(2,1)S(1)}, u32[]{:S(2)}, u32[]{:S(2)}) collective-permute-start(bf16[256,2048]{1,0:T(8,128)(2,1)S(1)} %collective-permute-done.refs_1_), channel_id=1, source_target_pairs={{0,1},{1,2},{2,3},{3,0},{4,5},{5,6},{6,7},{7,4},{8,9},{9,10},{10,1... | collective-permute-start | bytes 3145736 | tf_op jit(solution)/shard_map/ppermute | solution.py:743
  355.6 46.1 %collective-permute-start.22 = (bf16[1024,4096]{1,0:T(8,128)(2,1)}, bf16[1024,4096]{1,0:T(8,128)(2,1)}, u32[]{:S(2)}, u32[]{:S(2)}) collective-permute-start(bf16[1024,4096]{1,0:T(8,128)(2,1)} %weight_product.9), channel_id=1, source_target_pairs={{0,4},{4,0},{8,12},{12,8},{16,20},{20,16},{24,28},{28,24},{1,5},{5... | collective-permute-start | bytes 25165832 | tf_op jit(solution)/shard_map/ppermute | solution.py:732
  356.5 28.1 %collective-permute-start.17 = (bf16[256,2048]{1,0:T(8,128)(2,1)S(1)}, bf16[256,2048]{1,0:T(8,128)(2,1)S(1)}, u32[]{:S(2)}, u32[]{:S(2)}) collective-permute-start(bf16[256,2048]{1,0:T(8,128)(2,1)S(1)} %add_convert_fusion.5), channel_id=1, source_target_pairs={{0,1},{1,2},{2,3},{3,0},{4,5},{5,6},{6,7},{7,4},{8,9},{9,10},{10,1... | collective-permute-start | bytes 3145736 | tf_op jit(solution)/shard_map/ppermute | solution.py:743
  422.2 59.7 %collective-permute-start.25 = (bf16[1024,2048]{1,0:T(8,128)(2,1)}, bf16[1024,2048]{1,0:T(8,128)(2,1)}, u32[]{:S(2)}, u32[]{:S(2)}) collective-permute-start(bf16[1024,2048]{1,0:T(8,128)(2,1)} %weight_product.12), channel_id=1, source_target_pairs={{0,4},{4,0},{8,12},{12,8},{16,20},{20,16},{24,28},{28,24},{1,5},{5... | collective-permute-start | bytes 12582920 | tf_op jit(solution)/shard_map/ppermute | solution.py:732
  423.8 39.0 %collective-permute-start.23 = (bf16[256,2048]{1,0:T(8,128)(2,1)S(1)}, bf16[256,2048]{1,0:T(8,128)(2,1)S(1)}, u32[]{:S(2)}, u32[]{:S(2)}) collective-permute-start(bf16[256,2048]{1,0:T(8,128)(2,1)S(1)} %split.80), channel_id=1, source_target_pairs={{0,1},{1,2},{2,3},{3,0},{4,5},{5,6},{6,7},{7,4},{8,9},{9,10},{10,1... | collective-permute-start | bytes 3145736 | tf_op jit(solution)/shard_map/ppermute | solution.py:743
  500.0 140.0 %reduce-scatter.5.cloned.1.call-start = ((), (), s32[]{:S(2)}) async-start(), calls=%async_computation.8 | async-start | bytes 10485760 | tf_op jit(solution)/shard_map/reduce_scatter | solution.py:738
  500.5 195.1 %reduce-scatter.11.cloned.1.call-start = ((), (), s32[]{:S(2)}) async-start(), calls=%async_computation.11 | async-start | bytes 5242880 | tf_op jit(solution)/shard_map/reduce_scatter | solution.py:738
  501.3 236.6 %reduce-scatter.7.cloned.1.call-start = ((), (), s32[]{:S(2)}) async-start(), calls=%async_computation.9 | async-start | bytes 1966080 | tf_op jit(solution)/shard_map/reduce_scatter | solution.py:738
  501.3 53.6 %collective-permute-start.27 = (bf16[1024,768]{1,0:T(8,128)(2,1)}, bf16[1024,768]{1,0:T(8,128)(2,1)S(1)}, u32[]{:S(2)}, u32[]{:S(2)}) collective-permute-start(bf16[1024,768]{1,0:T(8,128)(2,1)} %weight_product.13), channel_id=1, source_target_pairs={{0,4},{4,0},{8,12},{12,8},{16,20},{20,16},{24,28},{28,24},{1,5},{5... | collective-permute-start | bytes 4718600 | tf_op jit(solution)/shard_map/ppermute | solution.py:732
  504.4 61.2 %collective-permute-start.26 = (bf16[256,2048]{1,0:T(8,128)(2,1)}, bf16[256,2048]{1,0:T(8,128)(2,1)}, u32[]{:S(2)}, u32[]{:S(2)}) collective-permute-start(bf16[256,2048]{1,0:T(8,128)(2,1)} %add_convert_fusion.4), channel_id=1, source_target_pairs={{0,1},{1,2},{2,3},{3,0},{4,5},{5,6},{6,7},{7,4},{8,9},{9,10},{10,1... | collective-permute-start | bytes 3145736 | tf_op jit(solution)/shard_map/ppermute | solution.py:743
  563.1 81.2 %collective-permute-start.35 = (bf16[256,512]{1,0:T(8,128)(2,1)S(1)}, bf16[256,512]{1,0:T(8,128)(2,1)S(1)}, u32[]{:S(2)}, u32[]{:S(2)}) collective-permute-start(bf16[256,512]{1,0:T(8,128)(2,1)S(1)} %add_convert_fusion.8), channel_id=1, source_target_pairs={{0,3},{1,0},{2,1},{3,2},{4,7},{5,4},{6,5},{7,6},{8,11},{9,8},{10,9... | collective-permute-start | bytes 786440 | tf_op jit(solution)/shard_map/ppermute | solution.py:743
  642.8 60.2 %collective-permute-start.28 = (bf16[256,2048]{1,0:T(8,128)(2,1)}, bf16[256,2048]{1,0:T(8,128)(2,1)}, u32[]{:S(2)}, u32[]{:S(2)}) collective-permute-start(bf16[256,2048]{1,0:T(8,128)(2,1)} %add_convert_fusion.3), channel_id=1, source_target_pairs={{0,1},{1,2},{2,3},{3,0},{4,5},{5,6},{6,7},{7,4},{8,9},{9,10},{10,1... | collective-permute-start | bytes 3145736 | tf_op jit(solution)/shard_map/ppermute | solution.py:743
  645.4 53.6 %collective-permute-start.36 = (bf16[256,512]{1,0:T(8,128)(2,1)S(1)}, bf16[256,512]{1,0:T(8,128)(2,1)}, u32[]{:S(2)}, u32[]{:S(2)}) collective-permute-start(bf16[256,512]{1,0:T(8,128)(2,1)S(1)} %add_convert_fusion.7), channel_id=1, source_target_pairs={{0,3},{1,0},{2,1},{3,2},{4,7},{5,4},{6,5},{7,6},{8,11},{9,8},{10,9... | collective-permute-start | bytes 786440 | tf_op jit(solution)/shard_map/ppermute | solution.py:743
  (55 other events, 979.3 us)
Sparse Core Ops, SparseCore 0:
  10.9 37.2 all-gather.4
  64.4 52.6 all-gather.6
  119.6 89.8 all-gather.8
  211.2 54.3 all-gather.10
  499.2 51.1 reduce-scatter.8
  553.5 86.3 reduce-scatter.4
  642.9 52.6 reduce-scatter.10
  698.9 30.8 reduce-scatter.6

commit v3 on v2

v3 whole, which is shorter than its diff:
```python
import functools
import math

import jax
import jax.numpy as jnp
from jax import lax
from jax.experimental import pallas as pl
from jax.experimental.pallas import tpu as pltpu
from jax.sharding import PartitionSpec as P

QUERY_HEADS = 32
KEY_VALUE_HEADS = 8
HEAD_SIZE = 64
PIECES = 4


EPSILON = 1e-05
ROPE_BASE = 500000.0
NEGATIVE = -1e30
GROUP_QUERY = QUERY_HEADS // KEY_VALUE_HEADS * HEAD_SIZE
GROUP_WIDTH = GROUP_QUERY + 2 * HEAD_SIZE
KERNEL_VMEM = 60 * 1024 * 1024
SMALL_COST = pl.CostEstimate(flops=1, bytes_accessed=1, transcendentals=0)


def layout(lengths, complete_rows):
    doc_ends = jnp.cumsum(lengths, axis=-1)
    row_index = jnp.arange(complete_rows, dtype=jnp.int32)
    piece_count = lengths.shape[-1]
    doc_ids = jnp.sum((row_index[None, :, None] >= doc_ends[:, None, :]).astype(jnp.int32), axis=2)
    starts = doc_ends - lengths
    chosen = doc_ids[:, :, None] == jnp.arange(piece_count, dtype=jnp.int32)[None, None, :]
    doc_begin = jnp.sum(jnp.where(chosen, starts[:, None, :], 0), axis=2) + jnp.where(
        doc_ids == piece_count, doc_ends[:, -1:], 0
    )
    return (doc_ids, row_index[None, :] - doc_begin)


def rope_tables(positions, head_dim):
    half_dim = head_dim // 2
    frequency = ROPE_BASE ** (-(jnp.arange(half_dim, dtype=jnp.float32) * (2.0 / head_dim)))
    angles = positions.astype(jnp.float32)[..., None] * frequency
    return (jnp.cos(angles), jnp.sin(angles))


def norm_rows(values):
    inverse = lax.rsqrt(jnp.mean(values * values, axis=-1, keepdims=True) + EPSILON)
    return (values * inverse, inverse)


def dot_nt(left, right):
    return lax.dot_general(
        left, right, (((1,), (1,)), ((), ())), preferred_element_type=jnp.float32
    )


def dot_nn(left, right):
    return jnp.dot(left, right, preferred_element_type=jnp.float32)


def dot_tn(left, right):
    return lax.dot_general(
        left, right, (((0,), (0,)), ((), ())), preferred_element_type=jnp.float32
    )


def tile_of(size, limit=512):
    tile = limit
    while size % tile:
        tile //= 2
    return tile


def parameters():
    return pltpu.CompilerParams(vmem_limit_bytes=KERNEL_VMEM)


def swap_halves(values):
    lane = lax.broadcasted_iota(jnp.int32, values.shape, 1)
    half = HEAD_SIZE // 2
    return jnp.where(
        lane % HEAD_SIZE < half, pltpu.roll(values, 128 - half, 1), pltpu.roll(values, half, 1)
    )


def turned(values, cosine, sine, start):
    result = values * cosine + swap_halves(values) * sine
    rotated = GROUP_WIDTH - HEAD_SIZE
    if start + 128 <= rotated:
        return result
    lane = lax.broadcasted_iota(jnp.int32, values.shape, 1)
    return jnp.where(lane < rotated - start, result, values)


def project_kernel(x_ref, gain_ref, weight_ref, cos_ref, sin_ref, *refs):
    normed_ref, joint_ref = refs[-2:]

    @pl.when(pl.program_id(0) == 0)
    def _():
        values = x_ref[...].astype(jnp.float32)
        inverse = lax.rsqrt(jnp.mean(values * values, axis=-1, keepdims=True) + EPSILON)
        normed_ref[...] = (values * inverse * gain_ref[...]).astype(jnp.bfloat16)

    product = dot_nn(normed_ref[...], weight_ref[...])
    for start in range(0, GROUP_WIDTH, 128):
        part = turned(product[:, start : start + 128], cos_ref[...], sin_ref[...], start)
        if start < GROUP_QUERY:
            part = part * HEAD_SIZE ** (-0.5)
        joint_ref[:, start : start + 128] = part.astype(jnp.bfloat16)


def project(x, gain, weight, cosine, sine, kept, index, count, groups):
    rows, depth = x.shape
    specs = [
        pl.BlockSpec((rows, depth), lambda g: (0, 0)),
        pl.BlockSpec((1, depth), lambda g: (0, 0)),
        pl.BlockSpec((depth, GROUP_WIDTH), lambda g: (0, g)),
        pl.BlockSpec((rows, 128), lambda g: (index, 0)),
        pl.BlockSpec((rows, 128), lambda g: (index, 0)),
    ]
    operands = [x, gain, weight, cosine, sine]
    aliases = {}
    if kept is not None:
        specs.extend([pl.BlockSpec(memory_space=pl.ANY)] * 2)
        aliases = {len(operands) + i: i for i in range(2)}
        operands.extend(kept)
    return pl.pallas_call(
        project_kernel,
        grid=(groups,),
        in_specs=specs,
        out_specs=[
            pl.BlockSpec((rows, depth), lambda g: (index, 0)),
            pl.BlockSpec((rows, GROUP_WIDTH), lambda g: (index, g)),
        ],
        out_shape=[
            jax.ShapeDtypeStruct((rows * count, depth), jnp.bfloat16),
            jax.ShapeDtypeStruct((rows * count, GROUP_WIDTH * groups), jnp.bfloat16),
        ],
        input_output_aliases=aliases,
        compiler_params=parameters(),
        cost_estimate=SMALL_COST,
        name="project",
    )(*operands)


def ring_offset(place, chunk, count, rows):
    return pl.multiple_of(lax.rem(place - chunk + count, count) * rows, rows)


def forward_kernel(
    count, place_ref, own_ref, all_ref, docq_ref, dock_ref, o_ref, lse_ref, bias, scores
):
    chunk = pl.program_id(1)
    place = place_ref[0]
    rows = own_ref.shape[0]
    heads = GROUP_QUERY // HEAD_SIZE
    row_index = lax.broadcasted_iota(jnp.int32, (rows, rows), 0)
    column_index = lax.broadcasted_iota(jnp.int32, (rows, rows), 1)

    def score(j, peaks):
        offset = ring_offset(place, j, count, rows)
        same = dock_ref[pl.ds(offset, rows), :] == docq_ref[...]
        same = same & ((row_index <= column_index) | (j < chunk))
        bias[...] = jnp.where(same, 0.0, NEGATIVE)
        keys = all_ref[pl.ds(offset, rows), GROUP_QUERY : GROUP_QUERY + HEAD_SIZE]
        result = []
        for head in range(heads):
            query = own_ref[:, head * HEAD_SIZE : (head + 1) * HEAD_SIZE]
            block = dot_nt(keys, query) + bias[...]
            scores[head, j] = block
            result.append(jnp.maximum(peaks[head], jnp.max(block, axis=0, keepdims=True)))
        return tuple(result)

    peaks = lax.fori_loop(
        0,
        chunk + 1,
        score,
        tuple(jnp.full((1, rows), NEGATIVE, jnp.float32) for _ in range(heads)),
    )

    def mix(j, carry):
        offset = ring_offset(place, j, count, rows)
        values = all_ref[pl.ds(offset, rows), GROUP_QUERY + HEAD_SIZE :]
        values = jnp.concatenate([values, jnp.ones_like(values)], axis=1)
        result = []
        for head in range(heads):
            probs = jnp.exp(scores[head, j] - peaks[head])
            total = carry[head][1] + jnp.sum(probs, axis=0, keepdims=True)
            result.append((carry[head][0] + dot_tn(probs.astype(jnp.bfloat16), values), total))
        return tuple(result)

    sums = lax.fori_loop(
        0,
        chunk + 1,
        mix,
        tuple(
            (
                jnp.zeros((rows, 2 * HEAD_SIZE), jnp.float32),
                jnp.zeros((1, rows), jnp.float32),
            )
            for _ in range(heads)
        ),
    )
    for head in range(heads):
        mixed, total = sums[head]
        o_ref[:, head * HEAD_SIZE : (head + 1) * HEAD_SIZE] = (
            mixed[:, :HEAD_SIZE] / mixed[:, HEAD_SIZE:]
        ).astype(jnp.bfloat16)
        lse_ref[head : head + 1, :] = peaks[head] + jnp.log(total)


def attention_forward(joint, docs, place, count, groups):
    total_rows = joint.shape[0]
    rows = total_rows // count

    def block(c, place_ref):
        return lax.rem(place_ref[0] - c + count, count)

    spec = pltpu.PrefetchScalarGridSpec(
        num_scalar_prefetch=1,
        grid=(groups, count),
        in_specs=[
            pl.BlockSpec((rows, GROUP_WIDTH), lambda g, c, p: (block(c, p), g)),
            pl.BlockSpec((total_rows, GROUP_WIDTH), lambda g, c, p: (0, g)),
            pl.BlockSpec((1, rows), lambda g, c, p: (0, block(c, p))),
            pl.BlockSpec((total_rows, 1), lambda g, c, p: (0, 0)),
        ],
        out_specs=[
            pl.BlockSpec((rows, GROUP_QUERY), lambda g, c, p: (block(c, p), g)),
            pl.BlockSpec((8, rows), lambda g, c, p: (g, block(c, p))),
        ],
        scratch_shapes=[
            pltpu.VMEM((rows, rows), jnp.float32),
            pltpu.VMEM((GROUP_QUERY // HEAD_SIZE, count, rows, rows), jnp.float32),
        ],
    )
    return pl.pallas_call(
        functools.partial(forward_kernel, count),
        grid_spec=spec,
        out_shape=[
            jax.ShapeDtypeStruct((total_rows, GROUP_QUERY * groups), jnp.bfloat16),
            jax.ShapeDtypeStruct((8 * groups, total_rows), jnp.float32),
        ],
        compiler_params=parameters(),
        cost_estimate=SMALL_COST,
        name="attend",
    )(place, joint, joint, docs[None, :], docs[:, None])


def backward_kernel(count, place_ref, *refs):
    own_ref, all_ref, o_ref = refs[:3]
    lse_ref, docq_ref, dock_ref, cos_ref, sin_ref = refs[3 + count : 8 + count]
    out_ref, bias, grad_out, sum_q, sum_kv = refs[8 + count :]
    chunk = pl.program_id(0)
    place = place_ref[0]
    rows = own_ref.shape[0]
    heads = GROUP_QUERY // HEAD_SIZE
    row_index = lax.broadcasted_iota(jnp.int32, (rows, rows), 0)
    column_index = lax.broadcasted_iota(jnp.int32, (rows, rows), 1)

    for index in range(count):

        @pl.when(lax.rem(place - chunk + count, count) == index)
        def _():
            grad_out[...] = refs[3 + index][...]

    @pl.when(chunk == 0)
    def _():
        sum_kv[...] = jnp.zeros_like(sum_kv)

    sum_q[...] = jnp.zeros_like(sum_q)
    owner = lax.broadcasted_iota(jnp.int32, (8, GROUP_QUERY), 0)
    head_of = lax.broadcasted_iota(jnp.int32, (8, GROUP_QUERY), 1) // HEAD_SIZE
    selector = jnp.where(owner == head_of, 1.0, 0.0).astype(jnp.bfloat16)
    both = o_ref[...].astype(jnp.float32) * grad_out[...].astype(jnp.float32)
    high = both.astype(jnp.bfloat16)
    low = (both - high.astype(jnp.float32)).astype(jnp.bfloat16)
    inner = dot_nt(selector, high) + dot_nt(selector, low)

    def block(j, carry):
        offset = ring_offset(place, j, count, rows)
        same = dock_ref[pl.ds(offset, rows), :] == docq_ref[...]
        same = same & ((row_index <= column_index) | (j < chunk))
        bias[...] = jnp.where(same, 0.0, NEGATIVE)
        keys = all_ref[pl.ds(offset, rows), GROUP_QUERY : GROUP_QUERY + HEAD_SIZE]
        values = all_ref[pl.ds(offset, rows), GROUP_QUERY + HEAD_SIZE :]
        key_sum = jnp.zeros((rows, HEAD_SIZE), jnp.float32)
        value_sum = jnp.zeros((rows, HEAD_SIZE), jnp.float32)
        for head in range(heads):
            lanes = slice(head * HEAD_SIZE, (head + 1) * HEAD_SIZE)
            query = own_ref[:, lanes]
            grad = grad_out[:, lanes]
            probs = jnp.exp(dot_nt(keys, query) + bias[...] - lse_ref[head : head + 1, :])
            grad_probs = dot_nt(values, grad)
            grad_scores = (probs * (grad_probs - inner[head : head + 1, :])).astype(jnp.bfloat16)
            value_sum += dot_nn(probs.astype(jnp.bfloat16), grad)
            key_sum += dot_nn(grad_scores, query)
            sum_q[:, lanes] += dot_tn(grad_scores, keys)
        sum_kv[pl.ds(offset, rows), :HEAD_SIZE] += key_sum
        sum_kv[pl.ds(offset, rows), HEAD_SIZE:] += value_sum
        return carry

    lax.fori_loop(0, chunk + 1, block, 0)
    own = pl.ds(ring_offset(place, chunk, count, rows), rows)
    for start in range(0, GROUP_QUERY, 128):
        part = turned(sum_q[:, start : start + 128], cos_ref[own, :], -sin_ref[own, :], start)
        out_ref[own, start : start + 128] = (part * HEAD_SIZE ** (-0.5)).astype(jnp.bfloat16)

    @pl.when(chunk == count - 1)
    def _():
        part = turned(sum_kv[...], cos_ref[...], -sin_ref[...], GROUP_QUERY)
        out_ref[:, GROUP_QUERY:] = part.astype(jnp.bfloat16)


def attention_backward(joint, attended, grads, lse, docs, cosine, sine, place, group):
    count = len(grads)
    total_rows = joint.shape[0]
    rows = total_rows // count

    def block(c, place_ref):
        return lax.rem(place_ref[0] - c + count, count)

    table = pl.BlockSpec((total_rows, 128), lambda c, p: (0, 0))
    spec = pltpu.PrefetchScalarGridSpec(
        num_scalar_prefetch=1,
        grid=(count,),
        in_specs=[
            pl.BlockSpec((rows, GROUP_WIDTH), lambda c, p: (block(c, p), group)),
            pl.BlockSpec((total_rows, GROUP_WIDTH), lambda c, p: (0, group)),
            pl.BlockSpec((rows, GROUP_QUERY), lambda c, p: (block(c, p), group)),
            *[pl.BlockSpec((rows, GROUP_QUERY), lambda c, p: (0, group))] * count,
            pl.BlockSpec((8, rows), lambda c, p: (group, block(c, p))),
            pl.BlockSpec((1, rows), lambda c, p: (0, block(c, p))),
            pl.BlockSpec((total_rows, 1), lambda c, p: (0, 0)),
            table,
            table,
        ],
        out_specs=pl.BlockSpec((total_rows, GROUP_WIDTH), lambda c, p: (0, 0)),
        scratch_shapes=[
            pltpu.VMEM((rows, rows), jnp.float32),
            pltpu.VMEM((rows, GROUP_QUERY), jnp.bfloat16),
            pltpu.VMEM((rows, GROUP_QUERY), jnp.float32),
            pltpu.VMEM((total_rows, 2 * HEAD_SIZE), jnp.float32),
        ],
    )
    return pl.pallas_call(
        functools.partial(backward_kernel, count),
        grid_spec=spec,
        out_shape=jax.ShapeDtypeStruct((total_rows, GROUP_WIDTH), jnp.bfloat16),
        compiler_params=parameters(),
        cost_estimate=SMALL_COST,
        name="attend_back",
    )(
        place,
        joint,
        joint,
        attended,
        *grads,
        lse,
        docs[None, :],
        docs[:, None],
        cosine,
        sine,
    )


def join_kernel(*refs):
    place = 0
    for ref in refs[:-1]:
        size = ref.shape[1]
        refs[-1][:, place : place + size] = ref[...]
        place += size


def join(parts, blocks):
    rows = parts[0].shape[0] // (max(blocks) + 1)
    width = sum(part.shape[1] for part in parts)
    return pl.pallas_call(
        join_kernel,
        grid=(1,),
        in_specs=[
            pl.BlockSpec((rows, part.shape[1]), lambda i, block=block: (block, 0))
            for part, block in zip(parts, blocks)
        ],
        out_specs=pl.BlockSpec((rows, width), lambda i: (0, 0)),
        out_shape=jax.ShapeDtypeStruct((rows, width), parts[0].dtype),
        compiler_params=parameters(),
        cost_estimate=SMALL_COST,
        name="join",
    )(*parts)


def transposed_kernel(count, parts, *refs):
    total = dot_nt(refs[0][...], refs[count][...])
    for index in range(1, count):
        total += dot_nt(refs[index][...], refs[count + index][...])
    rows = total.shape[0] // parts
    for index in range(parts):
        refs[2 * count + index][...] = total[index * rows : (index + 1) * rows].astype(
            jnp.bfloat16
        )


def transposed_product(xs, weight, block, parts):
    rows, depth = xs[0].shape
    width = weight.shape[0]
    tile = tile_of(width)
    specs = [pl.BlockSpec((rows, depth), lambda t: (0, 0))] * len(xs)
    for index in range(len(xs)):
        specs.append(pl.BlockSpec((tile, depth), lambda t, index=index: (t, block + index)))
    part = (rows // parts, width)
    return pl.pallas_call(
        functools.partial(transposed_kernel, len(xs), parts),
        grid=(width // tile,),
        in_specs=specs,
        out_specs=[pl.BlockSpec((part[0], tile), lambda t: (0, t))] * parts,
        out_shape=[jax.ShapeDtypeStruct(part, jnp.bfloat16)] * parts,
        compiler_params=parameters(),
        cost_estimate=SMALL_COST,
        name="transposed",
    )(*xs, *[weight] * len(xs))


def heads_kernel(count, *refs):
    parts = refs[:count]
    weight_ref = refs[count]
    tokens = refs[count + 1 : -1]
    out_ref = refs[-1]
    step = pl.program_id(0)
    width = parts[0].shape[1]
    for j in range(count):
        term = dot_nt(parts[j][...], weight_ref[:, j * width : (j + 1) * width])
        if j == 0:
            out_ref[...] = term
        else:
            out_ref[...] += term
    for index in range(len(tokens)):

        @pl.when(step == index)
        def _():
            out_ref[...] += tokens[index][...].astype(jnp.float32)


def heads_product(parts, weight, tokens):
    blocks = len(tokens)
    rows, width = tokens[0].shape
    depth = parts[0].shape[1]
    specs = [
        pl.BlockSpec((rows, depth), lambda i, j=j: (lax.rem(i + j, blocks), 0))
        for j in range(len(parts))
    ]
    whole = pl.BlockSpec((rows, width), lambda i: (0, 0), pipeline_mode=pl.Buffered(1))
    return pl.pallas_call(
        functools.partial(heads_kernel, len(parts)),
        grid=(blocks,),
        in_specs=[
            *specs,
            pl.BlockSpec(
                (width, depth * len(parts)), lambda i: (0, 0), pipeline_mode=pl.Buffered(1)
            ),
            *[whole] * blocks,
        ],
        out_specs=pl.BlockSpec((rows, width), lambda i: (i, 0)),
        out_shape=jax.ShapeDtypeStruct((rows * blocks, width), jnp.float32),
        compiler_params=parameters(),
        cost_estimate=SMALL_COST,
        name="heads_product",
    )(*parts, weight, *tokens)


def attended_kernel(partial_ref, last_ref, weight_ref, gain_ref, hidden_ref, normed_ref):
    values = partial_ref[...] + dot_nt(last_ref[...], weight_ref[...])

    @pl.when(pl.program_id(0) == 0)
    def _():
        hidden_ref[...] = values

    inverse = lax.rsqrt(jnp.mean(values * values, axis=-1, keepdims=True) + EPSILON)
    normed_ref[...] = (values * inverse * gain_ref[...]).astype(jnp.bfloat16)


def after_attention(partial, last, weight, gain, count):
    total_rows, width = partial.shape
    rows = total_rows // count
    depth = last.shape[1]
    return pl.pallas_call(
        attended_kernel,
        grid=(count,),
        in_specs=[
            pl.BlockSpec((rows, width), lambda i: (i, 0)),
            pl.BlockSpec((rows, depth), lambda i: (lax.rem(i + count - 1, count), 0)),
            pl.BlockSpec((width, depth), lambda i: (0, count - 1)),
            pl.BlockSpec((1, width), lambda i: (0, 0)),
        ],
        out_specs=[
            pl.BlockSpec((rows, width), lambda i: (0, 0)),
            pl.BlockSpec((rows, width), lambda i: (lax.rem(i + count - 1, count), 0)),
        ],
        out_shape=[
            jax.ShapeDtypeStruct((rows, width), jnp.float32),
            jax.ShapeDtypeStruct((total_rows, width), jnp.bfloat16),
        ],
        compiler_params=parameters(),
        cost_estimate=SMALL_COST,
        name="after_attention",
    )(partial, last, weight, gain)


def up_kernel(x_ref, gate_ref, up_ref, *refs):
    a_ref, u_ref, g_ref = refs[-3:]
    gate = dot_nn(x_ref[...], gate_ref[...])
    up = dot_nn(x_ref[...], up_ref[...])
    a_ref[...] = gate.astype(jnp.bfloat16)
    u_ref[...] = up.astype(jnp.bfloat16)
    g_ref[...] = (gate * jax.nn.sigmoid(gate) * up).astype(jnp.bfloat16)


def up_chunk(x, weight, kept, index, count):
    total_rows, depth = x.shape
    rows = total_rows // count
    hidden = weight.shape[1] // 3
    tile = tile_of(hidden)
    tiles = hidden // tile
    specs = [
        pl.BlockSpec((rows, depth), lambda t: (index, 0)),
        pl.BlockSpec((depth, tile), lambda t: (0, t)),
        pl.BlockSpec((depth, tile), lambda t: (0, tiles + t)),
    ]
    operands = [x, weight, weight]
    aliases = {}
    if kept is not None:
        specs.extend([pl.BlockSpec(memory_space=pl.ANY)] * 3)
        aliases = {len(operands) + i: i for i in range(3)}
        operands.extend(kept)
    return pl.pallas_call(
        up_kernel,
        grid=(tiles,),
        in_specs=specs,
        out_specs=[pl.BlockSpec((rows, tile), lambda t: (index, t))] * 3,
        out_shape=[jax.ShapeDtypeStruct((total_rows, hidden), jnp.bfloat16)] * 3,
        input_output_aliases=aliases,
        compiler_params=parameters(),
        cost_estimate=SMALL_COST,
        name="up_chunk",
    )(*operands)


def down_kernel(parts, tiles, *refs):
    down_ref, a_ref, u_ref, gate_ref, up_ref = refs[parts : parts + 5]
    da_ref, du_ref = refs[-5 - parts : -3 - parts]
    dx_refs = refs[-3 - parts : -3]
    da_kept, du_kept, e_out = refs[-3:]
    step = pl.program_id(0)

    @pl.when(step == 0)
    def _():
        rows = refs[0].shape[0]
        for index in range(parts):
            e_out[index * rows : (index + 1) * rows, :] = refs[index][...]

    @pl.when(step < tiles)
    def _():
        grad = dot_nn(e_out[...], down_ref[...])
        gate = a_ref[...].astype(jnp.float32)
        up = u_ref[...].astype(jnp.float32)
        sigmoid = jax.nn.sigmoid(gate)
        da = (grad * up * sigmoid * (1.0 + gate * (1.0 - sigmoid))).astype(jnp.bfloat16)
        du = (grad * gate * sigmoid).astype(jnp.bfloat16)
        da_ref[...] = da
        du_ref[...] = du
        tile = da.shape[1]
        for index in range(tiles):

            @pl.when(step == index)
            def _():
                da_kept[:, index * tile : (index + 1) * tile] = da
                du_kept[:, index * tile : (index + 1) * tile] = du

    @pl.when(step >= tiles)
    def _():
        total = dot_nt(da_kept[...], gate_ref[...]) + dot_nt(du_kept[...], up_ref[...])
        rows = total.shape[0] // parts
        for index in range(parts):
            dx_refs[index][...] = total[index * rows : (index + 1) * rows].astype(jnp.bfloat16)


def down_chunk(es, a, u, weight, kept, index, count):
    depth, width = weight.shape
    rows = len(es) * es[0].shape[0]
    hidden = width // 3
    tile = tile_of(hidden)
    tiles = hidden // tile
    row_tile = tile_of(depth)

    def column(t):
        return jnp.minimum(t, tiles - 1)

    def row(t):
        return jnp.maximum(t - tiles, 0)

    specs = [pl.BlockSpec(es[0].shape, lambda t: (0, 0))] * len(es) + [
        pl.BlockSpec((depth, tile), lambda t: (0, 2 * tiles + column(t))),
        pl.BlockSpec((rows, tile), lambda t: (index, column(t))),
        pl.BlockSpec((rows, tile), lambda t: (index, column(t))),
        pl.BlockSpec((row_tile, hidden), lambda t: (row(t), 0)),
        pl.BlockSpec((row_tile, hidden), lambda t: (row(t), 1)),
    ]
    operands = [*es, weight, a, u, weight, weight]
    part = es[0].shape
    shapes = [
        jax.ShapeDtypeStruct((rows * count, hidden), jnp.bfloat16),
        jax.ShapeDtypeStruct((rows * count, hidden), jnp.bfloat16),
        *[jax.ShapeDtypeStruct(part, jnp.bfloat16)] * len(es),
    ]
    aliases = {}
    if kept is not None:
        specs.extend([pl.BlockSpec(memory_space=pl.ANY)] * 2)
        aliases = {len(operands) + i: i for i in range(2)}
        operands.extend(kept)
    result = pl.pallas_call(
        functools.partial(down_kernel, len(es), tiles),
        grid=(tiles + depth // row_tile,),
        in_specs=specs,
        out_specs=[
            pl.BlockSpec((rows, tile), lambda t: (index, column(t))),
            pl.BlockSpec((rows, tile), lambda t: (index, column(t))),
            *[pl.BlockSpec((part[0], row_tile), lambda t: (0, row(t)))] * len(es),
        ],
        out_shape=shapes,
        input_output_aliases=aliases,
        scratch_shapes=[
            pltpu.VMEM((rows, hidden), jnp.bfloat16),
            pltpu.VMEM((rows, hidden), jnp.bfloat16),
            pltpu.VMEM((rows, depth), jnp.bfloat16),
        ],
        compiler_params=parameters(),
        cost_estimate=SMALL_COST,
        name="down_chunk",
    )(*operands)
    return result[:2], list(result[2:])


def weight_kernel(parts, count, blocks, split, place_ref, *refs):
    if parts == 1:
        x = refs[0][...]
    else:
        x = jnp.concatenate([ref[...] for ref in refs[:parts]], axis=0)
    ys = refs[parts : parts + count]
    step = pl.program_id(0)
    column = 0
    for y_ref in ys:
        width = y_ref.shape[1]
        piece = math.gcd(width, split) if width > split else width
        piece = math.gcd(piece, 1024) if piece > 1024 else piece
        for first in range(0, width, piece):
            total = dot_tn(x, y_ref[:, first : first + piece])
            start = column + first
            if len(refs) == parts + count + 1:
                refs[-1][:, start : start + piece] = total.astype(jnp.bfloat16)
                continue
            total += refs[parts + count][:, start : start + piece].astype(jnp.float32)
            total = total.astype(jnp.bfloat16)
            keep = step < blocks // 2 if start < split else lax.rem(step, 2) == 0
            keep_ref, send_ref = refs[-4:-2] if start < split else refs[-2:]
            columns = slice(start % split, start % split + piece)

            @pl.when(keep)
            def _():
                keep_ref[:, columns] = total

            @pl.when(jnp.logical_not(keep))
            def _():
                send_ref[:, columns] = total

        column += width


def weight_product(xs, ys, place, count, received):
    depth = xs[0].shape[1]
    rows = xs[0].shape[0]
    blocks = count // 2
    tile = depth // count
    total = sum(y.shape[1] for y in ys)
    split = -(-total // 256) * 128
    side = 1 if received is None else 0
    whole = pl.BlockSpec((tile, total), lambda t, p: (t, 0))
    if received is None:
        out_specs = whole
        out_shape = jax.ShapeDtypeStruct((depth // 2, total), jnp.bfloat16)
    else:
        half = blocks // 2
        out_specs = [
            pl.BlockSpec((tile, split), lambda t, p: (jnp.minimum(t, half - 1), 0)),
            pl.BlockSpec((tile, split), lambda t, p: (jnp.maximum(t - half, 0), 0)),
            pl.BlockSpec((tile, total - split), lambda t, p: (t // 2, 0)),
            pl.BlockSpec((tile, total - split), lambda t, p: (t // 2, 0)),
        ]
        out_shape = [
            jax.ShapeDtypeStruct((depth // 4, width), jnp.bfloat16)
            for width in (split, split, total - split, total - split)
        ]
    specs = [
        pl.BlockSpec((rows, tile), lambda t, p: (0, lax.bitwise_xor(p[0], 2 * t + side)))
    ] * len(xs)
    specs += [pl.BlockSpec(y.shape, lambda t, p: (0, 0)) for y in ys]
    operands = [*xs, *ys]
    if received is not None:
        specs.append(whole)
        operands.append(received)
    return pl.pallas_call(
        functools.partial(weight_kernel, len(xs), len(ys), blocks, split),
        grid_spec=pltpu.PrefetchScalarGridSpec(
            num_scalar_prefetch=1, grid=(blocks,), in_specs=specs, out_specs=out_specs
        ),
        out_shape=out_shape,
        compiler_params=parameters(),
        cost_estimate=SMALL_COST,
        name="weight_product",
    )(place, *operands)


def fold_kernel(count, *refs):
    for index in range(count):
        first, second = refs[2 * index : 2 * index + 2]
        keep, send = refs[2 * count + 2 * index : 2 * count + 2 * index + 2]
        rows = keep.shape[0]
        total = first[...].astype(jnp.float32) + second[...].astype(jnp.float32)
        total = total.astype(jnp.bfloat16)
        keep[...] = total[:rows]
        send[...] = total[rows:]


def fold(values):
    shapes = []
    for value in values[::2]:
        shape = (value.shape[0] // 2, value.shape[1])
        shapes.extend([jax.ShapeDtypeStruct(shape, jnp.bfloat16)] * 2)
    return pl.pallas_call(
        functools.partial(fold_kernel, len(values) // 2),
        out_shape=shapes,
        compiler_params=parameters(),
        cost_estimate=SMALL_COST,
        name="fold",
    )(*values)


def residual_kernel(parts, e_ref, hidden_ref, first_ref, second_ref, gain_ref, weight_ref, *refs):
    dh_ref, dz_ref = refs[:2]
    step = pl.program_id(0)

    @pl.when(step == 0)
    def _():
        values = hidden_ref[...]
        inverse = lax.rsqrt(jnp.mean(values * values, axis=-1, keepdims=True) + EPSILON)
        scaled = values * inverse
        grad = first_ref[...].astype(jnp.float32) + second_ref[...].astype(jnp.float32)
        grad = grad * gain_ref[...]
        projection = jnp.mean(grad * scaled, axis=-1, keepdims=True)
        total = e_ref[...].astype(jnp.float32) + inverse * (grad - scaled * projection)
        dh_ref[...] = total
        dz_ref[...] = total.astype(jnp.bfloat16)

    result = dot_nn(dz_ref[...], weight_ref[...]).astype(jnp.bfloat16)
    for index in range(parts):

        @pl.when(step == index)
        def _():
            refs[2 + index][...] = result


def residual_gradient(e, hidden_res, first, second, gain, weight, parts):
    rows, depth = e.shape
    tile = weight.shape[1] // parts
    whole = pl.BlockSpec((rows, depth), lambda t: (0, 0))
    result = pl.pallas_call(
        functools.partial(residual_kernel, parts),
        grid=(parts,),
        in_specs=[
            whole,
            whole,
            whole,
            whole,
            pl.BlockSpec((1, depth), lambda t: (0, 0)),
            pl.BlockSpec((depth, tile), lambda t: (0, t)),
        ],
        out_specs=[whole, whole] + [pl.BlockSpec((rows, tile), lambda t: (0, 0))] * parts,
        out_shape=[
            jax.ShapeDtypeStruct((rows, depth), jnp.float32),
            jax.ShapeDtypeStruct((rows, depth), jnp.bfloat16),
            *[jax.ShapeDtypeStruct((rows, tile), jnp.bfloat16)] * parts,
        ],
        compiler_params=parameters(),
        cost_estimate=SMALL_COST,
        name="residual_gradient",
    )(e, hidden_res, first, second, gain, weight)
    return result[0], result[1], list(result[2:])


def tie(value, *others):
    return lax.optimization_barrier((value, others))[0]


def together(*values):
    return lax.optimization_barrier(values)


def add(first, second):
    return (first.astype(jnp.float32) + second.astype(jnp.float32)).astype(jnp.bfloat16)


class Mover:
    def __init__(self):
        self.dp_count = lax.axis_size("dp")
        self.ring = lax.axis_size("tensor")
        self.steps = []
        step = 2
        while step < self.dp_count:
            self.steps.append(step)
            step *= 2

    def swap(self, value, step):
        return lax.ppermute(value, "dp", [(i, i ^ step) for i in range(self.dp_count)])

    def gather(self, shard):
        return lax.all_gather(shard, "dp", axis=0, tiled=True)

    def begin(self, pieces, level):
        orders = (self.steps[::-1], self.steps[:1] + self.steps[:0:-1])
        result = []
        for side in range(2):
            keep, send = pieces[2 * side : 2 * side + 2]
            result.extend([keep, self.swap(send, orders[side][level])])
        return result

    def advance(self, values, level=1):
        while level < len(self.steps):
            values = self.begin(fold(values), level)
            level += 1
        return values

    def hop(self, value, shift=1):
        return lax.ppermute(
            value, "tensor", [(i, (i + shift) % self.ring) for i in range(self.ring)]
        )

    def spread(self, value):
        ring = self.ring
        return [value] + [
            lax.ppermute(value, "tensor", [(i, (i - j) % ring) for i in range(ring)])
            for j in range(1, ring)
        ]

    def collect(self, parts):
        ring = self.ring
        total = parts[0]
        for j in range(1, ring):
            moved = lax.ppermute(
                parts[j].astype(jnp.bfloat16), "tensor", [(i, (i + j) % ring) for i in range(ring)]
            )
            total = total + moved.astype(jnp.float32)
        return total

    def exchange(self, parts):
        ring = self.ring
        return [parts[0]] + [
            lax.ppermute(parts[j], "tensor", [(i, (i + j) % ring) for i in range(ring)])
            for j in range(1, ring)
        ]


def total_of(values):
    return jnp.concatenate(
        [
            first.astype(jnp.float32) + second.astype(jnp.float32)
            for first, second in zip(values[::2], values[1::2])
        ],
        axis=1,
    )


def back_norm(grad_normed, scaled, inverse, scale_row):
    grad_scaled = grad_normed * scale_row
    projection = jnp.mean(grad_scaled * scaled, axis=-1, keepdims=True)
    return inverse * (grad_scaled - scaled * projection)


def per_device(
    tokens,
    seq_lengths,
    attention_gain,
    query_matrix,
    key_matrix,
    value_matrix,
    output_weight,
    feedforward_gain,
    gate_weight,
    up_weight,
    down_weight,
    cotangent,
):
    mover = Mover()
    dp_count = mover.dp_count
    ring = mover.ring
    dp_place = lax.axis_index("dp").astype(jnp.int32).reshape(1)
    ring_place = lax.axis_index("tensor")
    place = ring_place.astype(jnp.int32).reshape(1)
    _, local_rows, model_width = tokens.shape
    complete_rows = local_rows * ring
    hidden = gate_weight.shape[1]
    groups = key_matrix.shape[1] // HEAD_SIZE
    joint_width = groups * GROUP_WIDTH
    f32 = jnp.float32
    b16 = jnp.bfloat16

    doc_ids, positions = layout(seq_lengths, complete_rows)
    row_index = jnp.arange(complete_rows, dtype=jnp.int32)
    doc_ids = jnp.where(doc_ids[0] < PIECES, doc_ids[0], PIECES + row_index)

    def to_relative(values):
        view = values.reshape((ring, local_rows) + values.shape[1:])
        return jnp.roll(view, -(ring_place + 1), axis=0)[::-1].reshape(values.shape)

    doc_ids = to_relative(doc_ids)
    cosine, sine = rope_tables(to_relative(positions[0]), HEAD_SIZE)
    cosine_table = jnp.tile(cosine, (1, 128 // cosine.shape[1]))
    sine_table = jnp.tile(jnp.concatenate([-sine, sine], axis=1), (1, 128 // HEAD_SIZE))

    def grouped(query, key, value):
        pieces = []
        for g in range(groups):
            pieces.append(query[:, g * GROUP_QUERY : (g + 1) * GROUP_QUERY])
            pieces.append(key[:, g * HEAD_SIZE : (g + 1) * HEAD_SIZE])
            pieces.append(value[:, g * HEAD_SIZE : (g + 1) * HEAD_SIZE])
        return jnp.concatenate(pieces, axis=1)

    joint_matrix = grouped(query_matrix, key_matrix, value_matrix)
    own_gains = jnp.stack([attention_gain, feedforward_gain], axis=1)
    joint_full = mover.gather(
        jnp.concatenate([joint_matrix, jnp.pad(own_gains, ((0, 0), (0, 126)))], axis=1)
    )
    output_parts = mover.spread(output_weight.T)
    ff_shard = jnp.concatenate([gate_weight, up_weight, down_weight.T], axis=1)
    output_parts, cosine_table, sine_table, doc_ids, ff_shard, local_tokens = together(
        output_parts, cosine_table, sine_table, doc_ids, ff_shard, tokens[0]
    )
    token_chunks = [local_tokens, mover.hop(local_tokens)]
    output_ring = join(output_parts, [0] * ring)
    output_full = mover.gather(output_ring)
    ff_full = mover.gather(tie(ff_shard, output_ring))
    gains = joint_full[:, joint_width : joint_width + 2].T.astype(f32)
    gain_one, gain_two = gains[:1], gains[1:]

    def projection(kept, index):
        return project(
            token_chunks[index],
            gain_one,
            joint_full,
            cosine_table,
            sine_table,
            kept,
            index,
            ring,
            groups,
        )

    kept = projection(None, 0)
    for j in range(1, ring):
        token_chunks[j], kept = together(token_chunks[j], kept)
        if j + 1 < ring:
            token_chunks.append(mover.hop(token_chunks[j]))
        else:
            local_cotangent = tie(cotangent[0], token_chunks[j])
            moved = mover.hop(local_cotangent)
        kept = projection(kept, j)
    normed_one, joint = kept
    attended, totals = attention_forward(joint, doc_ids, place, ring, groups)
    moved, attended = together(moved, attended)
    cotangent_chunks = [local_cotangent, moved]
    attended_parts = [attended]
    while len(attended_parts) < ring:
        part = mover.hop(attended_parts[-1], -1)
        if len(attended_parts) == ring - 1:
            partial = heads_product(
                tie(attended_parts, attended_parts[-1]), output_full, token_chunks
            )
            part, partial = together(part, partial)
        attended_parts.append(part)
    moved, last = together(moved, attended_parts[-1])

    pairs = ring // 2
    moved = mover.hop(moved)
    hidden_res, normed_two = after_attention(partial, last, output_full, gain_two, ring)
    upward = up_chunk(normed_two, ff_full, None, 0, pairs)
    downward = None
    grads = []

    def chunks_of(pair):
        return [cotangent_chunks[(2 * pair + i) % ring] for i in (1, 2)]

    def lower(pair, kept):
        return down_chunk(chunks_of(pair), upward[0], upward[1], ff_full, kept, pair, pairs)

    for j in range(2, ring):
        if j > 2:
            moved = mover.hop(moved)
            if j % 2:
                downward, parts = lower((j - 3) // 2, downward)
                grads.extend(parts)
            else:
                upward = up_chunk(normed_two, ff_full, upward, j // 2 - 1, pairs)
        moved, upward, downward, grads = together(moved, upward, downward, grads)
        cotangent_chunks.append(moved)

    def weights(xs, ys, received=None):
        return weight_product(xs, ys, dp_place, dp_count, received)

    ordered = cotangent_chunks[1:] + cotangent_chunks[:1]
    total = grads[0]
    moved = mover.hop(total)
    upward = up_chunk(tie(normed_two, total), ff_full, upward, pairs - 1, pairs)
    product = upward[2]
    down_part = weights(ordered, [product])
    moved, upward, down_part = together(moved, upward, down_part)
    down_part = mover.swap(down_part, 1)
    for j in range(2, ring):
        total = add(moved, grads[j - 1])
        moved = mover.hop(total)
        if j == 2:
            downward, parts = lower(pairs - 1, tie(downward, total))
            grads.extend(parts)
            moved, downward, grads = together(moved, downward, grads)
            grad_gate, grad_up = downward
        if j == 3:
            gate_part = weights([tie(normed_two, total)], [grad_gate])
            up_part = weights([tie(normed_two, gate_part)], [grad_up])
            down_part = weights(tie(ordered, up_part), [product], down_part)
            moved, gate_part, up_part, down_part = together(moved, gate_part, up_part, down_part)
    grad_hidden, grad_branch, grad_parts = residual_gradient(
        local_cotangent, hidden_res, moved, grads[-1], gain_two, output_full, ring
    )

    grad_parts = mover.exchange(grad_parts)
    gate_part, up_part = mover.swap(gate_part, 1), mover.swap(up_part, 1)
    down_part = mover.begin(down_part, 0)
    branch = transposed_product([tie(product, grad_branch)], ff_full, 2, ring)
    gate_part = weights([tie(normed_two, branch)], [grad_gate], gate_part)
    grad_parts, branch, gate_part, up_part, down_part = together(
        grad_parts, branch, gate_part, up_part, down_part
    )
    grad_joint = []
    sent = 0
    moved = branch[0]
    for group in range(groups):
        moved = mover.hop(moved)
        grad_joint.append(
            attention_backward(
                joint,
                attended,
                tie(grad_parts, grad_joint),
                totals,
                doc_ids,
                cosine_table,
                sine_table,
                place,
                group,
            )
        )
        if group == 0:
            up_part = weights([tie(normed_two, grad_joint)], [grad_up], up_part)
            gate_part = mover.begin(gate_part, 0)
        else:
            up_part = mover.begin(up_part, 0)
        if group + 1 == groups:
            grads = transposed_product(grad_joint, joint_full, 0, ring)
        moved, grad_joint, grads, gate_part, up_part = together(
            moved, grad_joint, grads, gate_part, up_part
        )
        sent += 1
        if group + 1 < groups:
            moved = add(moved, branch[sent])
    if groups == 1:
        up_part = mover.begin(up_part, 0)
    branch_moved = moved
    attended_local = join(attended_parts, list(range(ring)))
    moved = grads[0]
    for j in range(1, ring):
        total = grads[1] if j == 1 else add(moved, grads[j])
        moved = mover.hop(total)
        if j == 1:
            gate_part, down_part = mover.advance(gate_part), mover.advance(down_part)
            output_part = weights([tie(grad_branch, total)], [attended_local])
            joint_part = weights([tie(normed_one, output_part)], grad_joint)
            output_part = mover.swap(output_part, 1)
            output_part = weights([tie(grad_branch, joint_part)], [attended_local], output_part)
            moved, joint_part, output_part, gate_part, down_part = together(
                moved, joint_part, output_part, gate_part, down_part
            )
        if j == 2:
            output_part = mover.begin(output_part, 0)
            joint_part = mover.swap(joint_part, 1)
            joint_part = weights([tie(normed_one, total)], grad_joint, joint_part)
            moved, joint_part, output_part = together(moved, joint_part, output_part)
        if j == 3:
            output_part = mover.advance(output_part)
            up_part = mover.advance(up_part)
            joint_part = mover.begin(joint_part, 0)
            moved, joint_part, output_part, up_part = together(
                moved, joint_part, output_part, up_part
            )
    joint_part = mover.advance(joint_part)
    for j in range(sent, ring - 1):
        branch_moved = mover.hop(add(branch_moved, branch[j]))
    output_out = mover.collect(jnp.split(total_of(output_part), ring, axis=1)).T
    scaled_one, inverse_one = norm_rows(local_tokens.astype(f32))
    local_one = moved.astype(f32) + grads[0].astype(f32)
    input_gradient = grad_hidden + back_norm(local_one, scaled_one, inverse_one, gain_one)
    block_output = (
        hidden_res + (branch_moved.astype(f32) + branch[-1].astype(f32))
    ).astype(b16)
    gate_out, up_out, joint_out = total_of(gate_part), total_of(up_part), total_of(joint_part)
    down_out = total_of(down_part).T

    sums = jnp.stack(
        [
            jnp.sum(joint_out * joint_matrix.astype(f32), axis=1) / attention_gain.astype(f32),
            jnp.sum(gate_out * gate_weight.astype(f32) + up_out * up_weight.astype(f32), axis=1)
            / feedforward_gain.astype(f32),
        ]
    )
    gain_out = sums
    for shift in range(1, ring):
        gain_out = gain_out + lax.ppermute(
            sums, "tensor", [(i, (i + shift) % ring) for i in range(ring)]
        )

    def ungrouped(first, width):
        return jnp.concatenate(
            [
                joint_out[:, g * GROUP_WIDTH + first : g * GROUP_WIDTH + first + width]
                for g in range(groups)
            ],
            axis=1,
        )

    return (
        block_output[None],
        input_gradient[None],
        gain_out[0],
        ungrouped(0, GROUP_QUERY),
        ungrouped(GROUP_QUERY, HEAD_SIZE),
        ungrouped(GROUP_QUERY + HEAD_SIZE, HEAD_SIZE),
        output_out,
        gain_out[1],
        gate_out,
        up_out,
        down_out,
    )


def solution(mesh):
    return jax.shard_map(
        per_device,
        mesh=mesh,
        in_specs=(
            P("dp", "tensor", None),
            P("dp", None),
            P("dp"),
            P("dp", "tensor"),
            P("dp", "tensor"),
            P("dp", "tensor"),
            P("tensor", "dp"),
            P("dp"),
            P("dp", "tensor"),
            P("dp", "tensor"),
            P("tensor", "dp"),
            P("dp", "tensor", None),
        ),
        out_specs=(
            P("dp", "tensor", None),
            P("dp", "tensor", None),
            P("dp"),
            P("dp", "tensor"),
            P("dp", "tensor"),
            P("dp", "tensor"),
            P("tensor", "dp"),
            P("dp"),
            P("dp", "tensor"),
            P("dp", "tensor"),
            P("tensor", "dp"),
        ),
        check_vma=False,
    )
```

time: 783 us -> 644 us (0.82)
  waiting for transfers between devices: 362 us -> 170 us
  Pallas kernels: 277 us -> 317 us
  starting transfers between devices: 45.6 us -> 68.5 us
  local copies, waits for them, and re-layouts: 34.5 us -> 23.6 us
    reduce_scatter x4 -> x0, waiting for transfers between devices: 168 us -> none  [scatter(): lax.psum_scatter(total, 'dp', scatter_dimension=0, tiled=True, axis_index...]
    pallas_call x23 -> x28, Pallas kernels: 176 us -> 208 us  [the longest x10 83.8 us: weight_product(): pl.pallas_call(functools.partial(weight_kernel, len(xs), len(ys), blocks,...]
    ppermute x3, waiting for transfers between devices: 34.7 us -> 10 us  [spread(): lax.ppermute(value, 'tensor', [(i, (i - j) % ring) for i in range(ring)])]
    ppermute x4 -> x25, starting transfers between devices: 0.65 us -> 23.1 us  [swap(): lax.ppermute(value, 'dp', [(i, i ^ step) for i in range(self.dp_count)])]
    ppermute x21 -> x18, waiting for transfers between devices: 139 us -> 120 us  [hop(): lax.ppermute(value, 'tensor', [(i, (i + shift) % self.ring) for i in rang...]
    split x7 -> x2, local copies, waits for them, and re-layouts: 13 us -> 0.07 us  [per_device(): output_out = mover.collect(jnp.split(total_of(output_part), ring, axis=1)).T]
    ppermute x4 -> x25, waiting for transfers between devices: 3.92 us -> 16.7 us  [swap(): lax.ppermute(value, 'dp', [(i, i ^ step) for i in range(self.dp_count)])]
    add x0 -> x9, other arithmetic: none -> 9.86 us  [total_of(): first.astype(jnp.float32) + second.astype(jnp.float32)]
  transfers between devices with their start and end apart: 45 -> 58, of which waited for: 16 -> 20; matrix products, arithmetic and copies ran while one was open for 8% -> 8% of each run, Pallas kernels for 36% -> 49%
where the time goes in v3:
time: 644 us; the launch traced here: 634 us
  Pallas kernels  317 us (49%)
  waiting for transfers between devices  170 us (26%)
  starting transfers between devices  68.5 us (11%)
  other arithmetic  40.1 us (6%)
  local copies, waits for them, and re-layouts  23.6 us (4%)
  between operations  15.2 us (2%)
    ppermute x18, waiting for transfers between devices, hop(): lax.ppermute(value, 'tensor', [(i, (i + shift) % self.ring) for i in rang...  120 us
    pallas_call x10, Pallas kernels, weight_product(): pl.pallas_call(functools.partial(weight_kernel, len(xs), len(ys), blocks,...  83.8 us
    pallas_call x2, Pallas kernels, down_chunk(): pl.pallas_call(functools.partial(down_kernel, len(es), tiles), grid=(tile...  45 us
    pallas_call x2, Pallas kernels, attention_backward(): pl.pallas_call(functools.partial(backward_kernel, count), grid_spec=spec,...  41.4 us
    ppermute x18, starting transfers between devices, hop(): lax.ppermute(value, 'tensor', [(i, (i + shift) % self.ring) for i in rang...  28.9 us
    pallas_call x2, Pallas kernels, up_chunk(): pl.pallas_call(up_kernel, grid=(tiles,), in_specs=specs, out_specs=[pl.Bl...  28.6 us
    ppermute x25, starting transfers between devices, swap(): lax.ppermute(value, 'dp', [(i, i ^ step) for i in range(self.dp_count)])  23.1 us
    pallas_call x1, Pallas kernels, attention_forward(): pl.pallas_call(functools.partial(forward_kernel, count), grid_spec=spec,...  22.3 us
  transfers between devices with their start and end apart: 58, of which 20 were waited for; matrix products, arithmetic and copies ran while one was open for 8% of the time, Pallas kernels for 49%

profile of v3, /device:TPU:0, one launch (start us, length us, event | category | flops | bytes accessed | tf_op | source)
XLA Modules:
  0.0 634.1 jit_solution(9636244061078713606)
XLA Ops:
  25.0 10.0 %collective-permute-done.1.refs_2_ = bf16[256,512]{1,0:T(8,128)(2,1)} collective-permute-done((bf16[256,512]{1,0:T(8,128)(2,1)S(1)}, bf16[256,512]{1,0:T(8,128)(2,1)}, u32[]{:S(2)}, u32[]{:S(2)}) %collective-permute-start.1) | collective-permute-done | bytes 262176 | tf_op jit(solution)/shard_map/ppermute | solution.py:849
  58.1 9.9 %collective-permute-done.3.x_ref.refs_5_ = bf16[256,2048]{1,0:T(8,128)(2,1)S(1)} collective-permute-done((bf16[256,2048]{1,0:T(8,128)(2,1)S(1)}, bf16[256,2048]{1,0:T(8,128)(2,1)S(1)}, u32[]{:S(2)}, u32[]{:S(2)}) %collective-permute-start.3) | collective-permute-done | bytes 1048608 | tf_op jit(solution)/shard_map/ppermute | solution.py:842
  74.5 18.8 %collective-permute-done.4.x_ref.refs_6_ = bf16[256,2048]{1,0:T(8,128)(2,1)S(1)} collective-permute-done((bf16[256,2048]{1,0:T(8,128)(2,1)S(1)}, bf16[256,2048]{1,0:T(8,128)(2,1)S(1)}, u32[]{:S(2)}, u32[]{:S(2)}) %collective-permute-start.4) | collective-permute-done | bytes 1048608 | tf_op jit(solution)/shard_map/ppermute | solution.py:842
  98.9 18.7 %collective-permute-done.5.x_ref.refs_7_ = bf16[256,2048]{1,0:T(8,128)(2,1)S(1)} collective-permute-done((bf16[256,2048]{1,0:T(8,128)(2,1)S(1)}, bf16[256,2048]{1,0:T(8,128)(2,1)S(1)}, u32[]{:S(2)}, u32[]{:S(2)}) %collective-permute-start.5) | collective-permute-done | bytes 1048608 | tf_op jit(solution)/shard_map/ppermute | solution.py:842
  125.0 22.3 %attend.1 = (bf16[1024,512]{1,0:T(8,128)(2,1)}, f32[16,1024]{1,0:T(8,128)}) custom-call(s32[1]{0:T(128)} %bitcast.10.place_ref, bf16[1024,768]{1,0:T(8,128)(2,1)} %get-tuple-element.270.own_ref.all_ref.refs_0_.refs_1_, bf16[1024,768]{1,0:T(8,128)(2,1)} %get-tuple-element.270.own_ref.all_ref.refs_0_.refs_1_, s32[1,1024]{1,0:T(1,128)} %bitcast.52, ...), custom_call_target="tpu_custom_call" | custom-call | flops 1 | bytes 1 | tf_op jit(solution)/shard_map/attend/pallas_call | solution.py:237
  151.1 19.6 %collective-permute-done.7.refs_1_ = bf16[1024,512]{1,0:T(8,128)(2,1)S(1)} collective-permute-done((bf16[1024,512]{1,0:T(8,128)(2,1)}, bf16[1024,512]{1,0:T(8,128)(2,1)S(1)}, u32[]{:S(2)}, u32[]{:S(2)}) %collective-permute-start.7) | collective-permute-done | bytes 1048608 | tf_op jit(solution)/shard_map/ppermute | solution.py:842
  174.7 18.8 %collective-permute-done.8.refs_2_ = bf16[1024,512]{1,0:T(8,128)(2,1)S(1)} collective-permute-done((bf16[1024,512]{1,0:T(8,128)(2,1)S(1)}, bf16[1024,512]{1,0:T(8,128)(2,1)S(1)}, u32[]{:S(2)}, u32[]{:S(2)}) %collective-permute-start.8) | collective-permute-done | bytes 1048608 | tf_op jit(solution)/shard_map/ppermute | solution.py:842
  198.0 13.9 %heads_product.1.partial_ref = f32[1024,2048]{1,0:T(8,128)} custom-call(bf16[1024,512]{1,0:T(8,128)(2,1)} %get-tuple-element.274.refs_0_.refs_2_, bf16[1024,512]{1,0:T(8,128)(2,1)} %copy-done.7, bf16[1024,512]{1,0:T(8,128)(2,1)} %copy-done.8, bf16[2048,2048]{1,0:T(8,128)(2,1)} %all-gather.6.cloned.1.call-done.refs_3_.weight_ref, bf16[256,2048]{1,0:T(8,128)(2,1)} %bitcast.34, ...), custom_call_target="tpu_custom_call" | custom-call | flops 1 | bytes 1 | tf_op jit(solution)/shard_map/heads_product/pallas_call | solution.py:453
  221.1 9.3 %after_attention.1 = (f32[256,2048]{1,0:T(8,128)}, bf16[1024,2048]{1,0:T(8,128)(2,1)}) custom-call(f32[1024,2048]{1,0:T(8,128)} %heads_product.1.partial_ref, bf16[1024,512]{1,0:T(8,128)(2,1)} %collective-permute-done.9.last_ref.refs_3_, bf16[2048,2048]{1,0:T(8,128)(2,1)} %all-gather.6.cloned.1.call-done.refs_3_.weight_ref, f32[1,2048]{1,0:T(1,128)} %copy.113.gain_ref), custom_call_target="tpu_custom_call" | custom-call | flops 1 | bytes 1 | tf_op jit(solution)/shard_map/after_attention/pallas_call | solution.py:486
  232.9 14.4 %up_chunk.2 = (bf16[1024,2048]{1,0:T(8,128)(2,1)}, bf16[1024,2048]{1,0:T(8,128)(2,1)}, bf16[1024,2048]{1,0:T(8,128)(2,1)}) custom-call(bf16[1024,2048]{1,0:T(8,128)(2,1)} %get-tuple-element.374.x_ref.refs_0_, bf16[2048,6144]{1,0:T(8,128)(2,1)} %all-gather.8.cloned.1.call-done.gate_ref.up_ref.refs_2_.refs_5_.refs_6_.refs_1_, ...), custom_call_target="tpu_custom_call" | custom-call | flops 1 | bytes 1 | tf_op jit(solution)/shard_map/up_chunk/pallas_call | solution.py:535
  248.8 22.5 %down_chunk.2 = (bf16[1024,2048]{1,0:T(8,128)(2,1)}, bf16[1024,2048]{1,0:T(8,128)(2,1)}, bf16[256,2048]{1,0:T(8,128)(2,1)}, bf16[256,2048]{1,0:T(8,128)(2,1)}) custom-call(bf16[256,2048]{1,0:T(8,128)(2,1)} %copy-done.3, bf16[256,2048]{1,0:T(8,128)(2,1)} %copy-done.4, ...), custom_call_target="tpu_custom_call" | custom-call | flops 1 | bytes 1 | tf_op jit(solution)/shard_map/down_chunk/pallas_call | solution.py:620
  274.5 14.2 %up_chunk.3 = (bf16[1024,2048]{1,0:T(8,128)(2,1)}, bf16[1024,2048]{1,0:T(8,128)(2,1)}, bf16[1024,2048]{1,0:T(8,128)(2,1)}) custom-call(bf16[1024,2048]{1,0:T(8,128)(2,1)} %get-tuple-element.374.x_ref.refs_0_, ...), custom_call_target="tpu_custom_call", output_to_operand_aliasing={{0}: (3, {}), {1}: (4, {}), {2}: (5, {})} | custom-call | flops 1 | bytes 1 | tf_op jit(solution)/shard_map/up_chunk/pallas_call | solution.py:535
  288.6 9.0 %weight_product.10 = bf16[1024,2048]{1,0:T(8,128)(2,1)} custom-call(s32[1]{0:T(128)} %bitcast.13.place_ref, bf16[256,2048]{1,0:T(8,128)(2,1)} %copy-done.3, bf16[256,2048]{1,0:T(8,128)(2,1)} %copy-done.4, bf16[256,2048]{1,0:T(8,128)(2,1)} %copy-done.5, bf16[256,2048]{1,0:T(8,128)(2,1)} %bitcast.39, bf16[1024,2048]{1,0:T(8,128)(2,1)} %get-tuple-element.344.refs_4_.refs_0_), custom_call_target="tpu_custom_call" | custom-call | flops 1 | bytes 1 | tf_op jit(solution)/shard_map/weight_product/pallas_call | solution.py:710
  301.6 22.5 %down_chunk.3 = (bf16[1024,2048]{1,0:T(8,128)(2,1)}, bf16[1024,2048]{1,0:T(8,128)(2,1)}, bf16[256,2048]{1,0:T(8,128)(2,1)}, bf16[256,2048]{1,0:T(8,128)(2,1)}) custom-call(bf16[256,2048]{1,0:T(8,128)(2,1)} %copy-done.5, bf16[256,2048]{1,0:T(8,128)(2,1)} %bitcast.40, ...), custom_call_target="tpu_custom_call", output_to_operand_aliasing={{0}: (7, {}), {1}: (8, {})} | custom-call | flops 1 | bytes 1 | tf_op jit(solution)/shard_map/down_chunk/pallas_call | solution.py:620
  348.1 10.9 %weight_product.13 = (bf16[512,1024]{1,0:T(8,128)(2,1)}, bf16[512,1024]{1,0:T(8,128)(2,1)}, bf16[512,1024]{1,0:T(8,128)(2,1)}, bf16[512,1024]{1,0:T(8,128)(2,1)}) custom-call(s32[1]{0:T(128)} %bitcast.13.place_ref, bf16[256,2048]{1,0:T(8,128)(2,1)} %copy-done.3, bf16[256,2048]{1,0:T(8,128)(2,1)} %copy-done.4, bf16[256,2048]{1,0:T(8,128)(2,1)} %copy-done.5, ...), custom_call_target="tpu_custom_call" | custom-call | flops 1 | bytes 1 | tf_op jit(solution)/shard_map/weight_product/pallas_call | solution.py:710
  361.6 10.6 %residual_gradient.1 = (f32[256,2048]{1,0:T(8,128)}, bf16[256,2048]{1,0:T(8,128)(2,1)}, bf16[256,512]{1,0:T(8,128)(2,1)}, bf16[256,512]{1,0:T(8,128)(2,1)}, bf16...) custom-call(bf16[256,2048]{1,0:T(8,128)(2,1)} %bitcast.42, f32[256,2048]{1,0:T(8,128)} %get-tuple-element.285.hidden_ref, ...), custom_call_target="tpu_custom_call" | custom-call | flops 1 | bytes 1 | tf_op jit(solution)/shard_map/residual_gradient/pallas_call | solution.py:775
  372.2 10.0 %collective-permute-done.16.refs_4_ = bf16[256,512]{1,0:T(8,128)(2,1)S(1)} collective-permute-done((bf16[256,512]{1,0:T(8,128)(2,1)}, bf16[256,512]{1,0:T(8,128)(2,1)S(1)}, u32[]{:S(2)}, u32[]{:S(2)}) %collective-permute-start.16) | collective-permute-done | bytes 262176 | tf_op jit(solution)/shard_map/ppermute | solution.py:866
  384.2 13.2 %transposed.2 = (bf16[256,2048]{1,0:T(8,128)(2,1)}, bf16[256,2048]{1,0:T(8,128)(2,1)}, bf16[256,2048]{1,0:T(8,128)(2,1)}, bf16[256,2048]{1,0:T(8,128)(2,1)}) custom-call(bf16[1024,2048]{1,0:T(8,128)(2,1)} %get-tuple-element.344.refs_4_.refs_0_, bf16[2048,6144]{1,0:T(8,128)(2,1)} %all-gather.8.cloned.1.call-done.gate_ref.up_ref.refs_2_.refs_5_.refs_6_.refs_1_), custom_call_target="tpu_custom_call" | custom-call | flops 1 | bytes 1 | tf_op jit(solution)/shard_map/transposed/pallas_call | solution.py:412
  397.4 10.6 %weight_product.14 = (bf16[512,1024]{1,0:T(8,128)(2,1)}, bf16[512,1024]{1,0:T(8,128)(2,1)}, bf16[512,1024]{1,0:T(8,128)(2,1)}, bf16[512,1024]{1,0:T(8,128)(2,1)}) custom-call(s32[1]{0:T(128)} %bitcast.13.place_ref, bf16[1024,2048]{1,0:T(8,128)(2,1)} %get-tuple-element.374.x_ref.refs_0_, bf16[1024,2048]{1,0:T(8,128)(2,1)} %get-tuple-element.325.refs_1_, ...), custom_call_target="tpu_custom_call" | custom-call | flops 1 | bytes 1 | tf_op jit(solution)/shard_map/weight_product/pallas_call | solution.py:710
  411.6 20.7 %attend_back.2.refs_0_.refs_1_ = bf16[1024,384]{1,0:T(8,128)(2,1)} custom-call(s32[1]{0:T(128)} %bitcast.10.place_ref, bf16[1024,768]{1,0:T(8,128)(2,1)} %get-tuple-element.270.own_ref.all_ref.refs_0_.refs_1_, bf16[1024,768]{1,0:T(8,128)(2,1)} %get-tuple-element.270.own_ref.all_ref.refs_0_.refs_1_, bf16[1024,512]{1,0:T(8,128)(2,1)} %get-tuple-element.274.refs_0_.refs_2_, ...), custom_call_target="tpu_custom_call" | custom-call | flops 1 | bytes 1 | tf_op jit(solution)/shard_map/attend_back/pallas_call | solution.py:346
  432.4 10.7 %weight_product.15 = (bf16[512,1024]{1,0:T(8,128)(2,1)}, bf16[512,1024]{1,0:T(8,128)(2,1)}, bf16[512,1024]{1,0:T(8,128)(2,1)}, bf16[512,1024]{1,0:T(8,128)(2,1)}) custom-call(s32[1]{0:T(128)} %bitcast.13.place_ref, bf16[1024,2048]{1,0:T(8,128)(2,1)} %get-tuple-element.374.x_ref.refs_0_, bf16[1024,2048]{1,0:T(8,128)(2,1)} %get-tuple-element.327.refs_1_, ...), custom_call_target="tpu_custom_call" | custom-call | flops 1 | bytes 1 | tf_op jit(solution)/shard_map/weight_product/pallas_call | solution.py:710
  447.6 20.7 %attend_back.3.refs_1_.refs_2_ = bf16[1024,384]{1,0:T(8,128)(2,1)} custom-call(s32[1]{0:T(128)} %bitcast.10.place_ref, bf16[1024,768]{1,0:T(8,128)(2,1)} %get-tuple-element.270.own_ref.all_ref.refs_0_.refs_1_, bf16[1024,768]{1,0:T(8,128)(2,1)} %get-tuple-element.270.own_ref.all_ref.refs_0_.refs_1_, bf16[1024,512]{1,0:T(8,128)(2,1)} %get-tuple-element.274.refs_0_.refs_2_, ...), custom_call_target="tpu_custom_call" | custom-call | flops 1 | bytes 1 | tf_op jit(solution)/shard_map/attend_back/pallas_call | solution.py:346
  529.3 9.3 %collective-permute-done.29 = bf16[256,2048]{1,0:T(8,128)(2,1)} collective-permute-done((bf16[256,2048]{1,0:T(8,128)(2,1)}, bf16[256,2048]{1,0:T(8,128)(2,1)}, u32[]{:S(2)}, u32[]{:S(2)}) %collective-permute-start.29) | collective-permute-done | bytes 1048608 | tf_op jit(solution)/shard_map/ppermute | solution.py:842
  580.4 9.3 %collective-permute-done.43 = bf16[256,1024]{1,0:T(8,128)(2,1)} collective-permute-done((bf16[256,1024]{1,0:T(8,128)(2,1)}, bf16[256,1024]{1,0:T(8,128)(2,1)}, u32[]{:S(2)}, u32[]{:S(2)}) %collective-permute-start.43) | collective-permute-done | bytes 524320 | tf_op jit(solution)/shard_map/ppermute | solution.py:822
  (326 shorter events, 269.0 us)
Async XLA Ops:
  7.2 42.1 %all-gather.4.cloned.1.call-start = ((), (), s32[]{:S(2)}) async-start(), calls=%async_computation | async-start | bytes 4128768 | tf_op jit(solution)/shard_map/all_gather | solution.py:825
  11.9 186.1 %all-gather.6.cloned.1.call-start = ((), (), s32[]{:S(2)}) async-start(), calls=%async_computation.1 | async-start | bytes 9437184 | tf_op jit(solution)/shard_map/all_gather | solution.py:825
  37.7 195.2 %all-gather.8.cloned.1.call-start = ((), (), s32[]{:S(2)}) async-start(), calls=%async_computation.2 | async-start | bytes 28311552 | tf_op jit(solution)/shard_map/all_gather | solution.py:825
  38.9 29.1 %collective-permute-start.3 = (bf16[256,2048]{1,0:T(8,128)(2,1)S(1)}, bf16[256,2048]{1,0:T(8,128)(2,1)S(1)}, u32[]{:S(2)}, u32[]{:S(2)}) collective-permute-start(bf16[256,2048]{1,0:T(8,128)(2,1)S(1)} %bitcast.35), channel_id=1, source_target_pairs={{0,1},{1,2},{2,3},{3,0},{4,5},{5,6},{6,7},{7,4},{8,9},{9,10},{10,1... | collective-permute-start | bytes 3145736 | tf_op jit(solution)/shard_map/ppermute | solution.py:842
  118.6 28.7 %collective-permute-start.6 = (bf16[256,2048]{1,0:T(8,128)(2,1)S(1)}, bf16[256,2048]{1,0:T(8,128)(2,1)S(1)}, u32[]{:S(2)}, u32[]{:S(2)}) collective-permute-start(bf16[256,2048]{1,0:T(8,128)(2,1)S(1)} %bitcast.43), channel_id=1, source_target_pairs={{0,1},{1,2},{2,3},{3,0},{4,5},{5,6},{6,7},{7,4},{8,9},{9,10},{10,1... | collective-permute-start | bytes 3145736 | tf_op jit(solution)/shard_map/ppermute | solution.py:842
  301.0 47.1 %collective-permute-start.15 = (bf16[1024,2048]{1,0:T(8,128)(2,1)}, bf16[1024,2048]{1,0:T(8,128)(2,1)}, u32[]{:S(2)}, u32[]{:S(2)}) collective-permute-start(bf16[1024,2048]{1,0:T(8,128)(2,1)} %weight_product.10), channel_id=1, source_target_pairs={{0,4},{4,0},{8,12},{12,8},{16,20},{20,16},{24,28},{28,24},{1,5},{5... | collective-permute-start | bytes 12582920 | tf_op jit(solution)/shard_map/ppermute | solution.py:822
  330.6 28.4 %collective-permute-start.14 = (bf16[256,2048]{1,0:T(8,128)(2,1)S(1)}, bf16[256,2048]{1,0:T(8,128)(2,1)S(1)}, u32[]{:S(2)}, u32[]{:S(2)}) collective-permute-start(bf16[256,2048]{1,0:T(8,128)(2,1)S(1)} %add_convert_fusion.5), channel_id=1, source_target_pairs={{0,1},{1,2},{2,3},{3,0},{4,5},{5,6},{6,7},{7,4},{8,9},{9,10},{10,1... | collective-permute-start | bytes 3145736 | tf_op jit(solution)/shard_map/ppermute | solution.py:842
  359.1 49.0 %collective-permute-start.20 = (bf16[1024,2048]{1,0:T(8,128)(2,1)}, bf16[1024,2048]{1,0:T(8,128)(2,1)}, u32[]{:S(2)}, u32[]{:S(2)}) collective-permute-start(bf16[1024,2048]{1,0:T(8,128)(2,1)} %weight_product.12), channel_id=1, source_target_pairs={{0,4},{4,0},{8,12},{12,8},{16,20},{20,16},{24,28},{28,24},{1,5},{5... | collective-permute-start | bytes 12582920 | tf_op jit(solution)/shard_map/ppermute | solution.py:822
  359.6 48.4 %collective-permute-start.21 = (bf16[512,1024]{1,0:T(8,128)(2,1)}, bf16[512,1024]{1,0:T(8,128)(2,1)S(1)}, u32[]{:S(2)}, u32[]{:S(2)}) collective-permute-start(bf16[512,1024]{1,0:T(8,128)(2,1)} %get-tuple-element.357), channel_id=1, source_target_pairs={{0,16},{4,20},{8,24},{12,28},{16,0},{20,4},{24,8},{28,12},{1,17},{... | collective-permute-start | bytes 3145736 | tf_op jit(solution)/shard_map/ppermute | solution.py:822
  359.9 48.1 %collective-permute-start.22 = (bf16[512,1024]{1,0:T(8,128)(2,1)}, bf16[512,1024]{1,0:T(8,128)(2,1)S(1)}, u32[]{:S(2)}, u32[]{:S(2)}) collective-permute-start(bf16[512,1024]{1,0:T(8,128)(2,1)} %get-tuple-element.359), channel_id=1, source_target_pairs={{0,8},{4,12},{8,0},{12,4},{16,24},{20,28},{24,16},{28,20},{1,9},{5... | collective-permute-start | bytes 3145736 | tf_op jit(solution)/shard_map/ppermute | solution.py:822
  409.1 34.0 %collective-permute-start.23 = (bf16[256,2048]{1,0:T(8,128)(2,1)}, bf16[256,2048]{1,0:T(8,128)(2,1)S(1)}, u32[]{:S(2)}, u32[]{:S(2)}) collective-permute-start(bf16[256,2048]{1,0:T(8,128)(2,1)} %get-tuple-element.360), channel_id=1, source_target_pairs={{0,1},{1,2},{2,3},{3,0},{4,5},{5,6},{6,7},{7,4},{8,9},{9,10},{10,1... | collective-permute-start | bytes 3145736 | tf_op jit(solution)/shard_map/ppermute | solution.py:842
  409.6 33.5 %collective-permute-start.24 = (bf16[512,1024]{1,0:T(8,128)(2,1)}, bf16[512,1024]{1,0:T(8,128)(2,1)}, u32[]{:S(2)}, u32[]{:S(2)}) collective-permute-start(bf16[512,1024]{1,0:T(8,128)(2,1)} %get-tuple-element.371), channel_id=1, source_target_pairs={{0,16},{4,20},{8,24},{12,28},{16,0},{20,4},{24,8},{28,12},{1,17},{... | collective-permute-start | bytes 3145736 | tf_op jit(solution)/shard_map/ppermute | solution.py:822
  411.1 32.0 %collective-permute-start.25 = (bf16[512,1024]{1,0:T(8,128)(2,1)}, bf16[512,1024]{1,0:T(8,128)(2,1)}, u32[]{:S(2)}, u32[]{:S(2)}) collective-permute-start(bf16[512,1024]{1,0:T(8,128)(2,1)} %get-tuple-element.373), channel_id=1, source_target_pairs={{0,8},{4,12},{8,0},{12,4},{16,24},{20,28},{24,16},{28,20},{1,9},{5... | collective-permute-start | bytes 3145736 | tf_op jit(solution)/shard_map/ppermute | solution.py:822
  443.5 34.8 %collective-permute-start.26 = (bf16[256,2048]{1,0:T(8,128)(2,1)S(1)}, bf16[256,2048]{1,0:T(8,128)(2,1)S(1)}, u32[]{:S(2)}, u32[]{:S(2)}) collective-permute-start(bf16[256,2048]{1,0:T(8,128)(2,1)S(1)} %add_convert_fusion.4), channel_id=1, source_target_pairs={{0,1},{1,2},{2,3},{3,0},{4,5},{5,6},{6,7},{7,4},{8,9},{9,10},{10,1... | collective-permute-start | bytes 3145736 | tf_op jit(solution)/shard_map/ppermute | solution.py:842
  445.6 32.7 %collective-permute-start.27 = (bf16[512,1024]{1,0:T(8,128)(2,1)}, bf16[512,1024]{1,0:T(8,128)(2,1)S(1)}, u32[]{:S(2)}, u32[]{:S(2)}) collective-permute-start(bf16[512,1024]{1,0:T(8,128)(2,1)} %get-tuple-element.396), channel_id=1, source_target_pairs={{0,16},{4,20},{8,24},{12,28},{16,0},{20,4},{24,8},{28,12},{1,17},{... | collective-permute-start | bytes 3145736 | tf_op jit(solution)/shard_map/ppermute | solution.py:822
  445.9 32.4 %collective-permute-start.28 = (bf16[512,1024]{1,0:T(8,128)(2,1)}, bf16[512,1024]{1,0:T(8,128)(2,1)}, u32[]{:S(2)}, u32[]{:S(2)}) collective-permute-start(bf16[512,1024]{1,0:T(8,128)(2,1)} %get-tuple-element.398), channel_id=1, source_target_pairs={{0,8},{4,12},{8,0},{12,4},{16,24},{20,28},{24,16},{28,20},{1,9},{5... | collective-permute-start | bytes 3145736 | tf_op jit(solution)/shard_map/ppermute | solution.py:822
  487.7 32.9 %collective-permute-start.30 = (bf16[256,2048]{1,0:T(8,128)(2,1)}, bf16[256,2048]{1,0:T(8,128)(2,1)}, u32[]{:S(2)}, u32[]{:S(2)}) collective-permute-start(bf16[256,2048]{1,0:T(8,128)(2,1)} %get-tuple-element.403), channel_id=1, source_target_pairs={{0,1},{1,2},{2,3},{3,0},{4,5},{5,6},{6,7},{7,4},{8,9},{9,10},{10,1... | collective-permute-start | bytes 3145736 | tf_op jit(solution)/shard_map/ppermute | solution.py:842
  489.2 31.5 %collective-permute-start.35 = (bf16[256,1024]{1,0:T(8,128)(2,1)}, bf16[256,1024]{1,0:T(8,128)(2,1)}, u32[]{:S(2)}, u32[]{:S(2)}) collective-permute-start(bf16[256,1024]{1,0:T(8,128)(2,1)} %get-tuple-element.429), channel_id=1, source_target_pairs={{0,16},{4,20},{8,24},{12,28},{16,0},{20,4},{24,8},{28,12},{1,17},{... | collective-permute-start | bytes 1572872 | tf_op jit(solution)/shard_map/ppermute | solution.py:822
  505.2 33.4 %collective-permute-start.29 = (bf16[256,2048]{1,0:T(8,128)(2,1)}, bf16[256,2048]{1,0:T(8,128)(2,1)}, u32[]{:S(2)}, u32[]{:S(2)}) collective-permute-start(bf16[256,2048]{1,0:T(8,128)(2,1)} %add_convert_fusion.3), channel_id=1, source_target_pairs={{0,1},{1,2},{2,3},{3,0},{4,5},{5,6},{6,7},{7,4},{8,9},{9,10},{10,1... | collective-permute-start | bytes 3145736 | tf_op jit(solution)/shard_map/ppermute | solution.py:842
  523.3 37.0 %collective-permute-start.36 = (bf16[256,2048]{1,0:T(8,128)(2,1)}, bf16[256,2048]{1,0:T(8,128)(2,1)}, u32[]{:S(2)}, u32[]{:S(2)}) collective-permute-start(bf16[256,2048]{1,0:T(8,128)(2,1)} %add_convert_fusion.1), channel_id=1, source_target_pairs={{0,1},{1,2},{2,3},{3,0},{4,5},{5,6},{6,7},{7,4},{8,9},{9,10},{10,1... | collective-permute-start | bytes 3145736 | tf_op jit(solution)/shard_map/ppermute | solution.py:842
  524.6 35.8 %collective-permute-start.38 = (bf16[512,1024]{1,0:T(8,128)(2,1)}, bf16[512,1024]{1,0:T(8,128)(2,1)}, u32[]{:S(2)}, u32[]{:S(2)}) collective-permute-start(bf16[512,1024]{1,0:T(8,128)(2,1)} %get-tuple-element.439), channel_id=1, source_target_pairs={{0,16},{4,20},{8,24},{12,28},{16,0},{20,4},{24,8},{28,12},{1,17},{... | collective-permute-start | bytes 3145736 | tf_op jit(solution)/shard_map/ppermute | solution.py:822
  525.1 35.2 %collective-permute-start.39 = (bf16[512,1024]{1,0:T(8,128)(2,1)}, bf16[512,1024]{1,0:T(8,128)(2,1)}, u32[]{:S(2)}, u32[]{:S(2)}) collective-permute-start(bf16[512,1024]{1,0:T(8,128)(2,1)} %get-tuple-element.441), channel_id=1, source_target_pairs={{0,8},{4,12},{8,0},{12,4},{16,24},{20,28},{24,16},{28,20},{1,9},{5... | collective-permute-start | bytes 3145736 | tf_op jit(solution)/shard_map/ppermute | solution.py:822
  538.6 34.6 %collective-permute-start.45 = (bf16[256,1024]{1,0:T(8,128)(2,1)}, bf16[256,1024]{1,0:T(8,128)(2,1)S(1)}, u32[]{:S(2)}, u32[]{:S(2)}) collective-permute-start(bf16[256,1024]{1,0:T(8,128)(2,1)} %get-tuple-element.461), channel_id=1, source_target_pairs={{0,8},{4,12},{8,0},{12,4},{16,24},{20,28},{24,16},{28,20},{1,9},{5... | collective-permute-start | bytes 1572872 | tf_op jit(solution)/shard_map/ppermute | solution.py:822
  545.4 28.3 %collective-permute-start.46 = (bf16[256,1024]{1,0:T(8,128)(2,1)}, bf16[256,1024]{1,0:T(8,128)(2,1)}, u32[]{:S(2)}, u32[]{:S(2)}) collective-permute-start(bf16[256,1024]{1,0:T(8,128)(2,1)} %get-tuple-element.463), channel_id=1, source_target_pairs={{0,16},{4,20},{8,24},{12,28},{16,0},{20,4},{24,8},{28,12},{1,17},{... | collective-permute-start | bytes 1572872 | tf_op jit(solution)/shard_map/ppermute | solution.py:822
  (93 other events, 1284.5 us)
Sparse Core Ops, SparseCore 0:
  12.0 37.2 all-gather.3
  51.2 54.3 all-gather.5
  107.5 125.3 all-gather.7

commit v4 on v3

--- a/solution.py
+++ b/solution.py
@@ -147,71 +147,88 @@
     return pl.multiple_of(lax.rem(place - chunk + count, count) * rows, rows)
 
 
+def stack_heads(target, source):
+    rows, width = source.shape
+    for head in range(width // HEAD_SIZE):
+        target[head * rows : (head + 1) * rows, :] = source[
+            :, head * HEAD_SIZE : (head + 1) * HEAD_SIZE
+        ]
+
+
+def fill_bias(bias, key_docs, query_docs, earlier):
+    rows = key_docs.shape[0]
+    row_index = lax.broadcasted_iota(jnp.int32, (rows, rows), 0)
+    column_index = lax.broadcasted_iota(jnp.int32, (rows, rows), 1)
+    same = (key_docs == query_docs) & ((row_index <= column_index) | earlier)
+    values = jnp.where(same, 0.0, NEGATIVE)
+    for first in range(0, bias.shape[1], rows):
+        bias[:, first : first + rows] = values
+
+
 def forward_kernel(
-    count, place_ref, own_ref, all_ref, docq_ref, dock_ref, o_ref, lse_ref, bias, scores
+    count,
+    place_ref,
+    own_ref,
+    all_ref,
+    docq_ref,
+    dock_ref,
+    o_ref,
+    lse_ref,
+    bias,
+    queries,
+    values_all,
+    mixed,
 ):
     chunk = pl.program_id(1)
     place = place_ref[0]
     rows = own_ref.shape[0]
     heads = GROUP_QUERY // HEAD_SIZE
-    row_index = lax.broadcasted_iota(jnp.int32, (rows, rows), 0)
-    column_index = lax.broadcasted_iota(jnp.int32, (rows, rows), 1)
-
-    def score(j, peaks):
+    stack_heads(queries, own_ref.at[:, :GROUP_QUERY])
+
+    @pl.when(chunk == 0)
+    def _():
+        values = all_ref[:, GROUP_QUERY:].astype(jnp.float32)
+        values_all[...] = values.T[HEAD_SIZE:].astype(jnp.bfloat16)
+
+    mixed[...] = jnp.zeros_like(mixed)
+
+    def block(j, carry):
+        peaks, total = carry
         offset = ring_offset(place, j, count, rows)
-        same = dock_ref[pl.ds(offset, rows), :] == docq_ref[...]
-        same = same & ((row_index <= column_index) | (j < chunk))
-        bias[...] = jnp.where(same, 0.0, NEGATIVE)
-        keys = all_ref[pl.ds(offset, rows), GROUP_QUERY : GROUP_QUERY + HEAD_SIZE]
-        result = []
-        for head in range(heads):
-            query = own_ref[:, head * HEAD_SIZE : (head + 1) * HEAD_SIZE]
-            block = dot_nt(keys, query) + bias[...]
-            scores[head, j] = block
-            result.append(jnp.maximum(peaks[head], jnp.max(block, axis=0, keepdims=True)))
-        return tuple(result)
-
-    peaks = lax.fori_loop(
+        piece = pl.ds(offset, rows)
+        fill_bias(bias, dock_ref[piece, :], docq_ref[...], j < chunk)
+        keys = all_ref[piece, GROUP_QUERY : GROUP_QUERY + HEAD_SIZE]
+        scores = dot_nt(keys, queries[...]) + bias[...]
+        higher = jnp.maximum(peaks, jnp.max(scores, axis=0, keepdims=True))
+        probs = jnp.exp(scores - higher)
+        scale = jnp.exp(peaks - higher)
+        mixed[...] = mixed[...] * scale + dot_nn(
+            values_all[:, piece], probs.astype(jnp.bfloat16)
+        )
+        return higher, total * scale + jnp.sum(probs, axis=0, keepdims=True)
+
+    peaks, total = lax.fori_loop(
         0,
         chunk + 1,
-        score,
-        tuple(jnp.full((1, rows), NEGATIVE, jnp.float32) for _ in range(heads)),
-    )
-
-    def mix(j, carry):
-        offset = ring_offset(place, j, count, rows)
-        values = all_ref[pl.ds(offset, rows), GROUP_QUERY + HEAD_SIZE :]
-        values = jnp.concatenate([values, jnp.ones_like(values)], axis=1)
-        result = []
-        for head in range(heads):
-            probs = jnp.exp(scores[head, j] - peaks[head])
-            total = carry[head][1] + jnp.sum(probs, axis=0, keepdims=True)
-            result.append((carry[head][0] + dot_tn(probs.astype(jnp.bfloat16), values), total))
-        return tuple(result)
-
-    sums = lax.fori_loop(
-        0,
-        chunk + 1,
-        mix,
-        tuple(
-            (
-                jnp.zeros((rows, 2 * HEAD_SIZE), jnp.float32),
-                jnp.zeros((1, rows), jnp.float32),
-            )
-            for _ in range(heads)
+        block,
+        (
+            jnp.full((1, heads * rows), NEGATIVE, jnp.float32),
+            jnp.zeros((1, heads * rows), jnp.float32),
         ),
     )
-    for head in range(heads):
-        mixed, total = sums[head]
-        o_ref[:, head * HEAD_SIZE : (head + 1) * HEAD_SIZE] = (
-            mixed[:, :HEAD_SIZE] / mixed[:, HEAD_SIZE:]
-        ).astype(jnp.bfloat16)
-        lse_ref[head : head + 1, :] = peaks[head] + jnp.log(total)
+    lse_ref[:1, :] = peaks + jnp.log(total)
+    result = mixed[...] / total
+    for head in range(0, heads, 2):
+        pair = jnp.concatenate(
+            [result[:, (head + i) * rows : (head + i + 1) * rows] for i in range(2)], axis=0
+        )
+        o_ref[:, head * HEAD_SIZE : (head + 2) * HEAD_SIZE] = pair.T.astype(jnp.bfloat16)
 
 
 def attention_forward(joint, docs, place, count, groups):
     total_rows = joint.shape[0]
     rows = total_rows // count
+    stacked = rows * GROUP_QUERY // HEAD_SIZE
 
     def block(c, place_ref):
         return lax.rem(place_ref[0] - c + count, count)
@@ -227,11 +244,13 @@
         ],
         out_specs=[
             pl.BlockSpec((rows, GROUP_QUERY), lambda g, c, p: (block(c, p), g)),
-            pl.BlockSpec((8, rows), lambda g, c, p: (g, block(c, p))),
+            pl.BlockSpec((8, stacked), lambda g, c, p: (g, block(c, p))),
         ],
         scratch_shapes=[
-            pltpu.VMEM((rows, rows), jnp.float32),
-            pltpu.VMEM((GROUP_QUERY // HEAD_SIZE, count, rows, rows), jnp.float32),
+            pltpu.VMEM((rows, stacked), jnp.float32),
+            pltpu.VMEM((stacked, HEAD_SIZE), jnp.bfloat16),
+            pltpu.VMEM((HEAD_SIZE, total_rows), jnp.bfloat16),
+            pltpu.VMEM((HEAD_SIZE, stacked), jnp.float32),
         ],
     )
     return pl.pallas_call(
@@ -239,7 +258,7 @@
         grid_spec=spec,
         out_shape=[
             jax.ShapeDtypeStruct((total_rows, GROUP_QUERY * groups), jnp.bfloat16),
-            jax.ShapeDtypeStruct((8 * groups, total_rows), jnp.float32),
+            jax.ShapeDtypeStruct((8 * groups, stacked * count), jnp.float32),
         ],
         compiler_params=parameters(),
         cost_estimate=SMALL_COST,
@@ -250,65 +269,62 @@
 def backward_kernel(count, place_ref, *refs):
     own_ref, all_ref, o_ref = refs[:3]
     lse_ref, docq_ref, dock_ref, cos_ref, sin_ref = refs[3 + count : 8 + count]
-    out_ref, bias, grad_out, sum_q, sum_kv = refs[8 + count :]
+    out_ref, bias, queries, grads, keys_all, values_all, sum_q, sum_k, sum_v = refs[8 + count :]
     chunk = pl.program_id(0)
     place = place_ref[0]
     rows = own_ref.shape[0]
     heads = GROUP_QUERY // HEAD_SIZE
-    row_index = lax.broadcasted_iota(jnp.int32, (rows, rows), 0)
-    column_index = lax.broadcasted_iota(jnp.int32, (rows, rows), 1)
-
+    stack_heads(queries, own_ref.at[:, :GROUP_QUERY])
     for index in range(count):
 
         @pl.when(lax.rem(place - chunk + count, count) == index)
         def _():
-            grad_out[...] = refs[3 + index][...]
+            stack_heads(grads, refs[3 + index])
 
     @pl.when(chunk == 0)
     def _():
-        sum_kv[...] = jnp.zeros_like(sum_kv)
+        keys_all[...] = all_ref[:, GROUP_QUERY : GROUP_QUERY + HEAD_SIZE]
+        values_all[...] = all_ref[:, GROUP_QUERY + HEAD_SIZE :]
+        sum_k[...] = jnp.zeros_like(sum_k)
+        sum_v[...] = jnp.zeros_like(sum_v)
 
     sum_q[...] = jnp.zeros_like(sum_q)
-    owner = lax.broadcasted_iota(jnp.int32, (8, GROUP_QUERY), 0)
-    head_of = lax.broadcasted_iota(jnp.int32, (8, GROUP_QUERY), 1) // HEAD_SIZE
-    selector = jnp.where(owner == head_of, 1.0, 0.0).astype(jnp.bfloat16)
-    both = o_ref[...].astype(jnp.float32) * grad_out[...].astype(jnp.float32)
-    high = both.astype(jnp.bfloat16)
-    low = (both - high.astype(jnp.float32)).astype(jnp.bfloat16)
-    inner = dot_nt(selector, high) + dot_nt(selector, low)
+    ones = jnp.ones((8, HEAD_SIZE), jnp.bfloat16)
+    inner = []
+    for head in range(heads):
+        attended = o_ref[:, head * HEAD_SIZE : (head + 1) * HEAD_SIZE].astype(jnp.float32)
+        both = attended * grads[head * rows : (head + 1) * rows, :].astype(jnp.float32)
+        high = both.astype(jnp.bfloat16)
+        low = (both - high.astype(jnp.float32)).astype(jnp.bfloat16)
+        inner.append((dot_nt(ones, high) + dot_nt(ones, low))[:1])
+    inner = jnp.concatenate(inner, axis=1)
 
     def block(j, carry):
         offset = ring_offset(place, j, count, rows)
-        same = dock_ref[pl.ds(offset, rows), :] == docq_ref[...]
-        same = same & ((row_index <= column_index) | (j < chunk))
-        bias[...] = jnp.where(same, 0.0, NEGATIVE)
-        keys = all_ref[pl.ds(offset, rows), GROUP_QUERY : GROUP_QUERY + HEAD_SIZE]
-        values = all_ref[pl.ds(offset, rows), GROUP_QUERY + HEAD_SIZE :]
-        key_sum = jnp.zeros((rows, HEAD_SIZE), jnp.float32)
-        value_sum = jnp.zeros((rows, HEAD_SIZE), jnp.float32)
-        for head in range(heads):
-            lanes = slice(head * HEAD_SIZE, (head + 1) * HEAD_SIZE)
-            query = own_ref[:, lanes]
-            grad = grad_out[:, lanes]
-            probs = jnp.exp(dot_nt(keys, query) + bias[...] - lse_ref[head : head + 1, :])
-            grad_probs = dot_nt(values, grad)
-            grad_scores = (probs * (grad_probs - inner[head : head + 1, :])).astype(jnp.bfloat16)
-            value_sum += dot_nn(probs.astype(jnp.bfloat16), grad)
-            key_sum += dot_nn(grad_scores, query)
-            sum_q[:, lanes] += dot_tn(grad_scores, keys)
-        sum_kv[pl.ds(offset, rows), :HEAD_SIZE] += key_sum
-        sum_kv[pl.ds(offset, rows), HEAD_SIZE:] += value_sum
+        piece = pl.ds(offset, rows)
+        fill_bias(bias, dock_ref[piece, :], docq_ref[...], j < chunk)
+        probs = jnp.exp(dot_nt(keys_all[piece, :], queries[...]) + bias[...] - lse_ref[:1, :])
+        grad_probs = dot_nt(values_all[piece, :], grads[...])
+        grad_scores = (probs * (grad_probs - inner)).astype(jnp.bfloat16)
+        sum_v[piece, :] += dot_nn(probs.astype(jnp.bfloat16), grads[...])
+        sum_k[piece, :] += dot_nn(grad_scores, queries[...])
+        sum_q[...] += dot_tn(grad_scores, keys_all[piece, :])
         return carry
 
     lax.fori_loop(0, chunk + 1, block, 0)
     own = pl.ds(ring_offset(place, chunk, count, rows), rows)
-    for start in range(0, GROUP_QUERY, 128):
-        part = turned(sum_q[:, start : start + 128], cos_ref[own, :], -sin_ref[own, :], start)
+    for first in range(0, heads, 2):
+        start = first * HEAD_SIZE
+        part = jnp.concatenate(
+            [sum_q[(first + i) * rows : (first + i + 1) * rows, :] for i in range(2)], axis=1
+        )
+        part = turned(part, cos_ref[own, :], -sin_ref[own, :], start)
         out_ref[own, start : start + 128] = (part * HEAD_SIZE ** (-0.5)).astype(jnp.bfloat16)
 
     @pl.when(chunk == count - 1)
     def _():
-        part = turned(sum_kv[...], cos_ref[...], -sin_ref[...], GROUP_QUERY)
+        part = jnp.concatenate([sum_k[...], sum_v[...]], axis=1)
+        part = turned(part, cos_ref[...], -sin_ref[...], GROUP_QUERY)
         out_ref[:, GROUP_QUERY:] = part.astype(jnp.bfloat16)
 
 
@@ -316,6 +332,7 @@
     count = len(grads)
     total_rows = joint.shape[0]
     rows = total_rows // count
+    stacked = rows * GROUP_QUERY // HEAD_SIZE
 
     def block(c, place_ref):
         return lax.rem(place_ref[0] - c + count, count)
@@ -329,7 +346,7 @@
             pl.BlockSpec((total_rows, GROUP_WIDTH), lambda c, p: (0, group)),
             pl.BlockSpec((rows, GROUP_QUERY), lambda c, p: (block(c, p), group)),
             *[pl.BlockSpec((rows, GROUP_QUERY), lambda c, p: (0, group))] * count,
-            pl.BlockSpec((8, rows), lambda c, p: (group, block(c, p))),
+            pl.BlockSpec((8, stacked), lambda c, p: (group, block(c, p))),
             pl.BlockSpec((1, rows), lambda c, p: (0, block(c, p))),
             pl.BlockSpec((total_rows, 1), lambda c, p: (0, 0)),
             table,
@@ -337,10 +354,11 @@
         ],
         out_specs=pl.BlockSpec((total_rows, GROUP_WIDTH), lambda c, p: (0, 0)),
         scratch_shapes=[
-            pltpu.VMEM((rows, rows), jnp.float32),
-            pltpu.VMEM((rows, GROUP_QUERY), jnp.bfloat16),
-            pltpu.VMEM((rows, GROUP_QUERY), jnp.float32),
-            pltpu.VMEM((total_rows, 2 * HEAD_SIZE), jnp.float32),
+            pltpu.VMEM((rows, stacked), jnp.float32),
+            *[pltpu.VMEM((stacked, HEAD_SIZE), jnp.bfloat16)] * 2,
+            *[pltpu.VMEM((total_rows, HEAD_SIZE), jnp.bfloat16)] * 2,
+            pltpu.VMEM((stacked, HEAD_SIZE), jnp.float32),
+            *[pltpu.VMEM((total_rows, HEAD_SIZE), jnp.float32)] * 2,
         ],
     )
     return pl.pallas_call(
@@ -401,13 +419,14 @@
         )
 
 
-def transposed_product(xs, weight, block, parts):
+def transposed_product(xs, weight, column, parts, block=0, blocks=1):
     rows, depth = xs[0].shape
+    rows //= blocks
     width = weight.shape[0]
     tile = tile_of(width)
-    specs = [pl.BlockSpec((rows, depth), lambda t: (0, 0))] * len(xs)
+    specs = [pl.BlockSpec((rows, depth), lambda t: (block, 0))] * len(xs)
     for index in range(len(xs)):
-        specs.append(pl.BlockSpec((tile, depth), lambda t, index=index: (t, block + index)))
+        specs.append(pl.BlockSpec((tile, depth), lambda t, index=index: (t, column + index)))
     part = (rows // parts, width)
     return pl.pallas_call(
         functools.partial(transposed_kernel, len(xs), parts),
@@ -640,47 +659,52 @@
     return result[:2], list(result[2:])
 
 
-def weight_kernel(parts, count, blocks, split, place_ref, *refs):
-    if parts == 1:
-        x = refs[0][...]
-    else:
-        x = jnp.concatenate([ref[...] for ref in refs[:parts]], axis=0)
-    ys = refs[parts : parts + count]
+def weight_kernel(counts, blocks, split, place_ref, *refs):
     step = pl.program_id(0)
+    total_refs = sum(parts + widths for parts, widths in counts)
+    received = refs[total_refs] if len(refs) > total_refs + 1 else None
+    place = 0
     column = 0
-    for y_ref in ys:
-        width = y_ref.shape[1]
-        piece = math.gcd(width, split) if width > split else width
-        piece = math.gcd(piece, 1024) if piece > 1024 else piece
-        for first in range(0, width, piece):
-            total = dot_tn(x, y_ref[:, first : first + piece])
-            start = column + first
-            if len(refs) == parts + count + 1:
-                refs[-1][:, start : start + piece] = total.astype(jnp.bfloat16)
-                continue
-            total += refs[parts + count][:, start : start + piece].astype(jnp.float32)
-            total = total.astype(jnp.bfloat16)
-            keep = step < blocks // 2 if start < split else lax.rem(step, 2) == 0
-            keep_ref, send_ref = refs[-4:-2] if start < split else refs[-2:]
-            columns = slice(start % split, start % split + piece)
-
-            @pl.when(keep)
-            def _():
-                keep_ref[:, columns] = total
-
-            @pl.when(jnp.logical_not(keep))
-            def _():
-                send_ref[:, columns] = total
-
-        column += width
-
-
-def weight_product(xs, ys, place, count, received):
-    depth = xs[0].shape[1]
-    rows = xs[0].shape[0]
+    for parts, widths in counts:
+        x = refs[place][...]
+        if parts > 1:
+            x = jnp.concatenate([ref[...] for ref in refs[place : place + parts]], axis=0)
+        for y_ref in refs[place + parts : place + parts + widths]:
+            width = y_ref.shape[1]
+            cuts = set(range(0, width, 1024)) | {width}
+            if column < split < column + width:
+                cuts.add(split - column)
+            cuts = sorted(cuts)
+            for first, last in zip(cuts[:-1], cuts[1:]):
+                total = dot_tn(x, y_ref[:, first:last])
+                start, end = column + first, column + last
+                if received is None:
+                    refs[-1][:, start:end] = total.astype(jnp.bfloat16)
+                    continue
+                total += received[:, start:end].astype(jnp.float32)
+                total = total.astype(jnp.bfloat16)
+                low = start < split
+                keep = step < blocks // 2 if low else lax.rem(step, 2) == 0
+                keep_ref, send_ref = refs[-4:-2] if low else refs[-2:]
+                columns = slice(start, end) if low else slice(start - split, end - split)
+
+                @pl.when(keep)
+                def _():
+                    keep_ref[:, columns] = total
+
+                @pl.when(jnp.logical_not(keep))
+                def _():
+                    send_ref[:, columns] = total
+
+            column += width
+        place += parts + widths
+
+
+def weight_product(pairs, place, count, received):
+    depth = pairs[0][0][0].shape[1]
     blocks = count // 2
     tile = depth // count
-    total = sum(y.shape[1] for y in ys)
+    total = sum(y.shape[1] for _, ys in pairs for y in ys)
     split = -(-total // 256) * 128
     side = 1 if received is None else 0
     whole = pl.BlockSpec((tile, total), lambda t, p: (t, 0))
@@ -699,16 +723,26 @@
             jax.ShapeDtypeStruct((depth // 4, width), jnp.bfloat16)
             for width in (split, split, total - split, total - split)
         ]
-    specs = [
-        pl.BlockSpec((rows, tile), lambda t, p: (0, lax.bitwise_xor(p[0], 2 * t + side)))
-    ] * len(xs)
-    specs += [pl.BlockSpec(y.shape, lambda t, p: (0, 0)) for y in ys]
-    operands = [*xs, *ys]
+    specs = []
+    operands = []
+    for xs, ys in pairs:
+        for x in xs:
+            specs.append(
+                pl.BlockSpec(
+                    (x.shape[0], tile), lambda t, p: (0, lax.bitwise_xor(p[0], 2 * t + side))
+                )
+            )
+        specs += [
+            pl.BlockSpec(y.shape, lambda t, p: (0, 0), pipeline_mode=pl.Buffered(1)) for y in ys
+        ]
+        operands.extend([*xs, *ys])
     if received is not None:
         specs.append(whole)
         operands.append(received)
     return pl.pallas_call(
-        functools.partial(weight_kernel, len(xs), len(ys), blocks, split),
+        functools.partial(
+            weight_kernel, [(len(xs), len(ys)) for xs, ys in pairs], blocks, split
+        ),
         grid_spec=pltpu.PrefetchScalarGridSpec(
             num_scalar_prefetch=1, grid=(blocks,), in_specs=specs, out_specs=out_specs
         ),
@@ -719,25 +753,39 @@
     )(place, *operands)
 
 
-def fold_kernel(count, *refs):
-    for index in range(count):
-        first, second = refs[2 * index : 2 * index + 2]
-        keep, send = refs[2 * count + 2 * index : 2 * count + 2 * index + 2]
-        rows = keep.shape[0]
-        total = first[...].astype(jnp.float32) + second[...].astype(jnp.float32)
-        total = total.astype(jnp.bfloat16)
-        keep[...] = total[:rows]
-        send[...] = total[rows:]
-
-
-def fold(values):
-    shapes = []
-    for value in values[::2]:
-        shape = (value.shape[0] // 2, value.shape[1])
-        shapes.extend([jax.ShapeDtypeStruct(shape, jnp.bfloat16)] * 2)
+def fold_kernel(counts, *refs):
+    outs = refs[sum(counts) :]
+    place = 0
+    row = 0
+    for index, count in enumerate(counts):
+        total = refs[place][...].astype(jnp.float32)
+        for ref in refs[place + 1 : place + count]:
+            total += ref[...].astype(jnp.float32)
+        out = outs[index % 2]
+        rows = total.shape[0]
+        out[row : row + rows, :] = total.astype(jnp.bfloat16)
+        row += rows * (index % 2)
+        place += count
+
+
+def fold(sums, rows):
+    counts = [len(terms) for pair in sums for terms in pair]
+    values = [value for pair in sums for terms in pair for value in terms]
+    widths = [terms[0].shape[1] for terms in sums[0]]
+    steps = 2 if all(width % 256 == 0 for width in widths) else 1
     return pl.pallas_call(
-        functools.partial(fold_kernel, len(values) // 2),
-        out_shape=shapes,
+        functools.partial(fold_kernel, counts),
+        grid=(steps,),
+        in_specs=[
+            pl.BlockSpec((rows, value.shape[1] // steps), lambda t: (1, t)) for value in values
+        ],
+        out_specs=[
+            pl.BlockSpec((rows * len(sums), width // steps), lambda t: (0, t))
+            for width in widths
+        ],
+        out_shape=[
+            jax.ShapeDtypeStruct((rows * len(sums), width), jnp.bfloat16) for width in widths
+        ],
         compiler_params=parameters(),
         cost_estimate=SMALL_COST,
         name="fold",
@@ -824,19 +872,34 @@
     def gather(self, shard):
         return lax.all_gather(shard, "dp", axis=0, tiled=True)
 
-    def begin(self, pieces, level):
+
+    def send(self, pieces, level):
         orders = (self.steps[::-1], self.steps[:1] + self.steps[:0:-1])
-        result = []
-        for side in range(2):
-            keep, send = pieces[2 * side : 2 * side + 2]
-            result.extend([keep, self.swap(send, orders[side][level])])
-        return result
-
-    def advance(self, values, level=1):
-        while level < len(self.steps):
-            values = self.begin(fold(values), level)
+        return [self.swap(piece, order[level]) for piece, order in zip(pieces, orders)]
+
+    def begin(self, pieces):
+        moved = self.send([pieces[1], pieces[3]], 0)
+        return [[pieces[0], moved[0]], [pieces[2], moved[1]]]
+
+    def fold(self, sums, level=1):
+        return fold(sums, sums[0][0][0].shape[0] >> level)
+
+    def advance(self, sums, folded):
+        level = 1
+        while True:
+            moved = self.send(folded, level)
             level += 1
-        return values
+            if level == len(self.steps):
+                return sums, moved
+            rows = moved[0].shape[0] // len(sums)
+            sums = [
+                [
+                    terms + [part[index * rows : (index + 1) * rows]]
+                    for terms, part in zip(pair, moved)
+                ]
+                for index, pair in enumerate(sums)
+            ]
+            folded = self.fold(sums, level)
 
     def hop(self, value, shift=1):
         return lax.ppermute(
@@ -868,14 +931,18 @@
         ]
 
 
-def total_of(values):
-    return jnp.concatenate(
-        [
-            first.astype(jnp.float32) + second.astype(jnp.float32)
-            for first, second in zip(values[::2], values[1::2])
-        ],
-        axis=1,
-    )
+def totals_of(sums, moved):
+    rows = moved[0].shape[0] // len(sums)
+    result = []
+    for index, pair in enumerate(sums):
+        halves = []
+        for terms, last in zip(pair, moved):
+            total = last[index * rows : (index + 1) * rows].astype(jnp.float32)
+            for term in terms:
+                total = total + term[:rows].astype(jnp.float32)
+            halves.append(total)
+        result.append(jnp.concatenate(halves, axis=1))
+    return result
 
 
 def back_norm(grad_normed, scaled, inverse, scale_row):
@@ -1012,7 +1079,7 @@
         cotangent_chunks.append(moved)
 
     def weights(xs, ys, received=None):
-        return weight_product(xs, ys, dp_place, dp_count, received)
+        return weight_product([(xs, ys)], dp_place, dp_count, received)
 
     ordered = cotangent_chunks[1:] + cotangent_chunks[:1]
     total = grads[0]
@@ -1028,30 +1095,45 @@
         if j == 2:
             downward, parts = lower(pairs - 1, tie(downward, total))
             grads.extend(parts)
-            moved, downward, grads = together(moved, downward, grads)
+            attended_local = join(tie(attended_parts, parts), list(range(ring)))
+            moved, downward, grads, attended_local = together(
+                moved, downward, grads, attended_local
+            )
             grad_gate, grad_up = downward
         if j == 3:
             gate_part = weights([tie(normed_two, total)], [grad_gate])
-            up_part = weights([tie(normed_two, gate_part)], [grad_up])
-            down_part = weights(tie(ordered, up_part), [product], down_part)
-            moved, gate_part, up_part, down_part = together(moved, gate_part, up_part, down_part)
+            branch = transposed_product(
+                [tie(product, gate_part)], ff_full, 2, ring // 2, 0, 2
+            )
+            down_part = weights(tie(ordered, branch), [product], down_part)
+            moved, gate_part, branch, down_part = together(moved, gate_part, branch, down_part)
+    gate_part = mover.swap(gate_part, 1)
+    down_part = mover.begin(down_part)
     grad_hidden, grad_branch, grad_parts = residual_gradient(
         local_cotangent, hidden_res, moved, grads[-1], gain_two, output_full, ring
     )
+    grad_hidden, grad_branch, grad_parts, gate_part = together(
+        grad_hidden, grad_branch, grad_parts, gate_part
+    )
 
     grad_parts = mover.exchange(grad_parts)
-    gate_part, up_part = mover.swap(gate_part, 1), mover.swap(up_part, 1)
-    down_part = mover.begin(down_part, 0)
-    branch = transposed_product([tie(product, grad_branch)], ff_full, 2, ring)
-    gate_part = weights([tie(normed_two, branch)], [grad_gate], gate_part)
-    grad_parts, branch, gate_part, up_part, down_part = together(
-        grad_parts, branch, gate_part, up_part, down_part
+    output_part = weights([grad_branch], [attended_local])
+    gate_part = weights([tie(normed_two, output_part)], [grad_gate], gate_part)
+    grad_parts, output_part, gate_part, down_part = together(
+        grad_parts, output_part, gate_part, down_part
     )
     grad_joint = []
     sent = 0
+    folded = []
     moved = branch[0]
     for group in range(groups):
         moved = mover.hop(moved)
+        sent += 1
+        if group == 0:
+            output_part = mover.swap(output_part, 1)
+            gate_part = mover.begin(gate_part)
+        else:
+            output_part = mover.begin(output_part)
         grad_joint.append(
             attention_backward(
                 joint,
@@ -1066,59 +1148,72 @@
             )
         )
         if group == 0:
-            up_part = weights([tie(normed_two, grad_joint)], [grad_up], up_part)
-            gate_part = mover.begin(gate_part, 0)
-        else:
-            up_part = mover.begin(up_part, 0)
+            output_part = weights(
+                [tie(grad_branch, grad_joint)], [attended_local], output_part
+            )
         if group + 1 == groups:
             grads = transposed_product(grad_joint, joint_full, 0, ring)
-        moved, grad_joint, grads, gate_part, up_part = together(
-            moved, grad_joint, grads, gate_part, up_part
+            folded = mover.fold(tie([gate_part, down_part], grads))
+        moved, grad_joint, grads, gate_part, output_part, folded = together(
+            moved, grad_joint, grads, gate_part, output_part, folded
         )
-        sent += 1
         if group + 1 < groups:
             moved = add(moved, branch[sent])
     if groups == 1:
-        up_part = mover.begin(up_part, 0)
+        output_part = mover.begin(output_part)
     branch_moved = moved
-    attended_local = join(attended_parts, list(range(ring)))
     moved = grads[0]
+
+    def last_weights(total, received):
+        return weight_product(
+            [([tie(normed_two, total)], [grad_up]), ([normed_one], grad_joint)],
+            dp_place,
+            dp_count,
+            received,
+        )
+
     for j in range(1, ring):
         total = grads[1] if j == 1 else add(moved, grads[j])
         moved = mover.hop(total)
         if j == 1:
-            gate_part, down_part = mover.advance(gate_part), mover.advance(down_part)
-            output_part = weights([tie(grad_branch, total)], [attended_local])
-            joint_part = weights([tie(normed_one, output_part)], grad_joint)
-            output_part = mover.swap(output_part, 1)
-            output_part = weights([tie(grad_branch, joint_part)], [attended_local], output_part)
-            moved, joint_part, output_part, gate_part, down_part = together(
-                moved, joint_part, output_part, gate_part, down_part
+            first_parts = mover.advance([gate_part, down_part], folded)
+            folded = mover.fold(tie([output_part], total))
+            last_part = last_weights(folded, None)
+            branch = branch + transposed_product(
+                [tie(product, last_part)], ff_full, 2, ring // 2, 1, 2
+            )
+            moved, last_part, branch, folded, first_parts = together(
+                moved, last_part, branch, folded, first_parts
             )
         if j == 2:
-            output_part = mover.begin(output_part, 0)
-            joint_part = mover.swap(joint_part, 1)
-            joint_part = weights([tie(normed_one, total)], grad_joint, joint_part)
-            moved, joint_part, output_part = together(moved, joint_part, output_part)
+            output_part = mover.advance([output_part], folded)
+            last_part = last_weights(total, mover.swap(last_part, 1))
+            gate_out, down_out = totals_of(*first_parts)
+            down_out = down_out.T
+            next_branch = add(branch_moved, branch[sent])
+            moved, last_part, output_part, gate_out, down_out, next_branch = together(
+                moved, last_part, output_part, gate_out, down_out, next_branch
+            )
         if j == 3:
-            output_part = mover.advance(output_part)
-            up_part = mover.advance(up_part)
-            joint_part = mover.begin(joint_part, 0)
-            moved, joint_part, output_part, up_part = together(
-                moved, joint_part, output_part, up_part
-            )
-    joint_part = mover.advance(joint_part)
-    for j in range(sent, ring - 1):
-        branch_moved = mover.hop(add(branch_moved, branch[j]))
-    output_out = mover.collect(jnp.split(total_of(output_part), ring, axis=1)).T
+            last_part = mover.begin(last_part)
+            branch_moved = mover.hop(tie(next_branch, total))
+            sent += 1
+            output_out = jnp.split(totals_of(*output_part)[0], ring, axis=1)
+            moved, last_part, output_out = together(moved, last_part, output_out)
+    folded, output_out = together(mover.fold([last_part]), output_out)
+    last_part = mover.advance([last_part], folded)
+    output_out = mover.collect(output_out[:-1] + [tie(output_out[-1], last_part)]).T
     scaled_one, inverse_one = norm_rows(local_tokens.astype(f32))
     local_one = moved.astype(f32) + grads[0].astype(f32)
     input_gradient = grad_hidden + back_norm(local_one, scaled_one, inverse_one, gain_one)
+    branch_moved = tie(branch_moved, last_part)
+    for j in range(sent, ring - 1):
+        branch_moved = mover.hop(add(branch_moved, branch[j]))
     block_output = (
         hidden_res + (branch_moved.astype(f32) + branch[-1].astype(f32))
     ).astype(b16)
-    gate_out, up_out, joint_out = total_of(gate_part), total_of(up_part), total_of(joint_part)
-    down_out = total_of(down_part).T
+    last_out = totals_of(*last_part)[0]
+    up_out, joint_out = last_out[:, :hidden], last_out[:, hidden:]
 
     sums = jnp.stack(
         [

time: 644 us -> 617 us (0.958)
  Pallas kernels: 317 us -> 297 us
  waiting for transfers between devices: 170 us -> 159 us
    pallas_call x15 -> x11, Pallas kernels: 101 us -> 89.1 us  [the longest x8 80.2 us: weight_product(): pl.pallas_call(functools.partial(weight_kernel, [(len(xs), len(ys)) for x...]
    ppermute x25 -> x18, starting transfers between devices: 23.1 us -> 13.9 us  [swap(): lax.ppermute(value, 'dp', [(i, i ^ step) for i in range(self.dp_count)])]
    ppermute x3, waiting for transfers between devices: 9.97 us -> 1.3 us  [exchange(): lax.ppermute(parts[j], 'tensor', [(i, (i + j) % ring) for i in range(ring)])]
    pallas_call x2, Pallas kernels: 41.4 us -> 33.9 us  [attention_backward(): pl.pallas_call(functools.partial(backward_kernel, count), grid_spec=spec,...]
    ppermute x25 -> x18, waiting for transfers between devices: 16.7 us -> 12.1 us  [swap(): lax.ppermute(value, 'dp', [(i, i ^ step) for i in range(self.dp_count)])]
    pallas_call x2 -> x3, Pallas kernels: 21 us -> 25.1 us  [transposed_product(): pl.pallas_call(functools.partial(transposed_kernel, len(xs), parts), grid...]
  transfers between devices with their start and end apart: 58 -> 51, of which waited for: 20 -> 22; matrix products, arithmetic and copies ran while one was open for 8% -> 9% of each run, Pallas kernels for 49% -> 49%
where the time goes in v4:
time: 617 us; the launch traced here: 608 us
  Pallas kernels  297 us (48%)
  waiting for transfers between devices  159 us (26%)
  starting transfers between devices  70.6 us (11%)
  other arithmetic  39.9 us (6%)
  local copies, waits for them, and re-layouts  26 us (4%)
  between operations  15.1 us (2%)
    ppermute x18, waiting for transfers between devices, hop(): lax.ppermute(value, 'tensor', [(i, (i + shift) % self.ring) for i in rang...  121 us
    pallas_call x8, Pallas kernels, weight_product(): pl.pallas_call(functools.partial(weight_kernel, [(len(xs), len(ys)) for x...  80.2 us
    pallas_call x2, Pallas kernels, down_chunk(): pl.pallas_call(functools.partial(down_kernel, len(es), tiles), grid=(tile...  45 us
    pallas_call x2, Pallas kernels, attention_backward(): pl.pallas_call(functools.partial(backward_kernel, count), grid_spec=spec,...  33.9 us
    ppermute x18, starting transfers between devices, hop(): lax.ppermute(value, 'tensor', [(i, (i + shift) % self.ring) for i in rang...  33.6 us
    pallas_call x2, Pallas kernels, up_chunk(): pl.pallas_call(up_kernel, grid=(tiles,), in_specs=specs, out_specs=[pl.Bl...  28.6 us
    pallas_call x3, Pallas kernels, transposed_product(): pl.pallas_call(functools.partial(transposed_kernel, len(xs), parts), grid...  25.1 us
    pallas_call x4, Pallas kernels, project(): pl.pallas_call(project_kernel, grid=(groups,), in_specs=specs, out_specs=...  19.4 us
  transfers between devices with their start and end apart: 51, of which 22 were waited for; matrix products, arithmetic and copies ran while one was open for 9% of the time, Pallas kernels for 49%

profile of v4, /device:TPU:0, one launch (start us, length us, event | category | flops | bytes accessed | tf_op | source)
XLA Modules:
  0.0 607.8 jit_solution(8731736663773306895)
XLA Ops:
  25.0 10.0 %collective-permute-done.1.refs_2_ = bf16[256,512]{1,0:T(8,128)(2,1)} collective-permute-done((bf16[256,512]{1,0:T(8,128)(2,1)S(1)}, bf16[256,512]{1,0:T(8,128)(2,1)}, u32[]{:S(2)}, u32[]{:S(2)}) %collective-permute-start.1) | collective-permute-done | bytes 262176 | tf_op jit(solution)/shard_map/ppermute | solution.py:912
  58.1 10.0 %collective-permute-done.3.x_ref.refs_5_ = bf16[256,2048]{1,0:T(8,128)(2,1)S(1)} collective-permute-done((bf16[256,2048]{1,0:T(8,128)(2,1)S(1)}, bf16[256,2048]{1,0:T(8,128)(2,1)S(1)}, u32[]{:S(2)}, u32[]{:S(2)}) %collective-permute-start.3) | collective-permute-done | bytes 1048608 | tf_op jit(solution)/shard_map/ppermute | solution.py:905
  74.5 18.8 %collective-permute-done.4.x_ref.refs_6_ = bf16[256,2048]{1,0:T(8,128)(2,1)S(1)} collective-permute-done((bf16[256,2048]{1,0:T(8,128)(2,1)S(1)}, bf16[256,2048]{1,0:T(8,128)(2,1)S(1)}, u32[]{:S(2)}, u32[]{:S(2)}) %collective-permute-start.4) | collective-permute-done | bytes 1048608 | tf_op jit(solution)/shard_map/ppermute | solution.py:905
  99.0 18.7 %collective-permute-done.5.x_ref.refs_7_ = bf16[256,2048]{1,0:T(8,128)(2,1)S(1)} collective-permute-done((bf16[256,2048]{1,0:T(8,128)(2,1)S(1)}, bf16[256,2048]{1,0:T(8,128)(2,1)S(1)}, u32[]{:S(2)}, u32[]{:S(2)}) %collective-permute-start.5) | collective-permute-done | bytes 1048608 | tf_op jit(solution)/shard_map/ppermute | solution.py:905
  124.2 17.8 %attend.1 = (bf16[1024,512]{1,0:T(8,128)(2,1)}, f32[16,4096]{1,0:T(8,128)}) custom-call(s32[1]{0:T(128)} %bitcast.10.place_ref, bf16[1024,768]{1,0:T(8,128)(2,1)} %get-tuple-element.285.own_ref.all_ref.refs_0_.refs_1_, bf16[1024,768]{1,0:T(8,128)(2,1)} %get-tuple-element.285.own_ref.all_ref.refs_0_.refs_1_, s32[1,1024]{1,0:T(1,128)} %bitcast.52, ...), custom_call_target="tpu_custom_call" | custom-call | flops 1 | bytes 1 | tf_op jit(solution)/shard_map/attend/pallas_call | solution.py:256
  145.7 19.6 %collective-permute-done.7.refs_1_ = bf16[1024,512]{1,0:T(8,128)(2,1)S(1)} collective-permute-done((bf16[1024,512]{1,0:T(8,128)(2,1)}, bf16[1024,512]{1,0:T(8,128)(2,1)S(1)}, u32[]{:S(2)}, u32[]{:S(2)}) %collective-permute-start.7) | collective-permute-done | bytes 1048608 | tf_op jit(solution)/shard_map/ppermute | solution.py:905
  169.4 18.6 %collective-permute-done.8.refs_2_ = bf16[1024,512]{1,0:T(8,128)(2,1)S(1)} collective-permute-done((bf16[1024,512]{1,0:T(8,128)(2,1)S(1)}, bf16[1024,512]{1,0:T(8,128)(2,1)S(1)}, u32[]{:S(2)}, u32[]{:S(2)}) %collective-permute-start.8) | collective-permute-done | bytes 1048608 | tf_op jit(solution)/shard_map/ppermute | solution.py:905
  192.8 13.9 %heads_product.1.partial_ref = f32[1024,2048]{1,0:T(8,128)} custom-call(bf16[1024,512]{1,0:T(8,128)(2,1)} %get-tuple-element.337.refs_0_.refs_2_, bf16[1024,512]{1,0:T(8,128)(2,1)} %copy-done.8, bf16[1024,512]{1,0:T(8,128)(2,1)} %copy-done.9, bf16[2048,2048]{1,0:T(8,128)(2,1)} %all-gather.6.cloned.1.call-done.refs_3_.weight_ref, bf16[256,2048]{1,0:T(8,128)(2,1)} %bitcast.34, ...), custom_call_target="tpu_custom_call" | custom-call | flops 1 | bytes 1 | tf_op jit(solution)/shard_map/heads_product/pallas_call | solution.py:472
  216.1 9.2 %after_attention.1 = (f32[256,2048]{1,0:T(8,128)}, bf16[1024,2048]{1,0:T(8,128)(2,1)}) custom-call(f32[1024,2048]{1,0:T(8,128)} %heads_product.1.partial_ref, bf16[1024,512]{1,0:T(8,128)(2,1)} %collective-permute-done.9.last_ref.refs_3_, bf16[2048,2048]{1,0:T(8,128)(2,1)} %all-gather.6.cloned.1.call-done.refs_3_.weight_ref, f32[1,2048]{1,0:T(1,128)} %copy.113.gain_ref), custom_call_target="tpu_custom_call" | custom-call | flops 1 | bytes 1 | tf_op jit(solution)/shard_map/after_attention/pallas_call | solution.py:505
  232.9 14.4 %up_chunk.2 = (bf16[1024,2048]{1,0:T(8,128)(2,1)}, bf16[1024,2048]{1,0:T(8,128)(2,1)}, bf16[1024,2048]{1,0:T(8,128)(2,1)}) custom-call(bf16[1024,2048]{1,0:T(8,128)(2,1)} %get-tuple-element.462.x_ref.refs_0_, bf16[2048,6144]{1,0:T(8,128)(2,1)} %all-gather.8.cloned.1.call-done.gate_ref.up_ref.refs_2_.refs_5_.refs_6_.refs_1_, ...), custom_call_target="tpu_custom_call" | custom-call | flops 1 | bytes 1 | tf_op jit(solution)/shard_map/up_chunk/pallas_call | solution.py:554
  248.9 22.4 %down_chunk.2 = (bf16[1024,2048]{1,0:T(8,128)(2,1)}, bf16[1024,2048]{1,0:T(8,128)(2,1)}, bf16[256,2048]{1,0:T(8,128)(2,1)}, bf16[256,2048]{1,0:T(8,128)(2,1)}) custom-call(bf16[256,2048]{1,0:T(8,128)(2,1)} %copy-done.3, bf16[256,2048]{1,0:T(8,128)(2,1)} %copy-done.4, ...), custom_call_target="tpu_custom_call" | custom-call | flops 1 | bytes 1 | tf_op jit(solution)/shard_map/down_chunk/pallas_call | solution.py:639
  274.5 14.1 %up_chunk.3 = (bf16[1024,2048]{1,0:T(8,128)(2,1)}, bf16[1024,2048]{1,0:T(8,128)(2,1)}, bf16[1024,2048]{1,0:T(8,128)(2,1)}) custom-call(bf16[1024,2048]{1,0:T(8,128)(2,1)} %get-tuple-element.462.x_ref.refs_0_, ...), custom_call_target="tpu_custom_call", output_to_operand_aliasing={{0}: (3, {}), {1}: (4, {}), {2}: (5, {})} | custom-call | flops 1 | bytes 1 | tf_op jit(solution)/shard_map/up_chunk/pallas_call | solution.py:554
  288.7 9.0 %weight_product.8 = bf16[1024,2048]{1,0:T(8,128)(2,1)} custom-call(s32[1]{0:T(128)} %bitcast.13.place_ref, bf16[256,2048]{1,0:T(8,128)(2,1)} %copy-done.3, bf16[256,2048]{1,0:T(8,128)(2,1)} %copy-done.4, bf16[256,2048]{1,0:T(8,128)(2,1)} %copy-done.5, bf16[256,2048]{1,0:T(8,128)(2,1)} %bitcast.39, bf16[1024,2048]{1,0:T(8,128)(2,1)} %get-tuple-element.451.refs_4_.refs_0_), custom_call_target="tpu_custom_call" | custom-call | flops 1 | bytes 1 | tf_op jit(solution)/shard_map/weight_product/pallas_call | solution.py:742
  301.7 22.5 %down_chunk.3 = (bf16[1024,2048]{1,0:T(8,128)(2,1)}, bf16[1024,2048]{1,0:T(8,128)(2,1)}, bf16[256,2048]{1,0:T(8,128)(2,1)}, bf16[256,2048]{1,0:T(8,128)(2,1)}) custom-call(bf16[256,2048]{1,0:T(8,128)(2,1)} %copy-done.5, bf16[256,2048]{1,0:T(8,128)(2,1)} %bitcast.40, ...), custom_call_target="tpu_custom_call", output_to_operand_aliasing={{0}: (7, {}), {1}: (8, {})} | custom-call | flops 1 | bytes 1 | tf_op jit(solution)/shard_map/down_chunk/pallas_call | solution.py:639
  330.7 8.8 %weight_product.9 = bf16[1024,2048]{1,0:T(8,128)(2,1)} custom-call(s32[1]{0:T(128)} %bitcast.13.place_ref, bf16[1024,2048]{1,0:T(8,128)(2,1)} %get-tuple-element.462.x_ref.refs_0_, bf16[1024,2048]{1,0:T(8,128)(2,1)} %get-tuple-element.344.refs_1_), custom_call_target="tpu_custom_call" | custom-call | flops 1 | bytes 1 | tf_op jit(solution)/shard_map/weight_product/pallas_call | solution.py:742
  348.1 10.9 %weight_product.10 = (bf16[512,1024]{1,0:T(8,128)(2,1)}, bf16[512,1024]{1,0:T(8,128)(2,1)}, bf16[512,1024]{1,0:T(8,128)(2,1)}, bf16[512,1024]{1,0:T(8,128)(2,1)}) custom-call(s32[1]{0:T(128)} %bitcast.13.place_ref, bf16[256,2048]{1,0:T(8,128)(2,1)} %copy-done.3, bf16[256,2048]{1,0:T(8,128)(2,1)} %copy-done.4, bf16[256,2048]{1,0:T(8,128)(2,1)} %copy-done.5, ...), custom_call_target="tpu_custom_call" | custom-call | flops 1 | bytes 1 | tf_op jit(solution)/shard_map/weight_product/pallas_call | solution.py:742
  361.2 10.6 %residual_gradient.1 = (f32[256,2048]{1,0:T(8,128)}, bf16[256,2048]{1,0:T(8,128)(2,1)}, bf16[256,512]{1,0:T(8,128)(2,1)}, bf16[256,512]{1,0:T(8,128)(2,1)}, bf16...) custom-call(bf16[256,2048]{1,0:T(8,128)(2,1)} %bitcast.42, f32[256,2048]{1,0:T(8,128)} %get-tuple-element.300.hidden_ref, ...), custom_call_target="tpu_custom_call" | custom-call | flops 1 | bytes 1 | tf_op jit(solution)/shard_map/residual_gradient/pallas_call | solution.py:823
  381.6 10.6 %weight_product.12 = (bf16[512,1024]{1,0:T(8,128)(2,1)}, bf16[512,1024]{1,0:T(8,128)(2,1)}, bf16[512,1024]{1,0:T(8,128)(2,1)}, bf16[512,1024]{1,0:T(8,128)(2,1)}) custom-call(s32[1]{0:T(128)} %bitcast.13.place_ref, bf16[1024,2048]{1,0:T(8,128)(2,1)} %get-tuple-element.462.x_ref.refs_0_, bf16[1024,2048]{1,0:T(8,128)(2,1)} %get-tuple-element.344.refs_1_, ...), custom_call_target="tpu_custom_call" | custom-call | flops 1 | bytes 1 | tf_op jit(solution)/shard_map/weight_product/pallas_call | solution.py:742
  401.9 16.9 %attend_back.2.refs_0_.refs_3_ = bf16[1024,384]{1,0:T(8,128)(2,1)} custom-call(s32[1]{0:T(128)} %bitcast.10.place_ref, bf16[1024,768]{1,0:T(8,128)(2,1)} %get-tuple-element.285.own_ref.all_ref.refs_0_.refs_1_, bf16[1024,768]{1,0:T(8,128)(2,1)} %get-tuple-element.285.own_ref.all_ref.refs_0_.refs_1_, bf16[1024,512]{1,0:T(8,128)(2,1)} %get-tuple-element.337.refs_0_.refs_2_, ...), custom_call_target="tpu_custom_call" | custom-call | flops 1 | bytes 1 | tf_op jit(solution)/shard_map/attend_back/pallas_call | solution.py:364
  431.1 17.0 %attend_back.3.refs_1_.refs_4_ = bf16[1024,384]{1,0:T(8,128)(2,1)} custom-call(s32[1]{0:T(128)} %bitcast.10.place_ref, bf16[1024,768]{1,0:T(8,128)(2,1)} %get-tuple-element.285.own_ref.all_ref.refs_0_.refs_1_, bf16[1024,768]{1,0:T(8,128)(2,1)} %get-tuple-element.285.own_ref.all_ref.refs_0_.refs_1_, bf16[1024,512]{1,0:T(8,128)(2,1)} %get-tuple-element.337.refs_0_.refs_2_, ...), custom_call_target="tpu_custom_call" | custom-call | flops 1 | bytes 1 | tf_op jit(solution)/shard_map/attend_back/pallas_call | solution.py:364
  465.4 12.1 %weight_product.14 = bf16[1024,2816]{1,0:T(8,128)(2,1)} custom-call(s32[1]{0:T(128)} %bitcast.13.place_ref, bf16[1024,2048]{1,0:T(8,128)(2,1)} %get-tuple-element.462.x_ref.refs_0_, bf16[1024,2048]{1,0:T(8,128)(2,1)} %get-tuple-element.447.refs_1_, bf16[1024,2048]{1,0:T(8,128)(2,1)} %get-tuple-element.448.refs_2_, ...), custom_call_target="tpu_custom_call" | custom-call | flops 1 | bytes 1 | tf_op jit(solution)/shard_map/weight_product/pallas_call | solution.py:742
  477.5 8.7 %transposed.5 = (bf16[256,2048]{1,0:T(8,128)(2,1)}, bf16[256,2048]{1,0:T(8,128)(2,1)}) custom-call(bf16[1024,2048]{1,0:T(8,128)(2,1)} %get-tuple-element.451.refs_4_.refs_0_, bf16[2048,6144]{1,0:T(8,128)(2,1)} %all-gather.8.cloned.1.call-done.gate_ref.up_ref.refs_2_.refs_5_.refs_6_.refs_1_), custom_call_target="tpu_custom_call" | custom-call | flops 1 | bytes 1 | tf_op jit(solution)/shard_map/transposed/pallas_call | solution.py:431
  502.0 16.6 %weight_product.15 = (bf16[512,1408]{1,0:T(8,128)(2,1)}, bf16[512,1408]{1,0:T(8,128)(2,1)}, bf16[512,1408]{1,0:T(8,128)(2,1)}, bf16[512,1408]{1,0:T(8,128)(2,1)}) custom-call(s32[1]{0:T(128)} %bitcast.13.place_ref, bf16[1024,2048]{1,0:T(8,128)(2,1)} %get-tuple-element.462.x_ref.refs_0_, bf16[1024,2048]{1,0:T(8,128)(2,1)} %get-tuple-element.447.refs_1_, ...), custom_call_target="tpu_custom_call" | custom-call | flops 1 | bytes 1 | tf_op jit(solution)/shard_map/weight_product/pallas_call | solution.py:742
  534.6 17.7 %collective-permute-done.37 = bf16[256,2048]{1,0:T(8,128)(2,1)} collective-permute-done((bf16[256,2048]{1,0:T(8,128)(2,1)}, bf16[256,2048]{1,0:T(8,128)(2,1)}, u32[]{:S(2)}, u32[]{:S(2)}) %collective-permute-start.37) | collective-permute-done | bytes 1048608 | tf_op jit(solution)/shard_map/ppermute | solution.py:905
  (307 shorter events, 243.7 us)
Async XLA Ops:
  7.2 42.1 %all-gather.4.cloned.1.call-start = ((), (), s32[]{:S(2)}) async-start(), calls=%async_computation | async-start | bytes 4128768 | tf_op jit(solution)/shard_map/all_gather | solution.py:873
  11.9 180.8 %all-gather.6.cloned.1.call-start = ((), (), s32[]{:S(2)}) async-start(), calls=%async_computation.1 | async-start | bytes 9437184 | tf_op jit(solution)/shard_map/all_gather | solution.py:873
  37.8 195.1 %all-gather.8.cloned.1.call-start = ((), (), s32[]{:S(2)}) async-start(), calls=%async_computation.2 | async-start | bytes 28311552 | tf_op jit(solution)/shard_map/all_gather | solution.py:873
  39.0 29.1 %collective-permute-start.3 = (bf16[256,2048]{1,0:T(8,128)(2,1)S(1)}, bf16[256,2048]{1,0:T(8,128)(2,1)S(1)}, u32[]{:S(2)}, u32[]{:S(2)}) collective-permute-start(bf16[256,2048]{1,0:T(8,128)(2,1)S(1)} %bitcast.35), channel_id=1, source_target_pairs={{0,1},{1,2},{2,3},{3,0},{4,5},{5,6},{6,7},{7,4},{8,9},{9,10},{10,1... | collective-permute-start | bytes 3145736 | tf_op jit(solution)/shard_map/ppermute | solution.py:905
  213.6 33.7 %collective-permute-start.10 = (bf16[256,2048]{1,0:T(8,128)(2,1)S(1)}, bf16[256,2048]{1,0:T(8,128)(2,1)S(1)}, u32[]{:S(2)}, u32[]{:S(2)}) collective-permute-start(bf16[256,2048]{1,0:T(8,128)(2,1)S(1)} %collective-permute-done.6.refs_0_), channel_id=1, source_target_pairs={{0,1},{1,2},{2,3},{3,0},{4,5},{5,6},{6,7},{7,4},{8,9},{9,10},{10,1... | collective-permute-start | bytes 3145736 | tf_op jit(solution)/shard_map/ppermute | solution.py:905
  247.3 27.2 %collective-permute-start.11 = (bf16[256,2048]{1,0:T(8,128)(2,1)S(1)}, bf16[256,2048]{1,0:T(8,128)(2,1)S(1)}, u32[]{:S(2)}, u32[]{:S(2)}) collective-permute-start(bf16[256,2048]{1,0:T(8,128)(2,1)S(1)} %collective-permute-done.10.refs_1_), channel_id=1, source_target_pairs={{0,1},{1,2},{2,3},{3,0},{4,5},{5,6},{6,7},{7,4},{8,9},{9,10},{10,1... | collective-permute-start | bytes 3145736 | tf_op jit(solution)/shard_map/ppermute | solution.py:905
  301.0 47.1 %collective-permute-start.15 = (bf16[1024,2048]{1,0:T(8,128)(2,1)}, bf16[1024,2048]{1,0:T(8,128)(2,1)}, u32[]{:S(2)}, u32[]{:S(2)}) collective-permute-start(bf16[1024,2048]{1,0:T(8,128)(2,1)} %weight_product.8), channel_id=1, source_target_pairs={{0,4},{4,0},{8,12},{12,8},{16,20},{20,16},{24,28},{28,24},{1,5},{5... | collective-permute-start | bytes 12582920 | tf_op jit(solution)/shard_map/ppermute | solution.py:870
  301.4 27.6 %collective-permute-start.13 = (bf16[256,2048]{1,0:T(8,128)(2,1)S(1)}, bf16[256,2048]{1,0:T(8,128)(2,1)S(1)}, u32[]{:S(2)}, u32[]{:S(2)}) collective-permute-start(bf16[256,2048]{1,0:T(8,128)(2,1)S(1)} %add_convert_fusion.6), channel_id=1, source_target_pairs={{0,1},{1,2},{2,3},{3,0},{4,5},{5,6},{6,7},{7,4},{8,9},{9,10},{10,1... | collective-permute-start | bytes 3145736 | tf_op jit(solution)/shard_map/ppermute | solution.py:905
  330.6 28.4 %collective-permute-start.14 = (bf16[256,2048]{1,0:T(8,128)(2,1)S(1)}, bf16[256,2048]{1,0:T(8,128)(2,1)S(1)}, u32[]{:S(2)}, u32[]{:S(2)}) collective-permute-start(bf16[256,2048]{1,0:T(8,128)(2,1)S(1)} %add_convert_fusion.5), channel_id=1, source_target_pairs={{0,1},{1,2},{2,3},{3,0},{4,5},{5,6},{6,7},{7,4},{8,9},{9,10},{10,1... | collective-permute-start | bytes 3145736 | tf_op jit(solution)/shard_map/ppermute | solution.py:905
  359.1 33.1 %collective-permute-start.21 = (bf16[512,1024]{1,0:T(8,128)(2,1)}, bf16[512,1024]{1,0:T(8,128)(2,1)S(1)}, u32[]{:S(2)}, u32[]{:S(2)}) collective-permute-start(bf16[512,1024]{1,0:T(8,128)(2,1)} %get-tuple-element.380), channel_id=1, source_target_pairs={{0,16},{4,20},{8,24},{12,28},{16,0},{20,4},{24,8},{28,12},{1,17},{... | collective-permute-start | bytes 3145736 | tf_op jit(solution)/shard_map/ppermute | solution.py:870
  359.6 32.7 %collective-permute-start.22 = (bf16[512,1024]{1,0:T(8,128)(2,1)}, bf16[512,1024]{1,0:T(8,128)(2,1)S(1)}, u32[]{:S(2)}, u32[]{:S(2)}) collective-permute-start(bf16[512,1024]{1,0:T(8,128)(2,1)} %get-tuple-element.382), channel_id=1, source_target_pairs={{0,8},{4,12},{8,0},{12,4},{16,24},{20,28},{24,16},{28,20},{1,9},{5... | collective-permute-start | bytes 3145736 | tf_op jit(solution)/shard_map/ppermute | solution.py:870
  393.7 32.3 %collective-permute-start.16 = (bf16[256,2048]{1,0:T(8,128)(2,1)}, bf16[256,2048]{1,0:T(8,128)(2,1)}, u32[]{:S(2)}, u32[]{:S(2)}) collective-permute-start(bf16[256,2048]{1,0:T(8,128)(2,1)} %get-tuple-element.357), channel_id=1, source_target_pairs={{0,1},{1,2},{2,3},{3,0},{4,5},{5,6},{6,7},{7,4},{8,9},{9,10},{10,1... | collective-permute-start | bytes 3145736 | tf_op jit(solution)/shard_map/ppermute | solution.py:905
  429.5 29.7 %collective-permute-start.26 = (bf16[256,2048]{1,0:T(8,128)(2,1)}, bf16[256,2048]{1,0:T(8,128)(2,1)S(1)}, u32[]{:S(2)}, u32[]{:S(2)}) collective-permute-start(bf16[256,2048]{1,0:T(8,128)(2,1)} %add_convert_fusion.4), channel_id=1, source_target_pairs={{0,1},{1,2},{2,3},{3,0},{4,5},{5,6},{6,7},{7,4},{8,9},{9,10},{10,1... | collective-permute-start | bytes 3145736 | tf_op jit(solution)/shard_map/ppermute | solution.py:905
  429.9 29.3 %collective-permute-start.27 = (bf16[512,1024]{1,0:T(8,128)(2,1)}, bf16[512,1024]{1,0:T(8,128)(2,1)S(1)}, u32[]{:S(2)}, u32[]{:S(2)}) collective-permute-start(bf16[512,1024]{1,0:T(8,128)(2,1)} %get-tuple-element.418), channel_id=1, source_target_pairs={{0,16},{4,20},{8,24},{12,28},{16,0},{20,4},{24,8},{28,12},{1,17},{... | collective-permute-start | bytes 3145736 | tf_op jit(solution)/shard_map/ppermute | solution.py:870
  430.4 28.8 %collective-permute-start.28 = (bf16[512,1024]{1,0:T(8,128)(2,1)}, bf16[512,1024]{1,0:T(8,128)(2,1)S(1)}, u32[]{:S(2)}, u32[]{:S(2)}) collective-permute-start(bf16[512,1024]{1,0:T(8,128)(2,1)} %get-tuple-element.420), channel_id=1, source_target_pairs={{0,8},{4,12},{8,0},{12,4},{16,24},{20,28},{24,16},{28,20},{1,9},{5... | collective-permute-start | bytes 3145736 | tf_op jit(solution)/shard_map/ppermute | solution.py:870
  459.2 27.0 %collective-permute-start.30 = (bf16[512,1024]{1,0:T(8,128)(2,1)}, bf16[512,1024]{1,0:T(8,128)(2,1)}, u32[]{:S(2)}, u32[]{:S(2)}) collective-permute-start(bf16[512,1024]{1,0:T(8,128)(2,1)} %get-tuple-element.458), channel_id=1, source_target_pairs={{0,8},{4,12},{8,0},{12,4},{16,24},{20,28},{24,16},{28,20},{1,9},{5... | collective-permute-start | bytes 3145736 | tf_op jit(solution)/shard_map/ppermute | solution.py:870
  491.4 28.0 %collective-permute-start.32 = (bf16[256,2048]{1,0:T(8,128)(2,1)}, bf16[256,2048]{1,0:T(8,128)(2,1)}, u32[]{:S(2)}, u32[]{:S(2)}) collective-permute-start(bf16[256,2048]{1,0:T(8,128)(2,1)} %add_convert_fusion.3), channel_id=1, source_target_pairs={{0,1},{1,2},{2,3},{3,0},{4,5},{5,6},{6,7},{7,4},{8,9},{9,10},{10,1... | collective-permute-start | bytes 3145736 | tf_op jit(solution)/shard_map/ppermute | solution.py:905
  491.8 26.9 %collective-permute-start.34 = (bf16[256,1024]{1,0:T(8,128)(2,1)}, bf16[256,1024]{1,0:T(8,128)(2,1)S(1)}, u32[]{:S(2)}, u32[]{:S(2)}) collective-permute-start(bf16[256,1024]{1,0:T(8,128)(2,1)} %get-tuple-element.468), channel_id=1, source_target_pairs={{0,8},{4,12},{8,0},{12,4},{16,24},{20,28},{24,16},{28,20},{1,9},{5... | collective-permute-start | bytes 1572872 | tf_op jit(solution)/shard_map/ppermute | solution.py:870
  519.4 33.5 %collective-permute-start.38 = (bf16[512,1408]{1,0:T(8,128)(2,1)}, bf16[512,1408]{1,0:T(8,128)(2,1)}, u32[]{:S(2)}, u32[]{:S(2)}) collective-permute-start(bf16[512,1408]{1,0:T(8,128)(2,1)} %get-tuple-element.487), channel_id=1, source_target_pairs={{0,16},{4,20},{8,24},{12,28},{16,0},{20,4},{24,8},{28,12},{1,17},{... | collective-permute-start | bytes 4325384 | tf_op jit(solution)/shard_map/ppermute | solution.py:870
  520.2 33.5 %collective-permute-start.39 = (bf16[512,1408]{1,0:T(8,128)(2,1)}, bf16[512,1408]{1,0:T(8,128)(2,1)}, u32[]{:S(2)}, u32[]{:S(2)}) collective-permute-start(bf16[512,1408]{1,0:T(8,128)(2,1)} %get-tuple-element.489), channel_id=1, source_target_pairs={{0,8},{4,12},{8,0},{12,4},{16,24},{20,28},{24,16},{28,20},{1,9},{5... | collective-permute-start | bytes 4325384 | tf_op jit(solution)/shard_map/ppermute | solution.py:870
  524.1 28.2 %collective-permute-start.37 = (bf16[256,2048]{1,0:T(8,128)(2,1)}, bf16[256,2048]{1,0:T(8,128)(2,1)}, u32[]{:S(2)}, u32[]{:S(2)}) collective-permute-start(bf16[256,2048]{1,0:T(8,128)(2,1)} %add_convert_fusion.1), channel_id=1, source_target_pairs={{0,1},{1,2},{2,3},{3,0},{4,5},{5,6},{6,7},{7,4},{8,9},{9,10},{10,1... | collective-permute-start | bytes 3145736 | tf_op jit(solution)/shard_map/ppermute | solution.py:905
  529.0 57.9 %collective-permute-start.36 = (bf16[256,2048]{1,0:T(8,128)(2,1)}, bf16[256,2048]{1,0:T(8,128)(2,1)}, u32[]{:S(2)}, u32[]{:S(2)}) collective-permute-start(bf16[256,2048]{1,0:T(8,128)(2,1)} %add_convert_fusion.2), channel_id=1, source_target_pairs={{0,1},{1,2},{2,3},{3,0},{4,5},{5,6},{6,7},{7,4},{8,9},{9,10},{10,1... | collective-permute-start | bytes 3145736 | tf_op jit(solution)/shard_map/ppermute | solution.py:905
  560.1 36.4 %collective-permute-start.45 = (bf16[256,512]{1,0:T(8,128)(2,1)S(1)}, bf16[256,512]{1,0:T(8,128)(2,1)S(1)}, u32[]{:S(2)}, u32[]{:S(2)}) collective-permute-start(bf16[256,512]{1,0:T(8,128)(2,1)S(1)} %copy-done.54), channel_id=1, source_target_pairs={{0,1},{1,2},{2,3},{3,0},{4,5},{5,6},{6,7},{7,4},{8,9},{9,10},{10,1... | collective-permute-start | bytes 786440 | tf_op jit(solution)/shard_map/ppermute | solution.py:920
  562.1 34.4 %collective-permute-start.46 = (bf16[256,512]{1,0:T(8,128)(2,1)}, bf16[256,512]{1,0:T(8,128)(2,1)S(1)}, u32[]{:S(2)}, u32[]{:S(2)}) collective-permute-start(bf16[256,512]{1,0:T(8,128)(2,1)} %get-tuple-element.516), channel_id=1, source_target_pairs={{0,2},{1,3},{2,0},{3,1},{4,6},{5,7},{6,4},{7,5},{8,10},{9,11},{10,... | collective-permute-start | bytes 786440 | tf_op jit(solution)/shard_map/ppermute | solution.py:920
  (87 other events, 1256.0 us)
Sparse Core Ops, SparseCore 0:
  12.0 37.2 all-gather.3
  51.2 54.3 all-gather.5
  107.5 125.3 all-gather.7

commit v5 on v4

--- a/solution.py
+++ b/solution.py
@@ -99,7 +99,7 @@
     def _():
         values = x_ref[...].astype(jnp.float32)
         inverse = lax.rsqrt(jnp.mean(values * values, axis=-1, keepdims=True) + EPSILON)
-        normed_ref[...] = (values * inverse * gain_ref[...]).astype(jnp.bfloat16)
+        normed_ref[...] = (values * inverse * gain_ref[:1, :]).astype(jnp.bfloat16)
 
     product = dot_nn(normed_ref[...], weight_ref[...])
     for start in range(0, GROUP_WIDTH, 128):
@@ -113,7 +113,7 @@
     rows, depth = x.shape
     specs = [
         pl.BlockSpec((rows, depth), lambda g: (0, 0)),
-        pl.BlockSpec((1, depth), lambda g: (0, 0)),
+        pl.BlockSpec((2, depth), lambda g: (0, 0)),
         pl.BlockSpec((depth, GROUP_WIDTH), lambda g: (0, g)),
         pl.BlockSpec((rows, 128), lambda g: (index, 0)),
         pl.BlockSpec((rows, 128), lambda g: (index, 0)),
@@ -382,6 +382,36 @@
     )
 
 
+def pack_kernel(groups, query_ref, key_ref, value_ref, gain_ref, joint_ref, out_ref):
+    for g in range(groups):
+        start = g * GROUP_WIDTH
+        columns = slice(g * HEAD_SIZE, (g + 1) * HEAD_SIZE)
+        joint_ref[:, start : start + GROUP_QUERY] = query_ref[
+            :, g * GROUP_QUERY : (g + 1) * GROUP_QUERY
+        ]
+        joint_ref[:, start + GROUP_QUERY : start + GROUP_WIDTH] = jnp.concatenate(
+            [key_ref[:, columns], value_ref[:, columns]], axis=1
+        )
+    width = groups * GROUP_WIDTH
+    out_ref[:, :width] = joint_ref[...]
+    out_ref[:, width:] = gain_ref[...].astype(jnp.float32).T.astype(jnp.bfloat16)
+
+
+def pack(query, key, value, gains, groups):
+    rows = query.shape[0]
+    width = groups * GROUP_WIDTH
+    return pl.pallas_call(
+        functools.partial(pack_kernel, groups),
+        out_shape=[
+            jax.ShapeDtypeStruct((rows, width), jnp.bfloat16),
+            jax.ShapeDtypeStruct((rows, width + 128), jnp.bfloat16),
+        ],
+        compiler_params=parameters(),
+        cost_estimate=SMALL_COST,
+        name="pack",
+    )(query, key, value, gains)
+
+
 def join_kernel(*refs):
     place = 0
     for ref in refs[:-1]:
@@ -443,10 +473,16 @@
 def heads_kernel(count, *refs):
     parts = refs[:count]
     weight_ref = refs[count]
-    tokens = refs[count + 1 : -1]
-    out_ref = refs[-1]
+    tokens = refs[count + 1 : -2]
+    out_ref, local_ref = refs[-2:]
     step = pl.program_id(0)
     width = parts[0].shape[1]
+
+    @pl.when(step == 0)
+    def _():
+        for j in range(count):
+            local_ref[:, j * width : (j + 1) * width] = parts[j][...]
+
     for j in range(count):
         term = dot_nt(parts[j][...], weight_ref[:, j * width : (j + 1) * width])
         if j == 0:
@@ -479,23 +515,32 @@
             ),
             *[whole] * blocks,
         ],
-        out_specs=pl.BlockSpec((rows, width), lambda i: (i, 0)),
-        out_shape=jax.ShapeDtypeStruct((rows * blocks, width), jnp.float32),
+        out_specs=[
+            pl.BlockSpec((rows, width), lambda i: (i, 0)),
+            pl.BlockSpec((rows, depth * len(parts)), lambda i: (0, 0)),
+        ],
+        out_shape=[
+            jax.ShapeDtypeStruct((rows * blocks, width), jnp.float32),
+            jax.ShapeDtypeStruct((rows, depth * len(parts)), jnp.bfloat16),
+        ],
         compiler_params=parameters(),
         cost_estimate=SMALL_COST,
         name="heads_product",
     )(*parts, weight, *tokens)
 
 
-def attended_kernel(partial_ref, last_ref, weight_ref, gain_ref, hidden_ref, normed_ref):
+def attended_kernel(
+    partial_ref, last_ref, weight_ref, gain_ref, hidden_ref, normed_ref, local_ref
+):
     values = partial_ref[...] + dot_nt(last_ref[...], weight_ref[...])
 
     @pl.when(pl.program_id(0) == 0)
     def _():
         hidden_ref[...] = values
+        local_ref[...] = last_ref[...]
 
     inverse = lax.rsqrt(jnp.mean(values * values, axis=-1, keepdims=True) + EPSILON)
-    normed_ref[...] = (values * inverse * gain_ref[...]).astype(jnp.bfloat16)
+    normed_ref[...] = (values * inverse * gain_ref[1:, :]).astype(jnp.bfloat16)
 
 
 def after_attention(partial, last, weight, gain, count):
@@ -509,15 +554,17 @@
             pl.BlockSpec((rows, width), lambda i: (i, 0)),
             pl.BlockSpec((rows, depth), lambda i: (lax.rem(i + count - 1, count), 0)),
             pl.BlockSpec((width, depth), lambda i: (0, count - 1)),
-            pl.BlockSpec((1, width), lambda i: (0, 0)),
+            pl.BlockSpec((2, width), lambda i: (0, 0)),
         ],
         out_specs=[
             pl.BlockSpec((rows, width), lambda i: (0, 0)),
             pl.BlockSpec((rows, width), lambda i: (lax.rem(i + count - 1, count), 0)),
+            pl.BlockSpec((rows, depth), lambda i: (0, 0)),
         ],
         out_shape=[
             jax.ShapeDtypeStruct((rows, width), jnp.float32),
             jax.ShapeDtypeStruct((total_rows, width), jnp.bfloat16),
+            jax.ShapeDtypeStruct((rows, depth), jnp.bfloat16),
         ],
         compiler_params=parameters(),
         cost_estimate=SMALL_COST,
@@ -537,13 +584,14 @@
 def up_chunk(x, weight, kept, index, count):
     total_rows, depth = x.shape
     rows = total_rows // count
-    hidden = weight.shape[1] // 3
+    hidden = (weight.shape[1] - depth) // 2
     tile = tile_of(hidden)
     tiles = hidden // tile
+    start = depth // tile
     specs = [
         pl.BlockSpec((rows, depth), lambda t: (index, 0)),
-        pl.BlockSpec((depth, tile), lambda t: (0, t)),
-        pl.BlockSpec((depth, tile), lambda t: (0, tiles + t)),
+        pl.BlockSpec((depth, tile), lambda t: (0, start + t)),
+        pl.BlockSpec((depth, tile), lambda t: (0, start + tiles + t)),
     ]
     operands = [x, weight, weight]
     aliases = {}
@@ -603,10 +651,10 @@
             dx_refs[index][...] = total[index * rows : (index + 1) * rows].astype(jnp.bfloat16)
 
 
-def down_chunk(es, a, u, weight, kept, index, count):
-    depth, width = weight.shape
+def down_chunk(es, a, u, down_weight, weight, kept, index, count):
+    depth, hidden = down_weight.shape
     rows = len(es) * es[0].shape[0]
-    hidden = width // 3
+    start = depth // hidden
     tile = tile_of(hidden)
     tiles = hidden // tile
     row_tile = tile_of(depth)
@@ -618,13 +666,13 @@
         return jnp.maximum(t - tiles, 0)
 
     specs = [pl.BlockSpec(es[0].shape, lambda t: (0, 0))] * len(es) + [
-        pl.BlockSpec((depth, tile), lambda t: (0, 2 * tiles + column(t))),
+        pl.BlockSpec((depth, tile), lambda t: (0, column(t))),
         pl.BlockSpec((rows, tile), lambda t: (index, column(t))),
         pl.BlockSpec((rows, tile), lambda t: (index, column(t))),
-        pl.BlockSpec((row_tile, hidden), lambda t: (row(t), 0)),
-        pl.BlockSpec((row_tile, hidden), lambda t: (row(t), 1)),
+        pl.BlockSpec((row_tile, hidden), lambda t: (row(t), start)),
+        pl.BlockSpec((row_tile, hidden), lambda t: (row(t), start + 1)),
     ]
-    operands = [*es, weight, a, u, weight, weight]
+    operands = [*es, down_weight, a, u, weight, weight]
     part = es[0].shape
     shapes = [
         jax.ShapeDtypeStruct((rows * count, hidden), jnp.bfloat16),
@@ -802,7 +850,7 @@
         inverse = lax.rsqrt(jnp.mean(values * values, axis=-1, keepdims=True) + EPSILON)
         scaled = values * inverse
         grad = first_ref[...].astype(jnp.float32) + second_ref[...].astype(jnp.float32)
-        grad = grad * gain_ref[...]
+        grad = grad * gain_ref[1:, :]
         projection = jnp.mean(grad * scaled, axis=-1, keepdims=True)
         total = e_ref[...].astype(jnp.float32) + inverse * (grad - scaled * projection)
         dh_ref[...] = total
@@ -818,7 +866,7 @@
 
 def residual_gradient(e, hidden_res, first, second, gain, weight, parts):
     rows, depth = e.shape
-    tile = weight.shape[1] // parts
+    tile = depth // parts
     whole = pl.BlockSpec((rows, depth), lambda t: (0, 0))
     result = pl.pallas_call(
         functools.partial(residual_kernel, parts),
@@ -828,7 +876,7 @@
             whole,
             whole,
             whole,
-            pl.BlockSpec((1, depth), lambda t: (0, 0)),
+            pl.BlockSpec((2, depth), lambda t: (0, 0)),
             pl.BlockSpec((depth, tile), lambda t: (0, t)),
         ],
         out_specs=[whole, whole] + [pl.BlockSpec((rows, tile), lambda t: (0, 0))] * parts,
@@ -992,35 +1040,25 @@
     cosine_table = jnp.tile(cosine, (1, 128 // cosine.shape[1]))
     sine_table = jnp.tile(jnp.concatenate([-sine, sine], axis=1), (1, 128 // HEAD_SIZE))
 
-    def grouped(query, key, value):
-        pieces = []
-        for g in range(groups):
-            pieces.append(query[:, g * GROUP_QUERY : (g + 1) * GROUP_QUERY])
-            pieces.append(key[:, g * HEAD_SIZE : (g + 1) * HEAD_SIZE])
-            pieces.append(value[:, g * HEAD_SIZE : (g + 1) * HEAD_SIZE])
-        return jnp.concatenate(pieces, axis=1)
-
-    joint_matrix = grouped(query_matrix, key_matrix, value_matrix)
-    own_gains = jnp.stack([attention_gain, feedforward_gain], axis=1)
-    joint_full = mover.gather(
-        jnp.concatenate([joint_matrix, jnp.pad(own_gains, ((0, 0), (0, 126)))], axis=1)
-    )
+    own_gains = jnp.pad(jnp.stack([attention_gain, feedforward_gain]), ((0, 126), (0, 0)))
+    joint_matrix, packed = pack(query_matrix, key_matrix, value_matrix, own_gains, groups)
+    joint_full = mover.gather(packed)
     output_parts = mover.spread(output_weight.T)
-    ff_shard = jnp.concatenate([gate_weight, up_weight, down_weight.T], axis=1)
-    output_parts, cosine_table, sine_table, doc_ids, ff_shard, local_tokens = together(
-        output_parts, cosine_table, sine_table, doc_ids, ff_shard, tokens[0]
-    )
+    up_shard = jnp.concatenate([gate_weight, up_weight], axis=1)
+    output_parts, cosine_table, sine_table, doc_ids, up_shard, down_shard = together(
+        output_parts, cosine_table, sine_table, doc_ids, up_shard, down_weight.T
+    )
+    local_tokens = tokens[0]
     token_chunks = [local_tokens, mover.hop(local_tokens)]
-    output_ring = join(output_parts, [0] * ring)
-    output_full = mover.gather(output_ring)
-    ff_full = mover.gather(tie(ff_shard, output_ring))
+    up_shard = join(output_parts + [up_shard], [0] * (ring + 1))
+    up_full = mover.gather(up_shard)
+    down_full = mover.gather(tie(down_shard, up_shard))
     gains = joint_full[:, joint_width : joint_width + 2].T.astype(f32)
-    gain_one, gain_two = gains[:1], gains[1:]
 
     def projection(kept, index):
         return project(
             token_chunks[index],
-            gain_one,
+            gains,
             joint_full,
             cosine_table,
             sine_table,
@@ -1032,7 +1070,7 @@
 
     kept = projection(None, 0)
     for j in range(1, ring):
-        token_chunks[j], kept = together(token_chunks[j], kept)
+        token_chunks[j], kept, gains = together(token_chunks[j], kept, gains)
         if j + 1 < ring:
             token_chunks.append(mover.hop(token_chunks[j]))
         else:
@@ -1047,17 +1085,17 @@
     while len(attended_parts) < ring:
         part = mover.hop(attended_parts[-1], -1)
         if len(attended_parts) == ring - 1:
-            partial = heads_product(
-                tie(attended_parts, attended_parts[-1]), output_full, token_chunks
+            partial, attended_local = heads_product(
+                tie(attended_parts, attended_parts[-1]), up_full, token_chunks
             )
-            part, partial = together(part, partial)
+            part, partial, attended_local = together(part, partial, attended_local)
         attended_parts.append(part)
     moved, last = together(moved, attended_parts[-1])
 
     pairs = ring // 2
     moved = mover.hop(moved)
-    hidden_res, normed_two = after_attention(partial, last, output_full, gain_two, ring)
-    upward = up_chunk(normed_two, ff_full, None, 0, pairs)
+    hidden_res, normed_two, attended_last = after_attention(partial, last, up_full, gains, ring)
+    upward = up_chunk(normed_two, up_full, None, 0, pairs)
     downward = None
     grads = []
 
@@ -1065,7 +1103,9 @@
         return [cotangent_chunks[(2 * pair + i) % ring] for i in (1, 2)]
 
     def lower(pair, kept):
-        return down_chunk(chunks_of(pair), upward[0], upward[1], ff_full, kept, pair, pairs)
+        return down_chunk(
+            chunks_of(pair), upward[0], upward[1], down_full, up_full, kept, pair, pairs
+        )
 
     for j in range(2, ring):
         if j > 2:
@@ -1074,7 +1114,7 @@
                 downward, parts = lower((j - 3) // 2, downward)
                 grads.extend(parts)
             else:
-                upward = up_chunk(normed_two, ff_full, upward, j // 2 - 1, pairs)
+                upward = up_chunk(normed_two, up_full, upward, j // 2 - 1, pairs)
         moved, upward, downward, grads = together(moved, upward, downward, grads)
         cotangent_chunks.append(moved)
 
@@ -1084,7 +1124,7 @@
     ordered = cotangent_chunks[1:] + cotangent_chunks[:1]
     total = grads[0]
     moved = mover.hop(total)
-    upward = up_chunk(tie(normed_two, total), ff_full, upward, pairs - 1, pairs)
+    upward = up_chunk(tie(normed_two, total), up_full, upward, pairs - 1, pairs)
     product = upward[2]
     down_part = weights(ordered, [product])
     moved, upward, down_part = together(moved, upward, down_part)
@@ -1095,29 +1135,26 @@
         if j == 2:
             downward, parts = lower(pairs - 1, tie(downward, total))
             grads.extend(parts)
-            attended_local = join(tie(attended_parts, parts), list(range(ring)))
-            moved, downward, grads, attended_local = together(
-                moved, downward, grads, attended_local
-            )
+            moved, downward, grads = together(moved, downward, grads)
             grad_gate, grad_up = downward
         if j == 3:
             gate_part = weights([tie(normed_two, total)], [grad_gate])
             branch = transposed_product(
-                [tie(product, gate_part)], ff_full, 2, ring // 2, 0, 2
+                [tie(product, gate_part)], down_full, 0, ring // 2, 0, 2
             )
             down_part = weights(tie(ordered, branch), [product], down_part)
             moved, gate_part, branch, down_part = together(moved, gate_part, branch, down_part)
     gate_part = mover.swap(gate_part, 1)
     down_part = mover.begin(down_part)
     grad_hidden, grad_branch, grad_parts = residual_gradient(
-        local_cotangent, hidden_res, moved, grads[-1], gain_two, output_full, ring
+        local_cotangent, hidden_res, moved, grads[-1], gains, up_full, ring
     )
     grad_hidden, grad_branch, grad_parts, gate_part = together(
         grad_hidden, grad_branch, grad_parts, gate_part
     )
 
     grad_parts = mover.exchange(grad_parts)
-    output_part = weights([grad_branch], [attended_local])
+    output_part = weights([grad_branch], [attended_local, attended_last])
     gate_part = weights([tie(normed_two, output_part)], [grad_gate], gate_part)
     grad_parts, output_part, gate_part, down_part = together(
         grad_parts, output_part, gate_part, down_part
@@ -1149,7 +1186,7 @@
         )
         if group == 0:
             output_part = weights(
-                [tie(grad_branch, grad_joint)], [attended_local], output_part
+                [tie(grad_branch, grad_joint)], [attended_local, attended_last], output_part
             )
         if group + 1 == groups:
             grads = transposed_product(grad_joint, joint_full, 0, ring)
@@ -1180,7 +1217,7 @@
             folded = mover.fold(tie([output_part], total))
             last_part = last_weights(folded, None)
             branch = branch + transposed_product(
-                [tie(product, last_part)], ff_full, 2, ring // 2, 1, 2
+                [tie(product, last_part)], down_full, 0, ring // 2, 1, 2
             )
             moved, last_part, branch, folded, first_parts = together(
                 moved, last_part, branch, folded, first_parts
@@ -1190,7 +1227,7 @@
             last_part = last_weights(total, mover.swap(last_part, 1))
             gate_out, down_out = totals_of(*first_parts)
             down_out = down_out.T
-            next_branch = add(branch_moved, branch[sent])
+            next_branch = add(tie(branch_moved, last_part), branch[sent])
             moved, last_part, output_part, gate_out, down_out, next_branch = together(
                 moved, last_part, output_part, gate_out, down_out, next_branch
             )
@@ -1205,7 +1242,7 @@
     output_out = mover.collect(output_out[:-1] + [tie(output_out[-1], last_part)]).T
     scaled_one, inverse_one = norm_rows(local_tokens.astype(f32))
     local_one = moved.astype(f32) + grads[0].astype(f32)
-    input_gradient = grad_hidden + back_norm(local_one, scaled_one, inverse_one, gain_one)
+    input_gradient = grad_hidden + back_norm(local_one, scaled_one, inverse_one, gains[:1])
     branch_moved = tie(branch_moved, last_part)
     for j in range(sent, ring - 1):
         branch_moved = mover.hop(add(branch_moved, branch[j]))

time: 617 us -> 606 us (0.982)
  waiting for transfers between devices: 159 us -> 148 us
    all_gather x3, waiting for transfers between devices: 10.2 us -> 0.02 us  [gather(): return lax.all_gather(shard, 'dp', axis=0, tiled=True)]
    slice x5 -> x1, local copies, waits for them, and re-layouts: 7.52 us -> 0.34 us  [per_device(): gains[:1]]
  transfers between devices with their start and end apart: 51 -> 51, of which waited for: 22 -> 16; matrix products, arithmetic and copies ran while one was open for 9% -> 9% of each run, Pallas kernels for 49% -> 50%
where the time goes in v5:
time: 606 us; the launch traced here: 597 us
  Pallas kernels  298 us (49%)
  waiting for transfers between devices  148 us (24%)
  starting transfers between devices  73.1 us (12%)
  other arithmetic  42.7 us (7%)
  local copies, waits for them, and re-layouts  20.1 us (3%)
  between operations  15 us (2%)
    ppermute x18, waiting for transfers between devices, hop(): lax.ppermute(value, 'tensor', [(i, (i + shift) % self.ring) for i in rang...  121 us
    pallas_call x8, Pallas kernels, weight_product(): pl.pallas_call(functools.partial(weight_kernel, [(len(xs), len(ys)) for x...  81.3 us
    pallas_call x2, Pallas kernels, down_chunk(): pl.pallas_call(functools.partial(down_kernel, len(es), tiles), grid=(tile...  44.8 us
    ppermute x18, starting transfers between devices, hop(): lax.ppermute(value, 'tensor', [(i, (i + shift) % self.ring) for i in rang...  35.8 us
    pallas_call x2, Pallas kernels, attention_backward(): pl.pallas_call(functools.partial(backward_kernel, count), grid_spec=spec,...  33.9 us
    pallas_call x2, Pallas kernels, up_chunk(): pl.pallas_call(up_kernel, grid=(tiles,), in_specs=specs, out_specs=[pl.Bl...  27.6 us
    pallas_call x3, Pallas kernels, transposed_product(): pl.pallas_call(functools.partial(transposed_kernel, len(xs), parts), grid...  25.2 us
    pallas_call x4, Pallas kernels, project(): pl.pallas_call(project_kernel, grid=(groups,), in_specs=specs, out_specs=...  18.9 us
  transfers between devices with their start and end apart: 51, of which 16 were waited for; matrix products, arithmetic and copies ran while one was open for 9% of the time, Pallas kernels for 50%

profile of v5, /device:TPU:0, one launch (start us, length us, event | category | flops | bytes accessed | tf_op | source)
XLA Modules:
  0.0 597.5 jit_solution(397960611985524452)
XLA Ops:
  26.3 9.2 %collective-permute-done.2.refs_2_ = bf16[256,512]{1,0:T(8,128)(2,1)} collective-permute-done((bf16[256,512]{1,0:T(8,128)(2,1)S(1)}, bf16[256,512]{1,0:T(8,128)(2,1)}, u32[]{:S(2)}, u32[]{:S(2)}) %collective-permute-start.2) | collective-permute-done | bytes 262176 | tf_op jit(solution)/shard_map/ppermute | solution.py:960
  55.6 14.6 %collective-permute-done.x_ref.refs_5_ = bf16[256,2048]{1,0:T(8,128)(2,1)S(1)} collective-permute-done((bf16[256,2048]{1,0:T(8,128)(2,1)S(1)}, bf16[256,2048]{1,0:T(8,128)(2,1)S(1)}, u32[]{:S(2)}, u32[]{:S(2)}) %collective-permute-start) | collective-permute-done | bytes 1048608 | tf_op jit(solution)/shard_map/ppermute | solution.py:953
  77.5 17.9 %collective-permute-done.4.x_ref.refs_6_ = bf16[256,2048]{1,0:T(8,128)(2,1)S(1)} collective-permute-done((bf16[256,2048]{1,0:T(8,128)(2,1)S(1)}, bf16[256,2048]{1,0:T(8,128)(2,1)S(1)}, u32[]{:S(2)}, u32[]{:S(2)}) %collective-permute-start.4) | collective-permute-done | bytes 1048608 | tf_op jit(solution)/shard_map/ppermute | solution.py:953
  101.9 18.0 %collective-permute-done.5.x_ref.refs_7_ = bf16[256,2048]{1,0:T(8,128)(2,1)} collective-permute-done((bf16[256,2048]{1,0:T(8,128)(2,1)S(1)}, bf16[256,2048]{1,0:T(8,128)(2,1)}, u32[]{:S(2)}, u32[]{:S(2)}) %collective-permute-start.5) | collective-permute-done | bytes 1048608 | tf_op jit(solution)/shard_map/ppermute | solution.py:953
  126.6 17.7 %attend.1 = (bf16[1024,512]{1,0:T(8,128)(2,1)}, f32[16,4096]{1,0:T(8,128)}) custom-call(s32[1]{0:T(128)} %bitcast.10.place_ref, bf16[1024,768]{1,0:T(8,128)(2,1)} %get-tuple-element.293.own_ref.all_ref.refs_0_.refs_1_, bf16[1024,768]{1,0:T(8,128)(2,1)} %get-tuple-element.293.own_ref.all_ref.refs_0_.refs_1_, s32[1,1024]{1,0:T(1,128)} %bitcast.52, ...), custom_call_target="tpu_custom_call" | custom-call | flops 1 | bytes 1 | tf_op jit(solution)/shard_map/attend/pallas_call | solution.py:256
  148.5 19.4 %collective-permute-done.7.refs_1_ = bf16[1024,512]{1,0:T(8,128)(2,1)S(1)} collective-permute-done((bf16[1024,512]{1,0:T(8,128)(2,1)}, bf16[1024,512]{1,0:T(8,128)(2,1)S(1)}, u32[]{:S(2)}, u32[]{:S(2)}) %collective-permute-start.7) | collective-permute-done | bytes 1048608 | tf_op jit(solution)/shard_map/ppermute | solution.py:953
  172.0 18.5 %collective-permute-done.8.refs_2_ = bf16[1024,512]{1,0:T(8,128)(2,1)} collective-permute-done((bf16[1024,512]{1,0:T(8,128)(2,1)S(1)}, bf16[1024,512]{1,0:T(8,128)(2,1)}, u32[]{:S(2)}, u32[]{:S(2)}) %collective-permute-start.8) | collective-permute-done | bytes 1048608 | tf_op jit(solution)/shard_map/ppermute | solution.py:953
  195.2 14.2 %heads_product.1 = (f32[1024,2048]{1,0:T(8,128)}, bf16[256,1536]{1,0:T(8,128)(2,1)}) custom-call(bf16[1024,512]{1,0:T(8,128)(2,1)} %get-tuple-element.297.refs_0_.refs_2_, bf16[1024,512]{1,0:T(8,128)(2,1)} %copy-done.41, bf16[1024,512]{1,0:T(8,128)(2,1)} %collective-permute-done.8.refs_2_, ...), custom_call_target="tpu_custom_call" | custom-call | flops 1 | bytes 1 | tf_op jit(solution)/shard_map/heads_product/pallas_call | solution.py:508
  217.5 9.3 %after_attention.1 = (f32[256,2048]{1,0:T(8,128)}, bf16[1024,2048]{1,0:T(8,128)(2,1)}, bf16[256,512]{1,0:T(8,128)(2,1)}) custom-call(f32[1024,2048]{1,0:T(8,128)} %get-tuple-element.307.partial_ref, bf16[1024,512]{1,0:T(8,128)(2,1)} %copy-done.42, bf16[2048,6144]{1,0:T(8,128)(2,1)} %all-gather.6.cloned.1.call-done.refs_3_.weight_ref.gate_ref.up_ref.refs_5_.refs_6_, ...), custom_call_target="tpu_custom_call" | custom-call | flops 1 | bytes 1 | tf_op jit(solution)/shard_map/after_attention/pallas_call | solution.py:550
  226.9 13.9 %up_chunk.2 = (bf16[1024,2048]{1,0:T(8,128)(2,1)}, bf16[1024,2048]{1,0:T(8,128)(2,1)}, bf16[1024,2048]{1,0:T(8,128)(2,1)}) custom-call(bf16[1024,2048]{1,0:T(8,128)(2,1)} %get-tuple-element.470.x_ref.refs_0_, bf16[2048,6144]{1,0:T(8,128)(2,1)} %all-gather.6.cloned.1.call-done.refs_3_.weight_ref.gate_ref.up_ref.refs_5_.refs_6_, ...), custom_call_target="tpu_custom_call" | custom-call | flops 1 | bytes 1 | tf_op jit(solution)/shard_map/up_chunk/pallas_call | solution.py:602
  241.7 22.4 %down_chunk.2 = (bf16[1024,2048]{1,0:T(8,128)(2,1)}, bf16[1024,2048]{1,0:T(8,128)(2,1)}, bf16[256,2048]{1,0:T(8,128)(2,1)}, bf16[256,2048]{1,0:T(8,128)(2,1)}) custom-call(bf16[256,2048]{1,0:T(8,128)(2,1)} %copy-done.5, bf16[256,2048]{1,0:T(8,128)(2,1)} %copy-done.6, bf16[2048,2048]{1,0:T(8,128)(2,1)} %all-gather.8.cloned.1.call-done.refs_2_.refs_1_, ...), custom_call_target="tpu_custom_call" | custom-call | flops 1 | bytes 1 | tf_op jit(solution)/shard_map/down_chunk/pallas_call | solution.py:687
  267.7 13.8 %up_chunk.3 = (bf16[1024,2048]{1,0:T(8,128)(2,1)}, bf16[1024,2048]{1,0:T(8,128)(2,1)}, bf16[1024,2048]{1,0:T(8,128)(2,1)}) custom-call(bf16[1024,2048]{1,0:T(8,128)(2,1)} %get-tuple-element.470.x_ref.refs_0_, ...), custom_call_target="tpu_custom_call", output_to_operand_aliasing={{0}: (3, {}), {1}: (4, {}), {2}: (5, {})} | custom-call | flops 1 | bytes 1 | tf_op jit(solution)/shard_map/up_chunk/pallas_call | solution.py:602
  281.4 9.0 %weight_product.8 = bf16[1024,2048]{1,0:T(8,128)(2,1)} custom-call(s32[1]{0:T(128)} %bitcast.13.place_ref, bf16[256,2048]{1,0:T(8,128)(2,1)} %copy-done.5, bf16[256,2048]{1,0:T(8,128)(2,1)} %copy-done.6, bf16[256,2048]{1,0:T(8,128)(2,1)} %copy-done.7, bf16[256,2048]{1,0:T(8,128)(2,1)} %bitcast.39, bf16[1024,2048]{1,0:T(8,128)(2,1)} %get-tuple-element.459.refs_4_.refs_0_), custom_call_target="tpu_custom_call" | custom-call | flops 1 | bytes 1 | tf_op jit(solution)/shard_map/weight_product/pallas_call | solution.py:790
  292.0 22.4 %down_chunk.3 = (bf16[1024,2048]{1,0:T(8,128)(2,1)}, bf16[1024,2048]{1,0:T(8,128)(2,1)}, bf16[256,2048]{1,0:T(8,128)(2,1)}, bf16[256,2048]{1,0:T(8,128)(2,1)}) custom-call(bf16[256,2048]{1,0:T(8,128)(2,1)} %copy-done.7, bf16[256,2048]{1,0:T(8,128)(2,1)} %bitcast.40, ...), custom_call_target="tpu_custom_call", output_to_operand_aliasing={{0}: (7, {}), {1}: (8, {})} | custom-call | flops 1 | bytes 1 | tf_op jit(solution)/shard_map/down_chunk/pallas_call | solution.py:687
  320.1 8.7 %weight_product.9 = bf16[1024,2048]{1,0:T(8,128)(2,1)} custom-call(s32[1]{0:T(128)} %bitcast.13.place_ref, bf16[1024,2048]{1,0:T(8,128)(2,1)} %get-tuple-element.470.x_ref.refs_0_, bf16[1024,2048]{1,0:T(8,128)(2,1)} %get-tuple-element.351.refs_1_), custom_call_target="tpu_custom_call" | custom-call | flops 1 | bytes 1 | tf_op jit(solution)/shard_map/weight_product/pallas_call | solution.py:790
  337.5 10.9 %weight_product.10 = (bf16[512,1024]{1,0:T(8,128)(2,1)}, bf16[512,1024]{1,0:T(8,128)(2,1)}, bf16[512,1024]{1,0:T(8,128)(2,1)}, bf16[512,1024]{1,0:T(8,128)(2,1)}) custom-call(s32[1]{0:T(128)} %bitcast.13.place_ref, bf16[256,2048]{1,0:T(8,128)(2,1)} %copy-done.5, bf16[256,2048]{1,0:T(8,128)(2,1)} %copy-done.6, bf16[256,2048]{1,0:T(8,128)(2,1)} %copy-done.7, ...), custom_call_target="tpu_custom_call" | custom-call | flops 1 | bytes 1 | tf_op jit(solution)/shard_map/weight_product/pallas_call | solution.py:790
  351.3 10.6 %residual_gradient.1 = (f32[256,2048]{1,0:T(8,128)}, bf16[256,2048]{1,0:T(8,128)(2,1)}, bf16[256,512]{1,0:T(8,128)(2,1)}, bf16[256,512]{1,0:T(8,128)(2,1)}, bf16...) custom-call(bf16[256,2048]{1,0:T(8,128)(2,1)} %bitcast.42, f32[256,2048]{1,0:T(8,128)} %get-tuple-element.311.hidden_ref, ...), custom_call_target="tpu_custom_call" | custom-call | flops 1 | bytes 1 | tf_op jit(solution)/shard_map/residual_gradient/pallas_call | solution.py:871
  371.4 10.6 %weight_product.12 = (bf16[512,1024]{1,0:T(8,128)(2,1)}, bf16[512,1024]{1,0:T(8,128)(2,1)}, bf16[512,1024]{1,0:T(8,128)(2,1)}, bf16[512,1024]{1,0:T(8,128)(2,1)}) custom-call(s32[1]{0:T(128)} %bitcast.13.place_ref, bf16[1024,2048]{1,0:T(8,128)(2,1)} %get-tuple-element.470.x_ref.refs_0_, bf16[1024,2048]{1,0:T(8,128)(2,1)} %get-tuple-element.351.refs_1_, ...), custom_call_target="tpu_custom_call" | custom-call | flops 1 | bytes 1 | tf_op jit(solution)/shard_map/weight_product/pallas_call | solution.py:790
  391.3 17.0 %attend_back.2.refs_0_.refs_3_ = bf16[1024,384]{1,0:T(8,128)(2,1)} custom-call(s32[1]{0:T(128)} %bitcast.10.place_ref, bf16[1024,768]{1,0:T(8,128)(2,1)} %get-tuple-element.293.own_ref.all_ref.refs_0_.refs_1_, bf16[1024,768]{1,0:T(8,128)(2,1)} %get-tuple-element.293.own_ref.all_ref.refs_0_.refs_1_, bf16[1024,512]{1,0:T(8,128)(2,1)} %get-tuple-element.297.refs_0_.refs_2_, ...), custom_call_target="tpu_custom_call" | custom-call | flops 1 | bytes 1 | tf_op jit(solution)/shard_map/attend_back/pallas_call | solution.py:364
  421.7 16.9 %attend_back.3.refs_1_.refs_4_ = bf16[1024,384]{1,0:T(8,128)(2,1)} custom-call(s32[1]{0:T(128)} %bitcast.10.place_ref, bf16[1024,768]{1,0:T(8,128)(2,1)} %get-tuple-element.293.own_ref.all_ref.refs_0_.refs_1_, bf16[1024,768]{1,0:T(8,128)(2,1)} %get-tuple-element.293.own_ref.all_ref.refs_0_.refs_1_, bf16[1024,512]{1,0:T(8,128)(2,1)} %get-tuple-element.297.refs_0_.refs_2_, ...), custom_call_target="tpu_custom_call" | custom-call | flops 1 | bytes 1 | tf_op jit(solution)/shard_map/attend_back/pallas_call | solution.py:364
  453.8 12.2 %weight_product.14 = bf16[1024,2816]{1,0:T(8,128)(2,1)} custom-call(s32[1]{0:T(128)} %bitcast.13.place_ref, bf16[1024,2048]{1,0:T(8,128)(2,1)} %get-tuple-element.470.x_ref.refs_0_, bf16[1024,2048]{1,0:T(8,128)(2,1)} %get-tuple-element.455.refs_1_, bf16[1024,2048]{1,0:T(8,128)(2,1)} %get-tuple-element.456.refs_2_, ...), custom_call_target="tpu_custom_call" | custom-call | flops 1 | bytes 1 | tf_op jit(solution)/shard_map/weight_product/pallas_call | solution.py:790
  466.0 8.8 %transposed.5 = (bf16[256,2048]{1,0:T(8,128)(2,1)}, bf16[256,2048]{1,0:T(8,128)(2,1)}) custom-call(bf16[1024,2048]{1,0:T(8,128)(2,1)} %get-tuple-element.459.refs_4_.refs_0_, bf16[2048,2048]{1,0:T(8,128)(2,1)} %all-gather.8.cloned.1.call-done.refs_2_.refs_1_), custom_call_target="tpu_custom_call" | custom-call | flops 1 | bytes 1 | tf_op jit(solution)/shard_map/transposed/pallas_call | solution.py:461
  488.9 17.3 %weight_product.15 = (bf16[512,1408]{1,0:T(8,128)(2,1)}, bf16[512,1408]{1,0:T(8,128)(2,1)}, bf16[512,1408]{1,0:T(8,128)(2,1)}, bf16[512,1408]{1,0:T(8,128)(2,1)}) custom-call(s32[1]{0:T(128)} %bitcast.13.place_ref, bf16[1024,2048]{1,0:T(8,128)(2,1)} %get-tuple-element.470.x_ref.refs_0_, bf16[1024,2048]{1,0:T(8,128)(2,1)} %get-tuple-element.455.refs_1_, ...), custom_call_target="tpu_custom_call" | custom-call | flops 1 | bytes 1 | tf_op jit(solution)/shard_map/weight_product/pallas_call | solution.py:790
  522.2 19.5 %collective-permute-done.37 = bf16[256,2048]{1,0:T(8,128)(2,1)} collective-permute-done((bf16[256,2048]{1,0:T(8,128)(2,1)}, bf16[256,2048]{1,0:T(8,128)(2,1)}, u32[]{:S(2)}, u32[]{:S(2)}) %collective-permute-start.37) | collective-permute-done | bytes 1048608 | tf_op jit(solution)/shard_map/ppermute | solution.py:953
  (287 shorter events, 229.6 us)
Async XLA Ops:
  7.2 41.7 %all-gather.4.cloned.1.call-start = ((), (), s32[]{:S(2)}) async-start(), calls=%async_computation | async-start | bytes 4128768 | tf_op jit(solution)/shard_map/all_gather | solution.py:921
  11.5 183.7 %all-gather.6.cloned.1.call-start = ((), (), s32[]{:S(2)}) async-start(), calls=%async_computation.1 | async-start | bytes 28311552 | tf_op jit(solution)/shard_map/all_gather | solution.py:921
  39.5 201.3 %all-gather.8.cloned.1.call-start = ((), (), s32[]{:S(2)}) async-start(), calls=%async_computation.2 | async-start | bytes 9437184 | tf_op jit(solution)/shard_map/all_gather | solution.py:921
  40.7 29.5 %collective-permute-start = (bf16[256,2048]{1,0:T(8,128)(2,1)S(1)}, bf16[256,2048]{1,0:T(8,128)(2,1)S(1)}, u32[]{:S(2)}, u32[]{:S(2)}) collective-permute-start(bf16[256,2048]{1,0:T(8,128)(2,1)S(1)} %bitcast.38), channel_id=1, source_target_pairs={{0,1},{1,2},{2,3},{3,0},{4,5},{5,6},{6,7},{7,4},{8,9},{9,10},{10,1... | collective-permute-start | bytes 3145736 | tf_op jit(solution)/shard_map/ppermute | solution.py:953
  190.5 26.0 %collective-permute-start.9 = (bf16[1024,512]{1,0:T(8,128)(2,1)}, bf16[1024,512]{1,0:T(8,128)(2,1)S(1)}, u32[]{:S(2)}, u32[]{:S(2)}) collective-permute-start(bf16[1024,512]{1,0:T(8,128)(2,1)} %collective-permute-done.8.refs_2_), channel_id=1, source_target_pairs={{0,3},{1,0},{2,1},{3,2},{4,7},{5,4},{6,5},{7,6},{8,11},{9,8},{10,9... | collective-permute-start | bytes 3145736 | tf_op jit(solution)/shard_map/ppermute | solution.py:953
  264.2 26.3 %collective-permute-start.12 = (bf16[256,2048]{1,0:T(8,128)(2,1)}, bf16[256,2048]{1,0:T(8,128)(2,1)S(1)}, u32[]{:S(2)}, u32[]{:S(2)}) collective-permute-start(bf16[256,2048]{1,0:T(8,128)(2,1)} %get-tuple-element.327), channel_id=1, source_target_pairs={{0,1},{1,2},{2,3},{3,0},{4,5},{5,6},{6,7},{7,4},{8,9},{9,10},{10,1... | collective-permute-start | bytes 3145736 | tf_op jit(solution)/shard_map/ppermute | solution.py:953
  290.5 47.0 %collective-permute-start.15 = (bf16[1024,2048]{1,0:T(8,128)(2,1)}, bf16[1024,2048]{1,0:T(8,128)(2,1)}, u32[]{:S(2)}, u32[]{:S(2)}) collective-permute-start(bf16[1024,2048]{1,0:T(8,128)(2,1)} %weight_product.8), channel_id=1, source_target_pairs={{0,4},{4,0},{8,12},{12,8},{16,20},{20,16},{24,28},{28,24},{1,5},{5... | collective-permute-start | bytes 12582920 | tf_op jit(solution)/shard_map/ppermute | solution.py:918
  290.9 27.6 %collective-permute-start.13 = (bf16[256,2048]{1,0:T(8,128)(2,1)S(1)}, bf16[256,2048]{1,0:T(8,128)(2,1)S(1)}, u32[]{:S(2)}, u32[]{:S(2)}) collective-permute-start(bf16[256,2048]{1,0:T(8,128)(2,1)S(1)} %add_convert_fusion.6), channel_id=1, source_target_pairs={{0,1},{1,2},{2,3},{3,0},{4,5},{5,6},{6,7},{7,4},{8,9},{9,10},{10,1... | collective-permute-start | bytes 3145736 | tf_op jit(solution)/shard_map/ppermute | solution.py:953
  320.1 28.3 %collective-permute-start.14 = (bf16[256,2048]{1,0:T(8,128)(2,1)S(1)}, bf16[256,2048]{1,0:T(8,128)(2,1)S(1)}, u32[]{:S(2)}, u32[]{:S(2)}) collective-permute-start(bf16[256,2048]{1,0:T(8,128)(2,1)S(1)} %add_convert_fusion.5), channel_id=1, source_target_pairs={{0,1},{1,2},{2,3},{3,0},{4,5},{5,6},{6,7},{7,4},{8,9},{9,10},{10,1... | collective-permute-start | bytes 3145736 | tf_op jit(solution)/shard_map/ppermute | solution.py:953
  348.5 33.5 %collective-permute-start.21 = (bf16[512,1024]{1,0:T(8,128)(2,1)}, bf16[512,1024]{1,0:T(8,128)(2,1)S(1)}, u32[]{:S(2)}, u32[]{:S(2)}) collective-permute-start(bf16[512,1024]{1,0:T(8,128)(2,1)} %get-tuple-element.388), channel_id=1, source_target_pairs={{0,16},{4,20},{8,24},{12,28},{16,0},{20,4},{24,8},{28,12},{1,17},{... | collective-permute-start | bytes 3145736 | tf_op jit(solution)/shard_map/ppermute | solution.py:918
  349.8 32.2 %collective-permute-start.22 = (bf16[512,1024]{1,0:T(8,128)(2,1)}, bf16[512,1024]{1,0:T(8,128)(2,1)S(1)}, u32[]{:S(2)}, u32[]{:S(2)}) collective-permute-start(bf16[512,1024]{1,0:T(8,128)(2,1)} %get-tuple-element.390), channel_id=1, source_target_pairs={{0,8},{4,12},{8,0},{12,4},{16,24},{20,28},{24,16},{28,20},{1,9},{5... | collective-permute-start | bytes 3145736 | tf_op jit(solution)/shard_map/ppermute | solution.py:918
  383.8 32.1 %collective-permute-start.16 = (bf16[256,2048]{1,0:T(8,128)(2,1)}, bf16[256,2048]{1,0:T(8,128)(2,1)}, u32[]{:S(2)}, u32[]{:S(2)}) collective-permute-start(bf16[256,2048]{1,0:T(8,128)(2,1)} %get-tuple-element.364), channel_id=1, source_target_pairs={{0,1},{1,2},{2,3},{3,0},{4,5},{5,6},{6,7},{7,4},{8,9},{9,10},{10,1... | collective-permute-start | bytes 3145736 | tf_op jit(solution)/shard_map/ppermute | solution.py:953
  418.9 30.9 %collective-permute-start.26 = (bf16[256,2048]{1,0:T(8,128)(2,1)}, bf16[256,2048]{1,0:T(8,128)(2,1)S(1)}, u32[]{:S(2)}, u32[]{:S(2)}) collective-permute-start(bf16[256,2048]{1,0:T(8,128)(2,1)} %add_convert_fusion.4), channel_id=1, source_target_pairs={{0,1},{1,2},{2,3},{3,0},{4,5},{5,6},{6,7},{7,4},{8,9},{9,10},{10,1... | collective-permute-start | bytes 3145736 | tf_op jit(solution)/shard_map/ppermute | solution.py:953
  419.2 30.6 %collective-permute-start.27 = (bf16[512,1024]{1,0:T(8,128)(2,1)}, bf16[512,1024]{1,0:T(8,128)(2,1)S(1)}, u32[]{:S(2)}, u32[]{:S(2)}) collective-permute-start(bf16[512,1024]{1,0:T(8,128)(2,1)} %get-tuple-element.426), channel_id=1, source_target_pairs={{0,16},{4,20},{8,24},{12,28},{16,0},{20,4},{24,8},{28,12},{1,17},{... | collective-permute-start | bytes 3145736 | tf_op jit(solution)/shard_map/ppermute | solution.py:918
  420.6 29.2 %collective-permute-start.28 = (bf16[512,1024]{1,0:T(8,128)(2,1)}, bf16[512,1024]{1,0:T(8,128)(2,1)S(1)}, u32[]{:S(2)}, u32[]{:S(2)}) collective-permute-start(bf16[512,1024]{1,0:T(8,128)(2,1)} %get-tuple-element.428), channel_id=1, source_target_pairs={{0,8},{4,12},{8,0},{12,4},{16,24},{20,28},{24,16},{28,20},{1,9},{5... | collective-permute-start | bytes 3145736 | tf_op jit(solution)/shard_map/ppermute | solution.py:918
  480.3 28.9 %collective-permute-start.32 = (bf16[256,2048]{1,0:T(8,128)(2,1)}, bf16[256,2048]{1,0:T(8,128)(2,1)}, u32[]{:S(2)}, u32[]{:S(2)}) collective-permute-start(bf16[256,2048]{1,0:T(8,128)(2,1)} %add_convert_fusion.3), channel_id=1, source_target_pairs={{0,1},{1,2},{2,3},{3,0},{4,5},{5,6},{6,7},{7,4},{8,9},{9,10},{10,1... | collective-permute-start | bytes 3145736 | tf_op jit(solution)/shard_map/ppermute | solution.py:953
  480.6 28.6 %collective-permute-start.34 = (bf16[256,1024]{1,0:T(8,128)(2,1)}, bf16[256,1024]{1,0:T(8,128)(2,1)S(1)}, u32[]{:S(2)}, u32[]{:S(2)}) collective-permute-start(bf16[256,1024]{1,0:T(8,128)(2,1)} %get-tuple-element.476), channel_id=1, source_target_pairs={{0,8},{4,12},{8,0},{12,4},{16,24},{20,28},{24,16},{28,20},{1,9},{5... | collective-permute-start | bytes 1572872 | tf_op jit(solution)/shard_map/ppermute | solution.py:918
  482.1 27.1 %collective-permute-start.35 = (bf16[256,1024]{1,0:T(8,128)(2,1)}, bf16[256,1024]{1,0:T(8,128)(2,1)}, u32[]{:S(2)}, u32[]{:S(2)}) collective-permute-start(bf16[256,1024]{1,0:T(8,128)(2,1)} %get-tuple-element.477), channel_id=1, source_target_pairs={{0,16},{4,20},{8,24},{12,28},{16,0},{20,4},{24,8},{28,12},{1,17},{... | collective-permute-start | bytes 1572872 | tf_op jit(solution)/shard_map/ppermute | solution.py:918
  509.2 33.6 %collective-permute-start.38 = (bf16[512,1408]{1,0:T(8,128)(2,1)}, bf16[512,1408]{1,0:T(8,128)(2,1)}, u32[]{:S(2)}, u32[]{:S(2)}) collective-permute-start(bf16[512,1408]{1,0:T(8,128)(2,1)} %get-tuple-element.496), channel_id=1, source_target_pairs={{0,16},{4,20},{8,24},{12,28},{16,0},{20,4},{24,8},{28,12},{1,17},{... | collective-permute-start | bytes 4325384 | tf_op jit(solution)/shard_map/ppermute | solution.py:918
  510.0 33.3 %collective-permute-start.39 = (bf16[512,1408]{1,0:T(8,128)(2,1)}, bf16[512,1408]{1,0:T(8,128)(2,1)}, u32[]{:S(2)}, u32[]{:S(2)}) collective-permute-start(bf16[512,1408]{1,0:T(8,128)(2,1)} %get-tuple-element.498), channel_id=1, source_target_pairs={{0,8},{4,12},{8,0},{12,4},{16,24},{20,28},{24,16},{28,20},{1,9},{5... | collective-permute-start | bytes 4325384 | tf_op jit(solution)/shard_map/ppermute | solution.py:918
  513.5 28.2 %collective-permute-start.37 = (bf16[256,2048]{1,0:T(8,128)(2,1)}, bf16[256,2048]{1,0:T(8,128)(2,1)}, u32[]{:S(2)}, u32[]{:S(2)}) collective-permute-start(bf16[256,2048]{1,0:T(8,128)(2,1)} %add_convert_fusion.1), channel_id=1, source_target_pairs={{0,1},{1,2},{2,3},{3,0},{4,5},{5,6},{6,7},{7,4},{8,9},{9,10},{10,1... | collective-permute-start | bytes 3145736 | tf_op jit(solution)/shard_map/ppermute | solution.py:953
  517.3 59.2 %collective-permute-start.36 = (bf16[256,2048]{1,0:T(8,128)(2,1)}, bf16[256,2048]{1,0:T(8,128)(2,1)}, u32[]{:S(2)}, u32[]{:S(2)}) collective-permute-start(bf16[256,2048]{1,0:T(8,128)(2,1)} %add_convert_fusion.2), channel_id=1, source_target_pairs={{0,1},{1,2},{2,3},{3,0},{4,5},{5,6},{6,7},{7,4},{8,9},{9,10},{10,1... | collective-permute-start | bytes 3145736 | tf_op jit(solution)/shard_map/ppermute | solution.py:953
  549.9 36.1 %collective-permute-start.45 = (bf16[256,512]{1,0:T(8,128)(2,1)S(1)}, bf16[256,512]{1,0:T(8,128)(2,1)S(1)}, u32[]{:S(2)}, u32[]{:S(2)}) collective-permute-start(bf16[256,512]{1,0:T(8,128)(2,1)S(1)} %split.17), channel_id=1, source_target_pairs={{0,1},{1,2},{2,3},{3,0},{4,5},{5,6},{6,7},{7,4},{8,9},{9,10},{10,1... | collective-permute-start | bytes 786440 | tf_op jit(solution)/shard_map/ppermute | solution.py:968
  552.3 33.8 %collective-permute-start.46 = (bf16[256,512]{1,0:T(8,128)(2,1)S(1)}, bf16[256,512]{1,0:T(8,128)(2,1)S(1)}, u32[]{:S(2)}, u32[]{:S(2)}) collective-permute-start(bf16[256,512]{1,0:T(8,128)(2,1)S(1)} %get-tuple-element.526), channel_id=1, source_target_pairs={{0,2},{1,3},{2,0},{3,1},{4,6},{5,7},{6,4},{7,5},{8,10},{9,11},{10,... | collective-permute-start | bytes 786440 | tf_op jit(solution)/shard_map/ppermute | solution.py:968
  (79 other events, 1256.2 us)
Sparse Core Ops, SparseCore 0:
  11.6 37.2 all-gather.3
  50.7 125.3 all-gather.5
  178.0 54.3 all-gather.7

commit v6 on v5

--- a/solution.py
+++ b/solution.py
@@ -414,28 +414,27 @@
 
 def join_kernel(*refs):
     place = 0
-    for ref in refs[:-1]:
+    for ref in refs[:-2]:
         size = ref.shape[1]
         refs[-1][:, place : place + size] = ref[...]
         place += size
 
 
-def join(parts, blocks):
-    rows = parts[0].shape[0] // (max(blocks) + 1)
+def join(parts, rest):
+    rows = rest.shape[0]
     width = sum(part.shape[1] for part in parts)
     return pl.pallas_call(
         join_kernel,
         grid=(1,),
-        in_specs=[
-            pl.BlockSpec((rows, part.shape[1]), lambda i, block=block: (block, 0))
-            for part, block in zip(parts, blocks)
-        ],
+        in_specs=[pl.BlockSpec(part.shape, lambda i: (0, 0)) for part in parts]
+        + [pl.BlockSpec(memory_space=pl.ANY)],
         out_specs=pl.BlockSpec((rows, width), lambda i: (0, 0)),
-        out_shape=jax.ShapeDtypeStruct((rows, width), parts[0].dtype),
+        out_shape=jax.ShapeDtypeStruct(rest.shape, rest.dtype),
+        input_output_aliases={len(parts): 0},
         compiler_params=parameters(),
         cost_estimate=SMALL_COST,
         name="join",
-    )(*parts)
+    )(*parts, rest)
 
 
 def transposed_kernel(count, parts, *refs):
@@ -842,7 +841,9 @@
 
 def residual_kernel(parts, e_ref, hidden_ref, first_ref, second_ref, gain_ref, weight_ref, *refs):
     dh_ref, dz_ref = refs[:2]
+    dh, dz = refs[-2:]
     step = pl.program_id(0)
+    tile = weight_ref.shape[1]
 
     @pl.when(step == 0)
     def _():
@@ -853,14 +854,17 @@
         grad = grad * gain_ref[1:, :]
         projection = jnp.mean(grad * scaled, axis=-1, keepdims=True)
         total = e_ref[...].astype(jnp.float32) + inverse * (grad - scaled * projection)
-        dh_ref[...] = total
-        dz_ref[...] = total.astype(jnp.bfloat16)
-
-    result = dot_nn(dz_ref[...], weight_ref[...]).astype(jnp.bfloat16)
+        dh[...] = total
+        dz[...] = total.astype(jnp.bfloat16)
+
+    result = dot_nn(dz[...], weight_ref[...]).astype(jnp.bfloat16)
     for index in range(parts):
 
         @pl.when(step == index)
         def _():
+            columns = slice(index * tile, (index + 1) * tile)
+            dh_ref[...] = dh[:, columns]
+            dz_ref[...] = dz[:, columns]
             refs[2 + index][...] = result
 
 
@@ -868,6 +872,7 @@
     rows, depth = e.shape
     tile = depth // parts
     whole = pl.BlockSpec((rows, depth), lambda t: (0, 0))
+    column = pl.BlockSpec((rows, tile), lambda t: (0, t))
     result = pl.pallas_call(
         functools.partial(residual_kernel, parts),
         grid=(parts,),
@@ -879,11 +884,15 @@
             pl.BlockSpec((2, depth), lambda t: (0, 0)),
             pl.BlockSpec((depth, tile), lambda t: (0, t)),
         ],
-        out_specs=[whole, whole] + [pl.BlockSpec((rows, tile), lambda t: (0, 0))] * parts,
+        out_specs=[column, column] + [pl.BlockSpec((rows, tile), lambda t: (0, 0))] * parts,
         out_shape=[
             jax.ShapeDtypeStruct((rows, depth), jnp.float32),
             jax.ShapeDtypeStruct((rows, depth), jnp.bfloat16),
             *[jax.ShapeDtypeStruct((rows, tile), jnp.bfloat16)] * parts,
+        ],
+        scratch_shapes=[
+            pltpu.VMEM((rows, depth), jnp.float32),
+            pltpu.VMEM((rows, depth), jnp.bfloat16),
         ],
         compiler_params=parameters(),
         cost_estimate=SMALL_COST,
@@ -1044,13 +1053,15 @@
     joint_matrix, packed = pack(query_matrix, key_matrix, value_matrix, own_gains, groups)
     joint_full = mover.gather(packed)
     output_parts = mover.spread(output_weight.T)
-    up_shard = jnp.concatenate([gate_weight, up_weight], axis=1)
+    up_shard = jnp.pad(
+        jnp.concatenate([gate_weight, up_weight], axis=1), ((0, 0), (model_width, 0))
+    )
     output_parts, cosine_table, sine_table, doc_ids, up_shard, down_shard = together(
         output_parts, cosine_table, sine_table, doc_ids, up_shard, down_weight.T
     )
     local_tokens = tokens[0]
     token_chunks = [local_tokens, mover.hop(local_tokens)]
-    up_shard = join(output_parts + [up_shard], [0] * (ring + 1))
+    up_shard = join(output_parts, up_shard)
     up_full = mover.gather(up_shard)
     down_full = mover.gather(tie(down_shard, up_shard))
     gains = joint_full[:, joint_width : joint_width + 2].T.astype(f32)
@@ -1219,17 +1230,17 @@
             branch = branch + transposed_product(
                 [tie(product, last_part)], down_full, 0, ring // 2, 1, 2
             )
-            moved, last_part, branch, folded, first_parts = together(
-                moved, last_part, branch, folded, first_parts
+            next_branch = add(branch_moved, branch[sent])
+            moved, last_part, branch, folded, first_parts, next_branch = together(
+                moved, last_part, branch, folded, first_parts, next_branch
             )
         if j == 2:
             output_part = mover.advance([output_part], folded)
             last_part = last_weights(total, mover.swap(last_part, 1))
             gate_out, down_out = totals_of(*first_parts)
             down_out = down_out.T
-            next_branch = add(tie(branch_moved, last_part), branch[sent])
-            moved, last_part, output_part, gate_out, down_out, next_branch = together(
-                moved, last_part, output_part, gate_out, down_out, next_branch
+            moved, last_part, output_part, gate_out, down_out = together(
+                moved, last_part, output_part, gate_out, down_out
             )
         if j == 3:
             last_part = mover.begin(last_part)

time: 606 us -> 604 us (level)
  transfers between devices with their start and end apart: 51 -> 51, of which waited for: 16 -> 17; matrix products, arithmetic and copies ran while one was open for 9% -> 9% of each run, Pallas kernels for 50% -> 49%
where the time goes in v6:
time: 604 us; the launch traced here: 596 us
  Pallas kernels  296 us (49%)
  waiting for transfers between devices  147 us (24%)
  starting transfers between devices  73.4 us (12%)
  other arithmetic  43.3 us (7%)
  local copies, waits for them, and re-layouts  20.1 us (3%)
  between operations  15.1 us (2%)
    ppermute x18, waiting for transfers between devices, hop(): lax.ppermute(value, 'tensor', [(i, (i + shift) % self.ring) for i in rang...  120 us
    pallas_call x8, Pallas kernels, weight_product(): pl.pallas_call(functools.partial(weight_kernel, [(len(xs), len(ys)) for x...  81.3 us
    pallas_call x2, Pallas kernels, down_chunk(): pl.pallas_call(functools.partial(down_kernel, len(es), tiles), grid=(tile...  44.7 us
    ppermute x18, starting transfers between devices, hop(): lax.ppermute(value, 'tensor', [(i, (i + shift) % self.ring) for i in rang...  35.5 us
    pallas_call x2, Pallas kernels, attention_backward(): pl.pallas_call(functools.partial(backward_kernel, count), grid_spec=spec,...  34 us
    pallas_call x2, Pallas kernels, up_chunk(): pl.pallas_call(up_kernel, grid=(tiles,), in_specs=specs, out_specs=[pl.Bl...  27.7 us
    pallas_call x3, Pallas kernels, transposed_product(): pl.pallas_call(functools.partial(transposed_kernel, len(xs), parts), grid...  25.1 us
    pallas_call x4, Pallas kernels, project(): pl.pallas_call(project_kernel, grid=(groups,), in_specs=specs, out_specs=...  18.9 us
  transfers between devices with their start and end apart: 51, of which 17 were waited for; matrix products, arithmetic and copies ran while one was open for 9% of the time, Pallas kernels for 49%

profile of v6, /device:TPU:0, one launch (start us, length us, event | category | flops | bytes accessed | tf_op | source)
XLA Modules:
  0.0 595.5 jit_solution(4259170148633438033)
XLA Ops:
  55.6 12.9 %collective-permute-done.x_ref.refs_5_ = bf16[256,2048]{1,0:T(8,128)(2,1)S(1)} collective-permute-done((bf16[256,2048]{1,0:T(8,128)(2,1)S(1)}, bf16[256,2048]{1,0:T(8,128)(2,1)S(1)}, u32[]{:S(2)}, u32[]{:S(2)}) %collective-permute-start) | collective-permute-done | bytes 1048608 | tf_op jit(solution)/shard_map/ppermute | solution.py:962
  76.0 17.9 %collective-permute-done.4.x_ref.refs_6_ = bf16[256,2048]{1,0:T(8,128)(2,1)S(1)} collective-permute-done((bf16[256,2048]{1,0:T(8,128)(2,1)S(1)}, bf16[256,2048]{1,0:T(8,128)(2,1)S(1)}, u32[]{:S(2)}, u32[]{:S(2)}) %collective-permute-start.4) | collective-permute-done | bytes 1048608 | tf_op jit(solution)/shard_map/ppermute | solution.py:962
  100.4 18.0 %collective-permute-done.5.x_ref.refs_7_ = bf16[256,2048]{1,0:T(8,128)(2,1)} collective-permute-done((bf16[256,2048]{1,0:T(8,128)(2,1)S(1)}, bf16[256,2048]{1,0:T(8,128)(2,1)}, u32[]{:S(2)}, u32[]{:S(2)}) %collective-permute-start.5) | collective-permute-done | bytes 1048608 | tf_op jit(solution)/shard_map/ppermute | solution.py:962
  125.0 17.7 %attend.1 = (bf16[1024,512]{1,0:T(8,128)(2,1)}, f32[16,4096]{1,0:T(8,128)}) custom-call(s32[1]{0:T(128)} %bitcast.10.place_ref, bf16[1024,768]{1,0:T(8,128)(2,1)} %get-tuple-element.291.own_ref.all_ref.refs_0_.refs_1_, bf16[1024,768]{1,0:T(8,128)(2,1)} %get-tuple-element.291.own_ref.all_ref.refs_0_.refs_1_, s32[1,1024]{1,0:T(1,128)} %bitcast.52, ...), custom_call_target="tpu_custom_call" | custom-call | flops 1 | bytes 1 | tf_op jit(solution)/shard_map/attend/pallas_call | solution.py:256
  146.7 19.6 %collective-permute-done.7.refs_1_ = bf16[1024,512]{1,0:T(8,128)(2,1)S(1)} collective-permute-done((bf16[1024,512]{1,0:T(8,128)(2,1)}, bf16[1024,512]{1,0:T(8,128)(2,1)S(1)}, u32[]{:S(2)}, u32[]{:S(2)}) %collective-permute-start.7) | collective-permute-done | bytes 1048608 | tf_op jit(solution)/shard_map/ppermute | solution.py:962
  170.2 18.7 %collective-permute-done.8.refs_2_ = bf16[1024,512]{1,0:T(8,128)(2,1)} collective-permute-done((bf16[1024,512]{1,0:T(8,128)(2,1)S(1)}, bf16[1024,512]{1,0:T(8,128)(2,1)}, u32[]{:S(2)}, u32[]{:S(2)}) %collective-permute-start.8) | collective-permute-done | bytes 1048608 | tf_op jit(solution)/shard_map/ppermute | solution.py:962
  193.3 14.2 %heads_product.1 = (f32[1024,2048]{1,0:T(8,128)}, bf16[256,1536]{1,0:T(8,128)(2,1)}) custom-call(bf16[1024,512]{1,0:T(8,128)(2,1)} %get-tuple-element.295.refs_0_.refs_2_, bf16[1024,512]{1,0:T(8,128)(2,1)} %copy-done.40, bf16[1024,512]{1,0:T(8,128)(2,1)} %collective-permute-done.8.refs_2_, ...), custom_call_target="tpu_custom_call" | custom-call | flops 1 | bytes 1 | tf_op jit(solution)/shard_map/heads_product/pallas_call | solution.py:507
  215.9 9.3 %after_attention.1 = (f32[256,2048]{1,0:T(8,128)}, bf16[1024,2048]{1,0:T(8,128)(2,1)}, bf16[256,512]{1,0:T(8,128)(2,1)}) custom-call(f32[1024,2048]{1,0:T(8,128)} %get-tuple-element.305.partial_ref, bf16[1024,512]{1,0:T(8,128)(2,1)} %copy-done.41, bf16[2048,6144]{1,0:T(8,128)(2,1)} %all-gather.6.cloned.1.call-done.refs_3_.weight_ref.gate_ref.up_ref.refs_5_.refs_6_, ...), custom_call_target="tpu_custom_call" | custom-call | flops 1 | bytes 1 | tf_op jit(solution)/shard_map/after_attention/pallas_call | solution.py:549
  225.3 13.9 %up_chunk.2 = (bf16[1024,2048]{1,0:T(8,128)(2,1)}, bf16[1024,2048]{1,0:T(8,128)(2,1)}, bf16[1024,2048]{1,0:T(8,128)(2,1)}) custom-call(bf16[1024,2048]{1,0:T(8,128)(2,1)} %get-tuple-element.470.x_ref.refs_0_, bf16[2048,6144]{1,0:T(8,128)(2,1)} %all-gather.6.cloned.1.call-done.refs_3_.weight_ref.gate_ref.up_ref.refs_5_.refs_6_, ...), custom_call_target="tpu_custom_call" | custom-call | flops 1 | bytes 1 | tf_op jit(solution)/shard_map/up_chunk/pallas_call | solution.py:601
  240.2 22.3 %down_chunk.2 = (bf16[1024,2048]{1,0:T(8,128)(2,1)}, bf16[1024,2048]{1,0:T(8,128)(2,1)}, bf16[256,2048]{1,0:T(8,128)(2,1)}, bf16[256,2048]{1,0:T(8,128)(2,1)}) custom-call(bf16[256,2048]{1,0:T(8,128)(2,1)} %copy-done.5, bf16[256,2048]{1,0:T(8,128)(2,1)} %copy-done.6, bf16[2048,2048]{1,0:T(8,128)(2,1)} %all-gather.8.cloned.1.call-done.refs_2_.refs_1_, ...), custom_call_target="tpu_custom_call" | custom-call | flops 1 | bytes 1 | tf_op jit(solution)/shard_map/down_chunk/pallas_call | solution.py:686
  266.0 13.8 %up_chunk.3 = (bf16[1024,2048]{1,0:T(8,128)(2,1)}, bf16[1024,2048]{1,0:T(8,128)(2,1)}, bf16[1024,2048]{1,0:T(8,128)(2,1)}) custom-call(bf16[1024,2048]{1,0:T(8,128)(2,1)} %get-tuple-element.470.x_ref.refs_0_, ...), custom_call_target="tpu_custom_call", output_to_operand_aliasing={{0}: (3, {}), {1}: (4, {}), {2}: (5, {})} | custom-call | flops 1 | bytes 1 | tf_op jit(solution)/shard_map/up_chunk/pallas_call | solution.py:601
  279.8 9.0 %weight_product.8 = bf16[1024,2048]{1,0:T(8,128)(2,1)} custom-call(s32[1]{0:T(128)} %bitcast.13.place_ref, bf16[256,2048]{1,0:T(8,128)(2,1)} %copy-done.5, bf16[256,2048]{1,0:T(8,128)(2,1)} %copy-done.6, bf16[256,2048]{1,0:T(8,128)(2,1)} %copy-done.7, bf16[256,2048]{1,0:T(8,128)(2,1)} %bitcast.39, bf16[1024,2048]{1,0:T(8,128)(2,1)} %get-tuple-element.457.refs_4_.refs_0_), custom_call_target="tpu_custom_call" | custom-call | flops 1 | bytes 1 | tf_op jit(solution)/shard_map/weight_product/pallas_call | solution.py:789
  290.4 22.4 %down_chunk.3 = (bf16[1024,2048]{1,0:T(8,128)(2,1)}, bf16[1024,2048]{1,0:T(8,128)(2,1)}, bf16[256,2048]{1,0:T(8,128)(2,1)}, bf16[256,2048]{1,0:T(8,128)(2,1)}) custom-call(bf16[256,2048]{1,0:T(8,128)(2,1)} %copy-done.7, bf16[256,2048]{1,0:T(8,128)(2,1)} %bitcast.40, ...), custom_call_target="tpu_custom_call", output_to_operand_aliasing={{0}: (7, {}), {1}: (8, {})} | custom-call | flops 1 | bytes 1 | tf_op jit(solution)/shard_map/down_chunk/pallas_call | solution.py:686
  318.5 8.7 %weight_product.9 = bf16[1024,2048]{1,0:T(8,128)(2,1)} custom-call(s32[1]{0:T(128)} %bitcast.13.place_ref, bf16[1024,2048]{1,0:T(8,128)(2,1)} %get-tuple-element.470.x_ref.refs_0_, bf16[1024,2048]{1,0:T(8,128)(2,1)} %get-tuple-element.349.refs_1_), custom_call_target="tpu_custom_call" | custom-call | flops 1 | bytes 1 | tf_op jit(solution)/shard_map/weight_product/pallas_call | solution.py:789
  327.2 8.6 %transposed.3 = (bf16[256,2048]{1,0:T(8,128)(2,1)}, bf16[256,2048]{1,0:T(8,128)(2,1)}) custom-call(bf16[1024,2048]{1,0:T(8,128)(2,1)} %get-tuple-element.457.refs_4_.refs_0_, bf16[2048,2048]{1,0:T(8,128)(2,1)} %all-gather.8.cloned.1.call-done.refs_2_.refs_1_), custom_call_target="tpu_custom_call" | custom-call | flops 1 | bytes 1 | tf_op jit(solution)/shard_map/transposed/pallas_call | solution.py:460
  335.8 10.9 %weight_product.10 = (bf16[512,1024]{1,0:T(8,128)(2,1)}, bf16[512,1024]{1,0:T(8,128)(2,1)}, bf16[512,1024]{1,0:T(8,128)(2,1)}, bf16[512,1024]{1,0:T(8,128)(2,1)}) custom-call(s32[1]{0:T(128)} %bitcast.13.place_ref, bf16[256,2048]{1,0:T(8,128)(2,1)} %copy-done.5, bf16[256,2048]{1,0:T(8,128)(2,1)} %copy-done.6, bf16[256,2048]{1,0:T(8,128)(2,1)} %copy-done.7, ...), custom_call_target="tpu_custom_call" | custom-call | flops 1 | bytes 1 | tf_op jit(solution)/shard_map/weight_product/pallas_call | solution.py:789
  350.1 10.3 %residual_gradient.1 = (f32[256,2048]{1,0:T(8,128)}, bf16[256,2048]{1,0:T(8,128)(2,1)}, bf16[256,512]{1,0:T(8,128)(2,1)}, bf16[256,512]{1,0:T(8,128)(2,1)}, bf16...) custom-call(bf16[256,2048]{1,0:T(8,128)(2,1)} %bitcast.42, f32[256,2048]{1,0:T(8,128)} %get-tuple-element.309.hidden_ref, ...), custom_call_target="tpu_custom_call" | custom-call | flops 1 | bytes 1 | tf_op jit(solution)/shard_map/residual_gradient/pallas_call | solution.py:876
  369.9 10.6 %weight_product.12 = (bf16[512,1024]{1,0:T(8,128)(2,1)}, bf16[512,1024]{1,0:T(8,128)(2,1)}, bf16[512,1024]{1,0:T(8,128)(2,1)}, bf16[512,1024]{1,0:T(8,128)(2,1)}) custom-call(s32[1]{0:T(128)} %bitcast.13.place_ref, bf16[1024,2048]{1,0:T(8,128)(2,1)} %get-tuple-element.470.x_ref.refs_0_, bf16[1024,2048]{1,0:T(8,128)(2,1)} %get-tuple-element.349.refs_1_, ...), custom_call_target="tpu_custom_call" | custom-call | flops 1 | bytes 1 | tf_op jit(solution)/shard_map/weight_product/pallas_call | solution.py:789
  389.4 17.0 %attend_back.2.refs_0_.refs_3_ = bf16[1024,384]{1,0:T(8,128)(2,1)} custom-call(s32[1]{0:T(128)} %bitcast.10.place_ref, bf16[1024,768]{1,0:T(8,128)(2,1)} %get-tuple-element.291.own_ref.all_ref.refs_0_.refs_1_, bf16[1024,768]{1,0:T(8,128)(2,1)} %get-tuple-element.291.own_ref.all_ref.refs_0_.refs_1_, bf16[1024,512]{1,0:T(8,128)(2,1)} %get-tuple-element.295.refs_0_.refs_2_, ...), custom_call_target="tpu_custom_call" | custom-call | flops 1 | bytes 1 | tf_op jit(solution)/shard_map/attend_back/pallas_call | solution.py:364
  420.2 16.9 %attend_back.3.refs_1_.refs_4_ = bf16[1024,384]{1,0:T(8,128)(2,1)} custom-call(s32[1]{0:T(128)} %bitcast.10.place_ref, bf16[1024,768]{1,0:T(8,128)(2,1)} %get-tuple-element.291.own_ref.all_ref.refs_0_.refs_1_, bf16[1024,768]{1,0:T(8,128)(2,1)} %get-tuple-element.291.own_ref.all_ref.refs_0_.refs_1_, bf16[1024,512]{1,0:T(8,128)(2,1)} %get-tuple-element.295.refs_0_.refs_2_, ...), custom_call_target="tpu_custom_call" | custom-call | flops 1 | bytes 1 | tf_op jit(solution)/shard_map/attend_back/pallas_call | solution.py:364
  452.2 12.2 %weight_product.14 = bf16[1024,2816]{1,0:T(8,128)(2,1)} custom-call(s32[1]{0:T(128)} %bitcast.13.place_ref, bf16[1024,2048]{1,0:T(8,128)(2,1)} %get-tuple-element.470.x_ref.refs_0_, bf16[1024,2048]{1,0:T(8,128)(2,1)} %get-tuple-element.453.refs_1_, bf16[1024,2048]{1,0:T(8,128)(2,1)} %get-tuple-element.454.refs_2_, ...), custom_call_target="tpu_custom_call" | custom-call | flops 1 | bytes 1 | tf_op jit(solution)/shard_map/weight_product/pallas_call | solution.py:789
  464.5 8.7 %transposed.5 = (bf16[256,2048]{1,0:T(8,128)(2,1)}, bf16[256,2048]{1,0:T(8,128)(2,1)}) custom-call(bf16[1024,2048]{1,0:T(8,128)(2,1)} %get-tuple-element.457.refs_4_.refs_0_, bf16[2048,2048]{1,0:T(8,128)(2,1)} %all-gather.8.cloned.1.call-done.refs_2_.refs_1_), custom_call_target="tpu_custom_call" | custom-call | flops 1 | bytes 1 | tf_op jit(solution)/shard_map/transposed/pallas_call | solution.py:460
  487.5 17.3 %weight_product.15 = (bf16[512,1408]{1,0:T(8,128)(2,1)}, bf16[512,1408]{1,0:T(8,128)(2,1)}, bf16[512,1408]{1,0:T(8,128)(2,1)}, bf16[512,1408]{1,0:T(8,128)(2,1)}) custom-call(s32[1]{0:T(128)} %bitcast.13.place_ref, bf16[1024,2048]{1,0:T(8,128)(2,1)} %get-tuple-element.470.x_ref.refs_0_, bf16[1024,2048]{1,0:T(8,128)(2,1)} %get-tuple-element.453.refs_1_, ...), custom_call_target="tpu_custom_call" | custom-call | flops 1 | bytes 1 | tf_op jit(solution)/shard_map/weight_product/pallas_call | solution.py:789
  521.5 19.3 %collective-permute-done.37 = bf16[256,2048]{1,0:T(8,128)(2,1)} collective-permute-done((bf16[256,2048]{1,0:T(8,128)(2,1)}, bf16[256,2048]{1,0:T(8,128)(2,1)}, u32[]{:S(2)}, u32[]{:S(2)}) %collective-permute-start.37) | collective-permute-done | bytes 1048608 | tf_op jit(solution)/shard_map/ppermute | solution.py:962
  (285 shorter events, 229.8 us)
Async XLA Ops:
  7.2 41.6 %all-gather.4.cloned.1.call-start = ((), (), s32[]{:S(2)}) async-start(), calls=%async_computation | async-start | bytes 4128768 | tf_op jit(solution)/shard_map/all_gather | solution.py:930
  11.5 181.8 %all-gather.6.cloned.1.call-start = ((), (), s32[]{:S(2)}) async-start(), calls=%async_computation.1 | async-start | bytes 28311552 | tf_op jit(solution)/shard_map/all_gather | solution.py:930
  37.9 201.3 %all-gather.8.cloned.1.call-start = ((), (), s32[]{:S(2)}) async-start(), calls=%async_computation.2 | async-start | bytes 9437184 | tf_op jit(solution)/shard_map/all_gather | solution.py:930
  39.1 29.4 %collective-permute-start = (bf16[256,2048]{1,0:T(8,128)(2,1)S(1)}, bf16[256,2048]{1,0:T(8,128)(2,1)S(1)}, u32[]{:S(2)}, u32[]{:S(2)}) collective-permute-start(bf16[256,2048]{1,0:T(8,128)(2,1)S(1)} %bitcast.38), channel_id=1, source_target_pairs={{0,1},{1,2},{2,3},{3,0},{4,5},{5,6},{6,7},{7,4},{8,9},{9,10},{10,1... | collective-permute-start | bytes 3145736 | tf_op jit(solution)/shard_map/ppermute | solution.py:962
  262.5 26.3 %collective-permute-start.12 = (bf16[256,2048]{1,0:T(8,128)(2,1)}, bf16[256,2048]{1,0:T(8,128)(2,1)S(1)}, u32[]{:S(2)}, u32[]{:S(2)}) collective-permute-start(bf16[256,2048]{1,0:T(8,128)(2,1)} %get-tuple-element.325), channel_id=1, source_target_pairs={{0,1},{1,2},{2,3},{3,0},{4,5},{5,6},{6,7},{7,4},{8,9},{9,10},{10,1... | collective-permute-start | bytes 3145736 | tf_op jit(solution)/shard_map/ppermute | solution.py:962
  288.8 47.0 %collective-permute-start.15 = (bf16[1024,2048]{1,0:T(8,128)(2,1)}, bf16[1024,2048]{1,0:T(8,128)(2,1)}, u32[]{:S(2)}, u32[]{:S(2)}) collective-permute-start(bf16[1024,2048]{1,0:T(8,128)(2,1)} %weight_product.8), channel_id=1, source_target_pairs={{0,4},{4,0},{8,12},{12,8},{16,20},{20,16},{24,28},{28,24},{1,5},{5... | collective-permute-start | bytes 12582920 | tf_op jit(solution)/shard_map/ppermute | solution.py:927
  289.2 27.6 %collective-permute-start.13 = (bf16[256,2048]{1,0:T(8,128)(2,1)S(1)}, bf16[256,2048]{1,0:T(8,128)(2,1)S(1)}, u32[]{:S(2)}, u32[]{:S(2)}) collective-permute-start(bf16[256,2048]{1,0:T(8,128)(2,1)S(1)} %add_convert_fusion.6), channel_id=1, source_target_pairs={{0,1},{1,2},{2,3},{3,0},{4,5},{5,6},{6,7},{7,4},{8,9},{9,10},{10,1... | collective-permute-start | bytes 3145736 | tf_op jit(solution)/shard_map/ppermute | solution.py:962
  318.4 28.3 %collective-permute-start.14 = (bf16[256,2048]{1,0:T(8,128)(2,1)S(1)}, bf16[256,2048]{1,0:T(8,128)(2,1)S(1)}, u32[]{:S(2)}, u32[]{:S(2)}) collective-permute-start(bf16[256,2048]{1,0:T(8,128)(2,1)S(1)} %add_convert_fusion.5), channel_id=1, source_target_pairs={{0,1},{1,2},{2,3},{3,0},{4,5},{5,6},{6,7},{7,4},{8,9},{9,10},{10,1... | collective-permute-start | bytes 3145736 | tf_op jit(solution)/shard_map/ppermute | solution.py:962
  346.8 33.6 %collective-permute-start.21 = (bf16[512,1024]{1,0:T(8,128)(2,1)}, bf16[512,1024]{1,0:T(8,128)(2,1)S(1)}, u32[]{:S(2)}, u32[]{:S(2)}) collective-permute-start(bf16[512,1024]{1,0:T(8,128)(2,1)} %get-tuple-element.386), channel_id=1, source_target_pairs={{0,16},{4,20},{8,24},{12,28},{16,0},{20,4},{24,8},{28,12},{1,17},{... | collective-permute-start | bytes 3145736 | tf_op jit(solution)/shard_map/ppermute | solution.py:927
  348.5 32.0 %collective-permute-start.22 = (bf16[512,1024]{1,0:T(8,128)(2,1)}, bf16[512,1024]{1,0:T(8,128)(2,1)S(1)}, u32[]{:S(2)}, u32[]{:S(2)}) collective-permute-start(bf16[512,1024]{1,0:T(8,128)(2,1)} %get-tuple-element.388), channel_id=1, source_target_pairs={{0,8},{4,12},{8,0},{12,4},{16,24},{20,28},{24,16},{28,20},{1,9},{5... | collective-permute-start | bytes 3145736 | tf_op jit(solution)/shard_map/ppermute | solution.py:927
  382.3 31.6 %collective-permute-start.16 = (bf16[256,2048]{1,0:T(8,128)(2,1)}, bf16[256,2048]{1,0:T(8,128)(2,1)}, u32[]{:S(2)}, u32[]{:S(2)}) collective-permute-start(bf16[256,2048]{1,0:T(8,128)(2,1)} %get-tuple-element.362), channel_id=1, source_target_pairs={{0,1},{1,2},{2,3},{3,0},{4,5},{5,6},{6,7},{7,4},{8,9},{9,10},{10,1... | collective-permute-start | bytes 3145736 | tf_op jit(solution)/shard_map/ppermute | solution.py:962
  417.1 31.2 %collective-permute-start.26 = (bf16[256,2048]{1,0:T(8,128)(2,1)}, bf16[256,2048]{1,0:T(8,128)(2,1)S(1)}, u32[]{:S(2)}, u32[]{:S(2)}) collective-permute-start(bf16[256,2048]{1,0:T(8,128)(2,1)} %add_convert_fusion.4), channel_id=1, source_target_pairs={{0,1},{1,2},{2,3},{3,0},{4,5},{5,6},{6,7},{7,4},{8,9},{9,10},{10,1... | collective-permute-start | bytes 3145736 | tf_op jit(solution)/shard_map/ppermute | solution.py:962
  417.4 30.8 %collective-permute-start.27 = (bf16[512,1024]{1,0:T(8,128)(2,1)}, bf16[512,1024]{1,0:T(8,128)(2,1)S(1)}, u32[]{:S(2)}, u32[]{:S(2)}) collective-permute-start(bf16[512,1024]{1,0:T(8,128)(2,1)} %get-tuple-element.424), channel_id=1, source_target_pairs={{0,16},{4,20},{8,24},{12,28},{16,0},{20,4},{24,8},{28,12},{1,17},{... | collective-permute-start | bytes 3145736 | tf_op jit(solution)/shard_map/ppermute | solution.py:927
  419.1 29.2 %collective-permute-start.28 = (bf16[512,1024]{1,0:T(8,128)(2,1)}, bf16[512,1024]{1,0:T(8,128)(2,1)S(1)}, u32[]{:S(2)}, u32[]{:S(2)}) collective-permute-start(bf16[512,1024]{1,0:T(8,128)(2,1)} %get-tuple-element.426), channel_id=1, source_target_pairs={{0,8},{4,12},{8,0},{12,4},{16,24},{20,28},{24,16},{28,20},{1,9},{5... | collective-permute-start | bytes 3145736 | tf_op jit(solution)/shard_map/ppermute | solution.py:927
  448.3 27.6 %collective-permute-start.30 = (bf16[512,1024]{1,0:T(8,128)(2,1)}, bf16[512,1024]{1,0:T(8,128)(2,1)}, u32[]{:S(2)}, u32[]{:S(2)}) collective-permute-start(bf16[512,1024]{1,0:T(8,128)(2,1)} %get-tuple-element.464), channel_id=1, source_target_pairs={{0,8},{4,12},{8,0},{12,4},{16,24},{20,28},{24,16},{28,20},{1,9},{5... | collective-permute-start | bytes 3145736 | tf_op jit(solution)/shard_map/ppermute | solution.py:927
  449.3 26.6 %collective-permute-start.31 = (bf16[512,1024]{1,0:T(8,128)(2,1)}, bf16[512,1024]{1,0:T(8,128)(2,1)}, u32[]{:S(2)}, u32[]{:S(2)}) collective-permute-start(bf16[512,1024]{1,0:T(8,128)(2,1)} %get-tuple-element.465), channel_id=1, source_target_pairs={{0,16},{4,20},{8,24},{12,28},{16,0},{20,4},{24,8},{28,12},{1,17},{... | collective-permute-start | bytes 3145736 | tf_op jit(solution)/shard_map/ppermute | solution.py:927
  449.6 26.2 %collective-permute-start.29 = (bf16[256,2048]{1,0:T(8,128)(2,1)}, bf16[256,2048]{1,0:T(8,128)(2,1)}, u32[]{:S(2)}, u32[]{:S(2)}) collective-permute-start(bf16[256,2048]{1,0:T(8,128)(2,1)} %get-tuple-element.441), channel_id=1, source_target_pairs={{0,1},{1,2},{2,3},{3,0},{4,5},{5,6},{6,7},{7,4},{8,9},{9,10},{10,1... | collective-permute-start | bytes 3145736 | tf_op jit(solution)/shard_map/ppermute | solution.py:962
  479.1 27.8 %collective-permute-start.32 = (bf16[256,2048]{1,0:T(8,128)(2,1)}, bf16[256,2048]{1,0:T(8,128)(2,1)}, u32[]{:S(2)}, u32[]{:S(2)}) collective-permute-start(bf16[256,2048]{1,0:T(8,128)(2,1)} %add_convert_fusion.2), channel_id=1, source_target_pairs={{0,1},{1,2},{2,3},{3,0},{4,5},{5,6},{6,7},{7,4},{8,9},{9,10},{10,1... | collective-permute-start | bytes 3145736 | tf_op jit(solution)/shard_map/ppermute | solution.py:962
  506.9 33.9 %collective-permute-start.38 = (bf16[512,1408]{1,0:T(8,128)(2,1)}, bf16[512,1408]{1,0:T(8,128)(2,1)}, u32[]{:S(2)}, u32[]{:S(2)}) collective-permute-start(bf16[512,1408]{1,0:T(8,128)(2,1)} %get-tuple-element.492), channel_id=1, source_target_pairs={{0,16},{4,20},{8,24},{12,28},{16,0},{20,4},{24,8},{28,12},{1,17},{... | collective-permute-start | bytes 4325384 | tf_op jit(solution)/shard_map/ppermute | solution.py:927
  508.6 33.3 %collective-permute-start.39 = (bf16[512,1408]{1,0:T(8,128)(2,1)}, bf16[512,1408]{1,0:T(8,128)(2,1)}, u32[]{:S(2)}, u32[]{:S(2)}) collective-permute-start(bf16[512,1408]{1,0:T(8,128)(2,1)} %get-tuple-element.494), channel_id=1, source_target_pairs={{0,8},{4,12},{8,0},{12,4},{16,24},{20,28},{24,16},{28,20},{1,9},{5... | collective-permute-start | bytes 4325384 | tf_op jit(solution)/shard_map/ppermute | solution.py:927
  512.6 28.2 %collective-permute-start.37 = (bf16[256,2048]{1,0:T(8,128)(2,1)}, bf16[256,2048]{1,0:T(8,128)(2,1)}, u32[]{:S(2)}, u32[]{:S(2)}) collective-permute-start(bf16[256,2048]{1,0:T(8,128)(2,1)} %add_convert_fusion.1), channel_id=1, source_target_pairs={{0,1},{1,2},{2,3},{3,0},{4,5},{5,6},{6,7},{7,4},{8,9},{9,10},{10,1... | collective-permute-start | bytes 3145736 | tf_op jit(solution)/shard_map/ppermute | solution.py:962
  515.1 59.4 %collective-permute-start.36 = (bf16[256,2048]{1,0:T(8,128)(2,1)}, bf16[256,2048]{1,0:T(8,128)(2,1)}, u32[]{:S(2)}, u32[]{:S(2)}) collective-permute-start(bf16[256,2048]{1,0:T(8,128)(2,1)} %add_convert_fusion.3), channel_id=1, source_target_pairs={{0,1},{1,2},{2,3},{3,0},{4,5},{5,6},{6,7},{7,4},{8,9},{9,10},{10,1... | collective-permute-start | bytes 3145736 | tf_op jit(solution)/shard_map/ppermute | solution.py:962
  547.7 36.4 %collective-permute-start.45 = (bf16[256,512]{1,0:T(8,128)(2,1)S(1)}, bf16[256,512]{1,0:T(8,128)(2,1)S(1)}, u32[]{:S(2)}, u32[]{:S(2)}) collective-permute-start(bf16[256,512]{1,0:T(8,128)(2,1)S(1)} %split.17), channel_id=1, source_target_pairs={{0,1},{1,2},{2,3},{3,0},{4,5},{5,6},{6,7},{7,4},{8,9},{9,10},{10,1... | collective-permute-start | bytes 786440 | tf_op jit(solution)/shard_map/ppermute | solution.py:977
  550.1 34.0 %collective-permute-start.46 = (bf16[256,512]{1,0:T(8,128)(2,1)S(1)}, bf16[256,512]{1,0:T(8,128)(2,1)S(1)}, u32[]{:S(2)}, u32[]{:S(2)}) collective-permute-start(bf16[256,512]{1,0:T(8,128)(2,1)S(1)} %get-tuple-element.522), channel_id=1, source_target_pairs={{0,2},{1,3},{2,0},{3,1},{4,6},{5,7},{6,4},{7,5},{8,10},{9,11},{10,... | collective-permute-start | bytes 786440 | tf_op jit(solution)/shard_map/ppermute | solution.py:977
  (78 other events, 1223.5 us)
Sparse Core Ops, SparseCore 0:
  11.6 37.2 all-gather.3
  50.7 125.3 all-gather.5
  178.0 54.3 all-gather.7

commit v7 on v6

--- a/solution.py
+++ b/solution.py
@@ -719,7 +719,7 @@
         for y_ref in refs[place + parts : place + parts + widths]:
             width = y_ref.shape[1]
             cuts = set(range(0, width, 1024)) | {width}
-            if column < split < column + width:
+            if column < split < column + width and split:
                 cuts.add(split - column)
             cuts = sorted(cuts)
             for first, last in zip(cuts[:-1], cuts[1:]):
@@ -730,6 +730,9 @@
                     continue
                 total += received[:, start:end].astype(jnp.float32)
                 total = total.astype(jnp.bfloat16)
+                if split == 0:
+                    refs[-1][:, start:end] = total
+                    continue
                 low = start < split
                 keep = step < blocks // 2 if low else lax.rem(step, 2) == 0
                 keep_ref, send_ref = refs[-4:-2] if low else refs[-2:]
@@ -747,15 +750,21 @@
         place += parts + widths
 
 
-def weight_product(pairs, place, count, received):
+def weight_product(pairs, place, count, received, ordered=False):
     depth = pairs[0][0][0].shape[1]
     blocks = count // 2
     tile = depth // count
     total = sum(y.shape[1] for _, ys in pairs for y in ys)
-    split = -(-total // 256) * 128
+    split = 0 if ordered else -(-total // 256) * 128
     side = 1 if received is None else 0
+
+    def source(t, p):
+        if ordered:
+            return 2 * t + lax.rem(p[0] + side, 2)
+        return lax.bitwise_xor(p[0], 2 * t + side)
+
     whole = pl.BlockSpec((tile, total), lambda t, p: (t, 0))
-    if received is None:
+    if received is None or ordered:
         out_specs = whole
         out_shape = jax.ShapeDtypeStruct((depth // 2, total), jnp.bfloat16)
     else:
@@ -774,11 +783,7 @@
     operands = []
     for xs, ys in pairs:
         for x in xs:
-            specs.append(
-                pl.BlockSpec(
-                    (x.shape[0], tile), lambda t, p: (0, lax.bitwise_xor(p[0], 2 * t + side))
-                )
-            )
+            specs.append(pl.BlockSpec((x.shape[0], tile), lambda t, p: (0, source(t, p))))
         specs += [
             pl.BlockSpec(y.shape, lambda t, p: (0, 0), pipeline_mode=pl.Buffered(1)) for y in ys
         ]
@@ -957,6 +962,17 @@
                 for index, pair in enumerate(sums)
             ]
             folded = self.fold(sums, level)
+
+    def advance_all(self, sums):
+        widths = {pair[0][0].shape[1] for pair in sums}
+        parts = [sums] if len(widths) == 1 else [[pair] for pair in sums]
+        return [self.advance(part, self.fold(part)) for part in parts]
+
+    def scatter(self, total):
+        groups = [list(range(core, self.dp_count, 2)) for core in range(2)]
+        return lax.psum_scatter(
+            total, "dp", scatter_dimension=0, tiled=True, axis_index_groups=groups
+        )
 
     def hop(self, value, shift=1):
         return lax.ppermute(
@@ -1137,7 +1153,7 @@
     moved = mover.hop(total)
     upward = up_chunk(tie(normed_two, total), up_full, upward, pairs - 1, pairs)
     product = upward[2]
-    down_part = weights(ordered, [product])
+    down_part = weight_product([(ordered, [product])], dp_place, dp_count, None, True)
     moved, upward, down_part = together(moved, upward, down_part)
     down_part = mover.swap(down_part, 1)
     for j in range(2, ring):
@@ -1153,10 +1169,12 @@
             branch = transposed_product(
                 [tie(product, gate_part)], down_full, 0, ring // 2, 0, 2
             )
-            down_part = weights(tie(ordered, branch), [product], down_part)
+            down_part = weight_product(
+                [(tie(ordered, branch), [product])], dp_place, dp_count, down_part, True
+            )
             moved, gate_part, branch, down_part = together(moved, gate_part, branch, down_part)
     gate_part = mover.swap(gate_part, 1)
-    down_part = mover.begin(down_part)
+    down_out = mover.scatter(down_part)
     grad_hidden, grad_branch, grad_parts = residual_gradient(
         local_cotangent, hidden_res, moved, grads[-1], gains, up_full, ring
     )
@@ -1167,19 +1185,15 @@
     grad_parts = mover.exchange(grad_parts)
     output_part = weights([grad_branch], [attended_local, attended_last])
     gate_part = weights([tie(normed_two, output_part)], [grad_gate], gate_part)
-    grad_parts, output_part, gate_part, down_part = together(
-        grad_parts, output_part, gate_part, down_part
-    )
+    grad_parts, output_part, gate_part = together(grad_parts, output_part, gate_part)
     grad_joint = []
     sent = 0
-    folded = []
     moved = branch[0]
     for group in range(groups):
         moved = mover.hop(moved)
         sent += 1
         if group == 0:
             output_part = mover.swap(output_part, 1)
-            gate_part = mover.begin(gate_part)
         else:
             output_part = mover.begin(output_part)
         grad_joint.append(
@@ -1201,9 +1215,8 @@
             )
         if group + 1 == groups:
             grads = transposed_product(grad_joint, joint_full, 0, ring)
-            folded = mover.fold(tie([gate_part, down_part], grads))
-        moved, grad_joint, grads, gate_part, output_part, folded = together(
-            moved, grad_joint, grads, gate_part, output_part, folded
+        moved, grad_joint, grads, output_part, down_out = together(
+            moved, grad_joint, grads, output_part, down_out
         )
         if group + 1 < groups:
             moved = add(moved, branch[sent])
@@ -1224,29 +1237,28 @@
         total = grads[1] if j == 1 else add(moved, grads[j])
         moved = mover.hop(total)
         if j == 1:
-            first_parts = mover.advance([gate_part, down_part], folded)
-            folded = mover.fold(tie([output_part], total))
-            last_part = last_weights(folded, None)
+            gate_part = mover.begin(gate_part)
+            last_part = last_weights(total, None)
             branch = branch + transposed_product(
                 [tie(product, last_part)], down_full, 0, ring // 2, 1, 2
             )
-            next_branch = add(branch_moved, branch[sent])
-            moved, last_part, branch, folded, first_parts, next_branch = together(
-                moved, last_part, branch, folded, first_parts, next_branch
+            moved, last_part, branch, output_part, gate_part = together(
+                moved, last_part, branch, output_part, gate_part
             )
         if j == 2:
-            output_part = mover.advance([output_part], folded)
-            last_part = last_weights(total, mover.swap(last_part, 1))
-            gate_out, down_out = totals_of(*first_parts)
-            down_out = down_out.T
-            moved, last_part, output_part, gate_out, down_out = together(
-                moved, last_part, output_part, gate_out, down_out
+            both_parts = tie([output_part, gate_part], total)
+            both_parts = mover.advance_all(both_parts)
+            next_branch = add(branch_moved, branch[sent])
+            last_part = last_weights(next_branch, mover.swap(last_part, 1))
+            moved, last_part, both_parts, next_branch = together(
+                moved, last_part, both_parts, next_branch
             )
         if j == 3:
             last_part = mover.begin(last_part)
             branch_moved = mover.hop(tie(next_branch, total))
             sent += 1
-            output_out = jnp.split(totals_of(*output_part)[0], ring, axis=1)
+            output_out, gate_out = [total for part in both_parts for total in totals_of(*part)]
+            output_out = jnp.split(output_out, ring, axis=1)
             moved, last_part, output_out = together(moved, last_part, output_out)
     folded, output_out = together(mover.fold([last_part]), output_out)
     last_part = mover.advance([last_part], folded)
@@ -1296,7 +1308,7 @@
         gain_out[1],
         gate_out,
         up_out,
-        down_out,
+        down_out.astype(f32).T,
     )
 
 

time: 604 us -> 600 us (level)
    ppermute x18 -> x14, starting transfers between devices: 15.4 us -> 11.1 us  [swap(): lax.ppermute(value, 'dp', [(i, i ^ step) for i in range(self.dp_count)])]
    ppermute x18 -> x14, waiting for transfers between devices: 11.4 us -> 13.7 us  [swap(): lax.ppermute(value, 'dp', [(i, i ^ step) for i in range(self.dp_count)])]
  transfers between devices with their start and end apart: 51 -> 48, of which waited for: 17 -> 17; matrix products, arithmetic and copies ran while one was open for 9% -> 9% of each run, Pallas kernels for 49% -> 49%
where the time goes in v7:
time: 600 us; the launch traced here: 591 us
  Pallas kernels  294 us (49%)
  waiting for transfers between devices  151 us (25%)
  starting transfers between devices  69.8 us (12%)
  other arithmetic  40.7 us (7%)
  local copies, waits for them, and re-layouts  21.6 us (4%)
  between operations  15 us (2%)
    ppermute x18, waiting for transfers between devices, hop(): lax.ppermute(value, 'tensor', [(i, (i + shift) % self.ring) for i in rang...  122 us
    pallas_call x8, Pallas kernels, weight_product(): pl.pallas_call(functools.partial(weight_kernel, [(len(xs), len(ys)) for x...  79.5 us
    pallas_call x2, Pallas kernels, down_chunk(): pl.pallas_call(functools.partial(down_kernel, len(es), tiles), grid=(tile...  44.8 us
    ppermute x18, starting transfers between devices, hop(): lax.ppermute(value, 'tensor', [(i, (i + shift) % self.ring) for i in rang...  36.1 us
    pallas_call x2, Pallas kernels, attention_backward(): pl.pallas_call(functools.partial(backward_kernel, count), grid_spec=spec,...  34.6 us
    pallas_call x2, Pallas kernels, up_chunk(): pl.pallas_call(up_kernel, grid=(tiles,), in_specs=specs, out_specs=[pl.Bl...  27.7 us
    pallas_call x3, Pallas kernels, transposed_product(): pl.pallas_call(functools.partial(transposed_kernel, len(xs), parts), grid...  25.1 us
    pallas_call x4, Pallas kernels, project(): pl.pallas_call(project_kernel, grid=(groups,), in_specs=specs, out_specs=...  18.9 us
  transfers between devices with their start and end apart: 48, of which 17 were waited for; matrix products, arithmetic and copies ran while one was open for 9% of the time, Pallas kernels for 49%

profile of v7, /device:TPU:0, one launch (start us, length us, event | category | flops | bytes accessed | tf_op | source)
XLA Modules:
  0.0 591.3 jit_solution(11910316609365692932)
XLA Ops:
  55.6 13.0 %collective-permute-done.x_ref.refs_5_ = bf16[256,2048]{1,0:T(8,128)(2,1)S(1)} collective-permute-done((bf16[256,2048]{1,0:T(8,128)(2,1)S(1)}, bf16[256,2048]{1,0:T(8,128)(2,1)S(1)}, u32[]{:S(2)}, u32[]{:S(2)}) %collective-permute-start) | collective-permute-done | bytes 1048608 | tf_op jit(solution)/shard_map/ppermute | solution.py:978
  76.0 17.8 %collective-permute-done.4.x_ref.refs_6_ = bf16[256,2048]{1,0:T(8,128)(2,1)S(1)} collective-permute-done((bf16[256,2048]{1,0:T(8,128)(2,1)S(1)}, bf16[256,2048]{1,0:T(8,128)(2,1)S(1)}, u32[]{:S(2)}, u32[]{:S(2)}) %collective-permute-start.4) | collective-permute-done | bytes 1048608 | tf_op jit(solution)/shard_map/ppermute | solution.py:978
  100.3 17.9 %collective-permute-done.5.x_ref.refs_7_ = bf16[256,2048]{1,0:T(8,128)(2,1)} collective-permute-done((bf16[256,2048]{1,0:T(8,128)(2,1)S(1)}, bf16[256,2048]{1,0:T(8,128)(2,1)}, u32[]{:S(2)}, u32[]{:S(2)}) %collective-permute-start.5) | collective-permute-done | bytes 1048608 | tf_op jit(solution)/shard_map/ppermute | solution.py:978
  124.8 17.7 %attend.1 = (bf16[1024,512]{1,0:T(8,128)(2,1)}, f32[16,4096]{1,0:T(8,128)}) custom-call(s32[1]{0:T(128)} %bitcast.10.place_ref, bf16[1024,768]{1,0:T(8,128)(2,1)} %get-tuple-element.265.own_ref.all_ref.refs_0_.refs_1_, bf16[1024,768]{1,0:T(8,128)(2,1)} %get-tuple-element.265.own_ref.all_ref.refs_0_.refs_1_, s32[1,1024]{1,0:T(1,128)} %bitcast.52, ...), custom_call_target="tpu_custom_call" | custom-call | flops 1 | bytes 1 | tf_op jit(solution)/shard_map/attend/pallas_call | solution.py:256
  146.5 19.6 %collective-permute-done.7.refs_1_ = bf16[1024,512]{1,0:T(8,128)(2,1)S(1)} collective-permute-done((bf16[1024,512]{1,0:T(8,128)(2,1)}, bf16[1024,512]{1,0:T(8,128)(2,1)S(1)}, u32[]{:S(2)}, u32[]{:S(2)}) %collective-permute-start.7) | collective-permute-done | bytes 1048608 | tf_op jit(solution)/shard_map/ppermute | solution.py:978
  170.0 18.8 %collective-permute-done.8.refs_2_ = bf16[1024,512]{1,0:T(8,128)(2,1)} collective-permute-done((bf16[1024,512]{1,0:T(8,128)(2,1)S(1)}, bf16[1024,512]{1,0:T(8,128)(2,1)}, u32[]{:S(2)}, u32[]{:S(2)}) %collective-permute-start.8) | collective-permute-done | bytes 1048608 | tf_op jit(solution)/shard_map/ppermute | solution.py:978
  193.1 14.3 %heads_product.1 = (f32[1024,2048]{1,0:T(8,128)}, bf16[256,1536]{1,0:T(8,128)(2,1)}) custom-call(bf16[1024,512]{1,0:T(8,128)(2,1)} %get-tuple-element.269.refs_0_.refs_2_, bf16[1024,512]{1,0:T(8,128)(2,1)} %copy-done.34, bf16[1024,512]{1,0:T(8,128)(2,1)} %collective-permute-done.8.refs_2_, ...), custom_call_target="tpu_custom_call" | custom-call | flops 1 | bytes 1 | tf_op jit(solution)/shard_map/heads_product/pallas_call | solution.py:507
  214.6 9.5 %after_attention.1 = (f32[256,2048]{1,0:T(8,128)}, bf16[1024,2048]{1,0:T(8,128)(2,1)}, bf16[256,512]{1,0:T(8,128)(2,1)}) custom-call(f32[1024,2048]{1,0:T(8,128)} %get-tuple-element.279.partial_ref, bf16[1024,512]{1,0:T(8,128)(2,1)} %collective-permute-done.9.last_ref, ...), custom_call_target="tpu_custom_call" | custom-call | flops 1 | bytes 1 | tf_op jit(solution)/shard_map/after_attention/pallas_call | solution.py:549
  224.1 13.9 %up_chunk.2 = (bf16[1024,2048]{1,0:T(8,128)(2,1)}, bf16[1024,2048]{1,0:T(8,128)(2,1)}, bf16[1024,2048]{1,0:T(8,128)(2,1)}) custom-call(bf16[1024,2048]{1,0:T(8,128)(2,1)} %get-tuple-element.408.x_ref.refs_0_, bf16[2048,6144]{1,0:T(8,128)(2,1)} %all-gather.6.cloned.1.call-done.refs_3_.weight_ref.gate_ref.up_ref.refs_5_.refs_6_, ...), custom_call_target="tpu_custom_call" | custom-call | flops 1 | bytes 1 | tf_op jit(solution)/shard_map/up_chunk/pallas_call | solution.py:601
  239.1 22.4 %down_chunk.2 = (bf16[1024,2048]{1,0:T(8,128)(2,1)}, bf16[1024,2048]{1,0:T(8,128)(2,1)}, bf16[256,2048]{1,0:T(8,128)(2,1)}, bf16[256,2048]{1,0:T(8,128)(2,1)}) custom-call(bf16[256,2048]{1,0:T(8,128)(2,1)} %copy-done.3, bf16[256,2048]{1,0:T(8,128)(2,1)} %copy-done.4, bf16[2048,2048]{1,0:T(8,128)(2,1)} %all-gather.8.cloned.1.call-done.refs_2_.refs_1_, ...), custom_call_target="tpu_custom_call" | custom-call | flops 1 | bytes 1 | tf_op jit(solution)/shard_map/down_chunk/pallas_call | solution.py:686
  265.7 13.8 %up_chunk.3 = (bf16[1024,2048]{1,0:T(8,128)(2,1)}, bf16[1024,2048]{1,0:T(8,128)(2,1)}, bf16[1024,2048]{1,0:T(8,128)(2,1)}) custom-call(bf16[1024,2048]{1,0:T(8,128)(2,1)} %get-tuple-element.408.x_ref.refs_0_, ...), custom_call_target="tpu_custom_call", output_to_operand_aliasing={{0}: (3, {}), {1}: (4, {}), {2}: (5, {})} | custom-call | flops 1 | bytes 1 | tf_op jit(solution)/shard_map/up_chunk/pallas_call | solution.py:601
  279.5 9.0 %weight_product.8 = bf16[1024,2048]{1,0:T(8,128)(2,1)} custom-call(s32[1]{0:T(128)} %bitcast.13.place_ref, bf16[256,2048]{1,0:T(8,128)(2,1)} %copy-done.3, bf16[256,2048]{1,0:T(8,128)(2,1)} %copy-done.4, bf16[256,2048]{1,0:T(8,128)(2,1)} %copy-done.5, bf16[256,2048]{1,0:T(8,128)(2,1)} %bitcast.39, bf16[1024,2048]{1,0:T(8,128)(2,1)} %get-tuple-element.393.refs_4_.refs_0_), custom_call_target="tpu_custom_call" | custom-call | flops 1 | bytes 1 | tf_op jit(solution)/shard_map/weight_product/pallas_call | solution.py:794
  291.1 22.4 %down_chunk.3 = (bf16[1024,2048]{1,0:T(8,128)(2,1)}, bf16[1024,2048]{1,0:T(8,128)(2,1)}, bf16[256,2048]{1,0:T(8,128)(2,1)}, bf16[256,2048]{1,0:T(8,128)(2,1)}) custom-call(bf16[256,2048]{1,0:T(8,128)(2,1)} %copy-done.5, bf16[256,2048]{1,0:T(8,128)(2,1)} %bitcast.40, ...), custom_call_target="tpu_custom_call", output_to_operand_aliasing={{0}: (7, {}), {1}: (8, {})} | custom-call | flops 1 | bytes 1 | tf_op jit(solution)/shard_map/down_chunk/pallas_call | solution.py:686
  319.3 8.7 %weight_product.9 = bf16[1024,2048]{1,0:T(8,128)(2,1)} custom-call(s32[1]{0:T(128)} %bitcast.13.place_ref, bf16[1024,2048]{1,0:T(8,128)(2,1)} %get-tuple-element.408.x_ref.refs_0_, bf16[1024,2048]{1,0:T(8,128)(2,1)} %get-tuple-element.323.refs_1_), custom_call_target="tpu_custom_call" | custom-call | flops 1 | bytes 1 | tf_op jit(solution)/shard_map/weight_product/pallas_call | solution.py:794
  328.1 8.6 %transposed.3 = (bf16[256,2048]{1,0:T(8,128)(2,1)}, bf16[256,2048]{1,0:T(8,128)(2,1)}) custom-call(bf16[1024,2048]{1,0:T(8,128)(2,1)} %get-tuple-element.393.refs_4_.refs_0_, bf16[2048,2048]{1,0:T(8,128)(2,1)} %all-gather.8.cloned.1.call-done.refs_2_.refs_1_), custom_call_target="tpu_custom_call" | custom-call | flops 1 | bytes 1 | tf_op jit(solution)/shard_map/transposed/pallas_call | solution.py:460
  336.7 9.7 %weight_product.10 = bf16[1024,2048]{1,0:T(8,128)(2,1)} custom-call(s32[1]{0:T(128)} %bitcast.13.place_ref, bf16[256,2048]{1,0:T(8,128)(2,1)} %copy-done.3, bf16[256,2048]{1,0:T(8,128)(2,1)} %copy-done.4, bf16[256,2048]{1,0:T(8,128)(2,1)} %copy-done.5, bf16[256,2048]{1,0:T(8,128)(2,1)} %bitcast.41, bf16[1024,2048]{1,0:T(8,128)(2,1)} %get-tuple-element.393.refs_4_.refs_0_, ...), custom_call_target="tpu_custom_call" | custom-call | flops 1 | bytes 1 | tf_op jit(solution)/shard_map/weight_product/pallas_call | solution.py:794
  347.4 10.7 %residual_gradient.1 = (f32[256,2048]{1,0:T(8,128)}, bf16[256,2048]{1,0:T(8,128)(2,1)}, bf16[256,512]{1,0:T(8,128)(2,1)}, bf16[256,512]{1,0:T(8,128)(2,1)}, bf16...) custom-call(bf16[256,2048]{1,0:T(8,128)(2,1)} %bitcast.42, f32[256,2048]{1,0:T(8,128)} %get-tuple-element.283.hidden_ref, ...), custom_call_target="tpu_custom_call" | custom-call | flops 1 | bytes 1 | tf_op jit(solution)/shard_map/residual_gradient/pallas_call | solution.py:881
  367.7 10.6 %weight_product.12 = (bf16[512,1024]{1,0:T(8,128)(2,1)}, bf16[512,1024]{1,0:T(8,128)(2,1)}, bf16[512,1024]{1,0:T(8,128)(2,1)}, bf16[512,1024]{1,0:T(8,128)(2,1)}) custom-call(s32[1]{0:T(128)} %bitcast.13.place_ref, bf16[1024,2048]{1,0:T(8,128)(2,1)} %get-tuple-element.408.x_ref.refs_0_, bf16[1024,2048]{1,0:T(8,128)(2,1)} %get-tuple-element.323.refs_1_, ...), custom_call_target="tpu_custom_call" | custom-call | flops 1 | bytes 1 | tf_op jit(solution)/shard_map/weight_product/pallas_call | solution.py:794
  385.6 17.7 %attend_back.2.refs_0_.refs_3_ = bf16[1024,384]{1,0:T(8,128)(2,1)} custom-call(s32[1]{0:T(128)} %bitcast.10.place_ref, bf16[1024,768]{1,0:T(8,128)(2,1)} %get-tuple-element.265.own_ref.all_ref.refs_0_.refs_1_, bf16[1024,768]{1,0:T(8,128)(2,1)} %get-tuple-element.265.own_ref.all_ref.refs_0_.refs_1_, bf16[1024,512]{1,0:T(8,128)(2,1)} %get-tuple-element.269.refs_0_.refs_2_, ...), custom_call_target="tpu_custom_call" | custom-call | flops 1 | bytes 1 | tf_op jit(solution)/shard_map/attend_back/pallas_call | solution.py:364
  416.6 17.0 %attend_back.3.refs_1_.refs_4_ = bf16[1024,384]{1,0:T(8,128)(2,1)} custom-call(s32[1]{0:T(128)} %bitcast.10.place_ref, bf16[1024,768]{1,0:T(8,128)(2,1)} %get-tuple-element.265.own_ref.all_ref.refs_0_.refs_1_, bf16[1024,768]{1,0:T(8,128)(2,1)} %get-tuple-element.265.own_ref.all_ref.refs_0_.refs_1_, bf16[1024,512]{1,0:T(8,128)(2,1)} %get-tuple-element.269.refs_0_.refs_2_, ...), custom_call_target="tpu_custom_call" | custom-call | flops 1 | bytes 1 | tf_op jit(solution)/shard_map/attend_back/pallas_call | solution.py:364
  442.6 12.1 %weight_product.14 = bf16[1024,2816]{1,0:T(8,128)(2,1)} custom-call(s32[1]{0:T(128)} %bitcast.13.place_ref, bf16[1024,2048]{1,0:T(8,128)(2,1)} %get-tuple-element.408.x_ref.refs_0_, bf16[1024,2048]{1,0:T(8,128)(2,1)} %get-tuple-element.389.refs_1_, bf16[1024,2048]{1,0:T(8,128)(2,1)} %get-tuple-element.390.refs_2_, ...), custom_call_target="tpu_custom_call" | custom-call | flops 1 | bytes 1 | tf_op jit(solution)/shard_map/weight_product/pallas_call | solution.py:794
  454.8 8.8 %transposed.5 = (bf16[256,2048]{1,0:T(8,128)(2,1)}, bf16[256,2048]{1,0:T(8,128)(2,1)}) custom-call(bf16[1024,2048]{1,0:T(8,128)(2,1)} %get-tuple-element.393.refs_4_.refs_0_, bf16[2048,2048]{1,0:T(8,128)(2,1)} %all-gather.8.cloned.1.call-done.refs_2_.refs_1_), custom_call_target="tpu_custom_call" | custom-call | flops 1 | bytes 1 | tf_op jit(solution)/shard_map/transposed/pallas_call | solution.py:460
  485.1 16.7 %weight_product.15 = (bf16[512,1408]{1,0:T(8,128)(2,1)}, bf16[512,1408]{1,0:T(8,128)(2,1)}, bf16[512,1408]{1,0:T(8,128)(2,1)}, bf16[512,1408]{1,0:T(8,128)(2,1)}) custom-call(s32[1]{0:T(128)} %bitcast.13.place_ref, bf16[1024,2048]{1,0:T(8,128)(2,1)} %get-tuple-element.408.x_ref.refs_0_, bf16[1024,2048]{1,0:T(8,128)(2,1)} %get-tuple-element.389.refs_1_, ...), custom_call_target="tpu_custom_call" | custom-call | flops 1 | bytes 1 | tf_op jit(solution)/shard_map/weight_product/pallas_call | solution.py:794
  514.2 19.5 %collective-permute-done.33 = bf16[256,2048]{1,0:T(8,128)(2,1)} collective-permute-done((bf16[256,2048]{1,0:T(8,128)(2,1)S(1)}, bf16[256,2048]{1,0:T(8,128)(2,1)}, u32[]{:S(2)}, u32[]{:S(2)}) %collective-permute-start.33) | collective-permute-done | bytes 1048608 | tf_op jit(solution)/shard_map/ppermute | solution.py:978
  (265 shorter events, 226.3 us)
Async XLA Ops:
  7.2 41.6 %all-gather.4.cloned.1.call-start = ((), (), s32[]{:S(2)}) async-start(), calls=%async_computation.1 | async-start | bytes 4128768 | tf_op jit(solution)/shard_map/all_gather | solution.py:935
  11.5 181.6 %all-gather.6.cloned.1.call-start = ((), (), s32[]{:S(2)}) async-start(), calls=%async_computation.2 | async-start | bytes 28311552 | tf_op jit(solution)/shard_map/all_gather | solution.py:935
  38.0 200.1 %all-gather.8.cloned.1.call-start = ((), (), s32[]{:S(2)}) async-start(), calls=%async_computation.3 | async-start | bytes 9437184 | tf_op jit(solution)/shard_map/all_gather | solution.py:935
  38.7 372.1 %reduce-scatter.2.cloned.1.call-start = ((), (), s32[]{:S(2)}) async-start(), calls=%async_computation.4 | async-start | bytes 5242880 | tf_op jit(solution)/shard_map/reduce_scatter | solution.py:973
  39.2 29.4 %collective-permute-start = (bf16[256,2048]{1,0:T(8,128)(2,1)S(1)}, bf16[256,2048]{1,0:T(8,128)(2,1)S(1)}, u32[]{:S(2)}, u32[]{:S(2)}) collective-permute-start(bf16[256,2048]{1,0:T(8,128)(2,1)S(1)} %bitcast.38), channel_id=1, source_target_pairs={{0,1},{1,2},{2,3},{3,0},{4,5},{5,6},{6,7},{7,4},{8,9},{9,10},{10,1... | collective-permute-start | bytes 3145736 | tf_op jit(solution)/shard_map/ppermute | solution.py:978
  261.5 27.1 %collective-permute-start.12 = (bf16[256,2048]{1,0:T(8,128)(2,1)}, bf16[256,2048]{1,0:T(8,128)(2,1)S(1)}, u32[]{:S(2)}, u32[]{:S(2)}) collective-permute-start(bf16[256,2048]{1,0:T(8,128)(2,1)} %get-tuple-element.299), channel_id=1, source_target_pairs={{0,1},{1,2},{2,3},{3,0},{4,5},{5,6},{6,7},{7,4},{8,9},{9,10},{10,1... | collective-permute-start | bytes 3145736 | tf_op jit(solution)/shard_map/ppermute | solution.py:978
  288.5 48.2 %collective-permute-start.15 = (bf16[1024,2048]{1,0:T(8,128)(2,1)}, bf16[1024,2048]{1,0:T(8,128)(2,1)}, u32[]{:S(2)}, u32[]{:S(2)}) collective-permute-start(bf16[1024,2048]{1,0:T(8,128)(2,1)} %weight_product.8), channel_id=1, source_target_pairs={{0,4},{4,0},{8,12},{12,8},{16,20},{20,16},{24,28},{28,24},{1,5},{5... | collective-permute-start | bytes 12582920 | tf_op jit(solution)/shard_map/ppermute | solution.py:932
  289.9 27.7 %collective-permute-start.13 = (bf16[256,2048]{1,0:T(8,128)(2,1)}, bf16[256,2048]{1,0:T(8,128)(2,1)S(1)}, u32[]{:S(2)}, u32[]{:S(2)}) collective-permute-start(bf16[256,2048]{1,0:T(8,128)(2,1)} %add_convert_fusion.6), channel_id=1, source_target_pairs={{0,1},{1,2},{2,3},{3,0},{4,5},{5,6},{6,7},{7,4},{8,9},{9,10},{10,1... | collective-permute-start | bytes 3145736 | tf_op jit(solution)/shard_map/ppermute | solution.py:978
  319.3 27.1 %collective-permute-start.14 = (bf16[256,2048]{1,0:T(8,128)(2,1)S(1)}, bf16[256,2048]{1,0:T(8,128)(2,1)S(1)}, u32[]{:S(2)}, u32[]{:S(2)}) collective-permute-start(bf16[256,2048]{1,0:T(8,128)(2,1)S(1)} %add_convert_fusion.5), channel_id=1, source_target_pairs={{0,1},{1,2},{2,3},{3,0},{4,5},{5,6},{6,7},{7,4},{8,9},{9,10},{10,1... | collective-permute-start | bytes 3145736 | tf_op jit(solution)/shard_map/ppermute | solution.py:978
  379.4 31.4 %collective-permute-start.16 = (bf16[256,2048]{1,0:T(8,128)(2,1)}, bf16[256,2048]{1,0:T(8,128)(2,1)S(1)}, u32[]{:S(2)}, u32[]{:S(2)}) collective-permute-start(bf16[256,2048]{1,0:T(8,128)(2,1)} %get-tuple-element.332), channel_id=1, source_target_pairs={{0,1},{1,2},{2,3},{3,0},{4,5},{5,6},{6,7},{7,4},{8,9},{9,10},{10,1... | collective-permute-start | bytes 3145736 | tf_op jit(solution)/shard_map/ppermute | solution.py:978
  412.2 29.4 %collective-permute-start.22 = (bf16[256,2048]{1,0:T(8,128)(2,1)}, bf16[256,2048]{1,0:T(8,128)(2,1)}, u32[]{:S(2)}, u32[]{:S(2)}) collective-permute-start(bf16[256,2048]{1,0:T(8,128)(2,1)} %add_convert_fusion.4), channel_id=1, source_target_pairs={{0,1},{1,2},{2,3},{3,0},{4,5},{5,6},{6,7},{7,4},{8,9},{9,10},{10,1... | collective-permute-start | bytes 3145736 | tf_op jit(solution)/shard_map/ppermute | solution.py:978
  412.8 28.8 %collective-permute-start.23 = (bf16[512,1024]{1,0:T(8,128)(2,1)}, bf16[512,1024]{1,0:T(8,128)(2,1)S(1)}, u32[]{:S(2)}, u32[]{:S(2)}) collective-permute-start(bf16[512,1024]{1,0:T(8,128)(2,1)} %get-tuple-element.383), channel_id=1, source_target_pairs={{0,16},{4,20},{8,24},{12,28},{16,0},{20,4},{24,8},{28,12},{1,17},{... | collective-permute-start | bytes 3145736 | tf_op jit(solution)/shard_map/ppermute | solution.py:932
  414.9 26.7 %collective-permute-start.24 = (bf16[512,1024]{1,0:T(8,128)(2,1)}, bf16[512,1024]{1,0:T(8,128)(2,1)S(1)}, u32[]{:S(2)}, u32[]{:S(2)}) collective-permute-start(bf16[512,1024]{1,0:T(8,128)(2,1)} %get-tuple-element.385), channel_id=1, source_target_pairs={{0,8},{4,12},{8,0},{12,4},{16,24},{20,28},{24,16},{28,20},{1,9},{5... | collective-permute-start | bytes 3145736 | tf_op jit(solution)/shard_map/ppermute | solution.py:932
  416.6 47.0 %collective-permute-start.26 = (bf16[512,1024]{1,0:T(8,128)(2,1)}, bf16[512,1024]{1,0:T(8,128)(2,1)}, u32[]{:S(2)}, u32[]{:S(2)}) collective-permute-start(bf16[512,1024]{1,0:T(8,128)(2,1)} %get-tuple-element.401), channel_id=1, source_target_pairs={{0,16},{4,20},{8,24},{12,28},{16,0},{20,4},{24,8},{28,12},{1,17},{... | collective-permute-start | bytes 3145736 | tf_op jit(solution)/shard_map/ppermute | solution.py:932
  433.5 30.0 %collective-permute-start.27 = (bf16[512,1024]{1,0:T(8,128)(2,1)}, bf16[512,1024]{1,0:T(8,128)(2,1)}, u32[]{:S(2)}, u32[]{:S(2)}) collective-permute-start(bf16[512,1024]{1,0:T(8,128)(2,1)} %get-tuple-element.403), channel_id=1, source_target_pairs={{0,8},{4,12},{8,0},{12,4},{16,24},{20,28},{24,16},{28,20},{1,9},{5... | collective-permute-start | bytes 3145736 | tf_op jit(solution)/shard_map/ppermute | solution.py:932
  441.6 26.0 %collective-permute-start.25 = (bf16[256,2048]{1,0:T(8,128)(2,1)}, bf16[256,2048]{1,0:T(8,128)(2,1)}, u32[]{:S(2)}, u32[]{:S(2)}) collective-permute-start(bf16[256,2048]{1,0:T(8,128)(2,1)} %get-tuple-element.387), channel_id=1, source_target_pairs={{0,1},{1,2},{2,3},{3,0},{4,5},{5,6},{6,7},{7,4},{8,9},{9,10},{10,1... | collective-permute-start | bytes 3145736 | tf_op jit(solution)/shard_map/ppermute | solution.py:978
  470.9 30.9 %collective-permute-start.28 = (bf16[256,2048]{1,0:T(8,128)(2,1)}, bf16[256,2048]{1,0:T(8,128)(2,1)}, u32[]{:S(2)}, u32[]{:S(2)}) collective-permute-start(bf16[256,2048]{1,0:T(8,128)(2,1)} %add_convert_fusion.3), channel_id=1, source_target_pairs={{0,1},{1,2},{2,3},{3,0},{4,5},{5,6},{6,7},{7,4},{8,9},{9,10},{10,1... | collective-permute-start | bytes 3145736 | tf_op jit(solution)/shard_map/ppermute | solution.py:978
  474.5 27.3 %collective-permute-start.30 = (bf16[512,1024]{1,0:T(8,128)(2,1)}, bf16[512,1024]{1,0:T(8,128)(2,1)S(1)}, u32[]{:S(2)}, u32[]{:S(2)}) collective-permute-start(bf16[512,1024]{1,0:T(8,128)(2,1)} %get-tuple-element.430), channel_id=1, source_target_pairs={{0,8},{4,12},{8,0},{12,4},{16,24},{20,28},{24,16},{28,20},{1,9},{5... | collective-permute-start | bytes 3145736 | tf_op jit(solution)/shard_map/ppermute | solution.py:932
  501.9 33.8 %collective-permute-start.34 = (bf16[512,1408]{1,0:T(8,128)(2,1)}, bf16[512,1408]{1,0:T(8,128)(2,1)}, u32[]{:S(2)}, u32[]{:S(2)}) collective-permute-start(bf16[512,1408]{1,0:T(8,128)(2,1)} %get-tuple-element.437), channel_id=1, source_target_pairs={{0,16},{4,20},{8,24},{12,28},{16,0},{20,4},{24,8},{28,12},{1,17},{... | collective-permute-start | bytes 4325384 | tf_op jit(solution)/shard_map/ppermute | solution.py:932
  503.6 32.9 %collective-permute-start.35 = (bf16[512,1408]{1,0:T(8,128)(2,1)}, bf16[512,1408]{1,0:T(8,128)(2,1)}, u32[]{:S(2)}, u32[]{:S(2)}) collective-permute-start(bf16[512,1408]{1,0:T(8,128)(2,1)} %get-tuple-element.439), channel_id=1, source_target_pairs={{0,8},{4,12},{8,0},{12,4},{16,24},{20,28},{24,16},{28,20},{1,9},{5... | collective-permute-start | bytes 4325384 | tf_op jit(solution)/shard_map/ppermute | solution.py:932
  505.6 28.1 %collective-permute-start.33 = (bf16[256,2048]{1,0:T(8,128)(2,1)S(1)}, bf16[256,2048]{1,0:T(8,128)(2,1)}, u32[]{:S(2)}, u32[]{:S(2)}) collective-permute-start(bf16[256,2048]{1,0:T(8,128)(2,1)S(1)} %add_convert_fusion.1), channel_id=1, source_target_pairs={{0,1},{1,2},{2,3},{3,0},{4,5},{5,6},{6,7},{7,4},{8,9},{9,10},{10,1... | collective-permute-start | bytes 3145736 | tf_op jit(solution)/shard_map/ppermute | solution.py:978
  508.3 62.0 %collective-permute-start.32 = (bf16[256,2048]{1,0:T(8,128)(2,1)}, bf16[256,2048]{1,0:T(8,128)(2,1)}, u32[]{:S(2)}, u32[]{:S(2)}) collective-permute-start(bf16[256,2048]{1,0:T(8,128)(2,1)} %add_convert_fusion.2), channel_id=1, source_target_pairs={{0,1},{1,2},{2,3},{3,0},{4,5},{5,6},{6,7},{7,4},{8,9},{9,10},{10,1... | collective-permute-start | bytes 3145736 | tf_op jit(solution)/shard_map/ppermute | solution.py:978
  542.7 37.2 %collective-permute-start.41 = (bf16[256,512]{1,0:T(8,128)(2,1)S(1)}, bf16[256,512]{1,0:T(8,128)(2,1)S(1)}, u32[]{:S(2)}, u32[]{:S(2)}) collective-permute-start(bf16[256,512]{1,0:T(8,128)(2,1)S(1)} %split.17), channel_id=1, source_target_pairs={{0,1},{1,2},{2,3},{3,0},{4,5},{5,6},{6,7},{7,4},{8,9},{9,10},{10,1... | collective-permute-start | bytes 786440 | tf_op jit(solution)/shard_map/ppermute | solution.py:993
  542.8 37.1 %collective-permute-start.42 = (bf16[256,512]{1,0:T(8,128)(2,1)}, bf16[256,512]{1,0:T(8,128)(2,1)S(1)}, u32[]{:S(2)}, u32[]{:S(2)}) collective-permute-start(bf16[256,512]{1,0:T(8,128)(2,1)} %get-tuple-element.470), channel_id=1, source_target_pairs={{0,2},{1,3},{2,0},{3,1},{4,6},{5,7},{6,4},{7,5},{8,10},{9,11},{10,... | collective-permute-start | bytes 786440 | tf_op jit(solution)/shard_map/ppermute | solution.py:993
  (69 other events, 965.8 us)
Sparse Core Ops, SparseCore 0:
  11.6 37.2 all-gather.3
  50.7 125.3 all-gather.5
  178.0 54.3 all-gather.7
  346.6 54.7 reduce-scatter.1

commit v8 on v7

--- a/solution.py
+++ b/solution.py
@@ -1242,17 +1242,16 @@
             branch = branch + transposed_product(
                 [tie(product, last_part)], down_full, 0, ring // 2, 1, 2
             )
-            moved, last_part, branch, output_part, gate_part = together(
-                moved, last_part, branch, output_part, gate_part
+            next_branch = add(branch_moved, branch[sent])
+            moved, last_part, branch, output_part, gate_part, next_branch = together(
+                moved, last_part, branch, output_part, gate_part, next_branch
             )
         if j == 2:
             both_parts = tie([output_part, gate_part], total)
             both_parts = mover.advance_all(both_parts)
-            next_branch = add(branch_moved, branch[sent])
-            last_part = last_weights(next_branch, mover.swap(last_part, 1))
-            moved, last_part, both_parts, next_branch = together(
-                moved, last_part, both_parts, next_branch
-            )
+            last_part = last_weights(total, mover.swap(last_part, 1))
+            moved, last_part, both_parts = together(moved, last_part, both_parts)
+            down_out = tie(down_out, both_parts)
         if j == 3:
             last_part = mover.begin(last_part)
             branch_moved = mover.hop(tie(next_branch, total))
@@ -1262,11 +1261,11 @@
             moved, last_part, output_out = together(moved, last_part, output_out)
     folded, output_out = together(mover.fold([last_part]), output_out)
     last_part = mover.advance([last_part], folded)
-    output_out = mover.collect(output_out[:-1] + [tie(output_out[-1], last_part)]).T
+    output_out = mover.collect(output_out[:-1] + [tie(output_out[-1], last_part[1][1])]).T
     scaled_one, inverse_one = norm_rows(local_tokens.astype(f32))
     local_one = moved.astype(f32) + grads[0].astype(f32)
     input_gradient = grad_hidden + back_norm(local_one, scaled_one, inverse_one, gains[:1])
-    branch_moved = tie(branch_moved, last_part)
+    branch_moved, last_part = together(branch_moved, last_part)
     for j in range(sent, ring - 1):
         branch_moved = mover.hop(add(branch_moved, branch[j]))
     block_output = (
@@ -1284,8 +1283,9 @@
     )
     gain_out = sums
     for shift in range(1, ring):
-        gain_out = gain_out + lax.ppermute(
-            sums, "tensor", [(i, (i + shift) % ring) for i in range(ring)]
+        gain_out = gain_out + tie(
+            lax.ppermute(sums, "tensor", [(i, (i + shift) % ring) for i in range(ring)]),
+            output_out,
         )
 
     def ungrouped(first, width):

time: 600 us -> 597 us (level)
  transfers between devices with their start and end apart: 48 -> 48, of which waited for: 17 -> 21; matrix products, arithmetic and copies ran while one was open for 9% -> 9% of each run, Pallas kernels for 49% -> 50%
where the time goes in v8:
time: 597 us; the launch traced here: 588 us
  Pallas kernels  294 us (49%)
  waiting for transfers between devices  148 us (25%)
  starting transfers between devices  69.6 us (12%)
  other arithmetic  40.8 us (7%)
  local copies, waits for them, and re-layouts  20.7 us (3%)
  between operations  14.9 us (2%)
    ppermute x18, waiting for transfers between devices, hop(): lax.ppermute(value, 'tensor', [(i, (i + shift) % self.ring) for i in rang...  121 us
    pallas_call x8, Pallas kernels, weight_product(): pl.pallas_call(functools.partial(weight_kernel, [(len(xs), len(ys)) for x...  79.8 us
    pallas_call x2, Pallas kernels, down_chunk(): pl.pallas_call(functools.partial(down_kernel, len(es), tiles), grid=(tile...  44.7 us
    ppermute x18, starting transfers between devices, hop(): lax.ppermute(value, 'tensor', [(i, (i + shift) % self.ring) for i in rang...  35.7 us
    pallas_call x2, Pallas kernels, attention_backward(): pl.pallas_call(functools.partial(backward_kernel, count), grid_spec=spec,...  34.5 us
    pallas_call x2, Pallas kernels, up_chunk(): pl.pallas_call(up_kernel, grid=(tiles,), in_specs=specs, out_specs=[pl.Bl...  27.7 us
    pallas_call x3, Pallas kernels, transposed_product(): pl.pallas_call(functools.partial(transposed_kernel, len(xs), parts), grid...  25.1 us
    pallas_call x4, Pallas kernels, project(): pl.pallas_call(project_kernel, grid=(groups,), in_specs=specs, out_specs=...  18.9 us
  transfers between devices with their start and end apart: 48, of which 21 were waited for; matrix products, arithmetic and copies ran while one was open for 9% of the time, Pallas kernels for 50%

profile of v8, /device:TPU:0, one launch (start us, length us, event | category | flops | bytes accessed | tf_op | source)
XLA Modules:
  0.0 587.7 jit_solution(9635983416021652535)
XLA Ops:
  55.6 12.9 %collective-permute-done.x_ref.refs_5_ = bf16[256,2048]{1,0:T(8,128)(2,1)S(1)} collective-permute-done((bf16[256,2048]{1,0:T(8,128)(2,1)S(1)}, bf16[256,2048]{1,0:T(8,128)(2,1)S(1)}, u32[]{:S(2)}, u32[]{:S(2)}) %collective-permute-start) | collective-permute-done | bytes 1048608 | tf_op jit(solution)/shard_map/ppermute | solution.py:978
  76.0 17.9 %collective-permute-done.4.x_ref.refs_6_ = bf16[256,2048]{1,0:T(8,128)(2,1)S(1)} collective-permute-done((bf16[256,2048]{1,0:T(8,128)(2,1)S(1)}, bf16[256,2048]{1,0:T(8,128)(2,1)S(1)}, u32[]{:S(2)}, u32[]{:S(2)}) %collective-permute-start.4) | collective-permute-done | bytes 1048608 | tf_op jit(solution)/shard_map/ppermute | solution.py:978
  100.4 17.9 %collective-permute-done.5.x_ref.refs_7_ = bf16[256,2048]{1,0:T(8,128)(2,1)} collective-permute-done((bf16[256,2048]{1,0:T(8,128)(2,1)S(1)}, bf16[256,2048]{1,0:T(8,128)(2,1)}, u32[]{:S(2)}, u32[]{:S(2)}) %collective-permute-start.5) | collective-permute-done | bytes 1048608 | tf_op jit(solution)/shard_map/ppermute | solution.py:978
  125.0 17.7 %attend.1 = (bf16[1024,512]{1,0:T(8,128)(2,1)}, f32[16,4096]{1,0:T(8,128)}) custom-call(s32[1]{0:T(128)} %bitcast.10.place_ref, bf16[1024,768]{1,0:T(8,128)(2,1)} %get-tuple-element.274.own_ref.all_ref.refs_0_.refs_1_, bf16[1024,768]{1,0:T(8,128)(2,1)} %get-tuple-element.274.own_ref.all_ref.refs_0_.refs_1_, s32[1,1024]{1,0:T(1,128)} %bitcast.52, ...), custom_call_target="tpu_custom_call" | custom-call | flops 1 | bytes 1 | tf_op jit(solution)/shard_map/attend/pallas_call | solution.py:256
  146.6 19.6 %collective-permute-done.7.refs_1_ = bf16[1024,512]{1,0:T(8,128)(2,1)S(1)} collective-permute-done((bf16[1024,512]{1,0:T(8,128)(2,1)}, bf16[1024,512]{1,0:T(8,128)(2,1)S(1)}, u32[]{:S(2)}, u32[]{:S(2)}) %collective-permute-start.7) | collective-permute-done | bytes 1048608 | tf_op jit(solution)/shard_map/ppermute | solution.py:978
  170.1 18.8 %collective-permute-done.8.refs_2_ = bf16[1024,512]{1,0:T(8,128)(2,1)} collective-permute-done((bf16[1024,512]{1,0:T(8,128)(2,1)S(1)}, bf16[1024,512]{1,0:T(8,128)(2,1)}, u32[]{:S(2)}, u32[]{:S(2)}) %collective-permute-start.8) | collective-permute-done | bytes 1048608 | tf_op jit(solution)/shard_map/ppermute | solution.py:978
  193.2 14.2 %heads_product.1 = (f32[1024,2048]{1,0:T(8,128)}, bf16[256,1536]{1,0:T(8,128)(2,1)}) custom-call(bf16[1024,512]{1,0:T(8,128)(2,1)} %get-tuple-element.278.refs_0_.refs_2_, bf16[1024,512]{1,0:T(8,128)(2,1)} %copy-done.38, bf16[1024,512]{1,0:T(8,128)(2,1)} %collective-permute-done.8.refs_2_, ...), custom_call_target="tpu_custom_call" | custom-call | flops 1 | bytes 1 | tf_op jit(solution)/shard_map/heads_product/pallas_call | solution.py:507
  215.8 9.4 %after_attention.1 = (f32[256,2048]{1,0:T(8,128)}, bf16[1024,2048]{1,0:T(8,128)(2,1)}, bf16[256,512]{1,0:T(8,128)(2,1)}) custom-call(f32[1024,2048]{1,0:T(8,128)} %get-tuple-element.288.partial_ref, bf16[1024,512]{1,0:T(8,128)(2,1)} %copy-done.39, bf16[2048,6144]{1,0:T(8,128)(2,1)} %all-gather.6.cloned.1.call-done.refs_3_.weight_ref.gate_ref.up_ref.refs_5_.refs_6_, ...), custom_call_target="tpu_custom_call" | custom-call | flops 1 | bytes 1 | tf_op jit(solution)/shard_map/after_attention/pallas_call | solution.py:549
  225.2 13.9 %up_chunk.2 = (bf16[1024,2048]{1,0:T(8,128)(2,1)}, bf16[1024,2048]{1,0:T(8,128)(2,1)}, bf16[1024,2048]{1,0:T(8,128)(2,1)}) custom-call(bf16[1024,2048]{1,0:T(8,128)(2,1)} %get-tuple-element.417.x_ref.refs_0_, bf16[2048,6144]{1,0:T(8,128)(2,1)} %all-gather.6.cloned.1.call-done.refs_3_.weight_ref.gate_ref.up_ref.refs_5_.refs_6_, ...), custom_call_target="tpu_custom_call" | custom-call | flops 1 | bytes 1 | tf_op jit(solution)/shard_map/up_chunk/pallas_call | solution.py:601
  240.1 22.3 %down_chunk.2 = (bf16[1024,2048]{1,0:T(8,128)(2,1)}, bf16[1024,2048]{1,0:T(8,128)(2,1)}, bf16[256,2048]{1,0:T(8,128)(2,1)}, bf16[256,2048]{1,0:T(8,128)(2,1)}) custom-call(bf16[256,2048]{1,0:T(8,128)(2,1)} %copy-done.5, bf16[256,2048]{1,0:T(8,128)(2,1)} %copy-done.6, bf16[2048,2048]{1,0:T(8,128)(2,1)} %all-gather.8.cloned.1.call-done.refs_2_.refs_1_, ...), custom_call_target="tpu_custom_call" | custom-call | flops 1 | bytes 1 | tf_op jit(solution)/shard_map/down_chunk/pallas_call | solution.py:686
  265.8 13.8 %up_chunk.3 = (bf16[1024,2048]{1,0:T(8,128)(2,1)}, bf16[1024,2048]{1,0:T(8,128)(2,1)}, bf16[1024,2048]{1,0:T(8,128)(2,1)}) custom-call(bf16[1024,2048]{1,0:T(8,128)(2,1)} %get-tuple-element.417.x_ref.refs_0_, ...), custom_call_target="tpu_custom_call", output_to_operand_aliasing={{0}: (3, {}), {1}: (4, {}), {2}: (5, {})} | custom-call | flops 1 | bytes 1 | tf_op jit(solution)/shard_map/up_chunk/pallas_call | solution.py:601
  279.6 9.0 %weight_product.8 = bf16[1024,2048]{1,0:T(8,128)(2,1)} custom-call(s32[1]{0:T(128)} %bitcast.13.place_ref, bf16[256,2048]{1,0:T(8,128)(2,1)} %copy-done.5, bf16[256,2048]{1,0:T(8,128)(2,1)} %copy-done.6, bf16[256,2048]{1,0:T(8,128)(2,1)} %copy-done.7, bf16[256,2048]{1,0:T(8,128)(2,1)} %bitcast.39, bf16[1024,2048]{1,0:T(8,128)(2,1)} %get-tuple-element.402.refs_4_.refs_0_), custom_call_target="tpu_custom_call" | custom-call | flops 1 | bytes 1 | tf_op jit(solution)/shard_map/weight_product/pallas_call | solution.py:794
  290.2 22.4 %down_chunk.3 = (bf16[1024,2048]{1,0:T(8,128)(2,1)}, bf16[1024,2048]{1,0:T(8,128)(2,1)}, bf16[256,2048]{1,0:T(8,128)(2,1)}, bf16[256,2048]{1,0:T(8,128)(2,1)}) custom-call(bf16[256,2048]{1,0:T(8,128)(2,1)} %copy-done.7, bf16[256,2048]{1,0:T(8,128)(2,1)} %bitcast.40, ...), custom_call_target="tpu_custom_call", output_to_operand_aliasing={{0}: (7, {}), {1}: (8, {})} | custom-call | flops 1 | bytes 1 | tf_op jit(solution)/shard_map/down_chunk/pallas_call | solution.py:686
  318.3 8.7 %weight_product.9 = bf16[1024,2048]{1,0:T(8,128)(2,1)} custom-call(s32[1]{0:T(128)} %bitcast.13.place_ref, bf16[1024,2048]{1,0:T(8,128)(2,1)} %get-tuple-element.417.x_ref.refs_0_, bf16[1024,2048]{1,0:T(8,128)(2,1)} %get-tuple-element.332.refs_1_), custom_call_target="tpu_custom_call" | custom-call | flops 1 | bytes 1 | tf_op jit(solution)/shard_map/weight_product/pallas_call | solution.py:794
  327.1 8.6 %transposed.3 = (bf16[256,2048]{1,0:T(8,128)(2,1)}, bf16[256,2048]{1,0:T(8,128)(2,1)}) custom-call(bf16[1024,2048]{1,0:T(8,128)(2,1)} %get-tuple-element.402.refs_4_.refs_0_, bf16[2048,2048]{1,0:T(8,128)(2,1)} %all-gather.8.cloned.1.call-done.refs_2_.refs_1_), custom_call_target="tpu_custom_call" | custom-call | flops 1 | bytes 1 | tf_op jit(solution)/shard_map/transposed/pallas_call | solution.py:460
  335.7 9.7 %weight_product.10 = bf16[1024,2048]{1,0:T(8,128)(2,1)} custom-call(s32[1]{0:T(128)} %bitcast.13.place_ref, bf16[256,2048]{1,0:T(8,128)(2,1)} %copy-done.5, bf16[256,2048]{1,0:T(8,128)(2,1)} %copy-done.6, bf16[256,2048]{1,0:T(8,128)(2,1)} %copy-done.7, bf16[256,2048]{1,0:T(8,128)(2,1)} %bitcast.41, bf16[1024,2048]{1,0:T(8,128)(2,1)} %get-tuple-element.402.refs_4_.refs_0_, ...), custom_call_target="tpu_custom_call" | custom-call | flops 1 | bytes 1 | tf_op jit(solution)/shard_map/weight_product/pallas_call | solution.py:794
  346.4 10.8 %residual_gradient.1 = (f32[256,2048]{1,0:T(8,128)}, bf16[256,2048]{1,0:T(8,128)(2,1)}, bf16[256,512]{1,0:T(8,128)(2,1)}, bf16[256,512]{1,0:T(8,128)(2,1)}, bf16...) custom-call(bf16[256,2048]{1,0:T(8,128)(2,1)} %bitcast.42, f32[256,2048]{1,0:T(8,128)} %get-tuple-element.292.hidden_ref, ...), custom_call_target="tpu_custom_call" | custom-call | flops 1 | bytes 1 | tf_op jit(solution)/shard_map/residual_gradient/pallas_call | solution.py:881
  366.8 10.8 %weight_product.12 = (bf16[512,1024]{1,0:T(8,128)(2,1)}, bf16[512,1024]{1,0:T(8,128)(2,1)}, bf16[512,1024]{1,0:T(8,128)(2,1)}, bf16[512,1024]{1,0:T(8,128)(2,1)}) custom-call(s32[1]{0:T(128)} %bitcast.13.place_ref, bf16[1024,2048]{1,0:T(8,128)(2,1)} %get-tuple-element.417.x_ref.refs_0_, bf16[1024,2048]{1,0:T(8,128)(2,1)} %get-tuple-element.332.refs_1_, ...), custom_call_target="tpu_custom_call" | custom-call | flops 1 | bytes 1 | tf_op jit(solution)/shard_map/weight_product/pallas_call | solution.py:794
  384.7 17.5 %attend_back.2.refs_0_.refs_3_ = bf16[1024,384]{1,0:T(8,128)(2,1)} custom-call(s32[1]{0:T(128)} %bitcast.10.place_ref, bf16[1024,768]{1,0:T(8,128)(2,1)} %get-tuple-element.274.own_ref.all_ref.refs_0_.refs_1_, bf16[1024,768]{1,0:T(8,128)(2,1)} %get-tuple-element.274.own_ref.all_ref.refs_0_.refs_1_, bf16[1024,512]{1,0:T(8,128)(2,1)} %get-tuple-element.278.refs_0_.refs_2_, ...), custom_call_target="tpu_custom_call" | custom-call | flops 1 | bytes 1 | tf_op jit(solution)/shard_map/attend_back/pallas_call | solution.py:364
  415.4 17.0 %attend_back.3.refs_1_.refs_4_ = bf16[1024,384]{1,0:T(8,128)(2,1)} custom-call(s32[1]{0:T(128)} %bitcast.10.place_ref, bf16[1024,768]{1,0:T(8,128)(2,1)} %get-tuple-element.274.own_ref.all_ref.refs_0_.refs_1_, bf16[1024,768]{1,0:T(8,128)(2,1)} %get-tuple-element.274.own_ref.all_ref.refs_0_.refs_1_, bf16[1024,512]{1,0:T(8,128)(2,1)} %get-tuple-element.278.refs_0_.refs_2_, ...), custom_call_target="tpu_custom_call" | custom-call | flops 1 | bytes 1 | tf_op jit(solution)/shard_map/attend_back/pallas_call | solution.py:364
  441.0 12.1 %weight_product.14 = bf16[1024,2816]{1,0:T(8,128)(2,1)} custom-call(s32[1]{0:T(128)} %bitcast.13.place_ref, bf16[1024,2048]{1,0:T(8,128)(2,1)} %get-tuple-element.417.x_ref.refs_0_, bf16[1024,2048]{1,0:T(8,128)(2,1)} %get-tuple-element.398.refs_1_, bf16[1024,2048]{1,0:T(8,128)(2,1)} %get-tuple-element.399.refs_2_, ...), custom_call_target="tpu_custom_call" | custom-call | flops 1 | bytes 1 | tf_op jit(solution)/shard_map/weight_product/pallas_call | solution.py:794
  453.1 8.7 %transposed.5 = (bf16[256,2048]{1,0:T(8,128)(2,1)}, bf16[256,2048]{1,0:T(8,128)(2,1)}) custom-call(bf16[1024,2048]{1,0:T(8,128)(2,1)} %get-tuple-element.402.refs_4_.refs_0_, bf16[2048,2048]{1,0:T(8,128)(2,1)} %all-gather.8.cloned.1.call-done.refs_2_.refs_1_), custom_call_target="tpu_custom_call" | custom-call | flops 1 | bytes 1 | tf_op jit(solution)/shard_map/transposed/pallas_call | solution.py:460
  477.0 16.7 %weight_product.15 = (bf16[512,1408]{1,0:T(8,128)(2,1)}, bf16[512,1408]{1,0:T(8,128)(2,1)}, bf16[512,1408]{1,0:T(8,128)(2,1)}, bf16[512,1408]{1,0:T(8,128)(2,1)}) custom-call(s32[1]{0:T(128)} %bitcast.13.place_ref, bf16[1024,2048]{1,0:T(8,128)(2,1)} %get-tuple-element.417.x_ref.refs_0_, bf16[1024,2048]{1,0:T(8,128)(2,1)} %get-tuple-element.398.refs_1_, ...), custom_call_target="tpu_custom_call" | custom-call | flops 1 | bytes 1 | tf_op jit(solution)/shard_map/weight_product/pallas_call | solution.py:794
  516.6 14.5 %collective-permute-done.33 = bf16[256,2048]{1,0:T(8,128)(2,1)} collective-permute-done((bf16[256,2048]{1,0:T(8,128)(2,1)}, bf16[256,2048]{1,0:T(8,128)(2,1)}, u32[]{:S(2)}, u32[]{:S(2)}) %collective-permute-start.33) | collective-permute-done | bytes 1048608 | tf_op jit(solution)/shard_map/ppermute | solution.py:978
  (273 shorter events, 227.6 us)
Async XLA Ops:
  7.2 41.6 %all-gather.4.cloned.1.call-start = ((), (), s32[]{:S(2)}) async-start(), calls=%async_computation.1 | async-start | bytes 4128768 | tf_op jit(solution)/shard_map/all_gather | solution.py:935
  11.5 181.7 %all-gather.6.cloned.1.call-start = ((), (), s32[]{:S(2)}) async-start(), calls=%async_computation.2 | async-start | bytes 28311552 | tf_op jit(solution)/shard_map/all_gather | solution.py:935
  38.0 201.2 %all-gather.8.cloned.1.call-start = ((), (), s32[]{:S(2)}) async-start(), calls=%async_computation.3 | async-start | bytes 9437184 | tf_op jit(solution)/shard_map/all_gather | solution.py:935
  38.7 371.0 %reduce-scatter.2.cloned.1.call-start = ((), (), s32[]{:S(2)}) async-start(), calls=%async_computation.4 | async-start | bytes 5242880 | tf_op jit(solution)/shard_map/reduce_scatter | solution.py:973
  39.2 29.4 %collective-permute-start = (bf16[256,2048]{1,0:T(8,128)(2,1)S(1)}, bf16[256,2048]{1,0:T(8,128)(2,1)S(1)}, u32[]{:S(2)}, u32[]{:S(2)}) collective-permute-start(bf16[256,2048]{1,0:T(8,128)(2,1)S(1)} %bitcast.38), channel_id=1, source_target_pairs={{0,1},{1,2},{2,3},{3,0},{4,5},{5,6},{6,7},{7,4},{8,9},{9,10},{10,1... | collective-permute-start | bytes 3145736 | tf_op jit(solution)/shard_map/ppermute | solution.py:978
  188.9 26.0 %collective-permute-start.9 = (bf16[1024,512]{1,0:T(8,128)(2,1)}, bf16[1024,512]{1,0:T(8,128)(2,1)S(1)}, u32[]{:S(2)}, u32[]{:S(2)}) collective-permute-start(bf16[1024,512]{1,0:T(8,128)(2,1)} %collective-permute-done.8.refs_2_), channel_id=1, source_target_pairs={{0,3},{1,0},{2,1},{3,2},{4,7},{5,4},{6,5},{7,6},{8,11},{9,8},{10,9... | collective-permute-start | bytes 3145736 | tf_op jit(solution)/shard_map/ppermute | solution.py:978
  262.4 26.2 %collective-permute-start.12 = (bf16[256,2048]{1,0:T(8,128)(2,1)}, bf16[256,2048]{1,0:T(8,128)(2,1)S(1)}, u32[]{:S(2)}, u32[]{:S(2)}) collective-permute-start(bf16[256,2048]{1,0:T(8,128)(2,1)} %get-tuple-element.308), channel_id=1, source_target_pairs={{0,1},{1,2},{2,3},{3,0},{4,5},{5,6},{6,7},{7,4},{8,9},{9,10},{10,1... | collective-permute-start | bytes 3145736 | tf_op jit(solution)/shard_map/ppermute | solution.py:978
  288.6 47.1 %collective-permute-start.15 = (bf16[1024,2048]{1,0:T(8,128)(2,1)}, bf16[1024,2048]{1,0:T(8,128)(2,1)}, u32[]{:S(2)}, u32[]{:S(2)}) collective-permute-start(bf16[1024,2048]{1,0:T(8,128)(2,1)} %weight_product.8), channel_id=1, source_target_pairs={{0,4},{4,0},{8,12},{12,8},{16,20},{20,16},{24,28},{28,24},{1,5},{5... | collective-permute-start | bytes 12582920 | tf_op jit(solution)/shard_map/ppermute | solution.py:932
  289.1 27.6 %collective-permute-start.13 = (bf16[256,2048]{1,0:T(8,128)(2,1)S(1)}, bf16[256,2048]{1,0:T(8,128)(2,1)S(1)}, u32[]{:S(2)}, u32[]{:S(2)}) collective-permute-start(bf16[256,2048]{1,0:T(8,128)(2,1)S(1)} %add_convert_fusion.6), channel_id=1, source_target_pairs={{0,1},{1,2},{2,3},{3,0},{4,5},{5,6},{6,7},{7,4},{8,9},{9,10},{10,1... | collective-permute-start | bytes 3145736 | tf_op jit(solution)/shard_map/ppermute | solution.py:978
  318.3 27.2 %collective-permute-start.14 = (bf16[256,2048]{1,0:T(8,128)(2,1)S(1)}, bf16[256,2048]{1,0:T(8,128)(2,1)S(1)}, u32[]{:S(2)}, u32[]{:S(2)}) collective-permute-start(bf16[256,2048]{1,0:T(8,128)(2,1)S(1)} %add_convert_fusion.5), channel_id=1, source_target_pairs={{0,1},{1,2},{2,3},{3,0},{4,5},{5,6},{6,7},{7,4},{8,9},{9,10},{10,1... | collective-permute-start | bytes 3145736 | tf_op jit(solution)/shard_map/ppermute | solution.py:978
  378.4 31.3 %collective-permute-start.16 = (bf16[256,2048]{1,0:T(8,128)(2,1)}, bf16[256,2048]{1,0:T(8,128)(2,1)S(1)}, u32[]{:S(2)}, u32[]{:S(2)}) collective-permute-start(bf16[256,2048]{1,0:T(8,128)(2,1)} %get-tuple-element.341), channel_id=1, source_target_pairs={{0,1},{1,2},{2,3},{3,0},{4,5},{5,6},{6,7},{7,4},{8,9},{9,10},{10,1... | collective-permute-start | bytes 3145736 | tf_op jit(solution)/shard_map/ppermute | solution.py:978
  411.1 29.5 %collective-permute-start.22 = (bf16[256,2048]{1,0:T(8,128)(2,1)}, bf16[256,2048]{1,0:T(8,128)(2,1)}, u32[]{:S(2)}, u32[]{:S(2)}) collective-permute-start(bf16[256,2048]{1,0:T(8,128)(2,1)} %add_convert_fusion.4), channel_id=1, source_target_pairs={{0,1},{1,2},{2,3},{3,0},{4,5},{5,6},{6,7},{7,4},{8,9},{9,10},{10,1... | collective-permute-start | bytes 3145736 | tf_op jit(solution)/shard_map/ppermute | solution.py:978
  411.8 28.8 %collective-permute-start.23 = (bf16[512,1024]{1,0:T(8,128)(2,1)}, bf16[512,1024]{1,0:T(8,128)(2,1)S(1)}, u32[]{:S(2)}, u32[]{:S(2)}) collective-permute-start(bf16[512,1024]{1,0:T(8,128)(2,1)} %get-tuple-element.392), channel_id=1, source_target_pairs={{0,16},{4,20},{8,24},{12,28},{16,0},{20,4},{24,8},{28,12},{1,17},{... | collective-permute-start | bytes 3145736 | tf_op jit(solution)/shard_map/ppermute | solution.py:932
  413.8 26.9 %collective-permute-start.24 = (bf16[512,1024]{1,0:T(8,128)(2,1)}, bf16[512,1024]{1,0:T(8,128)(2,1)}, u32[]{:S(2)}, u32[]{:S(2)}) collective-permute-start(bf16[512,1024]{1,0:T(8,128)(2,1)} %get-tuple-element.394), channel_id=1, source_target_pairs={{0,8},{4,12},{8,0},{12,4},{16,24},{20,28},{24,16},{28,20},{1,9},{5... | collective-permute-start | bytes 3145736 | tf_op jit(solution)/shard_map/ppermute | solution.py:932
  415.4 49.4 %collective-permute-start.26 = (bf16[512,1024]{1,0:T(8,128)(2,1)}, bf16[512,1024]{1,0:T(8,128)(2,1)S(1)}, u32[]{:S(2)}, u32[]{:S(2)}) collective-permute-start(bf16[512,1024]{1,0:T(8,128)(2,1)} %get-tuple-element.410), channel_id=1, source_target_pairs={{0,16},{4,20},{8,24},{12,28},{16,0},{20,4},{24,8},{28,12},{1,17},{... | collective-permute-start | bytes 3145736 | tf_op jit(solution)/shard_map/ppermute | solution.py:932
  432.5 32.3 %collective-permute-start.27 = (bf16[512,1024]{1,0:T(8,128)(2,1)}, bf16[512,1024]{1,0:T(8,128)(2,1)S(1)}, u32[]{:S(2)}, u32[]{:S(2)}) collective-permute-start(bf16[512,1024]{1,0:T(8,128)(2,1)} %get-tuple-element.412), channel_id=1, source_target_pairs={{0,8},{4,12},{8,0},{12,4},{16,24},{20,28},{24,16},{28,20},{1,9},{5... | collective-permute-start | bytes 3145736 | tf_op jit(solution)/shard_map/ppermute | solution.py:932
  440.6 25.9 %collective-permute-start.25 = (bf16[256,2048]{1,0:T(8,128)(2,1)}, bf16[256,2048]{1,0:T(8,128)(2,1)}, u32[]{:S(2)}, u32[]{:S(2)}) collective-permute-start(bf16[256,2048]{1,0:T(8,128)(2,1)} %get-tuple-element.396), channel_id=1, source_target_pairs={{0,1},{1,2},{2,3},{3,0},{4,5},{5,6},{6,7},{7,4},{8,9},{9,10},{10,1... | collective-permute-start | bytes 3145736 | tf_op jit(solution)/shard_map/ppermute | solution.py:978
  469.1 27.9 %collective-permute-start.28 = (bf16[256,2048]{1,0:T(8,128)(2,1)}, bf16[256,2048]{1,0:T(8,128)(2,1)}, u32[]{:S(2)}, u32[]{:S(2)}) collective-permute-start(bf16[256,2048]{1,0:T(8,128)(2,1)} %add_convert_fusion.2), channel_id=1, source_target_pairs={{0,1},{1,2},{2,3},{3,0},{4,5},{5,6},{6,7},{7,4},{8,9},{9,10},{10,1... | collective-permute-start | bytes 3145736 | tf_op jit(solution)/shard_map/ppermute | solution.py:978
  502.9 28.2 %collective-permute-start.33 = (bf16[256,2048]{1,0:T(8,128)(2,1)}, bf16[256,2048]{1,0:T(8,128)(2,1)}, u32[]{:S(2)}, u32[]{:S(2)}) collective-permute-start(bf16[256,2048]{1,0:T(8,128)(2,1)} %add_convert_fusion.1), channel_id=1, source_target_pairs={{0,1},{1,2},{2,3},{3,0},{4,5},{5,6},{6,7},{7,4},{8,9},{9,10},{10,1... | collective-permute-start | bytes 3145736 | tf_op jit(solution)/shard_map/ppermute | solution.py:978
  504.7 31.5 %collective-permute-start.34 = (bf16[512,1408]{1,0:T(8,128)(2,1)}, bf16[512,1408]{1,0:T(8,128)(2,1)}, u32[]{:S(2)}, u32[]{:S(2)}) collective-permute-start(bf16[512,1408]{1,0:T(8,128)(2,1)} %get-tuple-element.445), channel_id=1, source_target_pairs={{0,16},{4,20},{8,24},{12,28},{16,0},{20,4},{24,8},{28,12},{1,17},{... | collective-permute-start | bytes 4325384 | tf_op jit(solution)/shard_map/ppermute | solution.py:932
  506.5 31.2 %collective-permute-start.35 = (bf16[512,1408]{1,0:T(8,128)(2,1)}, bf16[512,1408]{1,0:T(8,128)(2,1)}, u32[]{:S(2)}, u32[]{:S(2)}) collective-permute-start(bf16[512,1408]{1,0:T(8,128)(2,1)} %get-tuple-element.447), channel_id=1, source_target_pairs={{0,8},{4,12},{8,0},{12,4},{16,24},{20,28},{24,16},{28,20},{1,9},{5... | collective-permute-start | bytes 4325384 | tf_op jit(solution)/shard_map/ppermute | solution.py:932
  512.7 41.0 %collective-permute-start.32 = (bf16[256,2048]{1,0:T(8,128)(2,1)}, bf16[256,2048]{1,0:T(8,128)(2,1)}, u32[]{:S(2)}, u32[]{:S(2)}) collective-permute-start(bf16[256,2048]{1,0:T(8,128)(2,1)} %add_convert_fusion.3), channel_id=1, source_target_pairs={{0,1},{1,2},{2,3},{3,0},{4,5},{5,6},{6,7},{7,4},{8,9},{9,10},{10,1... | collective-permute-start | bytes 3145736 | tf_op jit(solution)/shard_map/ppermute | solution.py:978
  544.0 30.8 %collective-permute-start.39 = (bf16[256,512]{1,0:T(8,128)(2,1)S(1)}, bf16[256,512]{1,0:T(8,128)(2,1)S(1)}, u32[]{:S(2)}, u32[]{:S(2)}) collective-permute-start(bf16[256,512]{1,0:T(8,128)(2,1)S(1)} %split.17), channel_id=1, source_target_pairs={{0,1},{1,2},{2,3},{3,0},{4,5},{5,6},{6,7},{7,4},{8,9},{9,10},{10,1... | collective-permute-start | bytes 786440 | tf_op jit(solution)/shard_map/ppermute | solution.py:993
  544.7 31.2 %collective-permute-start.40 = (bf16[256,512]{1,0:T(8,128)(2,1)S(1)}, bf16[256,512]{1,0:T(8,128)(2,1)S(1)}, u32[]{:S(2)}, u32[]{:S(2)}) collective-permute-start(bf16[256,512]{1,0:T(8,128)(2,1)S(1)} %get-tuple-element.484), channel_id=1, source_target_pairs={{0,2},{1,3},{2,0},{3,1},{4,6},{5,7},{6,4},{7,5},{8,10},{9,11},{10,... | collective-permute-start | bytes 786440 | tf_op jit(solution)/shard_map/ppermute | solution.py:993
  (73 other events, 1020.3 us)
Sparse Core Ops, SparseCore 0:
  11.6 37.2 all-gather.3
  50.7 125.3 all-gather.5
  178.0 54.3 all-gather.7
  345.7 54.5 reduce-scatter.1

commit v9 on v8

--- a/solution.py
+++ b/solution.py
@@ -1250,7 +1250,7 @@
             both_parts = tie([output_part, gate_part], total)
             both_parts = mover.advance_all(both_parts)
             last_part = last_weights(total, mover.swap(last_part, 1))
-            moved, last_part, both_parts = together(moved, last_part, both_parts)
+            moved, _, both_parts = together(moved, last_part, both_parts)
             down_out = tie(down_out, both_parts)
         if j == 3:
             last_part = mover.begin(last_part)

time: 597 us -> 595 us (level)
    ppermute x14, waiting for transfers between devices: 12.6 us -> 3.94 us  [swap(): lax.ppermute(value, 'dp', [(i, i ^ step) for i in range(self.dp_count)])]
  transfers between devices with their start and end apart: 48 -> 48, of which waited for: 21 -> 18; matrix products, arithmetic and copies ran while one was open for 9% -> 9% of each run, Pallas kernels for 50% -> 50%
where the time goes in v9:
time: 595 us; the launch traced here: 586 us
  Pallas kernels  294 us (49%)
  waiting for transfers between devices  144 us (24%)
  starting transfers between devices  71.8 us (12%)
  other arithmetic  40.8 us (7%)
  local copies, waits for them, and re-layouts  20.7 us (3%)
  between operations  14.9 us (3%)
    ppermute x18, waiting for transfers between devices, hop(): lax.ppermute(value, 'tensor', [(i, (i + shift) % self.ring) for i in rang...  125 us
    pallas_call x8, Pallas kernels, weight_product(): pl.pallas_call(functools.partial(weight_kernel, [(len(xs), len(ys)) for x...  79.7 us
    pallas_call x2, Pallas kernels, down_chunk(): pl.pallas_call(functools.partial(down_kernel, len(es), tiles), grid=(tile...  44.7 us
    ppermute x18, starting transfers between devices, hop(): lax.ppermute(value, 'tensor', [(i, (i + shift) % self.ring) for i in rang...  37.8 us
    pallas_call x2, Pallas kernels, attention_backward(): pl.pallas_call(functools.partial(backward_kernel, count), grid_spec=spec,...  34.5 us
    pallas_call x2, Pallas kernels, up_chunk(): pl.pallas_call(up_kernel, grid=(tiles,), in_specs=specs, out_specs=[pl.Bl...  27.7 us
    pallas_call x3, Pallas kernels, transposed_product(): pl.pallas_call(functools.partial(transposed_kernel, len(xs), parts), grid...  25.1 us
    pallas_call x4, Pallas kernels, project(): pl.pallas_call(project_kernel, grid=(groups,), in_specs=specs, out_specs=...  18.9 us
  transfers between devices with their start and end apart: 48, of which 18 were waited for; matrix products, arithmetic and copies ran while one was open for 9% of the time, Pallas kernels for 50%

profile of v9, /device:TPU:0, one launch (start us, length us, event | category | flops | bytes accessed | tf_op | source)
XLA Modules:
  0.0 585.7 jit_solution(15420243971479030234)
XLA Ops:
  55.6 12.9 %collective-permute-done.x_ref.refs_5_ = bf16[256,2048]{1,0:T(8,128)(2,1)S(1)} collective-permute-done((bf16[256,2048]{1,0:T(8,128)(2,1)S(1)}, bf16[256,2048]{1,0:T(8,128)(2,1)S(1)}, u32[]{:S(2)}, u32[]{:S(2)}) %collective-permute-start) | collective-permute-done | bytes 1048608 | tf_op jit(solution)/shard_map/ppermute | solution.py:978
  76.0 17.9 %collective-permute-done.4.x_ref.refs_6_ = bf16[256,2048]{1,0:T(8,128)(2,1)S(1)} collective-permute-done((bf16[256,2048]{1,0:T(8,128)(2,1)S(1)}, bf16[256,2048]{1,0:T(8,128)(2,1)S(1)}, u32[]{:S(2)}, u32[]{:S(2)}) %collective-permute-start.4) | collective-permute-done | bytes 1048608 | tf_op jit(solution)/shard_map/ppermute | solution.py:978
  100.4 17.9 %collective-permute-done.5.x_ref.refs_7_ = bf16[256,2048]{1,0:T(8,128)(2,1)} collective-permute-done((bf16[256,2048]{1,0:T(8,128)(2,1)S(1)}, bf16[256,2048]{1,0:T(8,128)(2,1)}, u32[]{:S(2)}, u32[]{:S(2)}) %collective-permute-start.5) | collective-permute-done | bytes 1048608 | tf_op jit(solution)/shard_map/ppermute | solution.py:978
  125.0 17.7 %attend.1 = (bf16[1024,512]{1,0:T(8,128)(2,1)}, f32[16,4096]{1,0:T(8,128)}) custom-call(s32[1]{0:T(128)} %bitcast.10.place_ref, bf16[1024,768]{1,0:T(8,128)(2,1)} %get-tuple-element.270.own_ref.all_ref.refs_0_.refs_1_, bf16[1024,768]{1,0:T(8,128)(2,1)} %get-tuple-element.270.own_ref.all_ref.refs_0_.refs_1_, s32[1,1024]{1,0:T(1,128)} %bitcast.52, ...), custom_call_target="tpu_custom_call" | custom-call | flops 1 | bytes 1 | tf_op jit(solution)/shard_map/attend/pallas_call | solution.py:256
  146.6 19.6 %collective-permute-done.7.refs_1_ = bf16[1024,512]{1,0:T(8,128)(2,1)S(1)} collective-permute-done((bf16[1024,512]{1,0:T(8,128)(2,1)}, bf16[1024,512]{1,0:T(8,128)(2,1)S(1)}, u32[]{:S(2)}, u32[]{:S(2)}) %collective-permute-start.7) | collective-permute-done | bytes 1048608 | tf_op jit(solution)/shard_map/ppermute | solution.py:978
  170.1 18.8 %collective-permute-done.8.refs_2_ = bf16[1024,512]{1,0:T(8,128)(2,1)} collective-permute-done((bf16[1024,512]{1,0:T(8,128)(2,1)S(1)}, bf16[1024,512]{1,0:T(8,128)(2,1)}, u32[]{:S(2)}, u32[]{:S(2)}) %collective-permute-start.8) | collective-permute-done | bytes 1048608 | tf_op jit(solution)/shard_map/ppermute | solution.py:978
  193.2 14.2 %heads_product.1 = (f32[1024,2048]{1,0:T(8,128)}, bf16[256,1536]{1,0:T(8,128)(2,1)}) custom-call(bf16[1024,512]{1,0:T(8,128)(2,1)} %get-tuple-element.274.refs_0_.refs_2_, bf16[1024,512]{1,0:T(8,128)(2,1)} %copy-done.38, bf16[1024,512]{1,0:T(8,128)(2,1)} %collective-permute-done.8.refs_2_, ...), custom_call_target="tpu_custom_call" | custom-call | flops 1 | bytes 1 | tf_op jit(solution)/shard_map/heads_product/pallas_call | solution.py:507
  215.8 9.4 %after_attention.1 = (f32[256,2048]{1,0:T(8,128)}, bf16[1024,2048]{1,0:T(8,128)(2,1)}, bf16[256,512]{1,0:T(8,128)(2,1)}) custom-call(f32[1024,2048]{1,0:T(8,128)} %get-tuple-element.284.partial_ref, bf16[1024,512]{1,0:T(8,128)(2,1)} %copy-done.39, bf16[2048,6144]{1,0:T(8,128)(2,1)} %all-gather.6.cloned.1.call-done.refs_3_.weight_ref.gate_ref.up_ref.refs_5_.refs_6_, ...), custom_call_target="tpu_custom_call" | custom-call | flops 1 | bytes 1 | tf_op jit(solution)/shard_map/after_attention/pallas_call | solution.py:549
  225.2 13.9 %up_chunk.2 = (bf16[1024,2048]{1,0:T(8,128)(2,1)}, bf16[1024,2048]{1,0:T(8,128)(2,1)}, bf16[1024,2048]{1,0:T(8,128)(2,1)}) custom-call(bf16[1024,2048]{1,0:T(8,128)(2,1)} %get-tuple-element.413.x_ref.refs_0_, bf16[2048,6144]{1,0:T(8,128)(2,1)} %all-gather.6.cloned.1.call-done.refs_3_.weight_ref.gate_ref.up_ref.refs_5_.refs_6_, ...), custom_call_target="tpu_custom_call" | custom-call | flops 1 | bytes 1 | tf_op jit(solution)/shard_map/up_chunk/pallas_call | solution.py:601
  240.1 22.3 %down_chunk.2 = (bf16[1024,2048]{1,0:T(8,128)(2,1)}, bf16[1024,2048]{1,0:T(8,128)(2,1)}, bf16[256,2048]{1,0:T(8,128)(2,1)}, bf16[256,2048]{1,0:T(8,128)(2,1)}) custom-call(bf16[256,2048]{1,0:T(8,128)(2,1)} %copy-done.5, bf16[256,2048]{1,0:T(8,128)(2,1)} %copy-done.6, bf16[2048,2048]{1,0:T(8,128)(2,1)} %all-gather.8.cloned.1.call-done.refs_2_.refs_1_, ...), custom_call_target="tpu_custom_call" | custom-call | flops 1 | bytes 1 | tf_op jit(solution)/shard_map/down_chunk/pallas_call | solution.py:686
  265.8 13.8 %up_chunk.3 = (bf16[1024,2048]{1,0:T(8,128)(2,1)}, bf16[1024,2048]{1,0:T(8,128)(2,1)}, bf16[1024,2048]{1,0:T(8,128)(2,1)}) custom-call(bf16[1024,2048]{1,0:T(8,128)(2,1)} %get-tuple-element.413.x_ref.refs_0_, ...), custom_call_target="tpu_custom_call", output_to_operand_aliasing={{0}: (3, {}), {1}: (4, {}), {2}: (5, {})} | custom-call | flops 1 | bytes 1 | tf_op jit(solution)/shard_map/up_chunk/pallas_call | solution.py:601
  279.6 9.0 %weight_product.8 = bf16[1024,2048]{1,0:T(8,128)(2,1)} custom-call(s32[1]{0:T(128)} %bitcast.13.place_ref, bf16[256,2048]{1,0:T(8,128)(2,1)} %copy-done.5, bf16[256,2048]{1,0:T(8,128)(2,1)} %copy-done.6, bf16[256,2048]{1,0:T(8,128)(2,1)} %copy-done.7, bf16[256,2048]{1,0:T(8,128)(2,1)} %bitcast.39, bf16[1024,2048]{1,0:T(8,128)(2,1)} %get-tuple-element.398.refs_4_.refs_0_), custom_call_target="tpu_custom_call" | custom-call | flops 1 | bytes 1 | tf_op jit(solution)/shard_map/weight_product/pallas_call | solution.py:794
  290.2 22.4 %down_chunk.3 = (bf16[1024,2048]{1,0:T(8,128)(2,1)}, bf16[1024,2048]{1,0:T(8,128)(2,1)}, bf16[256,2048]{1,0:T(8,128)(2,1)}, bf16[256,2048]{1,0:T(8,128)(2,1)}) custom-call(bf16[256,2048]{1,0:T(8,128)(2,1)} %copy-done.7, bf16[256,2048]{1,0:T(8,128)(2,1)} %bitcast.40, ...), custom_call_target="tpu_custom_call", output_to_operand_aliasing={{0}: (7, {}), {1}: (8, {})} | custom-call | flops 1 | bytes 1 | tf_op jit(solution)/shard_map/down_chunk/pallas_call | solution.py:686
  318.3 8.7 %weight_product.9 = bf16[1024,2048]{1,0:T(8,128)(2,1)} custom-call(s32[1]{0:T(128)} %bitcast.13.place_ref, bf16[1024,2048]{1,0:T(8,128)(2,1)} %get-tuple-element.413.x_ref.refs_0_, bf16[1024,2048]{1,0:T(8,128)(2,1)} %get-tuple-element.328.refs_1_), custom_call_target="tpu_custom_call" | custom-call | flops 1 | bytes 1 | tf_op jit(solution)/shard_map/weight_product/pallas_call | solution.py:794
  335.7 9.7 %weight_product.10 = bf16[1024,2048]{1,0:T(8,128)(2,1)} custom-call(s32[1]{0:T(128)} %bitcast.13.place_ref, bf16[256,2048]{1,0:T(8,128)(2,1)} %copy-done.5, bf16[256,2048]{1,0:T(8,128)(2,1)} %copy-done.6, bf16[256,2048]{1,0:T(8,128)(2,1)} %copy-done.7, bf16[256,2048]{1,0:T(8,128)(2,1)} %bitcast.41, bf16[1024,2048]{1,0:T(8,128)(2,1)} %get-tuple-element.398.refs_4_.refs_0_, ...), custom_call_target="tpu_custom_call" | custom-call | flops 1 | bytes 1 | tf_op jit(solution)/shard_map/weight_product/pallas_call | solution.py:794
  346.4 10.8 %residual_gradient.1 = (f32[256,2048]{1,0:T(8,128)}, bf16[256,2048]{1,0:T(8,128)(2,1)}, bf16[256,512]{1,0:T(8,128)(2,1)}, bf16[256,512]{1,0:T(8,128)(2,1)}, bf16...) custom-call(bf16[256,2048]{1,0:T(8,128)(2,1)} %bitcast.42, f32[256,2048]{1,0:T(8,128)} %get-tuple-element.288.hidden_ref, ...), custom_call_target="tpu_custom_call" | custom-call | flops 1 | bytes 1 | tf_op jit(solution)/shard_map/residual_gradient/pallas_call | solution.py:881
  366.8 10.8 %weight_product.12 = (bf16[512,1024]{1,0:T(8,128)(2,1)}, bf16[512,1024]{1,0:T(8,128)(2,1)}, bf16[512,1024]{1,0:T(8,128)(2,1)}, bf16[512,1024]{1,0:T(8,128)(2,1)}) custom-call(s32[1]{0:T(128)} %bitcast.13.place_ref, bf16[1024,2048]{1,0:T(8,128)(2,1)} %get-tuple-element.413.x_ref.refs_0_, bf16[1024,2048]{1,0:T(8,128)(2,1)} %get-tuple-element.328.refs_1_, ...), custom_call_target="tpu_custom_call" | custom-call | flops 1 | bytes 1 | tf_op jit(solution)/shard_map/weight_product/pallas_call | solution.py:794
  384.7 17.5 %attend_back.2.refs_0_.refs_3_ = bf16[1024,384]{1,0:T(8,128)(2,1)} custom-call(s32[1]{0:T(128)} %bitcast.10.place_ref, bf16[1024,768]{1,0:T(8,128)(2,1)} %get-tuple-element.270.own_ref.all_ref.refs_0_.refs_1_, bf16[1024,768]{1,0:T(8,128)(2,1)} %get-tuple-element.270.own_ref.all_ref.refs_0_.refs_1_, bf16[1024,512]{1,0:T(8,128)(2,1)} %get-tuple-element.274.refs_0_.refs_2_, ...), custom_call_target="tpu_custom_call" | custom-call | flops 1 | bytes 1 | tf_op jit(solution)/shard_map/attend_back/pallas_call | solution.py:364
  415.4 17.0 %attend_back.3.refs_1_.refs_4_ = bf16[1024,384]{1,0:T(8,128)(2,1)} custom-call(s32[1]{0:T(128)} %bitcast.10.place_ref, bf16[1024,768]{1,0:T(8,128)(2,1)} %get-tuple-element.270.own_ref.all_ref.refs_0_.refs_1_, bf16[1024,768]{1,0:T(8,128)(2,1)} %get-tuple-element.270.own_ref.all_ref.refs_0_.refs_1_, bf16[1024,512]{1,0:T(8,128)(2,1)} %get-tuple-element.274.refs_0_.refs_2_, ...), custom_call_target="tpu_custom_call" | custom-call | flops 1 | bytes 1 | tf_op jit(solution)/shard_map/attend_back/pallas_call | solution.py:364
  441.0 12.1 %weight_product.14 = bf16[1024,2816]{1,0:T(8,128)(2,1)} custom-call(s32[1]{0:T(128)} %bitcast.13.place_ref, bf16[1024,2048]{1,0:T(8,128)(2,1)} %get-tuple-element.413.x_ref.refs_0_, bf16[1024,2048]{1,0:T(8,128)(2,1)} %get-tuple-element.394.refs_1_, bf16[1024,2048]{1,0:T(8,128)(2,1)} %get-tuple-element.395.refs_2_, ...), custom_call_target="tpu_custom_call" | custom-call | flops 1 | bytes 1 | tf_op jit(solution)/shard_map/weight_product/pallas_call | solution.py:794
  453.1 8.7 %transposed.5 = (bf16[256,2048]{1,0:T(8,128)(2,1)}, bf16[256,2048]{1,0:T(8,128)(2,1)}) custom-call(bf16[1024,2048]{1,0:T(8,128)(2,1)} %get-tuple-element.398.refs_4_.refs_0_, bf16[2048,2048]{1,0:T(8,128)(2,1)} %all-gather.8.cloned.1.call-done.refs_2_.refs_1_), custom_call_target="tpu_custom_call" | custom-call | flops 1 | bytes 1 | tf_op jit(solution)/shard_map/transposed/pallas_call | solution.py:460
  477.0 16.7 %weight_product.15 = (bf16[512,1408]{1,0:T(8,128)(2,1)}, bf16[512,1408]{1,0:T(8,128)(2,1)}, bf16[512,1408]{1,0:T(8,128)(2,1)}, bf16[512,1408]{1,0:T(8,128)(2,1)}) custom-call(s32[1]{0:T(128)} %bitcast.13.place_ref, bf16[1024,2048]{1,0:T(8,128)(2,1)} %get-tuple-element.413.x_ref.refs_0_, bf16[1024,2048]{1,0:T(8,128)(2,1)} %get-tuple-element.394.refs_1_, ...), custom_call_target="tpu_custom_call" | custom-call | flops 1 | bytes 1 | tf_op jit(solution)/shard_map/weight_product/pallas_call | solution.py:794
  517.1 14.8 %collective-permute-done.33 = bf16[256,2048]{1,0:T(8,128)(2,1)} collective-permute-done((bf16[256,2048]{1,0:T(8,128)(2,1)}, bf16[256,2048]{1,0:T(8,128)(2,1)}, u32[]{:S(2)}, u32[]{:S(2)}) %collective-permute-start.33) | collective-permute-done | bytes 1048608 | tf_op jit(solution)/shard_map/ppermute | solution.py:978
  545.5 9.0 %collective-permute-done.32 = bf16[256,2048]{1,0:T(8,128)(2,1)} collective-permute-done((bf16[256,2048]{1,0:T(8,128)(2,1)}, bf16[256,2048]{1,0:T(8,128)(2,1)}, u32[]{:S(2)}, u32[]{:S(2)}) %collective-permute-start.32) | collective-permute-done | bytes 1048608 | tf_op jit(solution)/shard_map/ppermute | solution.py:978
  (273 shorter events, 225.1 us)
Async XLA Ops:
  7.2 41.6 %all-gather.4.cloned.1.call-start = ((), (), s32[]{:S(2)}) async-start(), calls=%async_computation.1 | async-start | bytes 4128768 | tf_op jit(solution)/shard_map/all_gather | solution.py:935
  11.5 181.7 %all-gather.6.cloned.1.call-start = ((), (), s32[]{:S(2)}) async-start(), calls=%async_computation.2 | async-start | bytes 28311552 | tf_op jit(solution)/shard_map/all_gather | solution.py:935
  38.0 201.2 %all-gather.8.cloned.1.call-start = ((), (), s32[]{:S(2)}) async-start(), calls=%async_computation.3 | async-start | bytes 9437184 | tf_op jit(solution)/shard_map/all_gather | solution.py:935
  38.7 371.0 %reduce-scatter.2.cloned.1.call-start = ((), (), s32[]{:S(2)}) async-start(), calls=%async_computation.4 | async-start | bytes 5242880 | tf_op jit(solution)/shard_map/reduce_scatter | solution.py:973
  39.2 29.4 %collective-permute-start = (bf16[256,2048]{1,0:T(8,128)(2,1)S(1)}, bf16[256,2048]{1,0:T(8,128)(2,1)S(1)}, u32[]{:S(2)}, u32[]{:S(2)}) collective-permute-start(bf16[256,2048]{1,0:T(8,128)(2,1)S(1)} %bitcast.38), channel_id=1, source_target_pairs={{0,1},{1,2},{2,3},{3,0},{4,5},{5,6},{6,7},{7,4},{8,9},{9,10},{10,1... | collective-permute-start | bytes 3145736 | tf_op jit(solution)/shard_map/ppermute | solution.py:978
  262.4 26.2 %collective-permute-start.12 = (bf16[256,2048]{1,0:T(8,128)(2,1)}, bf16[256,2048]{1,0:T(8,128)(2,1)S(1)}, u32[]{:S(2)}, u32[]{:S(2)}) collective-permute-start(bf16[256,2048]{1,0:T(8,128)(2,1)} %get-tuple-element.304), channel_id=1, source_target_pairs={{0,1},{1,2},{2,3},{3,0},{4,5},{5,6},{6,7},{7,4},{8,9},{9,10},{10,1... | collective-permute-start | bytes 3145736 | tf_op jit(solution)/shard_map/ppermute | solution.py:978
  288.6 47.1 %collective-permute-start.15 = (bf16[1024,2048]{1,0:T(8,128)(2,1)}, bf16[1024,2048]{1,0:T(8,128)(2,1)}, u32[]{:S(2)}, u32[]{:S(2)}) collective-permute-start(bf16[1024,2048]{1,0:T(8,128)(2,1)} %weight_product.8), channel_id=1, source_target_pairs={{0,4},{4,0},{8,12},{12,8},{16,20},{20,16},{24,28},{28,24},{1,5},{5... | collective-permute-start | bytes 12582920 | tf_op jit(solution)/shard_map/ppermute | solution.py:932
  289.1 27.6 %collective-permute-start.13 = (bf16[256,2048]{1,0:T(8,128)(2,1)S(1)}, bf16[256,2048]{1,0:T(8,128)(2,1)S(1)}, u32[]{:S(2)}, u32[]{:S(2)}) collective-permute-start(bf16[256,2048]{1,0:T(8,128)(2,1)S(1)} %add_convert_fusion.6), channel_id=1, source_target_pairs={{0,1},{1,2},{2,3},{3,0},{4,5},{5,6},{6,7},{7,4},{8,9},{9,10},{10,1... | collective-permute-start | bytes 3145736 | tf_op jit(solution)/shard_map/ppermute | solution.py:978
  318.3 27.2 %collective-permute-start.14 = (bf16[256,2048]{1,0:T(8,128)(2,1)S(1)}, bf16[256,2048]{1,0:T(8,128)(2,1)S(1)}, u32[]{:S(2)}, u32[]{:S(2)}) collective-permute-start(bf16[256,2048]{1,0:T(8,128)(2,1)S(1)} %add_convert_fusion.5), channel_id=1, source_target_pairs={{0,1},{1,2},{2,3},{3,0},{4,5},{5,6},{6,7},{7,4},{8,9},{9,10},{10,1... | collective-permute-start | bytes 3145736 | tf_op jit(solution)/shard_map/ppermute | solution.py:978
  378.4 31.3 %collective-permute-start.16 = (bf16[256,2048]{1,0:T(8,128)(2,1)}, bf16[256,2048]{1,0:T(8,128)(2,1)S(1)}, u32[]{:S(2)}, u32[]{:S(2)}) collective-permute-start(bf16[256,2048]{1,0:T(8,128)(2,1)} %get-tuple-element.337), channel_id=1, source_target_pairs={{0,1},{1,2},{2,3},{3,0},{4,5},{5,6},{6,7},{7,4},{8,9},{9,10},{10,1... | collective-permute-start | bytes 3145736 | tf_op jit(solution)/shard_map/ppermute | solution.py:978
  411.1 29.5 %collective-permute-start.22 = (bf16[256,2048]{1,0:T(8,128)(2,1)}, bf16[256,2048]{1,0:T(8,128)(2,1)}, u32[]{:S(2)}, u32[]{:S(2)}) collective-permute-start(bf16[256,2048]{1,0:T(8,128)(2,1)} %add_convert_fusion.4), channel_id=1, source_target_pairs={{0,1},{1,2},{2,3},{3,0},{4,5},{5,6},{6,7},{7,4},{8,9},{9,10},{10,1... | collective-permute-start | bytes 3145736 | tf_op jit(solution)/shard_map/ppermute | solution.py:978
  411.8 28.8 %collective-permute-start.23 = (bf16[512,1024]{1,0:T(8,128)(2,1)}, bf16[512,1024]{1,0:T(8,128)(2,1)S(1)}, u32[]{:S(2)}, u32[]{:S(2)}) collective-permute-start(bf16[512,1024]{1,0:T(8,128)(2,1)} %get-tuple-element.388), channel_id=1, source_target_pairs={{0,16},{4,20},{8,24},{12,28},{16,0},{20,4},{24,8},{28,12},{1,17},{... | collective-permute-start | bytes 3145736 | tf_op jit(solution)/shard_map/ppermute | solution.py:932
  413.8 26.8 %collective-permute-start.24 = (bf16[512,1024]{1,0:T(8,128)(2,1)}, bf16[512,1024]{1,0:T(8,128)(2,1)}, u32[]{:S(2)}, u32[]{:S(2)}) collective-permute-start(bf16[512,1024]{1,0:T(8,128)(2,1)} %get-tuple-element.390), channel_id=1, source_target_pairs={{0,8},{4,12},{8,0},{12,4},{16,24},{20,28},{24,16},{28,20},{1,9},{5... | collective-permute-start | bytes 3145736 | tf_op jit(solution)/shard_map/ppermute | solution.py:932
  415.4 49.3 %collective-permute-start.26 = (bf16[512,1024]{1,0:T(8,128)(2,1)}, bf16[512,1024]{1,0:T(8,128)(2,1)S(1)}, u32[]{:S(2)}, u32[]{:S(2)}) collective-permute-start(bf16[512,1024]{1,0:T(8,128)(2,1)} %get-tuple-element.406), channel_id=1, source_target_pairs={{0,16},{4,20},{8,24},{12,28},{16,0},{20,4},{24,8},{28,12},{1,17},{... | collective-permute-start | bytes 3145736 | tf_op jit(solution)/shard_map/ppermute | solution.py:932
  432.5 32.3 %collective-permute-start.27 = (bf16[512,1024]{1,0:T(8,128)(2,1)}, bf16[512,1024]{1,0:T(8,128)(2,1)S(1)}, u32[]{:S(2)}, u32[]{:S(2)}) collective-permute-start(bf16[512,1024]{1,0:T(8,128)(2,1)} %get-tuple-element.408), channel_id=1, source_target_pairs={{0,8},{4,12},{8,0},{12,4},{16,24},{20,28},{24,16},{28,20},{1,9},{5... | collective-permute-start | bytes 3145736 | tf_op jit(solution)/shard_map/ppermute | solution.py:932
  469.1 27.9 %collective-permute-start.28 = (bf16[256,2048]{1,0:T(8,128)(2,1)}, bf16[256,2048]{1,0:T(8,128)(2,1)}, u32[]{:S(2)}, u32[]{:S(2)}) collective-permute-start(bf16[256,2048]{1,0:T(8,128)(2,1)} %add_convert_fusion.2), channel_id=1, source_target_pairs={{0,1},{1,2},{2,3},{3,0},{4,5},{5,6},{6,7},{7,4},{8,9},{9,10},{10,1... | collective-permute-start | bytes 3145736 | tf_op jit(solution)/shard_map/ppermute | solution.py:978
  472.9 26.2 %collective-permute-start.30 = (bf16[512,1024]{1,0:T(8,128)(2,1)}, bf16[512,1024]{1,0:T(8,128)(2,1)S(1)}, u32[]{:S(2)}, u32[]{:S(2)}) collective-permute-start(bf16[512,1024]{1,0:T(8,128)(2,1)} %get-tuple-element.435), channel_id=1, source_target_pairs={{0,8},{4,12},{8,0},{12,4},{16,24},{20,28},{24,16},{28,20},{1,9},{5... | collective-permute-start | bytes 3145736 | tf_op jit(solution)/shard_map/ppermute | solution.py:932
  474.6 26.3 %collective-permute-start.31 = (bf16[512,1024]{1,0:T(8,128)(2,1)}, bf16[512,1024]{1,0:T(8,128)(2,1)}, u32[]{:S(2)}, u32[]{:S(2)}) collective-permute-start(bf16[512,1024]{1,0:T(8,128)(2,1)} %get-tuple-element.436), channel_id=1, source_target_pairs={{0,16},{4,20},{8,24},{12,28},{16,0},{20,4},{24,8},{28,12},{1,17},{... | collective-permute-start | bytes 3145736 | tf_op jit(solution)/shard_map/ppermute | solution.py:932
  493.6 38.2 %collective-permute-start.34 = (bf16[512,1408]{1,0:T(8,128)(2,1)}, bf16[512,1408]{1,0:T(8,128)(2,1)}, u32[]{:S(2)}, u32[]{:S(2)}) collective-permute-start(bf16[512,1408]{1,0:T(8,128)(2,1)} %get-tuple-element.416), channel_id=1, source_target_pairs={{0,16},{4,20},{8,24},{12,28},{16,0},{20,4},{24,8},{28,12},{1,17},{... | collective-permute-start | bytes 4325384 | tf_op jit(solution)/shard_map/ppermute | solution.py:932
  494.5 37.4 %collective-permute-start.35 = (bf16[512,1408]{1,0:T(8,128)(2,1)}, bf16[512,1408]{1,0:T(8,128)(2,1)}, u32[]{:S(2)}, u32[]{:S(2)}) collective-permute-start(bf16[512,1408]{1,0:T(8,128)(2,1)} %get-tuple-element.418), channel_id=1, source_target_pairs={{0,8},{4,12},{8,0},{12,4},{16,24},{20,28},{24,16},{28,20},{1,9},{5... | collective-permute-start | bytes 4325384 | tf_op jit(solution)/shard_map/ppermute | solution.py:932
  503.6 28.3 %collective-permute-start.33 = (bf16[256,2048]{1,0:T(8,128)(2,1)}, bf16[256,2048]{1,0:T(8,128)(2,1)}, u32[]{:S(2)}, u32[]{:S(2)}) collective-permute-start(bf16[256,2048]{1,0:T(8,128)(2,1)} %add_convert_fusion.1), channel_id=1, source_target_pairs={{0,1},{1,2},{2,3},{3,0},{4,5},{5,6},{6,7},{7,4},{8,9},{9,10},{10,1... | collective-permute-start | bytes 3145736 | tf_op jit(solution)/shard_map/ppermute | solution.py:978
  512.6 41.9 %collective-permute-start.32 = (bf16[256,2048]{1,0:T(8,128)(2,1)}, bf16[256,2048]{1,0:T(8,128)(2,1)}, u32[]{:S(2)}, u32[]{:S(2)}) collective-permute-start(bf16[256,2048]{1,0:T(8,128)(2,1)} %add_convert_fusion.3), channel_id=1, source_target_pairs={{0,1},{1,2},{2,3},{3,0},{4,5},{5,6},{6,7},{7,4},{8,9},{9,10},{10,1... | collective-permute-start | bytes 3145736 | tf_op jit(solution)/shard_map/ppermute | solution.py:978
  539.1 33.6 %collective-permute-start.39 = (bf16[256,512]{1,0:T(8,128)(2,1)S(1)}, bf16[256,512]{1,0:T(8,128)(2,1)S(1)}, u32[]{:S(2)}, u32[]{:S(2)}) collective-permute-start(bf16[256,512]{1,0:T(8,128)(2,1)S(1)} %split.17), channel_id=1, source_target_pairs={{0,1},{1,2},{2,3},{3,0},{4,5},{5,6},{6,7},{7,4},{8,9},{9,10},{10,1... | collective-permute-start | bytes 786440 | tf_op jit(solution)/shard_map/ppermute | solution.py:993
  540.9 32.8 %collective-permute-start.40 = (bf16[256,512]{1,0:T(8,128)(2,1)S(1)}, bf16[256,512]{1,0:T(8,128)(2,1)S(1)}, u32[]{:S(2)}, u32[]{:S(2)}) collective-permute-start(bf16[256,512]{1,0:T(8,128)(2,1)S(1)} %get-tuple-element.476), channel_id=1, source_target_pairs={{0,2},{1,3},{2,0},{3,1},{4,6},{5,7},{6,4},{7,5},{8,10},{9,11},{10,... | collective-permute-start | bytes 786440 | tf_op jit(solution)/shard_map/ppermute | solution.py:993
  (73 other events, 1034.6 us)
Sparse Core Ops, SparseCore 0:
  11.6 37.2 all-gather.3
  50.7 125.3 all-gather.5
  178.0 54.3 all-gather.7
  345.7 54.5 reduce-scatter.1

commit v10 on v9

--- a/solution.py
+++ b/solution.py
@@ -382,7 +382,9 @@
     )
 
 
-def pack_kernel(groups, query_ref, key_ref, value_ref, gain_ref, joint_ref, out_ref):
+def pack_kernel(
+    groups, query_ref, key_ref, value_ref, first_ref, second_ref, joint_ref, out_ref
+):
     for g in range(groups):
         start = g * GROUP_WIDTH
         columns = slice(g * HEAD_SIZE, (g + 1) * HEAD_SIZE)
@@ -394,10 +396,13 @@
         )
     width = groups * GROUP_WIDTH
     out_ref[:, :width] = joint_ref[...]
-    out_ref[:, width:] = gain_ref[...].astype(jnp.float32).T.astype(jnp.bfloat16)
-
-
-def pack(query, key, value, gains, groups):
+    row = lax.broadcasted_iota(jnp.int32, (128, query_ref.shape[0]), 0)
+    gains = jnp.where(row == 0, first_ref[...].astype(jnp.float32)[None, :], 0.0)
+    gains = jnp.where(row == 1, second_ref[...].astype(jnp.float32)[None, :], gains)
+    out_ref[:, width:] = gains.T.astype(jnp.bfloat16)
+
+
+def pack(query, key, value, first, second, groups):
     rows = query.shape[0]
     width = groups * GROUP_WIDTH
     return pl.pallas_call(
@@ -409,7 +414,7 @@
         compiler_params=parameters(),
         cost_estimate=SMALL_COST,
         name="pack",
-    )(query, key, value, gains)
+    )(query, key, value, first, second)
 
 
 def join_kernel(*refs):
@@ -1065,8 +1070,9 @@
     cosine_table = jnp.tile(cosine, (1, 128 // cosine.shape[1]))
     sine_table = jnp.tile(jnp.concatenate([-sine, sine], axis=1), (1, 128 // HEAD_SIZE))
 
-    own_gains = jnp.pad(jnp.stack([attention_gain, feedforward_gain]), ((0, 126), (0, 0)))
-    joint_matrix, packed = pack(query_matrix, key_matrix, value_matrix, own_gains, groups)
+    joint_matrix, packed = pack(
+        query_matrix, key_matrix, value_matrix, attention_gain, feedforward_gain, groups
+    )
     joint_full = mover.gather(packed)
     output_parts = mover.spread(output_weight.T)
     up_shard = jnp.pad(

time: 595 us -> 593 us (level)
  no operation moved by 1% of the time
where the time goes in v10:
time: 593 us; the launch traced here: 584 us
  Pallas kernels  294 us (50%)
  waiting for transfers between devices  143 us (24%)
  starting transfers between devices  72.3 us (12%)
  other arithmetic  40.2 us (7%)
  local copies, waits for them, and re-layouts  19.2 us (3%)
  between operations  14.9 us (3%)
    ppermute x18, waiting for transfers between devices, hop(): lax.ppermute(value, 'tensor', [(i, (i + shift) % self.ring) for i in rang...  123 us
    pallas_call x8, Pallas kernels, weight_product(): pl.pallas_call(functools.partial(weight_kernel, [(len(xs), len(ys)) for x...  79.9 us
    pallas_call x2, Pallas kernels, down_chunk(): pl.pallas_call(functools.partial(down_kernel, len(es), tiles), grid=(tile...  44.7 us
    ppermute x18, starting transfers between devices, hop(): lax.ppermute(value, 'tensor', [(i, (i + shift) % self.ring) for i in rang...  38.4 us
    pallas_call x2, Pallas kernels, attention_backward(): pl.pallas_call(functools.partial(backward_kernel, count), grid_spec=spec,...  34 us
    pallas_call x2, Pallas kernels, up_chunk(): pl.pallas_call(up_kernel, grid=(tiles,), in_specs=specs, out_specs=[pl.Bl...  27.7 us
    pallas_call x3, Pallas kernels, transposed_product(): pl.pallas_call(functools.partial(transposed_kernel, len(xs), parts), grid...  25.1 us
    pallas_call x4, Pallas kernels, project(): pl.pallas_call(project_kernel, grid=(groups,), in_specs=specs, out_specs=...  18.9 us
  transfers between devices with their start and end apart: 48, of which 18 were waited for; matrix products, arithmetic and copies ran while one was open for 9% of the time, Pallas kernels for 50%

profile of v10, /device:TPU:0, one launch (start us, length us, event | category | flops | bytes accessed | tf_op | source)
XLA Modules:
  0.0 583.6 jit_solution(12870384309454304192)
XLA Ops:
  54.5 12.1 %collective-permute-done.x_ref.refs_5_ = bf16[256,2048]{1,0:T(8,128)(2,1)S(1)} collective-permute-done((bf16[256,2048]{1,0:T(8,128)(2,1)S(1)}, bf16[256,2048]{1,0:T(8,128)(2,1)S(1)}, u32[]{:S(2)}, u32[]{:S(2)}) %collective-permute-start) | collective-permute-done | bytes 1048608 | tf_op jit(solution)/shard_map/ppermute | solution.py:983
  73.9 17.9 %collective-permute-done.4.x_ref.refs_6_ = bf16[256,2048]{1,0:T(8,128)(2,1)S(1)} collective-permute-done((bf16[256,2048]{1,0:T(8,128)(2,1)S(1)}, bf16[256,2048]{1,0:T(8,128)(2,1)S(1)}, u32[]{:S(2)}, u32[]{:S(2)}) %collective-permute-start.4) | collective-permute-done | bytes 1048608 | tf_op jit(solution)/shard_map/ppermute | solution.py:983
  98.4 17.9 %collective-permute-done.5.x_ref.refs_7_ = bf16[256,2048]{1,0:T(8,128)(2,1)} collective-permute-done((bf16[256,2048]{1,0:T(8,128)(2,1)S(1)}, bf16[256,2048]{1,0:T(8,128)(2,1)}, u32[]{:S(2)}, u32[]{:S(2)}) %collective-permute-start.5) | collective-permute-done | bytes 1048608 | tf_op jit(solution)/shard_map/ppermute | solution.py:983
  122.9 17.7 %attend.1 = (bf16[1024,512]{1,0:T(8,128)(2,1)}, f32[16,4096]{1,0:T(8,128)}) custom-call(s32[1]{0:T(128)} %bitcast.10.place_ref, bf16[1024,768]{1,0:T(8,128)(2,1)} %get-tuple-element.270.own_ref.all_ref.refs_0_.refs_1_, bf16[1024,768]{1,0:T(8,128)(2,1)} %get-tuple-element.270.own_ref.all_ref.refs_0_.refs_1_, s32[1,1024]{1,0:T(1,128)} %bitcast.52, ...), custom_call_target="tpu_custom_call" | custom-call | flops 1 | bytes 1 | tf_op jit(solution)/shard_map/attend/pallas_call | solution.py:256
  144.5 19.6 %collective-permute-done.7.refs_1_ = bf16[1024,512]{1,0:T(8,128)(2,1)S(1)} collective-permute-done((bf16[1024,512]{1,0:T(8,128)(2,1)}, bf16[1024,512]{1,0:T(8,128)(2,1)S(1)}, u32[]{:S(2)}, u32[]{:S(2)}) %collective-permute-start.7) | collective-permute-done | bytes 1048608 | tf_op jit(solution)/shard_map/ppermute | solution.py:983
  168.1 18.7 %collective-permute-done.8.refs_2_ = bf16[1024,512]{1,0:T(8,128)(2,1)} collective-permute-done((bf16[1024,512]{1,0:T(8,128)(2,1)S(1)}, bf16[1024,512]{1,0:T(8,128)(2,1)}, u32[]{:S(2)}, u32[]{:S(2)}) %collective-permute-start.8) | collective-permute-done | bytes 1048608 | tf_op jit(solution)/shard_map/ppermute | solution.py:983
  191.2 14.4 %heads_product.1 = (f32[1024,2048]{1,0:T(8,128)}, bf16[256,1536]{1,0:T(8,128)(2,1)}) custom-call(bf16[1024,512]{1,0:T(8,128)(2,1)} %get-tuple-element.274.refs_0_.refs_2_, bf16[1024,512]{1,0:T(8,128)(2,1)} %copy-done.38, bf16[1024,512]{1,0:T(8,128)(2,1)} %collective-permute-done.8.refs_2_, ...), custom_call_target="tpu_custom_call" | custom-call | flops 1 | bytes 1 | tf_op jit(solution)/shard_map/heads_product/pallas_call | solution.py:512
  213.6 9.4 %after_attention.1 = (f32[256,2048]{1,0:T(8,128)}, bf16[1024,2048]{1,0:T(8,128)(2,1)}, bf16[256,512]{1,0:T(8,128)(2,1)}) custom-call(f32[1024,2048]{1,0:T(8,128)} %get-tuple-element.284.partial_ref, bf16[1024,512]{1,0:T(8,128)(2,1)} %copy-done.39, bf16[2048,6144]{1,0:T(8,128)(2,1)} %all-gather.6.cloned.1.call-done.refs_3_.weight_ref.gate_ref.up_ref.refs_5_.refs_6_, ...), custom_call_target="tpu_custom_call" | custom-call | flops 1 | bytes 1 | tf_op jit(solution)/shard_map/after_attention/pallas_call | solution.py:554
  223.0 13.9 %up_chunk.2 = (bf16[1024,2048]{1,0:T(8,128)(2,1)}, bf16[1024,2048]{1,0:T(8,128)(2,1)}, bf16[1024,2048]{1,0:T(8,128)(2,1)}) custom-call(bf16[1024,2048]{1,0:T(8,128)(2,1)} %get-tuple-element.413.x_ref.refs_0_, bf16[2048,6144]{1,0:T(8,128)(2,1)} %all-gather.6.cloned.1.call-done.refs_3_.weight_ref.gate_ref.up_ref.refs_5_.refs_6_, ...), custom_call_target="tpu_custom_call" | custom-call | flops 1 | bytes 1 | tf_op jit(solution)/shard_map/up_chunk/pallas_call | solution.py:606
  237.9 22.3 %down_chunk.2 = (bf16[1024,2048]{1,0:T(8,128)(2,1)}, bf16[1024,2048]{1,0:T(8,128)(2,1)}, bf16[256,2048]{1,0:T(8,128)(2,1)}, bf16[256,2048]{1,0:T(8,128)(2,1)}) custom-call(bf16[256,2048]{1,0:T(8,128)(2,1)} %copy-done.5, bf16[256,2048]{1,0:T(8,128)(2,1)} %copy-done.6, bf16[2048,2048]{1,0:T(8,128)(2,1)} %all-gather.8.cloned.1.call-done.refs_2_.refs_1_, ...), custom_call_target="tpu_custom_call" | custom-call | flops 1 | bytes 1 | tf_op jit(solution)/shard_map/down_chunk/pallas_call | solution.py:691
  263.6 13.8 %up_chunk.3 = (bf16[1024,2048]{1,0:T(8,128)(2,1)}, bf16[1024,2048]{1,0:T(8,128)(2,1)}, bf16[1024,2048]{1,0:T(8,128)(2,1)}) custom-call(bf16[1024,2048]{1,0:T(8,128)(2,1)} %get-tuple-element.413.x_ref.refs_0_, ...), custom_call_target="tpu_custom_call", output_to_operand_aliasing={{0}: (3, {}), {1}: (4, {}), {2}: (5, {})} | custom-call | flops 1 | bytes 1 | tf_op jit(solution)/shard_map/up_chunk/pallas_call | solution.py:606
  277.4 9.0 %weight_product.8 = bf16[1024,2048]{1,0:T(8,128)(2,1)} custom-call(s32[1]{0:T(128)} %bitcast.13.place_ref, bf16[256,2048]{1,0:T(8,128)(2,1)} %copy-done.5, bf16[256,2048]{1,0:T(8,128)(2,1)} %copy-done.6, bf16[256,2048]{1,0:T(8,128)(2,1)} %copy-done.7, bf16[256,2048]{1,0:T(8,128)(2,1)} %bitcast.39, bf16[1024,2048]{1,0:T(8,128)(2,1)} %get-tuple-element.398.refs_4_.refs_0_), custom_call_target="tpu_custom_call" | custom-call | flops 1 | bytes 1 | tf_op jit(solution)/shard_map/weight_product/pallas_call | solution.py:799
  288.3 22.4 %down_chunk.3 = (bf16[1024,2048]{1,0:T(8,128)(2,1)}, bf16[1024,2048]{1,0:T(8,128)(2,1)}, bf16[256,2048]{1,0:T(8,128)(2,1)}, bf16[256,2048]{1,0:T(8,128)(2,1)}) custom-call(bf16[256,2048]{1,0:T(8,128)(2,1)} %copy-done.7, bf16[256,2048]{1,0:T(8,128)(2,1)} %bitcast.40, ...), custom_call_target="tpu_custom_call", output_to_operand_aliasing={{0}: (7, {}), {1}: (8, {})} | custom-call | flops 1 | bytes 1 | tf_op jit(solution)/shard_map/down_chunk/pallas_call | solution.py:691
  316.1 8.7 %weight_product.9 = bf16[1024,2048]{1,0:T(8,128)(2,1)} custom-call(s32[1]{0:T(128)} %bitcast.13.place_ref, bf16[1024,2048]{1,0:T(8,128)(2,1)} %get-tuple-element.413.x_ref.refs_0_, bf16[1024,2048]{1,0:T(8,128)(2,1)} %get-tuple-element.328.refs_1_), custom_call_target="tpu_custom_call" | custom-call | flops 1 | bytes 1 | tf_op jit(solution)/shard_map/weight_product/pallas_call | solution.py:799
  333.5 9.7 %weight_product.10 = bf16[1024,2048]{1,0:T(8,128)(2,1)} custom-call(s32[1]{0:T(128)} %bitcast.13.place_ref, bf16[256,2048]{1,0:T(8,128)(2,1)} %copy-done.5, bf16[256,2048]{1,0:T(8,128)(2,1)} %copy-done.6, bf16[256,2048]{1,0:T(8,128)(2,1)} %copy-done.7, bf16[256,2048]{1,0:T(8,128)(2,1)} %bitcast.41, bf16[1024,2048]{1,0:T(8,128)(2,1)} %get-tuple-element.398.refs_4_.refs_0_, ...), custom_call_target="tpu_custom_call" | custom-call | flops 1 | bytes 1 | tf_op jit(solution)/shard_map/weight_product/pallas_call | solution.py:799
  344.2 10.9 %residual_gradient.1 = (f32[256,2048]{1,0:T(8,128)}, bf16[256,2048]{1,0:T(8,128)(2,1)}, bf16[256,512]{1,0:T(8,128)(2,1)}, bf16[256,512]{1,0:T(8,128)(2,1)}, bf16...) custom-call(bf16[256,2048]{1,0:T(8,128)(2,1)} %bitcast.42, f32[256,2048]{1,0:T(8,128)} %get-tuple-element.288.hidden_ref, ...), custom_call_target="tpu_custom_call" | custom-call | flops 1 | bytes 1 | tf_op jit(solution)/shard_map/residual_gradient/pallas_call | solution.py:886
  364.6 11.0 %weight_product.12 = (bf16[512,1024]{1,0:T(8,128)(2,1)}, bf16[512,1024]{1,0:T(8,128)(2,1)}, bf16[512,1024]{1,0:T(8,128)(2,1)}, bf16[512,1024]{1,0:T(8,128)(2,1)}) custom-call(s32[1]{0:T(128)} %bitcast.13.place_ref, bf16[1024,2048]{1,0:T(8,128)(2,1)} %get-tuple-element.413.x_ref.refs_0_, bf16[1024,2048]{1,0:T(8,128)(2,1)} %get-tuple-element.328.refs_1_, ...), custom_call_target="tpu_custom_call" | custom-call | flops 1 | bytes 1 | tf_op jit(solution)/shard_map/weight_product/pallas_call | solution.py:799
  382.8 17.0 %attend_back.2.refs_0_.refs_3_ = bf16[1024,384]{1,0:T(8,128)(2,1)} custom-call(s32[1]{0:T(128)} %bitcast.10.place_ref, bf16[1024,768]{1,0:T(8,128)(2,1)} %get-tuple-element.270.own_ref.all_ref.refs_0_.refs_1_, bf16[1024,768]{1,0:T(8,128)(2,1)} %get-tuple-element.270.own_ref.all_ref.refs_0_.refs_1_, bf16[1024,512]{1,0:T(8,128)(2,1)} %get-tuple-element.274.refs_0_.refs_2_, ...), custom_call_target="tpu_custom_call" | custom-call | flops 1 | bytes 1 | tf_op jit(solution)/shard_map/attend_back/pallas_call | solution.py:364
  413.4 17.0 %attend_back.3.refs_1_.refs_4_ = bf16[1024,384]{1,0:T(8,128)(2,1)} custom-call(s32[1]{0:T(128)} %bitcast.10.place_ref, bf16[1024,768]{1,0:T(8,128)(2,1)} %get-tuple-element.270.own_ref.all_ref.refs_0_.refs_1_, bf16[1024,768]{1,0:T(8,128)(2,1)} %get-tuple-element.270.own_ref.all_ref.refs_0_.refs_1_, bf16[1024,512]{1,0:T(8,128)(2,1)} %get-tuple-element.274.refs_0_.refs_2_, ...), custom_call_target="tpu_custom_call" | custom-call | flops 1 | bytes 1 | tf_op jit(solution)/shard_map/attend_back/pallas_call | solution.py:364
  439.1 12.1 %weight_product.14 = bf16[1024,2816]{1,0:T(8,128)(2,1)} custom-call(s32[1]{0:T(128)} %bitcast.13.place_ref, bf16[1024,2048]{1,0:T(8,128)(2,1)} %get-tuple-element.413.x_ref.refs_0_, bf16[1024,2048]{1,0:T(8,128)(2,1)} %get-tuple-element.394.refs_1_, bf16[1024,2048]{1,0:T(8,128)(2,1)} %get-tuple-element.395.refs_2_, ...), custom_call_target="tpu_custom_call" | custom-call | flops 1 | bytes 1 | tf_op jit(solution)/shard_map/weight_product/pallas_call | solution.py:799
  451.2 8.7 %transposed.5 = (bf16[256,2048]{1,0:T(8,128)(2,1)}, bf16[256,2048]{1,0:T(8,128)(2,1)}) custom-call(bf16[1024,2048]{1,0:T(8,128)(2,1)} %get-tuple-element.398.refs_4_.refs_0_, bf16[2048,2048]{1,0:T(8,128)(2,1)} %all-gather.8.cloned.1.call-done.refs_2_.refs_1_), custom_call_target="tpu_custom_call" | custom-call | flops 1 | bytes 1 | tf_op jit(solution)/shard_map/transposed/pallas_call | solution.py:465
  474.5 16.7 %weight_product.15 = (bf16[512,1408]{1,0:T(8,128)(2,1)}, bf16[512,1408]{1,0:T(8,128)(2,1)}, bf16[512,1408]{1,0:T(8,128)(2,1)}, bf16[512,1408]{1,0:T(8,128)(2,1)}) custom-call(s32[1]{0:T(128)} %bitcast.13.place_ref, bf16[1024,2048]{1,0:T(8,128)(2,1)} %get-tuple-element.413.x_ref.refs_0_, bf16[1024,2048]{1,0:T(8,128)(2,1)} %get-tuple-element.394.refs_1_, ...), custom_call_target="tpu_custom_call" | custom-call | flops 1 | bytes 1 | tf_op jit(solution)/shard_map/weight_product/pallas_call | solution.py:799
  515.0 14.6 %collective-permute-done.33 = bf16[256,2048]{1,0:T(8,128)(2,1)} collective-permute-done((bf16[256,2048]{1,0:T(8,128)(2,1)}, bf16[256,2048]{1,0:T(8,128)(2,1)}, u32[]{:S(2)}, u32[]{:S(2)}) %collective-permute-start.33) | collective-permute-done | bytes 1048608 | tf_op jit(solution)/shard_map/ppermute | solution.py:983
  543.4 8.8 %collective-permute-done.32 = bf16[256,2048]{1,0:T(8,128)(2,1)} collective-permute-done((bf16[256,2048]{1,0:T(8,128)(2,1)}, bf16[256,2048]{1,0:T(8,128)(2,1)}, u32[]{:S(2)}, u32[]{:S(2)}) %collective-permute-start.32) | collective-permute-done | bytes 1048608 | tf_op jit(solution)/shard_map/ppermute | solution.py:983
  (270 shorter events, 224.2 us)
Async XLA Ops:
  7.2 40.5 %all-gather.4.cloned.1.call-start = ((), (), s32[]{:S(2)}) async-start(), calls=%async_computation.1 | async-start | bytes 4128768 | tf_op jit(solution)/shard_map/all_gather | solution.py:940
  9.5 181.7 %all-gather.6.cloned.1.call-start = ((), (), s32[]{:S(2)}) async-start(), calls=%async_computation.2 | async-start | bytes 28311552 | tf_op jit(solution)/shard_map/all_gather | solution.py:940
  36.3 200.8 %all-gather.8.cloned.1.call-start = ((), (), s32[]{:S(2)}) async-start(), calls=%async_computation.3 | async-start | bytes 9437184 | tf_op jit(solution)/shard_map/all_gather | solution.py:940
  37.0 370.4 %reduce-scatter.2.cloned.1.call-start = ((), (), s32[]{:S(2)}) async-start(), calls=%async_computation.4 | async-start | bytes 5242880 | tf_op jit(solution)/shard_map/reduce_scatter | solution.py:978
  37.5 29.1 %collective-permute-start = (bf16[256,2048]{1,0:T(8,128)(2,1)S(1)}, bf16[256,2048]{1,0:T(8,128)(2,1)S(1)}, u32[]{:S(2)}, u32[]{:S(2)}) collective-permute-start(bf16[256,2048]{1,0:T(8,128)(2,1)S(1)} %bitcast.38), channel_id=1, source_target_pairs={{0,1},{1,2},{2,3},{3,0},{4,5},{5,6},{6,7},{7,4},{8,9},{9,10},{10,1... | collective-permute-start | bytes 3145736 | tf_op jit(solution)/shard_map/ppermute | solution.py:983
  260.2 26.2 %collective-permute-start.12 = (bf16[256,2048]{1,0:T(8,128)(2,1)}, bf16[256,2048]{1,0:T(8,128)(2,1)S(1)}, u32[]{:S(2)}, u32[]{:S(2)}) collective-permute-start(bf16[256,2048]{1,0:T(8,128)(2,1)} %get-tuple-element.304), channel_id=1, source_target_pairs={{0,1},{1,2},{2,3},{3,0},{4,5},{5,6},{6,7},{7,4},{8,9},{9,10},{10,1... | collective-permute-start | bytes 3145736 | tf_op jit(solution)/shard_map/ppermute | solution.py:983
  286.5 47.1 %collective-permute-start.15 = (bf16[1024,2048]{1,0:T(8,128)(2,1)}, bf16[1024,2048]{1,0:T(8,128)(2,1)}, u32[]{:S(2)}, u32[]{:S(2)}) collective-permute-start(bf16[1024,2048]{1,0:T(8,128)(2,1)} %weight_product.8), channel_id=1, source_target_pairs={{0,4},{4,0},{8,12},{12,8},{16,20},{20,16},{24,28},{28,24},{1,5},{5... | collective-permute-start | bytes 12582920 | tf_op jit(solution)/shard_map/ppermute | solution.py:937
  286.9 27.6 %collective-permute-start.13 = (bf16[256,2048]{1,0:T(8,128)(2,1)S(1)}, bf16[256,2048]{1,0:T(8,128)(2,1)S(1)}, u32[]{:S(2)}, u32[]{:S(2)}) collective-permute-start(bf16[256,2048]{1,0:T(8,128)(2,1)S(1)} %add_convert_fusion.6), channel_id=1, source_target_pairs={{0,1},{1,2},{2,3},{3,0},{4,5},{5,6},{6,7},{7,4},{8,9},{9,10},{10,1... | collective-permute-start | bytes 3145736 | tf_op jit(solution)/shard_map/ppermute | solution.py:983
  316.1 27.2 %collective-permute-start.14 = (bf16[256,2048]{1,0:T(8,128)(2,1)S(1)}, bf16[256,2048]{1,0:T(8,128)(2,1)S(1)}, u32[]{:S(2)}, u32[]{:S(2)}) collective-permute-start(bf16[256,2048]{1,0:T(8,128)(2,1)S(1)} %add_convert_fusion.5), channel_id=1, source_target_pairs={{0,1},{1,2},{2,3},{3,0},{4,5},{5,6},{6,7},{7,4},{8,9},{9,10},{10,1... | collective-permute-start | bytes 3145736 | tf_op jit(solution)/shard_map/ppermute | solution.py:983
  376.6 30.8 %collective-permute-start.16 = (bf16[256,2048]{1,0:T(8,128)(2,1)}, bf16[256,2048]{1,0:T(8,128)(2,1)S(1)}, u32[]{:S(2)}, u32[]{:S(2)}) collective-permute-start(bf16[256,2048]{1,0:T(8,128)(2,1)} %get-tuple-element.337), channel_id=1, source_target_pairs={{0,1},{1,2},{2,3},{3,0},{4,5},{5,6},{6,7},{7,4},{8,9},{9,10},{10,1... | collective-permute-start | bytes 3145736 | tf_op jit(solution)/shard_map/ppermute | solution.py:983
  408.8 30.0 %collective-permute-start.22 = (bf16[256,2048]{1,0:T(8,128)(2,1)}, bf16[256,2048]{1,0:T(8,128)(2,1)}, u32[]{:S(2)}, u32[]{:S(2)}) collective-permute-start(bf16[256,2048]{1,0:T(8,128)(2,1)} %add_convert_fusion.4), channel_id=1, source_target_pairs={{0,1},{1,2},{2,3},{3,0},{4,5},{5,6},{6,7},{7,4},{8,9},{9,10},{10,1... | collective-permute-start | bytes 3145736 | tf_op jit(solution)/shard_map/ppermute | solution.py:983
  409.9 28.8 %collective-permute-start.23 = (bf16[512,1024]{1,0:T(8,128)(2,1)}, bf16[512,1024]{1,0:T(8,128)(2,1)S(1)}, u32[]{:S(2)}, u32[]{:S(2)}) collective-permute-start(bf16[512,1024]{1,0:T(8,128)(2,1)} %get-tuple-element.388), channel_id=1, source_target_pairs={{0,16},{4,20},{8,24},{12,28},{16,0},{20,4},{24,8},{28,12},{1,17},{... | collective-permute-start | bytes 3145736 | tf_op jit(solution)/shard_map/ppermute | solution.py:937
  411.5 27.2 %collective-permute-start.24 = (bf16[512,1024]{1,0:T(8,128)(2,1)}, bf16[512,1024]{1,0:T(8,128)(2,1)}, u32[]{:S(2)}, u32[]{:S(2)}) collective-permute-start(bf16[512,1024]{1,0:T(8,128)(2,1)} %get-tuple-element.390), channel_id=1, source_target_pairs={{0,8},{4,12},{8,0},{12,4},{16,24},{20,28},{24,16},{28,20},{1,9},{5... | collective-permute-start | bytes 3145736 | tf_op jit(solution)/shard_map/ppermute | solution.py:937
  412.9 50.0 %collective-permute-start.26 = (bf16[512,1024]{1,0:T(8,128)(2,1)}, bf16[512,1024]{1,0:T(8,128)(2,1)S(1)}, u32[]{:S(2)}, u32[]{:S(2)}) collective-permute-start(bf16[512,1024]{1,0:T(8,128)(2,1)} %get-tuple-element.406), channel_id=1, source_target_pairs={{0,16},{4,20},{8,24},{12,28},{16,0},{20,4},{24,8},{28,12},{1,17},{... | collective-permute-start | bytes 3145736 | tf_op jit(solution)/shard_map/ppermute | solution.py:937
  430.4 32.5 %collective-permute-start.27 = (bf16[512,1024]{1,0:T(8,128)(2,1)}, bf16[512,1024]{1,0:T(8,128)(2,1)S(1)}, u32[]{:S(2)}, u32[]{:S(2)}) collective-permute-start(bf16[512,1024]{1,0:T(8,128)(2,1)} %get-tuple-element.408), channel_id=1, source_target_pairs={{0,8},{4,12},{8,0},{12,4},{16,24},{20,28},{24,16},{28,20},{1,9},{5... | collective-permute-start | bytes 3145736 | tf_op jit(solution)/shard_map/ppermute | solution.py:937
  467.0 27.9 %collective-permute-start.28 = (bf16[256,2048]{1,0:T(8,128)(2,1)}, bf16[256,2048]{1,0:T(8,128)(2,1)}, u32[]{:S(2)}, u32[]{:S(2)}) collective-permute-start(bf16[256,2048]{1,0:T(8,128)(2,1)} %add_convert_fusion.2), channel_id=1, source_target_pairs={{0,1},{1,2},{2,3},{3,0},{4,5},{5,6},{6,7},{7,4},{8,9},{9,10},{10,1... | collective-permute-start | bytes 3145736 | tf_op jit(solution)/shard_map/ppermute | solution.py:983
  470.8 26.2 %collective-permute-start.30 = (bf16[512,1024]{1,0:T(8,128)(2,1)}, bf16[512,1024]{1,0:T(8,128)(2,1)S(1)}, u32[]{:S(2)}, u32[]{:S(2)}) collective-permute-start(bf16[512,1024]{1,0:T(8,128)(2,1)} %get-tuple-element.435), channel_id=1, source_target_pairs={{0,8},{4,12},{8,0},{12,4},{16,24},{20,28},{24,16},{28,20},{1,9},{5... | collective-permute-start | bytes 3145736 | tf_op jit(solution)/shard_map/ppermute | solution.py:937
  472.3 26.3 %collective-permute-start.31 = (bf16[512,1024]{1,0:T(8,128)(2,1)}, bf16[512,1024]{1,0:T(8,128)(2,1)}, u32[]{:S(2)}, u32[]{:S(2)}) collective-permute-start(bf16[512,1024]{1,0:T(8,128)(2,1)} %get-tuple-element.436), channel_id=1, source_target_pairs={{0,16},{4,20},{8,24},{12,28},{16,0},{20,4},{24,8},{28,12},{1,17},{... | collective-permute-start | bytes 3145736 | tf_op jit(solution)/shard_map/ppermute | solution.py:937
  491.1 38.5 %collective-permute-start.34 = (bf16[512,1408]{1,0:T(8,128)(2,1)}, bf16[512,1408]{1,0:T(8,128)(2,1)}, u32[]{:S(2)}, u32[]{:S(2)}) collective-permute-start(bf16[512,1408]{1,0:T(8,128)(2,1)} %get-tuple-element.416), channel_id=1, source_target_pairs={{0,16},{4,20},{8,24},{12,28},{16,0},{20,4},{24,8},{28,12},{1,17},{... | collective-permute-start | bytes 4325384 | tf_op jit(solution)/shard_map/ppermute | solution.py:937
  492.4 37.2 %collective-permute-start.35 = (bf16[512,1408]{1,0:T(8,128)(2,1)}, bf16[512,1408]{1,0:T(8,128)(2,1)}, u32[]{:S(2)}, u32[]{:S(2)}) collective-permute-start(bf16[512,1408]{1,0:T(8,128)(2,1)} %get-tuple-element.418), channel_id=1, source_target_pairs={{0,8},{4,12},{8,0},{12,4},{16,24},{20,28},{24,16},{28,20},{1,9},{5... | collective-permute-start | bytes 4325384 | tf_op jit(solution)/shard_map/ppermute | solution.py:937
  501.3 28.3 %collective-permute-start.33 = (bf16[256,2048]{1,0:T(8,128)(2,1)}, bf16[256,2048]{1,0:T(8,128)(2,1)}, u32[]{:S(2)}, u32[]{:S(2)}) collective-permute-start(bf16[256,2048]{1,0:T(8,128)(2,1)} %add_convert_fusion.1), channel_id=1, source_target_pairs={{0,1},{1,2},{2,3},{3,0},{4,5},{5,6},{6,7},{7,4},{8,9},{9,10},{10,1... | collective-permute-start | bytes 3145736 | tf_op jit(solution)/shard_map/ppermute | solution.py:983
  510.5 41.7 %collective-permute-start.32 = (bf16[256,2048]{1,0:T(8,128)(2,1)}, bf16[256,2048]{1,0:T(8,128)(2,1)}, u32[]{:S(2)}, u32[]{:S(2)}) collective-permute-start(bf16[256,2048]{1,0:T(8,128)(2,1)} %add_convert_fusion.3), channel_id=1, source_target_pairs={{0,1},{1,2},{2,3},{3,0},{4,5},{5,6},{6,7},{7,4},{8,9},{9,10},{10,1... | collective-permute-start | bytes 3145736 | tf_op jit(solution)/shard_map/ppermute | solution.py:983
  536.9 33.8 %collective-permute-start.39 = (bf16[256,512]{1,0:T(8,128)(2,1)S(1)}, bf16[256,512]{1,0:T(8,128)(2,1)S(1)}, u32[]{:S(2)}, u32[]{:S(2)}) collective-permute-start(bf16[256,512]{1,0:T(8,128)(2,1)S(1)} %split.17), channel_id=1, source_target_pairs={{0,1},{1,2},{2,3},{3,0},{4,5},{5,6},{6,7},{7,4},{8,9},{9,10},{10,1... | collective-permute-start | bytes 786440 | tf_op jit(solution)/shard_map/ppermute | solution.py:998
  538.4 33.2 %collective-permute-start.40 = (bf16[256,512]{1,0:T(8,128)(2,1)S(1)}, bf16[256,512]{1,0:T(8,128)(2,1)S(1)}, u32[]{:S(2)}, u32[]{:S(2)}) collective-permute-start(bf16[256,512]{1,0:T(8,128)(2,1)S(1)} %get-tuple-element.476), channel_id=1, source_target_pairs={{0,2},{1,3},{2,0},{3,1},{4,6},{5,7},{6,4},{7,5},{8,10},{9,11},{10,... | collective-permute-start | bytes 786440 | tf_op jit(solution)/shard_map/ppermute | solution.py:998
  (73 other events, 1024.8 us)
Sparse Core Ops, SparseCore 0:
  10.5 37.2 all-gather.3
  49.6 125.3 all-gather.5
  176.9 54.3 all-gather.7
  343.5 54.2 reduce-scatter.1

commit v11 on v10

--- a/solution.py
+++ b/solution.py
@@ -721,6 +721,7 @@
         x = refs[place][...]
         if parts > 1:
             x = jnp.concatenate([ref[...] for ref in refs[place : place + parts]], axis=0)
+        x = x.T
         for y_ref in refs[place + parts : place + parts + widths]:
             width = y_ref.shape[1]
             cuts = set(range(0, width, 1024)) | {width}
@@ -728,7 +729,7 @@
                 cuts.add(split - column)
             cuts = sorted(cuts)
             for first, last in zip(cuts[:-1], cuts[1:]):
-                total = dot_tn(x, y_ref[:, first:last])
+                total = dot_nn(x, y_ref[:, first:last])
                 start, end = column + first, column + last
                 if received is None:
                     refs[-1][:, start:end] = total.astype(jnp.bfloat16)

time: 593 us -> 593 us (level)
  no operation moved by 1% of the time
where the time goes in v11:
time: 593 us; the launch traced here: 584 us
  Pallas kernels  294 us (50%)
  waiting for transfers between devices  143 us (24%)
  starting transfers between devices  72.3 us (12%)
  other arithmetic  40.2 us (7%)
  local copies, waits for them, and re-layouts  19.2 us (3%)
  between operations  14.9 us (3%)
    ppermute x18, waiting for transfers between devices, hop(): lax.ppermute(value, 'tensor', [(i, (i + shift) % self.ring) for i in rang...  123 us
    pallas_call x8, Pallas kernels, weight_product(): pl.pallas_call(functools.partial(weight_kernel, [(len(xs), len(ys)) for x...  79.9 us
    pallas_call x2, Pallas kernels, down_chunk(): pl.pallas_call(functools.partial(down_kernel, len(es), tiles), grid=(tile...  44.7 us
    ppermute x18, starting transfers between devices, hop(): lax.ppermute(value, 'tensor', [(i, (i + shift) % self.ring) for i in rang...  38.4 us
    pallas_call x2, Pallas kernels, attention_backward(): pl.pallas_call(functools.partial(backward_kernel, count), grid_spec=spec,...  34 us
    pallas_call x2, Pallas kernels, up_chunk(): pl.pallas_call(up_kernel, grid=(tiles,), in_specs=specs, out_specs=[pl.Bl...  27.7 us
    pallas_call x3, Pallas kernels, transposed_product(): pl.pallas_call(functools.partial(transposed_kernel, len(xs), parts), grid...  25.1 us
    pallas_call x4, Pallas kernels, project(): pl.pallas_call(project_kernel, grid=(groups,), in_specs=specs, out_specs=...  18.9 us
  transfers between devices with their start and end apart: 48, of which 18 were waited for; matrix products, arithmetic and copies ran while one was open for 9% of the time, Pallas kernels for 50%

profile of v11, /device:TPU:0, one launch (start us, length us, event | category | flops | bytes accessed | tf_op | source)
XLA Modules:
  0.0 583.6 jit_solution(12870384309454304192)
XLA Ops:
  54.5 12.1 %collective-permute-done.x_ref.refs_5_ = bf16[256,2048]{1,0:T(8,128)(2,1)S(1)} collective-permute-done((bf16[256,2048]{1,0:T(8,128)(2,1)S(1)}, bf16[256,2048]{1,0:T(8,128)(2,1)S(1)}, u32[]{:S(2)}, u32[]{:S(2)}) %collective-permute-start) | collective-permute-done | bytes 1048608 | tf_op jit(solution)/shard_map/ppermute | solution.py:984
  73.9 17.9 %collective-permute-done.4.x_ref.refs_6_ = bf16[256,2048]{1,0:T(8,128)(2,1)S(1)} collective-permute-done((bf16[256,2048]{1,0:T(8,128)(2,1)S(1)}, bf16[256,2048]{1,0:T(8,128)(2,1)S(1)}, u32[]{:S(2)}, u32[]{:S(2)}) %collective-permute-start.4) | collective-permute-done | bytes 1048608 | tf_op jit(solution)/shard_map/ppermute | solution.py:984
  98.4 17.9 %collective-permute-done.5.x_ref.refs_7_ = bf16[256,2048]{1,0:T(8,128)(2,1)} collective-permute-done((bf16[256,2048]{1,0:T(8,128)(2,1)S(1)}, bf16[256,2048]{1,0:T(8,128)(2,1)}, u32[]{:S(2)}, u32[]{:S(2)}) %collective-permute-start.5) | collective-permute-done | bytes 1048608 | tf_op jit(solution)/shard_map/ppermute | solution.py:984
  122.9 17.7 %attend.1 = (bf16[1024,512]{1,0:T(8,128)(2,1)}, f32[16,4096]{1,0:T(8,128)}) custom-call(s32[1]{0:T(128)} %bitcast.10.place_ref, bf16[1024,768]{1,0:T(8,128)(2,1)} %get-tuple-element.270.own_ref.all_ref.refs_0_.refs_1_, bf16[1024,768]{1,0:T(8,128)(2,1)} %get-tuple-element.270.own_ref.all_ref.refs_0_.refs_1_, s32[1,1024]{1,0:T(1,128)} %bitcast.52, ...), custom_call_target="tpu_custom_call" | custom-call | flops 1 | bytes 1 | tf_op jit(solution)/shard_map/attend/pallas_call | solution.py:256
  144.5 19.6 %collective-permute-done.7.refs_1_ = bf16[1024,512]{1,0:T(8,128)(2,1)S(1)} collective-permute-done((bf16[1024,512]{1,0:T(8,128)(2,1)}, bf16[1024,512]{1,0:T(8,128)(2,1)S(1)}, u32[]{:S(2)}, u32[]{:S(2)}) %collective-permute-start.7) | collective-permute-done | bytes 1048608 | tf_op jit(solution)/shard_map/ppermute | solution.py:984
  168.1 18.7 %collective-permute-done.8.refs_2_ = bf16[1024,512]{1,0:T(8,128)(2,1)} collective-permute-done((bf16[1024,512]{1,0:T(8,128)(2,1)S(1)}, bf16[1024,512]{1,0:T(8,128)(2,1)}, u32[]{:S(2)}, u32[]{:S(2)}) %collective-permute-start.8) | collective-permute-done | bytes 1048608 | tf_op jit(solution)/shard_map/ppermute | solution.py:984
  191.2 14.4 %heads_product.1 = (f32[1024,2048]{1,0:T(8,128)}, bf16[256,1536]{1,0:T(8,128)(2,1)}) custom-call(bf16[1024,512]{1,0:T(8,128)(2,1)} %get-tuple-element.274.refs_0_.refs_2_, bf16[1024,512]{1,0:T(8,128)(2,1)} %copy-done.38, bf16[1024,512]{1,0:T(8,128)(2,1)} %collective-permute-done.8.refs_2_, ...), custom_call_target="tpu_custom_call" | custom-call | flops 1 | bytes 1 | tf_op jit(solution)/shard_map/heads_product/pallas_call | solution.py:512
  213.6 9.4 %after_attention.1 = (f32[256,2048]{1,0:T(8,128)}, bf16[1024,2048]{1,0:T(8,128)(2,1)}, bf16[256,512]{1,0:T(8,128)(2,1)}) custom-call(f32[1024,2048]{1,0:T(8,128)} %get-tuple-element.284.partial_ref, bf16[1024,512]{1,0:T(8,128)(2,1)} %copy-done.39, bf16[2048,6144]{1,0:T(8,128)(2,1)} %all-gather.6.cloned.1.call-done.refs_3_.weight_ref.gate_ref.up_ref.refs_5_.refs_6_, ...), custom_call_target="tpu_custom_call" | custom-call | flops 1 | bytes 1 | tf_op jit(solution)/shard_map/after_attention/pallas_call | solution.py:554
  223.0 13.9 %up_chunk.2 = (bf16[1024,2048]{1,0:T(8,128)(2,1)}, bf16[1024,2048]{1,0:T(8,128)(2,1)}, bf16[1024,2048]{1,0:T(8,128)(2,1)}) custom-call(bf16[1024,2048]{1,0:T(8,128)(2,1)} %get-tuple-element.413.x_ref.refs_0_, bf16[2048,6144]{1,0:T(8,128)(2,1)} %all-gather.6.cloned.1.call-done.refs_3_.weight_ref.gate_ref.up_ref.refs_5_.refs_6_, ...), custom_call_target="tpu_custom_call" | custom-call | flops 1 | bytes 1 | tf_op jit(solution)/shard_map/up_chunk/pallas_call | solution.py:606
  237.9 22.3 %down_chunk.2 = (bf16[1024,2048]{1,0:T(8,128)(2,1)}, bf16[1024,2048]{1,0:T(8,128)(2,1)}, bf16[256,2048]{1,0:T(8,128)(2,1)}, bf16[256,2048]{1,0:T(8,128)(2,1)}) custom-call(bf16[256,2048]{1,0:T(8,128)(2,1)} %copy-done.5, bf16[256,2048]{1,0:T(8,128)(2,1)} %copy-done.6, bf16[2048,2048]{1,0:T(8,128)(2,1)} %all-gather.8.cloned.1.call-done.refs_2_.refs_1_, ...), custom_call_target="tpu_custom_call" | custom-call | flops 1 | bytes 1 | tf_op jit(solution)/shard_map/down_chunk/pallas_call | solution.py:691
  263.6 13.8 %up_chunk.3 = (bf16[1024,2048]{1,0:T(8,128)(2,1)}, bf16[1024,2048]{1,0:T(8,128)(2,1)}, bf16[1024,2048]{1,0:T(8,128)(2,1)}) custom-call(bf16[1024,2048]{1,0:T(8,128)(2,1)} %get-tuple-element.413.x_ref.refs_0_, ...), custom_call_target="tpu_custom_call", output_to_operand_aliasing={{0}: (3, {}), {1}: (4, {}), {2}: (5, {})} | custom-call | flops 1 | bytes 1 | tf_op jit(solution)/shard_map/up_chunk/pallas_call | solution.py:606
  277.4 9.0 %weight_product.8 = bf16[1024,2048]{1,0:T(8,128)(2,1)} custom-call(s32[1]{0:T(128)} %bitcast.13.place_ref, bf16[256,2048]{1,0:T(8,128)(2,1)} %copy-done.5, bf16[256,2048]{1,0:T(8,128)(2,1)} %copy-done.6, bf16[256,2048]{1,0:T(8,128)(2,1)} %copy-done.7, bf16[256,2048]{1,0:T(8,128)(2,1)} %bitcast.39, bf16[1024,2048]{1,0:T(8,128)(2,1)} %get-tuple-element.398.refs_4_.refs_0_), custom_call_target="tpu_custom_call" | custom-call | flops 1 | bytes 1 | tf_op jit(solution)/shard_map/weight_product/pallas_call | solution.py:800
  288.3 22.4 %down_chunk.3 = (bf16[1024,2048]{1,0:T(8,128)(2,1)}, bf16[1024,2048]{1,0:T(8,128)(2,1)}, bf16[256,2048]{1,0:T(8,128)(2,1)}, bf16[256,2048]{1,0:T(8,128)(2,1)}) custom-call(bf16[256,2048]{1,0:T(8,128)(2,1)} %copy-done.7, bf16[256,2048]{1,0:T(8,128)(2,1)} %bitcast.40, ...), custom_call_target="tpu_custom_call", output_to_operand_aliasing={{0}: (7, {}), {1}: (8, {})} | custom-call | flops 1 | bytes 1 | tf_op jit(solution)/shard_map/down_chunk/pallas_call | solution.py:691
  316.1 8.7 %weight_product.9 = bf16[1024,2048]{1,0:T(8,128)(2,1)} custom-call(s32[1]{0:T(128)} %bitcast.13.place_ref, bf16[1024,2048]{1,0:T(8,128)(2,1)} %get-tuple-element.413.x_ref.refs_0_, bf16[1024,2048]{1,0:T(8,128)(2,1)} %get-tuple-element.328.refs_1_), custom_call_target="tpu_custom_call" | custom-call | flops 1 | bytes 1 | tf_op jit(solution)/shard_map/weight_product/pallas_call | solution.py:800
  333.5 9.7 %weight_product.10 = bf16[1024,2048]{1,0:T(8,128)(2,1)} custom-call(s32[1]{0:T(128)} %bitcast.13.place_ref, bf16[256,2048]{1,0:T(8,128)(2,1)} %copy-done.5, bf16[256,2048]{1,0:T(8,128)(2,1)} %copy-done.6, bf16[256,2048]{1,0:T(8,128)(2,1)} %copy-done.7, bf16[256,2048]{1,0:T(8,128)(2,1)} %bitcast.41, bf16[1024,2048]{1,0:T(8,128)(2,1)} %get-tuple-element.398.refs_4_.refs_0_, ...), custom_call_target="tpu_custom_call" | custom-call | flops 1 | bytes 1 | tf_op jit(solution)/shard_map/weight_product/pallas_call | solution.py:800
  344.2 10.9 %residual_gradient.1 = (f32[256,2048]{1,0:T(8,128)}, bf16[256,2048]{1,0:T(8,128)(2,1)}, bf16[256,512]{1,0:T(8,128)(2,1)}, bf16[256,512]{1,0:T(8,128)(2,1)}, bf16...) custom-call(bf16[256,2048]{1,0:T(8,128)(2,1)} %bitcast.42, f32[256,2048]{1,0:T(8,128)} %get-tuple-element.288.hidden_ref, ...), custom_call_target="tpu_custom_call" | custom-call | flops 1 | bytes 1 | tf_op jit(solution)/shard_map/residual_gradient/pallas_call | solution.py:887
  364.6 11.0 %weight_product.12 = (bf16[512,1024]{1,0:T(8,128)(2,1)}, bf16[512,1024]{1,0:T(8,128)(2,1)}, bf16[512,1024]{1,0:T(8,128)(2,1)}, bf16[512,1024]{1,0:T(8,128)(2,1)}) custom-call(s32[1]{0:T(128)} %bitcast.13.place_ref, bf16[1024,2048]{1,0:T(8,128)(2,1)} %get-tuple-element.413.x_ref.refs_0_, bf16[1024,2048]{1,0:T(8,128)(2,1)} %get-tuple-element.328.refs_1_, ...), custom_call_target="tpu_custom_call" | custom-call | flops 1 | bytes 1 | tf_op jit(solution)/shard_map/weight_product/pallas_call | solution.py:800
  382.8 17.0 %attend_back.2.refs_0_.refs_3_ = bf16[1024,384]{1,0:T(8,128)(2,1)} custom-call(s32[1]{0:T(128)} %bitcast.10.place_ref, bf16[1024,768]{1,0:T(8,128)(2,1)} %get-tuple-element.270.own_ref.all_ref.refs_0_.refs_1_, bf16[1024,768]{1,0:T(8,128)(2,1)} %get-tuple-element.270.own_ref.all_ref.refs_0_.refs_1_, bf16[1024,512]{1,0:T(8,128)(2,1)} %get-tuple-element.274.refs_0_.refs_2_, ...), custom_call_target="tpu_custom_call" | custom-call | flops 1 | bytes 1 | tf_op jit(solution)/shard_map/attend_back/pallas_call | solution.py:364
  413.4 17.0 %attend_back.3.refs_1_.refs_4_ = bf16[1024,384]{1,0:T(8,128)(2,1)} custom-call(s32[1]{0:T(128)} %bitcast.10.place_ref, bf16[1024,768]{1,0:T(8,128)(2,1)} %get-tuple-element.270.own_ref.all_ref.refs_0_.refs_1_, bf16[1024,768]{1,0:T(8,128)(2,1)} %get-tuple-element.270.own_ref.all_ref.refs_0_.refs_1_, bf16[1024,512]{1,0:T(8,128)(2,1)} %get-tuple-element.274.refs_0_.refs_2_, ...), custom_call_target="tpu_custom_call" | custom-call | flops 1 | bytes 1 | tf_op jit(solution)/shard_map/attend_back/pallas_call | solution.py:364
  439.1 12.1 %weight_product.14 = bf16[1024,2816]{1,0:T(8,128)(2,1)} custom-call(s32[1]{0:T(128)} %bitcast.13.place_ref, bf16[1024,2048]{1,0:T(8,128)(2,1)} %get-tuple-element.413.x_ref.refs_0_, bf16[1024,2048]{1,0:T(8,128)(2,1)} %get-tuple-element.394.refs_1_, bf16[1024,2048]{1,0:T(8,128)(2,1)} %get-tuple-element.395.refs_2_, ...), custom_call_target="tpu_custom_call" | custom-call | flops 1 | bytes 1 | tf_op jit(solution)/shard_map/weight_product/pallas_call | solution.py:800
  451.2 8.7 %transposed.5 = (bf16[256,2048]{1,0:T(8,128)(2,1)}, bf16[256,2048]{1,0:T(8,128)(2,1)}) custom-call(bf16[1024,2048]{1,0:T(8,128)(2,1)} %get-tuple-element.398.refs_4_.refs_0_, bf16[2048,2048]{1,0:T(8,128)(2,1)} %all-gather.8.cloned.1.call-done.refs_2_.refs_1_), custom_call_target="tpu_custom_call" | custom-call | flops 1 | bytes 1 | tf_op jit(solution)/shard_map/transposed/pallas_call | solution.py:465
  474.5 16.7 %weight_product.15 = (bf16[512,1408]{1,0:T(8,128)(2,1)}, bf16[512,1408]{1,0:T(8,128)(2,1)}, bf16[512,1408]{1,0:T(8,128)(2,1)}, bf16[512,1408]{1,0:T(8,128)(2,1)}) custom-call(s32[1]{0:T(128)} %bitcast.13.place_ref, bf16[1024,2048]{1,0:T(8,128)(2,1)} %get-tuple-element.413.x_ref.refs_0_, bf16[1024,2048]{1,0:T(8,128)(2,1)} %get-tuple-element.394.refs_1_, ...), custom_call_target="tpu_custom_call" | custom-call | flops 1 | bytes 1 | tf_op jit(solution)/shard_map/weight_product/pallas_call | solution.py:800
  515.0 14.6 %collective-permute-done.33 = bf16[256,2048]{1,0:T(8,128)(2,1)} collective-permute-done((bf16[256,2048]{1,0:T(8,128)(2,1)}, bf16[256,2048]{1,0:T(8,128)(2,1)}, u32[]{:S(2)}, u32[]{:S(2)}) %collective-permute-start.33) | collective-permute-done | bytes 1048608 | tf_op jit(solution)/shard_map/ppermute | solution.py:984
  543.4 8.8 %collective-permute-done.32 = bf16[256,2048]{1,0:T(8,128)(2,1)} collective-permute-done((bf16[256,2048]{1,0:T(8,128)(2,1)}, bf16[256,2048]{1,0:T(8,128)(2,1)}, u32[]{:S(2)}, u32[]{:S(2)}) %collective-permute-start.32) | collective-permute-done | bytes 1048608 | tf_op jit(solution)/shard_map/ppermute | solution.py:984
  (270 shorter events, 224.2 us)
Async XLA Ops:
  7.2 40.5 %all-gather.4.cloned.1.call-start = ((), (), s32[]{:S(2)}) async-start(), calls=%async_computation.1 | async-start | bytes 4128768 | tf_op jit(solution)/shard_map/all_gather | solution.py:941
  9.5 181.7 %all-gather.6.cloned.1.call-start = ((), (), s32[]{:S(2)}) async-start(), calls=%async_computation.2 | async-start | bytes 28311552 | tf_op jit(solution)/shard_map/all_gather | solution.py:941
  36.3 200.8 %all-gather.8.cloned.1.call-start = ((), (), s32[]{:S(2)}) async-start(), calls=%async_computation.3 | async-start | bytes 9437184 | tf_op jit(solution)/shard_map/all_gather | solution.py:941
  37.0 370.4 %reduce-scatter.2.cloned.1.call-start = ((), (), s32[]{:S(2)}) async-start(), calls=%async_computation.4 | async-start | bytes 5242880 | tf_op jit(solution)/shard_map/reduce_scatter | solution.py:979
  37.5 29.1 %collective-permute-start = (bf16[256,2048]{1,0:T(8,128)(2,1)S(1)}, bf16[256,2048]{1,0:T(8,128)(2,1)S(1)}, u32[]{:S(2)}, u32[]{:S(2)}) collective-permute-start(bf16[256,2048]{1,0:T(8,128)(2,1)S(1)} %bitcast.38), channel_id=1, source_target_pairs={{0,1},{1,2},{2,3},{3,0},{4,5},{5,6},{6,7},{7,4},{8,9},{9,10},{10,1... | collective-permute-start | bytes 3145736 | tf_op jit(solution)/shard_map/ppermute | solution.py:984
  260.2 26.2 %collective-permute-start.12 = (bf16[256,2048]{1,0:T(8,128)(2,1)}, bf16[256,2048]{1,0:T(8,128)(2,1)S(1)}, u32[]{:S(2)}, u32[]{:S(2)}) collective-permute-start(bf16[256,2048]{1,0:T(8,128)(2,1)} %get-tuple-element.304), channel_id=1, source_target_pairs={{0,1},{1,2},{2,3},{3,0},{4,5},{5,6},{6,7},{7,4},{8,9},{9,10},{10,1... | collective-permute-start | bytes 3145736 | tf_op jit(solution)/shard_map/ppermute | solution.py:984
  286.5 47.1 %collective-permute-start.15 = (bf16[1024,2048]{1,0:T(8,128)(2,1)}, bf16[1024,2048]{1,0:T(8,128)(2,1)}, u32[]{:S(2)}, u32[]{:S(2)}) collective-permute-start(bf16[1024,2048]{1,0:T(8,128)(2,1)} %weight_product.8), channel_id=1, source_target_pairs={{0,4},{4,0},{8,12},{12,8},{16,20},{20,16},{24,28},{28,24},{1,5},{5... | collective-permute-start | bytes 12582920 | tf_op jit(solution)/shard_map/ppermute | solution.py:938
  286.9 27.6 %collective-permute-start.13 = (bf16[256,2048]{1,0:T(8,128)(2,1)S(1)}, bf16[256,2048]{1,0:T(8,128)(2,1)S(1)}, u32[]{:S(2)}, u32[]{:S(2)}) collective-permute-start(bf16[256,2048]{1,0:T(8,128)(2,1)S(1)} %add_convert_fusion.6), channel_id=1, source_target_pairs={{0,1},{1,2},{2,3},{3,0},{4,5},{5,6},{6,7},{7,4},{8,9},{9,10},{10,1... | collective-permute-start | bytes 3145736 | tf_op jit(solution)/shard_map/ppermute | solution.py:984
  316.1 27.2 %collective-permute-start.14 = (bf16[256,2048]{1,0:T(8,128)(2,1)S(1)}, bf16[256,2048]{1,0:T(8,128)(2,1)S(1)}, u32[]{:S(2)}, u32[]{:S(2)}) collective-permute-start(bf16[256,2048]{1,0:T(8,128)(2,1)S(1)} %add_convert_fusion.5), channel_id=1, source_target_pairs={{0,1},{1,2},{2,3},{3,0},{4,5},{5,6},{6,7},{7,4},{8,9},{9,10},{10,1... | collective-permute-start | bytes 3145736 | tf_op jit(solution)/shard_map/ppermute | solution.py:984
  376.6 30.8 %collective-permute-start.16 = (bf16[256,2048]{1,0:T(8,128)(2,1)}, bf16[256,2048]{1,0:T(8,128)(2,1)S(1)}, u32[]{:S(2)}, u32[]{:S(2)}) collective-permute-start(bf16[256,2048]{1,0:T(8,128)(2,1)} %get-tuple-element.337), channel_id=1, source_target_pairs={{0,1},{1,2},{2,3},{3,0},{4,5},{5,6},{6,7},{7,4},{8,9},{9,10},{10,1... | collective-permute-start | bytes 3145736 | tf_op jit(solution)/shard_map/ppermute | solution.py:984
  408.8 30.0 %collective-permute-start.22 = (bf16[256,2048]{1,0:T(8,128)(2,1)}, bf16[256,2048]{1,0:T(8,128)(2,1)}, u32[]{:S(2)}, u32[]{:S(2)}) collective-permute-start(bf16[256,2048]{1,0:T(8,128)(2,1)} %add_convert_fusion.4), channel_id=1, source_target_pairs={{0,1},{1,2},{2,3},{3,0},{4,5},{5,6},{6,7},{7,4},{8,9},{9,10},{10,1... | collective-permute-start | bytes 3145736 | tf_op jit(solution)/shard_map/ppermute | solution.py:984
  409.9 28.8 %collective-permute-start.23 = (bf16[512,1024]{1,0:T(8,128)(2,1)}, bf16[512,1024]{1,0:T(8,128)(2,1)S(1)}, u32[]{:S(2)}, u32[]{:S(2)}) collective-permute-start(bf16[512,1024]{1,0:T(8,128)(2,1)} %get-tuple-element.388), channel_id=1, source_target_pairs={{0,16},{4,20},{8,24},{12,28},{16,0},{20,4},{24,8},{28,12},{1,17},{... | collective-permute-start | bytes 3145736 | tf_op jit(solution)/shard_map/ppermute | solution.py:938
  411.5 27.2 %collective-permute-start.24 = (bf16[512,1024]{1,0:T(8,128)(2,1)}, bf16[512,1024]{1,0:T(8,128)(2,1)}, u32[]{:S(2)}, u32[]{:S(2)}) collective-permute-start(bf16[512,1024]{1,0:T(8,128)(2,1)} %get-tuple-element.390), channel_id=1, source_target_pairs={{0,8},{4,12},{8,0},{12,4},{16,24},{20,28},{24,16},{28,20},{1,9},{5... | collective-permute-start | bytes 3145736 | tf_op jit(solution)/shard_map/ppermute | solution.py:938
  412.9 50.0 %collective-permute-start.26 = (bf16[512,1024]{1,0:T(8,128)(2,1)}, bf16[512,1024]{1,0:T(8,128)(2,1)S(1)}, u32[]{:S(2)}, u32[]{:S(2)}) collective-permute-start(bf16[512,1024]{1,0:T(8,128)(2,1)} %get-tuple-element.406), channel_id=1, source_target_pairs={{0,16},{4,20},{8,24},{12,28},{16,0},{20,4},{24,8},{28,12},{1,17},{... | collective-permute-start | bytes 3145736 | tf_op jit(solution)/shard_map/ppermute | solution.py:938
  430.4 32.5 %collective-permute-start.27 = (bf16[512,1024]{1,0:T(8,128)(2,1)}, bf16[512,1024]{1,0:T(8,128)(2,1)S(1)}, u32[]{:S(2)}, u32[]{:S(2)}) collective-permute-start(bf16[512,1024]{1,0:T(8,128)(2,1)} %get-tuple-element.408), channel_id=1, source_target_pairs={{0,8},{4,12},{8,0},{12,4},{16,24},{20,28},{24,16},{28,20},{1,9},{5... | collective-permute-start | bytes 3145736 | tf_op jit(solution)/shard_map/ppermute | solution.py:938
  467.0 27.9 %collective-permute-start.28 = (bf16[256,2048]{1,0:T(8,128)(2,1)}, bf16[256,2048]{1,0:T(8,128)(2,1)}, u32[]{:S(2)}, u32[]{:S(2)}) collective-permute-start(bf16[256,2048]{1,0:T(8,128)(2,1)} %add_convert_fusion.2), channel_id=1, source_target_pairs={{0,1},{1,2},{2,3},{3,0},{4,5},{5,6},{6,7},{7,4},{8,9},{9,10},{10,1... | collective-permute-start | bytes 3145736 | tf_op jit(solution)/shard_map/ppermute | solution.py:984
  470.8 26.2 %collective-permute-start.30 = (bf16[512,1024]{1,0:T(8,128)(2,1)}, bf16[512,1024]{1,0:T(8,128)(2,1)S(1)}, u32[]{:S(2)}, u32[]{:S(2)}) collective-permute-start(bf16[512,1024]{1,0:T(8,128)(2,1)} %get-tuple-element.435), channel_id=1, source_target_pairs={{0,8},{4,12},{8,0},{12,4},{16,24},{20,28},{24,16},{28,20},{1,9},{5... | collective-permute-start | bytes 3145736 | tf_op jit(solution)/shard_map/ppermute | solution.py:938
  472.3 26.3 %collective-permute-start.31 = (bf16[512,1024]{1,0:T(8,128)(2,1)}, bf16[512,1024]{1,0:T(8,128)(2,1)}, u32[]{:S(2)}, u32[]{:S(2)}) collective-permute-start(bf16[512,1024]{1,0:T(8,128)(2,1)} %get-tuple-element.436), channel_id=1, source_target_pairs={{0,16},{4,20},{8,24},{12,28},{16,0},{20,4},{24,8},{28,12},{1,17},{... | collective-permute-start | bytes 3145736 | tf_op jit(solution)/shard_map/ppermute | solution.py:938
  491.1 38.5 %collective-permute-start.34 = (bf16[512,1408]{1,0:T(8,128)(2,1)}, bf16[512,1408]{1,0:T(8,128)(2,1)}, u32[]{:S(2)}, u32[]{:S(2)}) collective-permute-start(bf16[512,1408]{1,0:T(8,128)(2,1)} %get-tuple-element.416), channel_id=1, source_target_pairs={{0,16},{4,20},{8,24},{12,28},{16,0},{20,4},{24,8},{28,12},{1,17},{... | collective-permute-start | bytes 4325384 | tf_op jit(solution)/shard_map/ppermute | solution.py:938
  492.4 37.2 %collective-permute-start.35 = (bf16[512,1408]{1,0:T(8,128)(2,1)}, bf16[512,1408]{1,0:T(8,128)(2,1)}, u32[]{:S(2)}, u32[]{:S(2)}) collective-permute-start(bf16[512,1408]{1,0:T(8,128)(2,1)} %get-tuple-element.418), channel_id=1, source_target_pairs={{0,8},{4,12},{8,0},{12,4},{16,24},{20,28},{24,16},{28,20},{1,9},{5... | collective-permute-start | bytes 4325384 | tf_op jit(solution)/shard_map/ppermute | solution.py:938
  501.3 28.3 %collective-permute-start.33 = (bf16[256,2048]{1,0:T(8,128)(2,1)}, bf16[256,2048]{1,0:T(8,128)(2,1)}, u32[]{:S(2)}, u32[]{:S(2)}) collective-permute-start(bf16[256,2048]{1,0:T(8,128)(2,1)} %add_convert_fusion.1), channel_id=1, source_target_pairs={{0,1},{1,2},{2,3},{3,0},{4,5},{5,6},{6,7},{7,4},{8,9},{9,10},{10,1... | collective-permute-start | bytes 3145736 | tf_op jit(solution)/shard_map/ppermute | solution.py:984
  510.5 41.7 %collective-permute-start.32 = (bf16[256,2048]{1,0:T(8,128)(2,1)}, bf16[256,2048]{1,0:T(8,128)(2,1)}, u32[]{:S(2)}, u32[]{:S(2)}) collective-permute-start(bf16[256,2048]{1,0:T(8,128)(2,1)} %add_convert_fusion.3), channel_id=1, source_target_pairs={{0,1},{1,2},{2,3},{3,0},{4,5},{5,6},{6,7},{7,4},{8,9},{9,10},{10,1... | collective-permute-start | bytes 3145736 | tf_op jit(solution)/shard_map/ppermute | solution.py:984
  536.9 33.8 %collective-permute-start.39 = (bf16[256,512]{1,0:T(8,128)(2,1)S(1)}, bf16[256,512]{1,0:T(8,128)(2,1)S(1)}, u32[]{:S(2)}, u32[]{:S(2)}) collective-permute-start(bf16[256,512]{1,0:T(8,128)(2,1)S(1)} %split.17), channel_id=1, source_target_pairs={{0,1},{1,2},{2,3},{3,0},{4,5},{5,6},{6,7},{7,4},{8,9},{9,10},{10,1... | collective-permute-start | bytes 786440 | tf_op jit(solution)/shard_map/ppermute | solution.py:999
  538.4 33.2 %collective-permute-start.40 = (bf16[256,512]{1,0:T(8,128)(2,1)S(1)}, bf16[256,512]{1,0:T(8,128)(2,1)S(1)}, u32[]{:S(2)}, u32[]{:S(2)}) collective-permute-start(bf16[256,512]{1,0:T(8,128)(2,1)S(1)} %get-tuple-element.476), channel_id=1, source_target_pairs={{0,2},{1,3},{2,0},{3,1},{4,6},{5,7},{6,4},{7,5},{8,10},{9,11},{10,... | collective-permute-start | bytes 786440 | tf_op jit(solution)/shard_map/ppermute | solution.py:999
  (73 other events, 1024.8 us)
Sparse Core Ops, SparseCore 0:
  10.5 37.2 all-gather.3
  49.6 125.3 all-gather.5
  176.9 54.3 all-gather.7
  343.5 54.2 reduce-scatter.1
